TPU v7x, 32 devices: a whole 2x2x4 slice. The times are simulated.
32 devices in a mesh: groups: 2 (over x), row: 16 (over z, y, core).
Axes of the slice: x: 2, y: 2, z: 4, core: 2. Of those that a mesh axis runs over, the one named last changes fastest.
Arguments:
- right_sides: float32 [16, 65536], P(None, ('groups', 'row')), parts along dimension 1, may hold values from -80 to 80
- nugget: float32 [65536], P(('groups', 'row')), parts along dimension 0, may hold values from 0.25 to 2
- left_factors: bfloat16 [1024, 16, 2048], P(('groups', 'row')), parts along dimension 0, may hold values from -0.125 to 0.125
- right_factors: bfloat16 [1024, 16, 2048], P(('groups', 'row')), parts along dimension 0, may hold values from -0.125 to 0.125
- tile_column: int32 [1024, 1], P(('groups', 'row')), parts along dimension 0, may hold values from 0 to 15; in each aligned block of 32 rows (0 to 31, 32 to 63, ...) at most 4 rows name the same one
- live_slots: int32 [32], P(('groups', 'row')), parts along dimension 0, may hold values from 16 to 32, as said below
Outputs:
- solution: float32 [16, 65536], P(None, ('groups', 'row')), parts along dimension 1
- residual: float32 [16, 65536], P(None, ('groups', 'row')), parts along dimension 1
There are 2 independent parts, one for each index of `groups`. A program takes and returns all parts, laid end to end along the dimension named above; each array names one. Nothing has to cross between parts.
Inputs may be any that keep to these rules, and one draw needn't show every extreme that they name: `tile_column`: among the 32 slots of one tile row at most 4 name the same tile column, a bound that some block reaches. `live_slots`: every tile row uses at least half of its 32 slots, and some tile row uses all of them.
All inputs are finite; a program needn't handle non-finite values.
Results may differ from a plain program's by a relative error of at most 0.0063.
Values may be sent and summed in bfloat16 or wider, within the bound.
No kernel may reach another device: no remote copies, remote signals or barrier semaphores. Data moves between devices by JAX's collectives and lax.ppermute only.
A program may use at most 64 MiB of HBM per device.

v0:
```python
import jax
import jax.numpy as jnp
from jax import lax
from jax.sharding import PartitionSpec as P

ITERS = 2


group_span = 8


def gram_solve(matrix, target):
    factor = jnp.linalg.cholesky(matrix)
    return jax.scipy.linalg.cho_solve((factor, True), target)


def pair_gram(former, latter):
    return jnp.dot(former, latter.T, precision=lax.Precision.HIGHEST)


def shards(right_sides, nugget, left_factors, right_factors, tile_column, live_slots):
    exact = lax.Precision.HIGHEST
    devices = lax.axis_size("row")
    slot_count = left_factors.shape[0]
    rhs_count = right_sides.shape[0]
    tile_width = left_factors.shape[2]
    columns = tile_column[:, 0]
    slot_index = jnp.arange(slot_count, dtype=jnp.int32)
    used_slots = live_slots[0]
    group_turns = (used_slots + group_span - 1) // group_span
    live_mask = (slot_index < used_slots).astype(jnp.float32)

    def group_projection(turn_index, direction_low, far_part):
        offset = turn_index * group_span
        left_block = lax.dynamic_slice_in_dim(left_factors, offset, group_span, 0)
        mask_block = lax.dynamic_slice_in_dim(live_mask, offset, group_span, 0)
        near_part = jnp.einsum(
            "krb,nb->krn", left_block, direction_low, preferred_element_type=jnp.float32
        )
        projection = ((near_part + far_part) * mask_block[:, None, None]).astype(jnp.bfloat16)
        own_term = jnp.einsum(
            "krb,krn->nb", left_block, projection, preferred_element_type=jnp.float32
        )
        return (offset, projection, own_term)

    solution = jnp.zeros_like(right_sides)
    residual = right_sides
    direction = right_sides
    res_gram = lax.psum(pair_gram(residual, residual), "row")
    for iteration in range(ITERS):
        direction_low = direction.astype(jnp.bfloat16)
        panels = lax.all_gather(direction_low, "row", axis=1, tiled=True).reshape(
            rhs_count, devices, tile_width
        )

        def one_group(turn_index, carry):
            own_rows, spread = carry
            offset = turn_index * group_span
            right_block = lax.dynamic_slice_in_dim(right_factors, offset, group_span, 0)
            column_block = lax.dynamic_slice_in_dim(columns, offset, group_span, 0)
            far_panels = jnp.take(panels, column_block, axis=1)
            far_part = jnp.einsum(
                "krb,nkb->krn", right_block, far_panels, preferred_element_type=jnp.float32
            )
            offset, projection, own_term = group_projection(turn_index, direction_low, far_part)
            moved = jnp.einsum(
                "krb,krn->nkb", right_block, projection, preferred_element_type=jnp.float32
            )
            return (own_rows + own_term, spread.at[:, column_block].add(moved))

        start = (
            jnp.zeros((rhs_count, tile_width), jnp.float32),
            jnp.zeros((rhs_count, devices, tile_width), jnp.float32),
        )
        own_rows, spread = lax.fori_loop(0, group_turns, one_group, start)
        summed = lax.psum_scatter(spread, "row", scatter_dimension=1, tiled=True)
        applied = nugget[None, :] * direction + (own_rows + summed.reshape(rhs_count, tile_width))
        curvature = lax.psum(pair_gram(direction, applied), "row")
        step_size = gram_solve(curvature, res_gram)
        solution = solution + jnp.dot(step_size.T, direction, precision=exact)
        residual = residual - jnp.dot(step_size.T, applied, precision=exact)
        if iteration + 1 < ITERS:
            next_gram = lax.psum(pair_gram(residual, residual), "row")
        if iteration + 1 < ITERS:
            update_mix = gram_solve(res_gram, next_gram)
            direction = residual + jnp.dot(update_mix.T, direction, precision=exact)
            res_gram = next_gram
    return (solution, residual)


def solution(mesh):
    return jax.shard_map(
        shards,
        mesh=mesh,
        in_specs=(
            P(None, ("groups", "row")),
            P(("groups", "row")),
            P(("groups", "row"), None, None),
            P(("groups", "row"), None, None),
            P(("groups", "row"), None),
            P(("groups", "row")),
        ),
        out_specs=(P(None, ("groups", "row")), P(None, ("groups", "row"))),
        check_vma=False,
    )
```

profile of v0, /device:TPU:0, one launch (start us, length us, event | category | flops | bytes accessed | tf_op | source)
XLA Modules:
  0.0 430.3 jit_solution(12311923803354846671)
XLA Ops:
  9.5 42.0 %all-gather.3.cloned.1.call-done = bf16[16,32768]{1,0:T(8,128)(2,1)} async-done(((bf16[16,2048]{1,0:T(8,128)(2,1)}), bf16[16,32768]{1,0:T(8,128)(2,1)}) %all-gather.3.cloned.1.call-update) | async-done | bytes 1048592 | tf_op jit(solution)/shard_map/all_gather | solution.py:52
  51.5 2.5 copy.51
  55.6 34.5 %while.24 = (s32[]{:T(128)}, f32[16,2048]{1,0:T(8,128)S(1)}, f32[16,16,2048]{2,0,1:T(8,128)}, s32[]{:T(128)}, bf16[32,16,2048]{2,1,0:T(8,128)(2,1)S(1)}, /*index...) while((s32[]{:T(128)}, f32[16,2048]{1,0:T(8,128)S(1)}, ...), condition=%wide.region_2.4_spmd, body=%wide.region_0.0_spmd.sunk | while | flops 34118708 | bytes 8253915 | solution.py:75
  55.7 1.8 gather_fusion
  60.7 3.4 scatter_fusion
  64.4 1.8 gather_fusion
  69.3 3.4 scatter_fusion
  78.0 3.3 scatter_fusion
  81.6 1.8 gather_fusion
  86.6 3.4 scatter_fusion
  91.3 59.3 %reduce-scatter.3.cloned.1.call-done = f32[16,1,2048]{2,0,1:T(8,128)} async-done(((f32[16,16,2048]{2,0,1:T(8,128)}), f32[16,1,2048]{2,0,1:T(8,128)}) %reduce-scatter.3.cloned.1.call-update) | async-done | bytes 131088 | tf_op jit(solution)/shard_map/reduce_scatter | solution.py:76
  151.7 57.7 %all-reduce = (f32[16,16]{0,1:T(8,128)S(1)}, f32[16,16]{0,1:T(8,128)S(1)}) all-reduce(f32[16,16]{0,1:T(8,128)S(1)} %fusion.66, f32[16,16]{0,1:T(8,128)S(1)} %convolution_bitcast_fusion.2), channel_id=1, replica_groups=mesh['groups'=2,'row'=16] {'row'}, use_global_device_ids=true, to_apply=%region_7.10 | all-reduce | flops 512 | bytes 4096 | tf_op jit(solution)/shard_map/psum | solution.py:49
  219.4 30.0 %psum.30 = f32[16,16]{1,0:T(8,128)S(1)} all-reduce(f32[16,16]{1,0:T(8,128)S(1)} %fusion.68), channel_id=1, replica_groups=mesh['groups'=2,'row'=16] {'row'}, use_global_device_ids=true, to_apply=%region_8.12 | all-reduce | flops 256 | bytes 2048 | tf_op jit(solution)/shard_map/psum | solution.py:83
  250.9 35.3 %all-gather.5.cloned.1.call-done = bf16[16,32768]{1,0:T(8,128)(2,1)} async-done(((bf16[16,2048]{1,0:T(8,128)(2,1)}), bf16[16,32768]{1,0:T(8,128)(2,1)}) %all-gather.5.cloned.1.call-update) | async-done | bytes 1048592 | tf_op jit(solution)/shard_map/all_gather | solution.py:52
  286.2 2.3 copy.50
  290.2 34.5 %while.25 = (s32[]{:T(128)}, f32[16,2048]{1,0:T(8,128)S(1)}, f32[16,16,2048]{2,0,1:T(8,128)}, s32[]{:T(128)}, bf16[32,16,2048]{2,1,0:T(8,128)(2,1)S(1)}, /*index...) while((s32[]{:T(128)}, f32[16,2048]{1,0:T(8,128)S(1)}, ...), condition=%wide.region_11.15_spmd, body=%wide.region_9.14_spmd.sunk | while | flops 34118708 | bytes 8253915 | solution.py:75
  290.3 1.8 gather_fusion.1
  295.2 3.4 scatter_fusion.1
  303.9 3.4 scatter_fusion.1
  312.6 3.3 scatter_fusion.1
  321.1 3.4 scatter_fusion.1
  325.1 60.1 %reduce-scatter.5.cloned.1.call-done = f32[16,1,2048]{2,0,1:T(8,128)} async-done(((f32[16,16,2048]{2,0,1:T(8,128)}), f32[16,1,2048]{2,0,1:T(8,128)}) %reduce-scatter.5.cloned.1.call-update) | async-done | bytes 131088 | tf_op jit(solution)/shard_map/reduce_scatter | solution.py:76
  386.4 30.0 %psum.31 = f32[16,16]{0,1:T(8,128)S(1)} all-reduce(f32[16,16]{0,1:T(8,128)S(1)} %fusion.45), channel_id=1, replica_groups=mesh['groups'=2,'row'=16] {'row'}, use_global_device_ids=true, to_apply=%region_13.17 | all-reduce | flops 256 | bytes 2048 | tf_op jit(solution)/shard_map/psum | solution.py:78
  421.8 1.9 convolution_subtract_fusion
  (126 shorter events, 60.1 us)
Async XLA Ops:
  7.2 44.3 %all-gather.3.cloned.1.call-start = ((), (), s32[]{:S(2)}) async-start(), calls=%async_computation.2 | async-start | bytes 1114112 | tf_op jit(solution)/shard_map/all_gather | solution.py:52
  8.8 141.8 %reduce-scatter.3.cloned.1.call-start = ((), (), s32[]{:S(2)}) async-start(), calls=%async_computation.3 | async-start | bytes 2228224 | tf_op jit(solution)/shard_map/reduce_scatter | solution.py:76
  51.5 4.1 copy-start
  51.5 4.1 copy-start.5
  51.5 4.1 copy-start.8
  90.1 0.9 copy-start.1
  90.1 60.4 %copy-start.7 = (f32[2048]{0:T(1024)S(1)}, f32[2048]{0:T(1024)}, u32[]{:S(2)}) copy-start(f32[2048]{0:T(1024)} %param.16) | copy-start | bytes 24580
  90.2 196.0 %all-gather.5.cloned.1.call-start = ((), (), s32[]{:S(2)}) async-start(), calls=%async_computation.4 | async-start | bytes 1114112 | tf_op jit(solution)/shard_map/all_gather | solution.py:52
  219.2 71.0 %copy-start.3 = (f32[16,2048]{1,0:T(8,128)}, f32[16,2048]{1,0:T(8,128)S(1)}, u32[]{:S(2)}) copy-start(f32[16,2048]{1,0:T(8,128)S(1)} %convolution_subtract_fusion.1) | copy-start | bytes 393220
  250.8 134.4 %reduce-scatter.5.cloned.1.call-start = ((), (), s32[]{:S(2)}) async-start(), calls=%async_computation.5 | async-start | bytes 2228224 | tf_op jit(solution)/shard_map/reduce_scatter | solution.py:76
  286.2 4.0 copy-start.6
  324.7 60.5 %copy-start.2 = (f32[16,2048]{1,0:T(8,128)S(1)}, f32[16,2048]{1,0:T(8,128)}, u32[]{:S(2)}) copy-start(f32[16,2048]{1,0:T(8,128)} %get-tuple-element.194) | copy-start | bytes 393220
  324.7 97.1 %copy-start.4 = (f32[16,2048]{1,0:T(8,128)S(1)}, f32[16,2048]{1,0:T(8,128)}, u32[]{:S(2)}) copy-start(f32[16,2048]{1,0:T(8,128)} %copy-done.3) | copy-start | bytes 393220
Sparse Core Ops, SparseCore 0:
  10.8 40.6 all-gather.2
  90.3 60.2 reduce-scatter.2
  251.0 35.1 all-gather.4
  324.9 60.2 reduce-scatter.4
where the time goes:
time: 432 us; the launch traced here: 430 us
  waiting for transfers between devices  197 us (46%)
  blocking collectives  118 us (27%)
  other arithmetic  41.1 us (10%)
  matrix products  35.3 us (8%)
  local copies, waits for them, and re-layouts  24.2 us (6%)
  between operations  14.6 us (3%)
    reduce_scatter x2, waiting for transfers between devices, shards(): summed = lax.psum_scatter(spread, 'row', scatter_dimension=1, tiled=True)  119 us
    all_gather x2, waiting for transfers between devices, shards(): lax.all_gather(direction_low, 'row', axis=1, tiled=True)  77.3 us
    psum x1, blocking collectives, shards(): res_gram = lax.psum(pair_gram(residual, residual), 'row')  57.7 us
    psum x1, blocking collectives, shards(): next_gram = lax.psum(pair_gram(residual, residual), 'row')  30 us
    psum x1, blocking collectives, shards(): curvature = lax.psum(pair_gram(direction, applied), 'row')  30 us
    scatter-add x8, other arithmetic, one_group(): return (own_rows + own_term, spread.at[:, column_block].add(moved))  26.8 us
    gather x8, local copies, waits for them, and re-layouts, one_group(): far_panels = jnp.take(panels, column_block, axis=1)  14.4 us
    dot_general x8, matrix products, one_group(): jnp.einsum('krb,nkb->krn', right_block, far_panels, preferred_element_typ...  11.1 us
  transfers between devices with their start and end apart: 4, of which 4 were waited for; matrix products, arithmetic and copies ran while one was open for 0% of the time, Pallas kernels for 0%

commit v1 on v0

v1 whole, which is shorter than its diff:
```python
import functools

import jax
import jax.numpy as jnp
from jax import lax
from jax.experimental import pallas as pl
from jax.experimental.pallas import tpu as pltpu
from jax.sharding import PartitionSpec as P

ITERS = 2
LANES = 128
F32 = jnp.float32
BF16 = jnp.bfloat16
EXACT = lax.Precision.HIGHEST
NN = (((1,), (0,)), ((), ()))
NT = (((1,), (1,)), ((), ()))


def lane_group(shape, rhs):
    return lax.broadcasted_iota(jnp.int32, shape, len(shape) - 1) // rhs


def encode(small, rhs):
    group = lane_group(small.shape, rhs)
    high = small.astype(BF16).astype(F32)
    rest = small - high
    middle = rest.astype(BF16).astype(F32)
    low = rest - middle
    picked = jnp.where(group == 0, high, jnp.where(group == 1, middle, jnp.where(group == 2, low, 0.0)))
    return picked.astype(BF16)


def fold(wide, rhs):
    shift = LANES // 2
    while shift >= rhs:
        wide = wide + pltpu.roll(wide, shift, 1)
        shift //= 2
    return wide


def repeat_rows(block, rhs):
    return jnp.concatenate([block] * (LANES // rhs), axis=0)


def right_divide(top, bottom, rhs):
    both = jnp.concatenate([top, bottom], axis=0)
    lane = lax.broadcasted_iota(jnp.int32, both.shape, 1) % rhs
    for k in range(rhs):
        row = both[k : k + 1, :]
        column = both[:, k : k + 1]
        scaled = column * (1.0 / both[k : k + 1, k : k + 1])
        both = jnp.where(lane == k, scaled, both - scaled * row)
    return both[rhs:, :]


def left_multiply(square, block, rhs):
    return lax.dot_general(square[:, :rhs], block, NN, precision=EXACT, preferred_element_type=F32)


def flat(ref, chunks):
    return jnp.concatenate([ref[c] for c in range(chunks)], axis=1)


def open_kernel(rhs, chunks, right_ref, message_ref):
    block = right_ref[...]
    for c in range(chunks):
        message_ref[c] = block[:, c * LANES : (c + 1) * LANES].astype(BF16)
    gram = lax.dot_general(block, repeat_rows(block, rhs), NT, precision=EXACT, preferred_element_type=F32)
    message_ref[chunks] = encode(gram, rhs)


def gathered_gram(held_ref, other_ref, chunks, rhs):
    half = held_ref.shape[0]
    total = held_ref[0, chunks].astype(F32)
    for i in range(1, half):
        total = total + held_ref[i, chunks].astype(F32)
    for i in range(half):
        total = total + other_ref[i, chunks].astype(F32)
    return fold(total, rhs)


def projections(held_ref, other_ref, left_ref, right_ref, slot_ref, panel_ref, rhs, chunks):
    half = held_ref.shape[0]
    for i in range(half):
        for c in range(chunks):
            at = slice(c * LANES, (c + 1) * LANES)
            panel_ref[i * rhs : (i + 1) * rhs, at] = held_ref[i, c]
            panel_ref[(half + i) * rhs : (half + i + 1) * rhs, at] = other_ref[i, c]
    far = lax.dot_general(right_ref[...], panel_ref[...], NT, preferred_element_type=F32)
    own = repeat_rows(panel_ref[:rhs, :], rhs)
    near = lax.dot_general(left_ref[...], own, NT, preferred_element_type=F32)
    slot = slot_ref[...]
    group = lane_group(slot.shape, rhs)
    total = jnp.zeros(slot.shape, F32)
    per = LANES // rhs
    for j in range(2 * half // per):
        total = total + jnp.where(slot == group + j * per, far[:, j * LANES : (j + 1) * LANES], 0.0)
    return near + fold(total, rhs)


def spread_out(projected, left_ref, right_ref, slot_ref, send_ref, keep_ref, own_ref, rhs, chunks):
    slot = slot_ref[...]
    group = lane_group(slot.shape, rhs)
    per = LANES // rhs
    panels = 2 * keep_ref.shape[0] // chunks
    turned = [
        jnp.where(slot == group + j * per, projected, 0.0).T.astype(BF16) for j in range(panels // per)
    ]
    turned = jnp.concatenate(turned, axis=0)
    own_turned = projected.T[:rhs].astype(BF16)
    own_ref[...] = lax.dot_general(own_turned, left_ref[...], NN, preferred_element_type=F32)
    step = 2 * LANES
    for block in range(chunks // 2):
        at = slice(block * step, (block + 1) * step)
        moved = lax.dot_general(turned, right_ref[:, at], NN, preferred_element_type=F32)
        for i in range(panels):
            for b in range(2):
                piece = moved[i * rhs : (i + 1) * rhs, b * LANES : (b + 1) * LANES]
                c = 2 * block + b
                if i < panels // 2:
                    keep_ref[i * chunks + c] = piece
                else:
                    send_ref[(i - panels // 2) * chunks + c] = piece.astype(BF16)


def curvature_part(direction, nugget, projected, rhs):
    rounded = projected.astype(BF16).astype(F32)
    weighted = lax.dot_general(
        direction * nugget, repeat_rows(direction, rhs), NT, precision=EXACT, preferred_element_type=F32
    )
    first = lax.dot_general(projected.T[:rhs], rounded, NN, precision=EXACT, preferred_element_type=F32)
    second = lax.dot_general(rounded.T[:rhs], projected, NN, precision=EXACT, preferred_element_type=F32)
    return weighted + 0.5 * (first + second)


def first_kernel(
    rhs, chunks, direction_ref, nugget_ref, held_ref, other_ref, left_ref, right_ref, slot_ref,
    send_ref, keep_ref, own_ref, part_ref, gram_ref, projected_ref, panel_ref,
):
    gram_ref[...] = gathered_gram(held_ref, other_ref, chunks, rhs)
    projected = projections(held_ref, other_ref, left_ref, right_ref, slot_ref, panel_ref, rhs, chunks)
    projected = jnp.where(slot_ref[...] >= 0, projected, 0.0)
    projected_ref[...] = projected
    spread_out(projected, left_ref, right_ref, slot_ref, send_ref, keep_ref, own_ref, rhs, chunks)
    part = curvature_part(direction_ref[...], nugget_ref[...], projected, rhs)
    part_ref[...] = part
    send_ref[send_ref.shape[0] - 1] = encode(part, rhs)


def halve_kernel(rhs, keep_ref, part_ref, got_ref, *out):
    *sends, kept_ref, total_ref = out
    count = kept_ref.shape[0]
    total = part_ref[...] + fold(got_ref[got_ref.shape[0] - 1].astype(F32), rhs)
    total_ref[...] = total
    code = encode(total, rhs)
    kept_ref[...] = keep_ref[:count] + got_ref[:count].astype(F32)
    at = count
    for send in sends:
        size = send.shape[0] - 1
        send[:size] = (keep_ref[at : at + size] + got_ref[at : at + size].astype(F32)).astype(BF16)
        send[size] = code
        at += size


def gathered_product(keep_ref, own_ref, part_ref, got, direction, nugget, rhs, chunks):
    total = keep_ref[...]
    code = jnp.zeros(part_ref.shape, F32)
    for ref in got:
        total = total + ref[:chunks].astype(F32)
        code = code + ref[chunks].astype(F32)
    applied = nugget * direction + own_ref[...] + jnp.concatenate([total[c] for c in range(chunks)], axis=1)
    return applied, part_ref[...] + fold(code, rhs)


def middle_kernel(rhs, chunks, count, direction_ref, nugget_ref, own_ref, keep_ref, part_ref, gram_ref, *rest):
    got, (message_ref, residual_ref, solution_ref) = rest[:count], rest[count:]
    direction = direction_ref[...]
    applied, curvature = gathered_product(
        keep_ref, own_ref, part_ref, got, direction, nugget_ref[...], rhs, chunks
    )
    step = right_divide(curvature, gram_ref[...], rhs)
    residual = direction - left_multiply(step, applied, rhs)
    residual_ref[...] = residual
    solution_ref[...] = left_multiply(step, direction, rhs)
    for c in range(chunks):
        message_ref[c] = residual[:, c * LANES : (c + 1) * LANES].astype(BF16)
    gram = lax.dot_general(residual, repeat_rows(residual, rhs), NT, precision=EXACT, preferred_element_type=F32)
    message_ref[chunks] = encode(gram, rhs)


def second_kernel(
    rhs, chunks, right_side_ref, residual_ref, nugget_ref, gram_ref, before_ref, held_ref, other_ref,
    left_ref, right_ref, slot_ref,
    send_ref, keep_ref, own_ref, part_ref, next_gram_ref, direction_ref, panel_ref,
):
    next_gram = gathered_gram(held_ref, other_ref, chunks, rhs)
    next_gram_ref[...] = next_gram
    mix = right_divide(gram_ref[...], next_gram, rhs)
    direction = residual_ref[...] + left_multiply(mix, right_side_ref[...], rhs)
    direction_ref[...] = direction
    projected = projections(held_ref, other_ref, left_ref, right_ref, slot_ref, panel_ref, rhs, chunks)
    mixing = repeat_rows(jnp.where(lane_group(mix.shape, rhs) == 0, mix, 0.0), rhs)
    projected = projected + lax.dot_general(
        before_ref[...], mixing, NT, precision=EXACT, preferred_element_type=F32
    )
    projected = jnp.where(slot_ref[...] >= 0, projected, 0.0)
    spread_out(projected, left_ref, right_ref, slot_ref, send_ref, keep_ref, own_ref, rhs, chunks)
    part = curvature_part(direction, nugget_ref[...], projected, rhs)
    part_ref[...] = part
    send_ref[send_ref.shape[0] - 1] = encode(part, rhs)


def last_kernel(rhs, chunks, count, direction_ref, nugget_ref, own_ref, keep_ref, part_ref, gram_ref, *rest):
    got, (residual_ref, solution_ref, out_solution_ref, out_residual_ref) = rest[:count], rest[count:]
    direction = direction_ref[...]
    applied, curvature = gathered_product(
        keep_ref, own_ref, part_ref, got, direction, nugget_ref[...], rhs, chunks
    )
    step = right_divide(curvature, gram_ref[...], rhs)
    out_solution_ref[...] = solution_ref[...] + left_multiply(step, direction, rhs)
    out_residual_ref[...] = residual_ref[...] - left_multiply(step, applied, rhs)


def call(kernel, outs, *args, scratch=()):
    whole = pl.BlockSpec(memory_space=pltpu.VMEM)
    return pl.pallas_call(
        kernel,
        out_shape=[jax.ShapeDtypeStruct(shape, dtype) for shape, dtype in outs],
        in_specs=[whole] * len(args),
        out_specs=[whole] * len(outs),
        scratch_shapes=list(scratch),
        compiler_params=pltpu.CompilerParams(vmem_limit_bytes=40 * 1024 * 1024),
    )(*args)


def shards(right_sides, nugget, left_factors, right_factors, tile_column, live_slots):
    devices = lax.axis_size("row")
    bits = devices.bit_length() - 1
    low_bits = bits - 2
    slots, rank, width = left_factors.shape
    rhs = right_sides.shape[0]
    chunks = width // LANES
    half = devices // 2

    def swap(array, offset):
        return lax.ppermute(array, "row", [(i, i ^ offset) for i in range(devices)])

    place = tile_column[:, 0] ^ lax.axis_index("row")
    ordered = place >> low_bits
    for b in range(low_bits):
        ordered = ordered | (((place >> b) & 1) << (bits - 1 - b))
    ordered = jnp.where(jnp.arange(slots, dtype=jnp.int32) < live_slots[0], ordered, -1)
    slot = jnp.broadcast_to(ordered[:, None, None], (slots, rank, LANES)).reshape(slots * rank, LANES)

    left = left_factors.reshape(slots * rank, width)
    right = right_factors.reshape(slots * rank, width)
    nugget = nugget[None, :]

    def gather(message):
        held = jnp.stack([message] + [swap(message, k << low_bits) for k in range(1, 4)])
        for b in range(low_bits - 1, 0, -1):
            held = jnp.concatenate([held, swap(held, 1 << b)])
        return held, swap(held, 1)

    small = (rhs, LANES)
    panel = (rhs, width)
    message_shape = ((chunks + 1, rhs, LANES), BF16)

    def reduced(send, keep, part):
        got = swap(send, 1)
        count = half
        for b in range(1, low_bits):
            count //= 2
            outs = [
                ((count * chunks + 1, rhs, LANES), BF16), ((count * chunks, rhs, LANES), F32), (small, F32)
            ]
            send, keep, part = call(functools.partial(halve_kernel, rhs), outs, keep, part, got)
            got = swap(send, 1 << b)
        outs = [message_shape] * 3 + [((chunks, rhs, LANES), F32), (small, F32)]
        *sends, keep, part = call(functools.partial(halve_kernel, rhs), outs, keep, part, got)
        return keep, part, [swap(sends[k - 1], k << low_bits) for k in range(1, 4)]

    spread_outs = [
        ((half * chunks + 1, rhs, LANES), BF16),
        ((half * chunks, rhs, LANES), F32),
        (panel, F32),
        (small, F32),
        (small, F32),
    ]
    scratch = [pltpu.VMEM((devices * rhs, width), BF16)]

    (message,) = call(functools.partial(open_kernel, rhs, chunks), [message_shape], right_sides)
    held, other = gather(message)
    send, keep, own, part, gram, before = call(
        functools.partial(first_kernel, rhs, chunks),
        spread_outs + [((slots * rank, LANES), F32)],
        right_sides, nugget, held, other, left, right, slot,
        scratch=scratch,
    )
    keep, part, got = reduced(send, keep, part)
    message, residual, solution = call(
        functools.partial(middle_kernel, rhs, chunks, len(got)),
        [message_shape, (panel, F32), (panel, F32)],
        right_sides, nugget, own, keep, part, gram, *got,
    )
    held, other = gather(message)
    send, keep, own, part, next_gram, direction = call(
        functools.partial(second_kernel, rhs, chunks),
        spread_outs + [(panel, F32)],
        right_sides, residual, nugget, gram, before, held, other, left, right, slot,
        scratch=scratch,
    )
    keep, part, got = reduced(send, keep, part)
    return tuple(
        call(
            functools.partial(last_kernel, rhs, chunks, len(got)),
            [(panel, F32), (panel, F32)],
            direction, nugget, own, keep, part, next_gram, *got, residual, solution,
        )
    )


def solution(mesh):
    return jax.shard_map(
        shards,
        mesh=mesh,
        in_specs=(
            P(None, ("groups", "row")),
            P(("groups", "row")),
            P(("groups", "row"), None, None),
            P(("groups", "row"), None, None),
            P(("groups", "row"), None),
            P(("groups", "row")),
        ),
        out_specs=(P(None, ("groups", "row")), P(None, ("groups", "row"))),
        check_vma=False,
    )
```

time: 432 us -> 101 us (0.23)
  waiting for transfers between devices: 197 us -> 49.2 us
  blocking collectives: 118 us -> 0 us
  other arithmetic: 41.1 us -> 0.74 us
  matrix products: 35.3 us -> 0 us
  starting transfers between devices: 0.16 us -> 26.2 us
  local copies, waits for them, and re-layouts: 24.2 us -> 4.02 us
  Pallas kernels: 0 us -> 19.4 us
  between operations: 14.6 us -> 1.43 us
    reduce_scatter x2 -> x0, waiting for transfers between devices: 119 us -> none  [shards(): summed = lax.psum_scatter(spread, 'row', scatter_dimension=1, tiled=True)]
    psum x3 -> x0, blocking collectives: 118 us -> none  [the longest x1 57.7 us: shards(): res_gram = lax.psum(pair_gram(residual, residual), 'row')]
    all_gather x2 -> x0, waiting for transfers between devices: 77.3 us -> none  [shards(): lax.all_gather(direction_low, 'row', axis=1, tiled=True)]
    ppermute x0 -> x20, waiting for transfers between devices: none -> 49.2 us  [swap(): return lax.ppermute(array, 'row', [(i, i ^ offset) for i in range(devices)])]
    dot_general x41 -> x0, matrix products: 34.3 us -> none  [the longest x8 11.1 us: one_group(): jnp.einsum('krb,nkb->krn', right_block, far_panels, preferred_element_typ...]
    scatter-add x8 -> x0, other arithmetic: 26.8 us -> none  [one_group(): return (own_rows + own_term, spread.at[:, column_block].add(moved))]
    ppermute x0 -> x20, starting transfers between devices: none -> 26.2 us  [swap(): return lax.ppermute(array, 'row', [(i, i ^ offset) for i in range(devices)])]
    pallas_call x0 -> x9, Pallas kernels: none -> 19.4 us  [call(): pl.pallas_call(kernel, out_shape=[jax.ShapeDtypeStruct(shape, dtype) for...]
  transfers between devices with their start and end apart: 4 -> 20, of which waited for: 4 -> 17; matrix products, arithmetic and copies ran while one was open for 0% -> 1% of each run, Pallas kernels for 0% -> 0%
where the time goes in v1:
time: 101 us
  waiting for transfers between devices  49.2 us (49%)
  starting transfers between devices  26.2 us (26%)
  Pallas kernels  19.4 us (19%)
  local copies, waits for them, and re-layouts  4.02 us (4%)
  between operations  1.43 us (1%)
    ppermute x20, waiting for transfers between devices, swap(): return lax.ppermute(array, 'row', [(i, i ^ offset) for i in range(devices)])  49.2 us
    ppermute x20, starting transfers between devices, swap(): return lax.ppermute(array, 'row', [(i, i ^ offset) for i in range(devices)])  26.2 us
    pallas_call x9, Pallas kernels, call(): pl.pallas_call(kernel, out_shape=[jax.ShapeDtypeStruct(shape, dtype) for...  19.4 us
    unnamed x22, local copies, waits for them, and re-layouts  3.67 us
  transfers between devices with their start and end apart: 20, of which 17 were waited for; matrix products, arithmetic and copies ran while one was open for 1% of the time, Pallas kernels for 0%

profile of v1, /device:TPU:0, one launch (start us, length us, event | category | flops | bytes accessed | tf_op | source)
XLA Modules:
  0.0 101.0 jit_solution(12675836739525209196)
XLA Ops:
  2.6 5.1 %collective-permute-start.2 = (bf16[17,16,128]{2,1,0:T(8,128)(2,1)S(1)}, bf16[17,16,128]{2,1,0:T(8,128)(2,1)S(1)}, u32[]{:S(2)}, u32[]{:S(2)}) collective-permute-start(bf16[17,16,128]{2,1,0:T(8,128)(2,1)S(1)} %shard_map.77), channel_id=1, source_target_pairs={{0,12},{1,13},{2,14},{3,15},{4,8},{5,9},{6,10},{7,11},{8,4},{9,5},... | collective-permute-start | bytes 208904 | tf_op jit(solution)/shard_map/ppermute | solution.py:246
  8.4 2.0 %collective-permute-done.2 = bf16[17,16,128]{2,1,0:T(8,128)(2,1)S(1)} collective-permute-done((bf16[17,16,128]{2,1,0:T(8,128)(2,1)S(1)}, bf16[17,16,128]{2,1,0:T(8,128)(2,1)S(1)}, u32[]{:S(2)}, u32[]{:S(2)}) %collective-permute-start.2) | collective-permute-done | bytes 69664 | tf_op jit(solution)/shard_map/ppermute | solution.py:246
  10.4 3.2 %collective-permute-done.1 = bf16[17,16,128]{2,1,0:T(8,128)(2,1)S(1)} collective-permute-done((bf16[17,16,128]{2,1,0:T(8,128)(2,1)S(1)}, bf16[17,16,128]{2,1,0:T(8,128)(2,1)S(1)}, u32[]{:S(2)}, u32[]{:S(2)}) %collective-permute-start.1) | collective-permute-done | bytes 69664 | tf_op jit(solution)/shard_map/ppermute | solution.py:246
  15.3 6.6 %collective-permute-done.3 = bf16[4,17,16,128]{3,2,1,0:T(8,128)(2,1)S(1)} collective-permute-done((bf16[4,17,16,128]{3,2,1,0:T(8,128)(2,1)S(1)}, bf16[4,17,16,128]{3,2,1,0:T(8,128)(2,1)S(1)}, u32[]{:S(2)}, u32[]{:S(2)}) %collective-permute-start.3) | collective-permute-done | bytes 278560 | tf_op jit(solution)/shard_map/ppermute | solution.py:246
  26.6 5.0 %shard_map.78 = (bf16[129,16,128]{2,1,0:T(8,128)(2,1)S(1)}, f32[128,16,128]{2,1,0:T(8,128)S(1)}, f32[16,2048]{1,0:T(8,128)S(1)}, f32[16,128]{1,0:T(8,128)S(1)}, ...) custom-call(f32[16,2048]{1,0:T(8,128)S(1)} %copy-done.4, f32[1,2048]{1,0:T(1,128)S(1)} %bitcast.29, ...), custom_call_target="tpu_custom_call" | custom-call | tf_op jit(solution)/shard_map/pallas_call | solution.py:226
  31.8 1.8 %collective-permute-done.5.got_ref = bf16[129,16,128]{2,1,0:T(8,128)(2,1)S(1)} collective-permute-done((bf16[129,16,128]{2,1,0:T(8,128)(2,1)S(1)}, bf16[129,16,128]{2,1,0:T(8,128)(2,1)S(1)}, u32[]{:S(2)}, u32[]{:S(2)}) %collective-permute-start.5) | collective-permute-done | bytes 528416 | tf_op jit(solution)/shard_map/ppermute | solution.py:246
  33.9 1.8 %collective-permute-start.6 = (bf16[65,16,128]{2,1,0:T(8,128)(2,1)S(1)}, bf16[65,16,128]{2,1,0:T(8,128)(2,1)S(1)}, u32[]{:S(2)}, u32[]{:S(2)}) collective-permute-start(bf16[65,16,128]{2,1,0:T(8,128)(2,1)S(1)} %get-tuple-element.39), channel_id=1, source_target_pairs={{0,2},{1,3},{2,0},{3,1},{4,6},{5,7},{6,4},{7,5},{8,10},{9,11},{10,... | collective-permute-start | bytes 798728 | tf_op jit(solution)/shard_map/ppermute | solution.py:246
  35.7 6.7 %collective-permute-done.6.got_ref = bf16[65,16,128]{2,1,0:T(8,128)(2,1)S(1)} collective-permute-done((bf16[65,16,128]{2,1,0:T(8,128)(2,1)S(1)}, bf16[65,16,128]{2,1,0:T(8,128)(2,1)S(1)}, u32[]{:S(2)}, u32[]{:S(2)}) %collective-permute-start.6) | collective-permute-done | bytes 266272 | tf_op jit(solution)/shard_map/ppermute | solution.py:246
  42.8 2.0 %collective-permute-start.8 = (bf16[17,16,128]{2,1,0:T(8,128)(2,1)S(1)}, bf16[17,16,128]{2,1,0:T(8,128)(2,1)S(1)}, u32[]{:S(2)}, u32[]{:S(2)}) collective-permute-start(bf16[17,16,128]{2,1,0:T(8,128)(2,1)S(1)} %get-tuple-element.44), channel_id=1, source_target_pairs={{0,8},{1,9},{2,10},{3,11},{4,12},{5,13},{6,14},{7,15},{8,0},{9,1},... | collective-permute-start | bytes 208904 | tf_op jit(solution)/shard_map/ppermute | solution.py:246
  44.9 2.2 %collective-permute-start.9 = (bf16[17,16,128]{2,1,0:T(8,128)(2,1)S(1)}, bf16[17,16,128]{2,1,0:T(8,128)(2,1)S(1)}, u32[]{:S(2)}, u32[]{:S(2)}) collective-permute-start(bf16[17,16,128]{2,1,0:T(8,128)(2,1)S(1)} %get-tuple-element.45), channel_id=1, source_target_pairs={{0,12},{1,13},{2,14},{3,15},{4,8},{5,9},{6,10},{7,11},{8,4},{9,5},... | collective-permute-start | bytes 208904 | tf_op jit(solution)/shard_map/ppermute | solution.py:246
  47.1 3.0 %collective-permute-done.8.rest_1_ = bf16[17,16,128]{2,1,0:T(8,128)(2,1)S(1)} collective-permute-done((bf16[17,16,128]{2,1,0:T(8,128)(2,1)S(1)}, bf16[17,16,128]{2,1,0:T(8,128)(2,1)S(1)}, u32[]{:S(2)}, u32[]{:S(2)}) %collective-permute-start.8) | collective-permute-done | bytes 69664 | tf_op jit(solution)/shard_map/ppermute | solution.py:246
  51.1 2.7 %shard_map.81 = (bf16[17,16,128]{2,1,0:T(8,128)(2,1)S(1)}, f32[16,2048]{1,0:T(8,128)S(1)}, f32[16,2048]{1,0:T(8,128)S(1)}) custom-call(f32[16,2048]{1,0:T(8,128)S(1)} %copy-done.5, f32[1,2048]{1,0:T(1,128)S(1)} %bitcast.30, f32[16,2048]{1,0:T(8,128)S(1)} %get-tuple-element.33.own_ref, f32[16,16,128]{2,1,0:T(8,128)S(1)} %get-tuple-element.40.keep_ref, ...), custom_call_target="tpu_custom_call" | custom-call | tf_op jit(solution)/shard_map/pallas_call | solution.py:226
  53.8 2.2 %collective-permute-start.12 = (bf16[17,16,128]{2,1,0:T(8,128)(2,1)S(1)}, bf16[17,16,128]{2,1,0:T(8,128)(2,1)S(1)}, u32[]{:S(2)}, u32[]{:S(2)}) collective-permute-start(bf16[17,16,128]{2,1,0:T(8,128)(2,1)S(1)} %get-tuple-element.48), channel_id=1, source_target_pairs={{0,12},{1,13},{2,14},{3,15},{4,8},{5,9},{6,10},{7,11},{8,4},{9,5},... | collective-permute-start | bytes 208904 | tf_op jit(solution)/shard_map/ppermute | solution.py:246
  56.4 1.9 %collective-permute-start.10 = (bf16[17,16,128]{2,1,0:T(8,128)(2,1)S(1)}, bf16[17,16,128]{2,1,0:T(8,128)(2,1)S(1)}, u32[]{:S(2)}, u32[]{:S(2)}) collective-permute-start(bf16[17,16,128]{2,1,0:T(8,128)(2,1)S(1)} %get-tuple-element.48), channel_id=1, source_target_pairs={{0,4},{1,5},{2,6},{3,7},{4,0},{5,1},{6,2},{7,3},{8,12},{9,13},{10,... | collective-permute-start | bytes 208904 | tf_op jit(solution)/shard_map/ppermute | solution.py:246
  58.3 1.9 %collective-permute-done.12 = bf16[17,16,128]{2,1,0:T(8,128)(2,1)S(1)} collective-permute-done((bf16[17,16,128]{2,1,0:T(8,128)(2,1)S(1)}, bf16[17,16,128]{2,1,0:T(8,128)(2,1)S(1)}, u32[]{:S(2)}, u32[]{:S(2)}) %collective-permute-start.12) | collective-permute-done | bytes 69664 | tf_op jit(solution)/shard_map/ppermute | solution.py:246
  63.4 4.9 %collective-permute-done.13 = bf16[4,17,16,128]{3,2,1,0:T(8,128)(2,1)S(1)} collective-permute-done((bf16[4,17,16,128]{3,2,1,0:T(8,128)(2,1)S(1)}, bf16[4,17,16,128]{3,2,1,0:T(8,128)(2,1)S(1)}, u32[]{:S(2)}, u32[]{:S(2)}) %collective-permute-start.13) | collective-permute-done | bytes 278560 | tf_op jit(solution)/shard_map/ppermute | solution.py:246
  68.4 1.9 %collective-permute-done.14.other_ref = bf16[8,17,16,128]{3,2,1,0:T(8,128)(2,1)S(1)} collective-permute-done((bf16[8,17,16,128]{3,2,1,0:T(8,128)(2,1)S(1)}, bf16[8,17,16,128]{3,2,1,0:T(8,128)(2,1)S(1)}, u32[]{:S(2)}, u32[]{:S(2)}) %collective-permute-start.14) | collective-permute-done | bytes 557088 | tf_op jit(solution)/shard_map/ppermute | solution.py:246
  70.4 7.1 %shard_map.82 = (bf16[129,16,128]{2,1,0:T(8,128)(2,1)S(1)}, f32[128,16,128]{2,1,0:T(8,128)S(1)}, f32[16,2048]{1,0:T(8,128)S(1)}, f32[16,128]{1,0:T(8,128)S(1)}, ...) custom-call(f32[16,2048]{1,0:T(8,128)S(1)} %copy-done.5, f32[16,2048]{1,0:T(8,128)S(1)} %get-tuple-element.46.residual_ref.rest_3_, ...), custom_call_target="tpu_custom_call" | custom-call | tf_op jit(solution)/shard_map/pallas_call | solution.py:226
  77.7 1.8 %collective-permute-done.15.got_ref = bf16[129,16,128]{2,1,0:T(8,128)(2,1)S(1)} collective-permute-done((bf16[129,16,128]{2,1,0:T(8,128)(2,1)S(1)}, bf16[129,16,128]{2,1,0:T(8,128)(2,1)S(1)}, u32[]{:S(2)}, u32[]{:S(2)}) %collective-permute-start.15) | collective-permute-done | bytes 528416 | tf_op jit(solution)/shard_map/ppermute | solution.py:246
  81.4 6.9 %collective-permute-done.16.got_ref = bf16[65,16,128]{2,1,0:T(8,128)(2,1)S(1)} collective-permute-done((bf16[65,16,128]{2,1,0:T(8,128)(2,1)S(1)}, bf16[65,16,128]{2,1,0:T(8,128)(2,1)S(1)}, u32[]{:S(2)}, u32[]{:S(2)}) %collective-permute-start.16) | collective-permute-done | bytes 266272 | tf_op jit(solution)/shard_map/ppermute | solution.py:246
  89.4 2.9 %collective-permute-start.18 = (bf16[17,16,128]{2,1,0:T(8,128)(2,1)S(1)}, bf16[17,16,128]{2,1,0:T(8,128)(2,1)S(1)}, u32[]{:S(2)}, u32[]{:S(2)}) collective-permute-start(bf16[17,16,128]{2,1,0:T(8,128)(2,1)S(1)} %get-tuple-element.61), channel_id=1, source_target_pairs={{0,8},{1,9},{2,10},{3,11},{4,12},{5,13},{6,14},{7,15},{8,0},{9,1},... | collective-permute-start | bytes 208904 | tf_op jit(solution)/shard_map/ppermute | solution.py:246
  93.4 3.3 %collective-permute-done.18.rest_1_ = bf16[17,16,128]{2,1,0:T(8,128)(2,1)S(1)} collective-permute-done((bf16[17,16,128]{2,1,0:T(8,128)(2,1)S(1)}, bf16[17,16,128]{2,1,0:T(8,128)(2,1)S(1)}, u32[]{:S(2)}, u32[]{:S(2)}) %collective-permute-start.18) | collective-permute-done | bytes 69664 | tf_op jit(solution)/shard_map/ppermute | solution.py:246
  96.6 1.8 %collective-permute-done.19.rest_2_ = bf16[17,16,128]{2,1,0:T(8,128)(2,1)S(1)} collective-permute-done((bf16[17,16,128]{2,1,0:T(8,128)(2,1)S(1)}, bf16[17,16,128]{2,1,0:T(8,128)(2,1)S(1)}, u32[]{:S(2)}, u32[]{:S(2)}) %collective-permute-start.19) | collective-permute-done | bytes 69664 | tf_op jit(solution)/shard_map/ppermute | solution.py:246
  98.4 2.6 %shard_map.85 = (f32[16,2048]{1,0:T(8,128)}, f32[16,2048]{1,0:T(8,128)}) custom-call(f32[16,2048]{1,0:T(8,128)S(1)} %get-tuple-element.49.direction_ref, f32[1,2048]{1,0:T(1,128)S(1)} %bitcast.32, f32[16,2048]{1,0:T(8,128)S(1)} %get-tuple-element.50.own_ref, f32[16,16,128]{2,1,0:T(8,128)S(1)} %get-tuple-element.57.keep_ref, ...), custom_call_target="tpu_custom_call" | custom-call | tf_op jit(solution)/shard_map/pallas_call | solution.py:226
  (55 shorter events, 18.2 us)
Async XLA Ops:
  0.6 23.5 %copy-start = (bf16[32,16,2048]{2,1,0:T(8,128)(2,1)S(1)}, bf16[32,16,2048]{2,1,0:T(8,128)(2,1)}, u32[]{:S(2)}) copy-start(bf16[32,16,2048]{2,1,0:T(8,128)(2,1)} %param.8) | copy-start | bytes 6291460
  1.7 22.4 %copy-start.6 = (f32[2048]{0:T(1024)S(1)}, f32[2048]{0:T(1024)}, u32[]{:S(2)}) copy-start(f32[2048]{0:T(1024)} %param.7) | copy-start | bytes 24580
  2.6 7.8 %collective-permute-start.2 = (bf16[17,16,128]{2,1,0:T(8,128)(2,1)S(1)}, bf16[17,16,128]{2,1,0:T(8,128)(2,1)S(1)}, u32[]{:S(2)}, u32[]{:S(2)}) collective-permute-start(bf16[17,16,128]{2,1,0:T(8,128)(2,1)S(1)} %shard_map.77), channel_id=1, source_target_pairs={{0,12},{1,13},{2,14},{3,15},{4,8},{5,9},{6,10},{7,11},{8,4},{9,5},... | collective-permute-start | bytes 208904 | tf_op jit(solution)/shard_map/ppermute | solution.py:246
  7.7 5.9 %collective-permute-start.1 = (bf16[17,16,128]{2,1,0:T(8,128)(2,1)S(1)}, bf16[17,16,128]{2,1,0:T(8,128)(2,1)S(1)}, u32[]{:S(2)}, u32[]{:S(2)}) collective-permute-start(bf16[17,16,128]{2,1,0:T(8,128)(2,1)S(1)} %shard_map.77), channel_id=1, source_target_pairs={{0,8},{1,9},{2,10},{3,11},{4,12},{5,13},{6,14},{7,15},{8,0},{9,1},... | collective-permute-start | bytes 208904 | tf_op jit(solution)/shard_map/ppermute | solution.py:246
  7.8 5.9 %collective-permute-start = (bf16[17,16,128]{2,1,0:T(8,128)(2,1)S(1)}, bf16[17,16,128]{2,1,0:T(8,128)(2,1)S(1)}, u32[]{:S(2)}, u32[]{:S(2)}) collective-permute-start(bf16[17,16,128]{2,1,0:T(8,128)(2,1)S(1)} %shard_map.77), channel_id=1, source_target_pairs={{0,4},{1,5},{2,6},{3,7},{4,0},{5,1},{6,2},{7,3},{8,12},{9,13},{10,... | collective-permute-start | bytes 208904 | tf_op jit(solution)/shard_map/ppermute | solution.py:246
  13.7 8.2 %collective-permute-start.3 = (bf16[4,17,16,128]{3,2,1,0:T(8,128)(2,1)S(1)}, bf16[4,17,16,128]{3,2,1,0:T(8,128)(2,1)S(1)}, u32[]{:S(2)}, u32[]{:S(2)}) collective-permute-start(bf16[4,17,16,128]{3,2,1,0:T(8,128)(2,1)S(1)} %pad_maximum_fusion), channel_id=1, source_target_pairs={{0,2},{1,3},{2,0},{3,1},{4,6},{5,7},{6,4},{7,5},{8,10},{9,11},{10,... | collective-permute-start | bytes 835592 | tf_op jit(solution)/shard_map/ppermute | solution.py:246
  22.0 2.0 %collective-permute-start.4 = (bf16[8,17,16,128]{3,2,1,0:T(8,128)(2,1)S(1)}, bf16[8,17,16,128]{3,2,1,0:T(8,128)(2,1)S(1)}, u32[]{:S(2)}, u32[]{:S(2)}) collective-permute-start(bf16[8,17,16,128]{3,2,1,0:T(8,128)(2,1)S(1)} %constant_dynamic-update-slice_fusion.held_ref), channel_id=1, source_target_pairs={{0,1},{1,0},{2,3},{3,2},{4,5},{5,4},{6,7},{7,6},{8,9},{9,8},{10,11... | collective-permute-start | bytes 1671176 | tf_op jit(solution)/shard_map/ppermute | solution.py:246
  31.6 19.5 %copy-start.5 = (f32[16,2048]{1,0:T(8,128)S(1)}, f32[16,2048]{1,0:T(8,128)}, u32[]{:S(2)}) copy-start(f32[16,2048]{1,0:T(8,128)} %right_side_ref.1) | copy-start | bytes 393220
  31.6 2.0 %collective-permute-start.5 = (bf16[129,16,128]{2,1,0:T(8,128)(2,1)S(1)}, bf16[129,16,128]{2,1,0:T(8,128)(2,1)S(1)}, u32[]{:S(2)}, u32[]{:S(2)}) collective-permute-start(bf16[129,16,128]{2,1,0:T(8,128)(2,1)S(1)} %get-tuple-element.36), channel_id=1, source_target_pairs={{0,1},{1,0},{2,3},{3,2},{4,5},{5,4},{6,7},{7,6},{8,9},{9,8},{10,11... | collective-permute-start | bytes 1585160 | tf_op jit(solution)/shard_map/ppermute | solution.py:246
  33.6 36.8 %copy-start.2 = (bf16[32,16,2048]{2,1,0:T(8,128)(2,1)S(1)}, bf16[32,16,2048]{2,1,0:T(8,128)(2,1)}, u32[]{:S(2)}) copy-start(bf16[32,16,2048]{2,1,0:T(8,128)(2,1)} %param.9) | copy-start | bytes 6291460
  33.9 8.5 %collective-permute-start.6 = (bf16[65,16,128]{2,1,0:T(8,128)(2,1)S(1)}, bf16[65,16,128]{2,1,0:T(8,128)(2,1)S(1)}, u32[]{:S(2)}, u32[]{:S(2)}) collective-permute-start(bf16[65,16,128]{2,1,0:T(8,128)(2,1)S(1)} %get-tuple-element.39), channel_id=1, source_target_pairs={{0,2},{1,3},{2,0},{3,1},{4,6},{5,7},{6,4},{7,5},{8,10},{9,11},{10,... | collective-permute-start | bytes 798728 | tf_op jit(solution)/shard_map/ppermute | solution.py:246
  42.6 4.4 %collective-permute-start.7 = (bf16[17,16,128]{2,1,0:T(8,128)(2,1)S(1)}, bf16[17,16,128]{2,1,0:T(8,128)(2,1)S(1)}, u32[]{:S(2)}, u32[]{:S(2)}) collective-permute-start(bf16[17,16,128]{2,1,0:T(8,128)(2,1)S(1)} %get-tuple-element.43), channel_id=1, source_target_pairs={{0,4},{1,5},{2,6},{3,7},{4,0},{5,1},{6,2},{7,3},{8,12},{9,13},{10,... | collective-permute-start | bytes 208904 | tf_op jit(solution)/shard_map/ppermute | solution.py:246
  42.8 7.2 %collective-permute-start.8 = (bf16[17,16,128]{2,1,0:T(8,128)(2,1)S(1)}, bf16[17,16,128]{2,1,0:T(8,128)(2,1)S(1)}, u32[]{:S(2)}, u32[]{:S(2)}) collective-permute-start(bf16[17,16,128]{2,1,0:T(8,128)(2,1)S(1)} %get-tuple-element.44), channel_id=1, source_target_pairs={{0,8},{1,9},{2,10},{3,11},{4,12},{5,13},{6,14},{7,15},{8,0},{9,1},... | collective-permute-start | bytes 208904 | tf_op jit(solution)/shard_map/ppermute | solution.py:246
  44.9 6.2 %collective-permute-start.9 = (bf16[17,16,128]{2,1,0:T(8,128)(2,1)S(1)}, bf16[17,16,128]{2,1,0:T(8,128)(2,1)S(1)}, u32[]{:S(2)}, u32[]{:S(2)}) collective-permute-start(bf16[17,16,128]{2,1,0:T(8,128)(2,1)S(1)} %get-tuple-element.45), channel_id=1, source_target_pairs={{0,12},{1,13},{2,14},{3,15},{4,8},{5,9},{6,10},{7,11},{8,4},{9,5},... | collective-permute-start | bytes 208904 | tf_op jit(solution)/shard_map/ppermute | solution.py:246
  53.8 6.4 %collective-permute-start.12 = (bf16[17,16,128]{2,1,0:T(8,128)(2,1)S(1)}, bf16[17,16,128]{2,1,0:T(8,128)(2,1)S(1)}, u32[]{:S(2)}, u32[]{:S(2)}) collective-permute-start(bf16[17,16,128]{2,1,0:T(8,128)(2,1)S(1)} %get-tuple-element.48), channel_id=1, source_target_pairs={{0,12},{1,13},{2,14},{3,15},{4,8},{5,9},{6,10},{7,11},{8,4},{9,5},... | collective-permute-start | bytes 208904 | tf_op jit(solution)/shard_map/ppermute | solution.py:246
  56.1 5.6 %collective-permute-start.11 = (bf16[17,16,128]{2,1,0:T(8,128)(2,1)S(1)}, bf16[17,16,128]{2,1,0:T(8,128)(2,1)S(1)}, u32[]{:S(2)}, u32[]{:S(2)}) collective-permute-start(bf16[17,16,128]{2,1,0:T(8,128)(2,1)S(1)} %get-tuple-element.48), channel_id=1, source_target_pairs={{0,8},{1,9},{2,10},{3,11},{4,12},{5,13},{6,14},{7,15},{8,0},{9,1},... | collective-permute-start | bytes 208904 | tf_op jit(solution)/shard_map/ppermute | solution.py:246
  56.4 5.3 %collective-permute-start.10 = (bf16[17,16,128]{2,1,0:T(8,128)(2,1)S(1)}, bf16[17,16,128]{2,1,0:T(8,128)(2,1)S(1)}, u32[]{:S(2)}, u32[]{:S(2)}) collective-permute-start(bf16[17,16,128]{2,1,0:T(8,128)(2,1)S(1)} %get-tuple-element.48), channel_id=1, source_target_pairs={{0,4},{1,5},{2,6},{3,7},{4,0},{5,1},{6,2},{7,3},{8,12},{9,13},{10,... | collective-permute-start | bytes 208904 | tf_op jit(solution)/shard_map/ppermute | solution.py:246
  61.7 6.6 %collective-permute-start.13 = (bf16[4,17,16,128]{3,2,1,0:T(8,128)(2,1)S(1)}, bf16[4,17,16,128]{3,2,1,0:T(8,128)(2,1)S(1)}, u32[]{:S(2)}, u32[]{:S(2)}) collective-permute-start(bf16[4,17,16,128]{3,2,1,0:T(8,128)(2,1)S(1)} %pad_maximum_fusion.1), channel_id=1, source_target_pairs={{0,2},{1,3},{2,0},{3,1},{4,6},{5,7},{6,4},{7,5},{8,10},{9,11},{10,... | collective-permute-start | bytes 835592 | tf_op jit(solution)/shard_map/ppermute | solution.py:246
  68.4 2.0 %collective-permute-start.14 = (bf16[8,17,16,128]{3,2,1,0:T(8,128)(2,1)S(1)}, bf16[8,17,16,128]{3,2,1,0:T(8,128)(2,1)S(1)}, u32[]{:S(2)}, u32[]{:S(2)}) collective-permute-start(bf16[8,17,16,128]{3,2,1,0:T(8,128)(2,1)S(1)} %constant_dynamic-update-slice_fusion.5.held_ref), channel_id=1, source_target_pairs={{0,1},{1,0},{2,3},{3,2},{4,5},{5,4},{6,7},{7,6},{8,9},{9,8},{10,11... | collective-permute-start | bytes 1671176 | tf_op jit(solution)/shard_map/ppermute | solution.py:246
  77.5 1.9 %collective-permute-start.15 = (bf16[129,16,128]{2,1,0:T(8,128)(2,1)S(1)}, bf16[129,16,128]{2,1,0:T(8,128)(2,1)S(1)}, u32[]{:S(2)}, u32[]{:S(2)}) collective-permute-start(bf16[129,16,128]{2,1,0:T(8,128)(2,1)S(1)} %get-tuple-element.53), channel_id=1, source_target_pairs={{0,1},{1,0},{2,3},{3,2},{4,5},{5,4},{6,7},{7,6},{8,9},{9,8},{10,11... | collective-permute-start | bytes 1585160 | tf_op jit(solution)/shard_map/ppermute | solution.py:246
  79.7 8.5 %collective-permute-start.16 = (bf16[65,16,128]{2,1,0:T(8,128)(2,1)S(1)}, bf16[65,16,128]{2,1,0:T(8,128)(2,1)S(1)}, u32[]{:S(2)}, u32[]{:S(2)}) collective-permute-start(bf16[65,16,128]{2,1,0:T(8,128)(2,1)S(1)} %get-tuple-element.56), channel_id=1, source_target_pairs={{0,2},{1,3},{2,0},{3,1},{4,6},{5,7},{6,4},{7,5},{8,10},{9,11},{10,... | collective-permute-start | bytes 798728 | tf_op jit(solution)/shard_map/ppermute | solution.py:246
  88.5 4.9 %collective-permute-start.17 = (bf16[17,16,128]{2,1,0:T(8,128)(2,1)S(1)}, bf16[17,16,128]{2,1,0:T(8,128)(2,1)S(1)}, u32[]{:S(2)}, u32[]{:S(2)}) collective-permute-start(bf16[17,16,128]{2,1,0:T(8,128)(2,1)S(1)} %get-tuple-element.60), channel_id=1, source_target_pairs={{0,4},{1,5},{2,6},{3,7},{4,0},{5,1},{6,2},{7,3},{8,12},{9,13},{10,... | collective-permute-start | bytes 208904 | tf_op jit(solution)/shard_map/ppermute | solution.py:246
  89.4 7.2 %collective-permute-start.18 = (bf16[17,16,128]{2,1,0:T(8,128)(2,1)S(1)}, bf16[17,16,128]{2,1,0:T(8,128)(2,1)S(1)}, u32[]{:S(2)}, u32[]{:S(2)}) collective-permute-start(bf16[17,16,128]{2,1,0:T(8,128)(2,1)S(1)} %get-tuple-element.61), channel_id=1, source_target_pairs={{0,8},{1,9},{2,10},{3,11},{4,12},{5,13},{6,14},{7,15},{8,0},{9,1},... | collective-permute-start | bytes 208904 | tf_op jit(solution)/shard_map/ppermute | solution.py:246
  92.3 6.1 %collective-permute-start.19 = (bf16[17,16,128]{2,1,0:T(8,128)(2,1)S(1)}, bf16[17,16,128]{2,1,0:T(8,128)(2,1)S(1)}, u32[]{:S(2)}, u32[]{:S(2)}) collective-permute-start(bf16[17,16,128]{2,1,0:T(8,128)(2,1)S(1)} %get-tuple-element.62), channel_id=1, source_target_pairs={{0,12},{1,13},{2,14},{3,15},{4,8},{5,9},{6,10},{7,11},{8,4},{9,5},... | collective-permute-start | bytes 208904 | tf_op jit(solution)/shard_map/ppermute | solution.py:246
  (3 other events, 3.6 us)

commit v2 on v0

v2 whole, which is shorter than its diff:
```python
import functools

import jax
import jax.numpy as jnp
from jax import lax
from jax.experimental import pallas as pl
from jax.experimental.pallas import tpu as pltpu
from jax.sharding import PartitionSpec as P

LANES = 128
F32 = jnp.float32
BF16 = jnp.bfloat16
EXACT = lax.Precision.HIGHEST
NN = (((1,), (0,)), ((), ()))
NT = (((1,), (1,)), ((), ()))


def lanes_of(block):
    return lax.broadcasted_iota(jnp.int32, block.shape, len(block.shape) - 1)


def pair_of(first, second, rhs):
    parts = [first] if second is None else [first, second]
    rest = jnp.zeros((rhs, LANES - rhs * len(parts)), F32)
    return jnp.concatenate(parts + [rest], axis=1)


def encode(pair, rhs):
    high = pair.astype(BF16).astype(F32)
    rest = pair - high
    middle = rest.astype(BF16).astype(F32)
    low = rest - middle
    return (high + pltpu.roll(middle, 2 * rhs, 1) + pltpu.roll(low, 4 * rhs, 1)).astype(BF16)


def decode(code, rhs):
    total = code + pltpu.roll(code, LANES - 2 * rhs, 1) + pltpu.roll(code, LANES - 4 * rhs, 1)
    return jnp.where(lanes_of(total) < 2 * rhs, total, 0.0)


def second_of(pair, rhs):
    return pltpu.roll(pair, LANES - rhs, 1)


def right_divide(top, bottom, rhs):
    both = jnp.concatenate([top, bottom], axis=0)
    lane = lanes_of(both)
    both = jnp.where(lane < rhs, both, 0.0)
    one = lane[:1]
    for k in range(0, rhs, 2):
        col_0 = jnp.broadcast_to(both[:, k : k + 1], both.shape)
        col_1 = jnp.broadcast_to(both[:, k + 1 : k + 2], both.shape)
        a, b = col_0[k : k + 1], col_1[k : k + 1]
        c, d = col_0[k + 1 : k + 2], col_1[k + 1 : k + 2]
        inverse = 1.0 / (a * d - b * c)
        row_0 = jnp.where(one == k, -1.0, jnp.where(one == k + 1, 0.0, both[k : k + 1]))
        row_1 = jnp.where(one == k, 0.0, jnp.where(one == k + 1, -1.0, both[k + 1 : k + 2]))
        new_0 = (d * row_0 - b * row_1) * inverse
        new_1 = (a * row_1 - c * row_0) * inverse
        both = jnp.where((lane == k) | (lane == k + 1), 0.0, both) - col_0 * new_0 - col_1 * new_1
    return both[rhs:, :]


def left_multiply(square, block, rhs):
    return lax.dot_general(square[:, :rhs], block, NN, precision=EXACT, preferred_element_type=F32)


def gram(former, latter):
    return lax.dot_general(former, latter, NT, precision=EXACT, preferred_element_type=F32)


def rows_of(ref, chunks):
    panels, _, rhs, lanes = ref.shape
    return jnp.concatenate([ref[:, c].reshape(panels * rhs, lanes) for c in range(chunks)], axis=1)


def store_message(message_ref, block, rhs, at=0):
    for c in range(block.shape[1] // LANES):
        message_ref[at + c] = block[:, c * LANES : (c + 1) * LANES].astype(message_ref.dtype)


def far_terms(total, panels, right_ref, slot, bases, rhs, chunks):
    rows = jnp.concatenate([rows_of(ref, chunks) for ref in panels], axis=0)
    far = lax.dot_general(rows, right_ref[...], NT, preferred_element_type=F32)
    at = 0
    for base, ref in zip(bases, panels):
        for i in range(ref.shape[0]):
            total = total + jnp.where(slot == base + i, far[at : at + rhs], 0.0)
            at += rhs
    return total


def codes_of(panels_ref, chunks):
    count, held = panels_ref.shape[:2]
    code = jnp.zeros(panels_ref.shape[2:], F32)
    for i in range(count if held > chunks else 0):
        code = code + panels_ref[i, chunks].astype(F32)
    return code


def spread_terms(projected, right_ref, slot, base, out_ref, count, rhs, chunks, extra=None):
    masked = [jnp.where(slot == base + i, projected, 0.0).astype(BF16) for i in range(count)]
    masked = jnp.concatenate(masked, axis=0)
    step = 2 * LANES
    for block in range(chunks // 2):
        at = slice(block * step, (block + 1) * step)
        moved = lax.dot_general(masked, right_ref[:, at], NN, preferred_element_type=F32)
        for i in range(count):
            for b in range(2):
                piece = moved[i * rhs : (i + 1) * rhs, b * LANES : (b + 1) * LANES]
                if i == 0 and extra is not None:
                    place = block * step + b * LANES
                    piece = piece + extra[:, place : place + LANES]
                out_ref[i * chunks + 2 * block + b] = piece.astype(out_ref.dtype)


def open_kernel(rhs, right_side_hbm, message_ref, right_side_ref, sem):
    copy = pltpu.make_async_copy(right_side_hbm, right_side_ref, sem)
    copy.start()
    copy.wait()
    store_message(message_ref, right_side_ref[...], rhs)


def load_kernel(
    rhs, rank, place_of, own_ref, column_ref, live_ref, nugget_hbm, left_hbm, right_hbm,
    nugget_ref, left_ref, right_ref, slot_ref, near_ref, pair_ref, nugget_sem, left_sem, right_sem,
):
    nugget_copy = pltpu.make_async_copy(nugget_hbm, nugget_ref, nugget_sem)
    left_copy = pltpu.make_async_copy(left_hbm, left_ref, left_sem)
    right_copy = pltpu.make_async_copy(right_hbm, right_ref, right_sem)
    nugget_copy.start()
    left_copy.start()
    right_copy.start()
    me = lax.axis_index("row")
    slot_of = lax.broadcasted_iota(jnp.int32, (1, slot_ref.shape[1]), 1) // rank
    slot = jnp.full(slot_of.shape, -1, jnp.int32)
    for s in range(column_ref.shape[0]):
        place = jnp.where(s < live_ref[0], place_of(column_ref[s] ^ me), -1)
        slot = jnp.where(slot_of == s, place, slot)
    slot_ref[...] = jnp.broadcast_to(slot, slot_ref.shape)
    own = own_ref[...]
    nugget_copy.wait()
    pair_ref[...] = pair_of(gram(own * nugget_ref[...], own), gram(own, own), rhs)
    left_copy.wait()
    near_ref[...] = lax.dot_general(own.astype(BF16), left_ref[...], NT, preferred_element_type=F32)
    right_copy.wait()


def near_kernel(own_ref, left_ref, near_ref):
    near_ref[...] = lax.dot_general(own_ref[...].astype(BF16), left_ref[...], NT, preferred_element_type=F32)


def add_kernel(rhs, chunks, bases, first, right_ref, slot_ref, *rest):
    panels, (part_ref, code_ref, out_ref, code_out_ref) = rest[: len(bases)], rest[len(bases) :]
    slot = slot_ref[...]
    total, code = part_ref[...], code_ref[...]
    if first:
        total, code = jnp.where(slot >= 0, total, 0.0), jnp.zeros(code.shape, F32)
    total = far_terms(total, panels, right_ref, slot, bases, rhs, chunks)
    for ref in panels:
        code = code + codes_of(ref, chunks)
    out_ref[...] = total
    code_out_ref[...] = code


def symmetric_product(projected):
    rounded = projected.astype(BF16).astype(F32)
    first = gram(projected, rounded)
    return 0.5 * (first + first.T)


def first_kernel(
    rhs, chunks, base, panels_ref, right_ref, slot_ref, before_ref, pair_ref,
    send_ref, total_ref, projected_ref,
):
    slot = slot_ref[...]
    projected = far_terms(before_ref[...], [panels_ref], right_ref, slot, [base], rhs, chunks)
    projected_ref[...] = projected
    total = pair_ref[...] + pair_of(symmetric_product(projected), None, rhs)
    total_ref[...] = total
    count = send_ref.shape[0] // chunks
    spread_terms(projected, right_ref, slot, base, send_ref, count, rhs, chunks)
    send_ref[count * chunks] = encode(total, rhs)


def second_kernel(
    rhs, chunks, base, panels_ref, right_ref, slot_ref, before_ref, code_ref,
    right_side_ref, residual_ref, nugget_ref, gram_ref, earlier_ref,
    send_ref, total_ref, projected_ref, direction_ref, next_gram_ref,
):
    slot = slot_ref[...]
    next_gram = decode(code_ref[...] + codes_of(panels_ref, chunks), rhs)
    next_gram_ref[...] = next_gram
    mix = right_divide(gram_ref[...], next_gram, rhs)
    projected = far_terms(before_ref[...], [panels_ref], right_ref, slot, [base], rhs, chunks)
    projected = projected + left_multiply(mix, earlier_ref[...], rhs)
    projected_ref[...] = projected
    direction = residual_ref[...] + left_multiply(mix, right_side_ref[...], rhs)
    direction_ref[...] = direction
    total = pair_of(gram(direction * nugget_ref[...], direction) + symmetric_product(projected), None, rhs)
    total_ref[...] = total
    count = send_ref.shape[0] // chunks
    spread_terms(projected, right_ref, slot, base, send_ref, count, rhs, chunks)
    send_ref[count * chunks] = encode(total, rhs)


def spread_kernel(rhs, chunks, base, projected_ref, right_ref, slot_ref, out_ref):
    spread_terms(
        projected_ref[...], right_ref, slot_ref[...], base, out_ref, out_ref.shape[0] // chunks, rhs, chunks
    )


def spread_own_kernel(rhs, chunks, base, projected_ref, left_ref, right_ref, slot_ref, out_ref):
    projected = projected_ref[...]
    own = lax.dot_general(projected.astype(BF16), left_ref[...], NN, preferred_element_type=F32)
    spread_terms(
        projected, right_ref, slot_ref[...], base, out_ref, out_ref.shape[0] // chunks, rhs, chunks, own
    )


def join_kernel(keep_ref, got_ref, sum_ref):
    sum_ref[...] = keep_ref[...] + got_ref[...].astype(F32)


def split_kernel(rhs, keep_ref, pair_ref, got_ref, total_ref, *sends):
    total = pair_ref[...] + decode(got_ref[got_ref.shape[0] - 1].astype(F32), rhs)
    total_ref[...] = total
    end = keep_ref.shape[0]
    for i, send in enumerate(sends):
        size = send.shape[0] - (1 if i == 0 else 0)
        send[:size] = (keep_ref[end - size : end] + got_ref[end - size : end].astype(F32)).astype(BF16)
        end -= size
    sends[0][sends[0].shape[0] - 1] = encode(total, rhs)


def part_kernel(rhs, at, stay, keep_ref, pair_ref, got_ref, *out):
    chunks = got_ref.shape[0]
    total = pair_ref[...]
    out = list(out)
    if chunks % 2:
        chunks -= 1
        total = total + decode(got_ref[chunks].astype(F32), rhs)
        out.pop(0)[...] = total
    if stay:
        out.pop(0)[...] = keep_ref[at : at + stay] + got_ref[:stay].astype(F32)
    if chunks > stay:
        (send,) = out
        send[: chunks - stay] = (keep_ref[at + stay : at + chunks] + got_ref[stay:chunks].astype(F32)).astype(
            BF16
        )
        send[chunks - stay] = encode(total, rhs)


def message_kernel(rhs, panel_ref, pair_ref, message_ref):
    message_ref[: panel_ref.shape[0]] = panel_ref[...].astype(BF16)
    message_ref[panel_ref.shape[0]] = encode(pair_ref[...], rhs)


def code_kernel(rhs, pair_ref, code_ref):
    code_ref[...] = encode(pair_ref[...], rhs)


def pair_kernel(rhs, pair_ref, got_ref, total_ref):
    total_ref[...] = pair_ref[...] + decode(got_ref[...].astype(F32), rhs)


def gathered_product(keep_ref, pair_ref, got, direction, nugget, rhs, chunks):
    total = keep_ref[...]
    code = jnp.zeros(pair_ref.shape, F32)
    for ref in got:
        total = total + ref[:chunks].astype(F32)
        code = code + ref[chunks].astype(F32)
    applied = nugget * direction + jnp.concatenate([total[c] for c in range(chunks)], axis=1)
    return applied, pair_ref[...] + decode(code, rhs)


def middle_kernel(rhs, chunks, direction_ref, nugget_ref, keep_ref, pair_ref, *rest):
    got, (message_ref, residual_ref, solution_ref, gram_ref) = rest[:-4], rest[-4:]
    direction = direction_ref[...]
    applied, pair = gathered_product(keep_ref, pair_ref, got, direction, nugget_ref[...], rhs, chunks)
    first_gram = second_of(pair, rhs)
    gram_ref[...] = first_gram
    step = right_divide(pair, first_gram, rhs)
    residual = direction - left_multiply(step, applied, rhs)
    residual_ref[...] = residual
    store_message(message_ref, residual, rhs)
    message_ref[chunks] = encode(pair_of(gram(residual, residual), None, rhs), rhs)
    solution_ref[...] = left_multiply(step, direction, rhs)


def last_kernel(rhs, chunks, direction_ref, nugget_ref, keep_ref, pair_ref, gram_ref, *rest):
    got, (residual_ref, solution_ref, out_solution_ref, out_residual_ref) = rest[:-4], rest[-4:]
    direction = direction_ref[...]
    applied, pair = gathered_product(keep_ref, pair_ref, got, direction, nugget_ref[...], rhs, chunks)
    step = right_divide(pair, gram_ref[...], rhs)
    out_solution_ref[...] = solution_ref[...] + left_multiply(step, direction, rhs)
    out_residual_ref[...] = residual_ref[...] - left_multiply(step, applied, rhs)


def call(kernel, outs, *args, far=(), scalars=(), fixed=(), scratch=()):
    whole = pl.BlockSpec(memory_space=pltpu.VMEM)
    spaces = {i: pltpu.HBM for i in far} | {i: pltpu.SMEM for i in scalars}
    return pl.pallas_call(
        kernel,
        out_shape=[
            pltpu.VMEM(shape, dtype) if i in fixed else jax.ShapeDtypeStruct(shape, dtype)
            for i, (shape, dtype) in enumerate(outs)
        ],
        in_specs=[pl.BlockSpec(memory_space=spaces[i]) if i in spaces else whole for i in range(len(args))],
        out_specs=[whole] * len(outs),
        scratch_shapes=list(scratch),
        cost_estimate=pl.CostEstimate(flops=0, bytes_accessed=0, transcendentals=0),
        compiler_params=pltpu.CompilerParams(vmem_limit_bytes=32 * 1024 * 1024),
    )(*args)


def after(value, *others):
    return lax.optimization_barrier((value, *others))[0]


def shards(right_sides, nugget, left_factors, right_factors, tile_column, live_slots):
    devices = lax.axis_size("row")
    bits = devices.bit_length() - 1
    low_bits = bits - 2
    slots, rank, width = left_factors.shape
    rhs = right_sides.shape[0]
    chunks = width // LANES
    part = functools.partial

    def swap(array, offset):
        return lax.ppermute(array, "row", [(i, i ^ offset) for i in range(devices)])

    groups = []
    for k in range(4):
        group = [k << low_bits]
        for b in range(low_bits - 1, 1, -1):
            group = group + [o | (1 << b) for o in group]
        groups.append(group)
    m = len(groups[0])
    held_offsets = sum(groups, [])
    late_offsets = [o | 2 for o in held_offsets]
    offsets = held_offsets + [o | 1 for o in held_offsets] + late_offsets + [o | 1 for o in late_offsets]
    held, held_other, late, late_other = (4 * m * i for i in range(4))

    def place_of(offset):
        place = (offset >> low_bits) * m
        for b in range(low_bits - 1, 1, -1):
            place = place + (((offset >> b) & 1) << (low_bits - 1 - b))
        return place + (offset & 1) * held_other + ((offset >> 1) & 1) * late

    assert [place_of(o) for o in offsets] == list(range(devices))

    small = ((rhs, LANES), F32)
    panel = ((rhs, width), F32)
    row_block = ((rhs, slots * rank), F32)

    def plain(count):
        return ((count * chunks, rhs, LANES), BF16)

    def coded(count):
        return ((count * chunks + 1, rhs, LANES), BF16)

    def kept(count):
        return ((count * chunks, rhs, LANES), F32)

    def gather(message, early):
        mine = [message[None]] + [swap(message, k << low_bits)[None] for k in range(1, 4)]
        near, code, slot, right = early
        mine[1] = after(mine[1], near)
        for b in range(low_bits - 1, 1, -1):
            mine = [jnp.concatenate([g, swap(g, 1 << b)]) for g in mine]
        beside = [swap(jnp.concatenate(mine[i : i + 2]), 2) for i in (0, 2)]
        own_core = jnp.concatenate(mine)
        other_core = swap(own_core, 1)
        add = part(add_kernel, rhs, chunks)
        near, code = call(
            part(add, (held, held_other), True), [row_block, small],
            right, slot, own_core, other_core, near, code,
        )
        beside = after(jnp.concatenate(beside), near)
        other_beside = swap(beside, 1)
        near, code = call(part(add, (late,), False), [row_block, small], right, slot, beside, near, code)
        return other_beside, near, code

    def reduce(send, pair, projected, left, right, slot):
        got = swap(send, 1)
        (send,) = call(part(spread_kernel, rhs, chunks, held_other), [plain(4 * m)], projected, right, slot)
        (keep,) = call(
            part(spread_kernel, rhs, chunks, late), [kept(4 * m)], after(projected, send), right, slot
        )
        got_held = swap(send, 1)
        pair, send_c, send_b, send_a = call(
            part(split_kernel, rhs),
            [small, coded(m), plain(m), plain(2 * m)],
            keep, pair, got,
        )
        got_c, got_b, got_a = swap(send_c, 2), swap(send_b, 2), swap(send_a, 2)
        (keep,) = call(
            part(spread_own_kernel, rhs, chunks, held), [kept(4 * m)], after(projected, send_c), left, right, slot
        )
        (keep,) = call(join_kernel, [kept(4 * m)], keep, got_held)
        got_c = after(got_c, keep)
        size = m * chunks
        if m == 1:
            pair, send_c = call(
                part(part_kernel, rhs, 3 * size, 0), [small, coded(1)], keep, pair, got_c
            )
            last_c = swap(send_c, 3 << low_bits)
            (send_b,) = call(
                part(part_kernel, rhs, 2 * size, 0), [coded(1)], keep, pair, got_b
            )
            last_b = swap(send_b, 2 << low_bits)
            mine, send_a = call(
                part(part_kernel, rhs, 0, size), [kept(1), coded(1)], keep, pair, got_a
            )
            return mine, pair, [swap(send_a, 1 << low_bits), last_b, last_c]
        (pair,) = call(part(pair_kernel, rhs), [small], pair, got_c[-1])
        got = jnp.concatenate([got_a, got_b, got_c[:-1]])
        (keep,) = call(join_kernel, [kept(4 * m)], keep, got)
        four = [keep[i * size : (i + 1) * size] for i in range(4)]
        for b in range(2, low_bits):
            (code,) = call(part(code_kernel, rhs), [((rhs, LANES), BF16)], pair)
            (pair,) = call(part(pair_kernel, rhs), [small], pair, swap(code, 1 << b))
            half = four[0].shape[0] // 2
            four = [x[:half] + swap(x[half:].astype(BF16), 1 << b).astype(F32) for x in four]
        sends = [call(part(message_kernel, rhs), [coded(1)], x, pair)[0] for x in four[1:]]
        return four[0], pair, [swap(x, (k + 1) << low_bits) for k, x in enumerate(sends)]

    def in_hbm(array):
        return pltpu.with_memory_space_constraint(array, pltpu.HBM)

    semaphore = pltpu.SemaphoreType.DMA
    factor = ((slots * rank, width), BF16)
    message, right_sides = call(
        part(open_kernel, rhs), [plain(1), panel], in_hbm(right_sides), far=(0,), fixed=(1,), scratch=[semaphore]
    )
    nugget, left, right, slot, near, pair = call(
        part(load_kernel, rhs, rank, place_of),
        [((1, width), F32), factor, factor, ((rhs, slots * rank), jnp.int32), row_block, small],
        right_sides, tile_column[:, 0], live_slots, in_hbm(nugget[None, :]),
        in_hbm(left_factors.reshape(slots * rank, width)), in_hbm(right_factors.reshape(slots * rank, width)),
        far=(3, 4, 5), scalars=(1, 2), fixed=(0, 1, 2), scratch=[semaphore] * 3,
    )
    other, near, _ = gather(message, (near, pair, slot, right))
    send, pair, earlier = call(
        part(first_kernel, rhs, chunks, late_other),
        [coded(4 * m), small, row_block],
        other, right, slot, near, pair,
    )
    mine, pair, got = reduce(send, pair, earlier, left, right, slot)
    message, residual, solution, first_gram = call(
        part(middle_kernel, rhs, chunks),
        [coded(1), panel, panel, small],
        right_sides, nugget, mine, pair, *got,
    )
    (near,) = call(near_kernel, [row_block], residual, left)
    other, near, code = gather(message, (near, first_gram, slot, right))
    send, pair, projected, direction, next_gram = call(
        part(second_kernel, rhs, chunks, late_other),
        [coded(4 * m), small, row_block, panel, small],
        other, right, slot, near, code, right_sides, residual, nugget, first_gram, earlier,
    )
    mine, pair, got = reduce(send, pair, projected, left, right, slot)
    return tuple(
        call(
            part(last_kernel, rhs, chunks),
            [panel, panel],
            direction, nugget, mine, pair, next_gram, *got, residual, solution,
        )
    )


def solution(mesh):
    return jax.shard_map(
        shards,
        mesh=mesh,
        in_specs=(
            P(None, ("groups", "row")),
            P(("groups", "row")),
            P(("groups", "row"), None, None),
            P(("groups", "row"), None, None),
            P(("groups", "row"), None),
            P(("groups", "row")),
        ),
        out_specs=(P(None, ("groups", "row")), P(None, ("groups", "row"))),
        check_vma=False,
    )
```

time: 432 us -> 89.8 us (0.21)
  waiting for transfers between devices: 197 us -> 39.1 us
  blocking collectives: 118 us -> 0 us
  other arithmetic: 41.1 us -> 0.19 us
  matrix products: 35.3 us -> 0 us
  starting transfers between devices: 0.16 us -> 29.1 us
  local copies, waits for them, and re-layouts: 24.2 us -> 0.65 us
  Pallas kernels: 0 us -> 19 us
  between operations: 14.6 us -> 1.53 us
    reduce_scatter x2 -> x0, waiting for transfers between devices: 119 us -> none  [shards(): summed = lax.psum_scatter(spread, 'row', scatter_dimension=1, tiled=True)]
    psum x3 -> x0, blocking collectives: 118 us -> none  [the longest x1 57.7 us: shards(): res_gram = lax.psum(pair_gram(residual, residual), 'row')]
    all_gather x2 -> x0, waiting for transfers between devices: 77.3 us -> none  [shards(): lax.all_gather(direction_low, 'row', axis=1, tiled=True)]
    ppermute x0 -> x30, waiting for transfers between devices: none -> 39.1 us  [swap(): return lax.ppermute(array, 'row', [(i, i ^ offset) for i in range(devices)])]
    dot_general x41 -> x0, matrix products: 34.3 us -> none  [the longest x8 11.1 us: one_group(): jnp.einsum('krb,nkb->krn', right_block, far_panels, preferred_element_typ...]
    ppermute x0 -> x30, starting transfers between devices: none -> 29.1 us  [swap(): return lax.ppermute(array, 'row', [(i, i ^ offset) for i in range(devices)])]
    scatter-add x8 -> x0, other arithmetic: 26.8 us -> none  [one_group(): return (own_rows + own_term, spread.at[:, column_block].add(moved))]
    pallas_call x0 -> x27, Pallas kernels: none -> 19 us  [call(): pl.pallas_call(kernel, out_shape=[pltpu.VMEM(shape, dtype) if i in fixed...]
  transfers between devices with their start and end apart: 4 -> 30, of which waited for: 4 -> 19; matrix products, arithmetic and copies ran while one was open for 0% -> 0% of each run, Pallas kernels for 0% -> 11%
where the time goes in v2:
time: 89.8 us; the launch traced here: 89.6 us
  waiting for transfers between devices  39.1 us (44%)
  starting transfers between devices  29.1 us (32%)
  Pallas kernels  19 us (21%)
  between operations  1.53 us (2%)
    ppermute x30, waiting for transfers between devices, swap(): return lax.ppermute(array, 'row', [(i, i ^ offset) for i in range(devices)])  39.1 us
    ppermute x30, starting transfers between devices, swap(): return lax.ppermute(array, 'row', [(i, i ^ offset) for i in range(devices)])  29.1 us
    pallas_call x27, Pallas kernels, call(): pl.pallas_call(kernel, out_shape=[pltpu.VMEM(shape, dtype) if i in fixed...  19 us
  transfers between devices with their start and end apart: 30, of which 19 were waited for; matrix products, arithmetic and copies ran while one was open for 0% of the time, Pallas kernels for 11%

profile of v2, /device:TPU:0, one launch (start us, length us, event | category | flops | bytes accessed | tf_op | source)
XLA Modules:
  0.0 89.6 jit_solution(2836211645661231948)
XLA Ops:
  1.6 3.1 %collective-permute-start = (bf16[16,16,128]{2,1,0:T(8,128)(2,1)S(1)}, bf16[16,16,128]{2,1,0:T(8,128)(2,1)S(1)}, u32[]{:S(2)}, u32[]{:S(2)}) collective-permute-start(bf16[16,16,128]{2,1,0:T(8,128)(2,1)S(1)} %get-tuple-element.57), channel_id=1, source_target_pairs={{0,4},{1,5},{2,6},{3,7},{4,0},{5,1},{6,2},{7,3},{8,12},{9,13},{10,... | collective-permute-start | bytes 196616 | tf_op jit(solution)/shard_map/ppermute | solution.py:331
  4.6 2.5 %collective-permute-start.3 = (bf16[16,16,128]{2,1,0:T(8,128)(2,1)S(1)}, bf16[16,16,128]{2,1,0:T(8,128)(2,1)S(1)}, u32[]{:S(2)}, u32[]{:S(2)}) collective-permute-start(bf16[16,16,128]{2,1,0:T(8,128)(2,1)S(1)} %get-tuple-element.57), channel_id=1, source_target_pairs={{0,12},{1,13},{2,14},{3,15},{4,8},{5,9},{6,10},{7,11},{8,4},{9,5},... | collective-permute-start | bytes 196616 | tf_op jit(solution)/shard_map/ppermute | solution.py:331
  8.6 2.8 %shard_map.78 = (f32[1,2048]{1,0:T(1,128)S(1)}, bf16[512,2048]{1,0:T(8,128)(2,1)S(1)}, bf16[512,2048]{1,0:T(8,128)(2,1)S(1)}, s32[16,512]{1,0:T(8,128)S(1)}, f32...) custom-call(f32[16,2048]{1,0:T(8,128)S(1)} %get-tuple-element.55.own_ref.direction_ref.right_side_ref, s32[32]{0:T(128)S(1)} %bitcast.16, ...), custom_call_target="tpu_custom_call" | custom-call | tf_op jit(solution)/shard_map/pallas_call | solution.py:303
  11.5 2.1 %collective-permute-done.2 = bf16[16,16,128]{2,1,0:T(8,128)(2,1)S(1)} collective-permute-done((bf16[16,16,128]{2,1,0:T(8,128)(2,1)S(1)}, bf16[16,16,128]{2,1,0:T(8,128)(2,1)S(1)}, u32[]{:S(2)}, u32[]{:S(2)}) %collective-permute-start.2) | collective-permute-done | bytes 65568 | tf_op jit(solution)/shard_map/ppermute | solution.py:331
  13.7 1.6 %collective-permute-start.4 = (bf16[2,16,16,128]{3,2,1,0:T(8,128)(2,1)S(1)}, bf16[2,16,16,128]{3,2,1,0:T(8,128)(2,1)S(1)}, u32[]{:S(2)}, u32[]{:S(2)}) collective-permute-start(bf16[2,16,16,128]{3,2,1,0:T(8,128)(2,1)S(1)} %pad_maximum_fusion.7), channel_id=1, source_target_pairs={{0,2},{1,3},{2,0},{3,1},{4,6},{5,7},{6,4},{7,5},{8,10},{9,11},{10,... | collective-permute-start | bytes 393224 | tf_op jit(solution)/shard_map/ppermute | solution.py:331
  15.8 4.3 %collective-permute-done.4 = bf16[2,16,16,128]{3,2,1,0:T(8,128)(2,1)S(1)} collective-permute-done((bf16[2,16,16,128]{3,2,1,0:T(8,128)(2,1)S(1)}, bf16[2,16,16,128]{3,2,1,0:T(8,128)(2,1)S(1)}, u32[]{:S(2)}, u32[]{:S(2)}) %collective-permute-start.4) | collective-permute-done | bytes 131104 | tf_op jit(solution)/shard_map/ppermute | solution.py:331
  20.1 2.4 %collective-permute-done.1 = bf16[2,16,16,128]{3,2,1,0:T(8,128)(2,1)S(1)} collective-permute-done((bf16[2,16,16,128]{3,2,1,0:T(8,128)(2,1)S(1)}, bf16[2,16,16,128]{3,2,1,0:T(8,128)(2,1)S(1)}, u32[]{:S(2)}, u32[]{:S(2)}) %collective-permute-start.1) | collective-permute-done | bytes 131104 | tf_op jit(solution)/shard_map/ppermute | solution.py:331
  28.1 1.5 %collective-permute-start.10 = (bf16[32,16,128]{2,1,0:T(8,128)(2,1)S(1)}, bf16[32,16,128]{2,1,0:T(8,128)(2,1)S(1)}, u32[]{:S(2)}, u32[]{:S(2)}) collective-permute-start(bf16[32,16,128]{2,1,0:T(8,128)(2,1)S(1)} %get-tuple-element.77), channel_id=1, source_target_pairs={{0,2},{1,3},{2,0},{3,1},{4,6},{5,7},{6,4},{7,5},{8,10},{9,11},{10,... | collective-permute-start | bytes 393224 | tf_op jit(solution)/shard_map/ppermute | solution.py:331
  30.1 1.5 %collective-permute-start.12 = (bf16[16,16,128]{2,1,0:T(8,128)(2,1)S(1)}, bf16[16,16,128]{2,1,0:T(8,128)(2,1)S(1)}, u32[]{:S(2)}, u32[]{:S(2)}) collective-permute-start(bf16[16,16,128]{2,1,0:T(8,128)(2,1)S(1)} %get-tuple-element.80), channel_id=1, source_target_pairs={{0,2},{1,3},{2,0},{3,1},{4,6},{5,7},{6,4},{7,5},{8,10},{9,11},{10,... | collective-permute-start | bytes 196616 | tf_op jit(solution)/shard_map/ppermute | solution.py:331
  32.4 3.3 %collective-permute-done.9.got_ref = bf16[17,16,128]{2,1,0:T(8,128)(2,1)S(1)} collective-permute-done((bf16[17,16,128]{2,1,0:T(8,128)(2,1)S(1)}, bf16[17,16,128]{2,1,0:T(8,128)(2,1)S(1)}, u32[]{:S(2)}, u32[]{:S(2)}) %collective-permute-start.9) | collective-permute-done | bytes 69664 | tf_op jit(solution)/shard_map/ppermute | solution.py:331
  37.4 1.7 %collective-permute-start.14 = (bf16[17,16,128]{2,1,0:T(8,128)(2,1)S(1)}, bf16[17,16,128]{2,1,0:T(8,128)(2,1)S(1)}, u32[]{:S(2)}, u32[]{:S(2)}) collective-permute-start(bf16[17,16,128]{2,1,0:T(8,128)(2,1)S(1)} %get-tuple-element.81), channel_id=1, source_target_pairs={{0,12},{1,13},{2,14},{3,15},{4,8},{5,9},{6,10},{7,11},{8,4},{9,5},... | collective-permute-start | bytes 208904 | tf_op jit(solution)/shard_map/ppermute | solution.py:331
  40.2 4.2 %collective-permute-done.13.rest_1_ = bf16[17,16,128]{2,1,0:T(8,128)(2,1)S(1)} collective-permute-done((bf16[17,16,128]{2,1,0:T(8,128)(2,1)S(1)}, bf16[17,16,128]{2,1,0:T(8,128)(2,1)S(1)}, u32[]{:S(2)}, u32[]{:S(2)}) %collective-permute-start.13) | collective-permute-done | bytes 69664 | tf_op jit(solution)/shard_map/ppermute | solution.py:331
  44.7 1.5 %shard_map.90 = (bf16[17,16,128]{2,1,0:T(8,128)(2,1)S(1)}, f32[16,2048]{1,0:T(8,128)S(1)}, f32[16,2048]{1,0:T(8,128)S(1)}, f32[16,128]{1,0:T(8,128)S(1)}) custom-call(f32[16,2048]{1,0:T(8,128)S(1)} %get-tuple-element.55.own_ref.direction_ref.right_side_ref, f32[1,2048]{1,0:T(1,128)S(1)} %get-tuple-element.56.nugget_ref, ...), custom_call_target="tpu_custom_call" | custom-call | tf_op jit(solution)/shard_map/pallas_call | solution.py:303
  47.3 1.9 %collective-permute-start.18 = (bf16[17,16,128]{2,1,0:T(8,128)(2,1)S(1)}, bf16[17,16,128]{2,1,0:T(8,128)(2,1)S(1)}, u32[]{:S(2)}, u32[]{:S(2)}) collective-permute-start(bf16[17,16,128]{2,1,0:T(8,128)(2,1)S(1)} %get-tuple-element.82), channel_id=1, source_target_pairs={{0,12},{1,13},{2,14},{3,15},{4,8},{5,9},{6,10},{7,11},{8,4},{9,5},... | collective-permute-start | bytes 208904 | tf_op jit(solution)/shard_map/ppermute | solution.py:331
  50.6 3.0 %collective-permute-done.18 = bf16[17,16,128]{2,1,0:T(8,128)(2,1)S(1)} collective-permute-done((bf16[17,16,128]{2,1,0:T(8,128)(2,1)S(1)}, bf16[17,16,128]{2,1,0:T(8,128)(2,1)S(1)}, u32[]{:S(2)}, u32[]{:S(2)}) %collective-permute-start.18) | collective-permute-done | bytes 69664 | tf_op jit(solution)/shard_map/ppermute | solution.py:331
  53.6 2.4 %collective-permute-done.17 = bf16[17,16,128]{2,1,0:T(8,128)(2,1)S(1)} collective-permute-done((bf16[17,16,128]{2,1,0:T(8,128)(2,1)S(1)}, bf16[17,16,128]{2,1,0:T(8,128)(2,1)S(1)}, u32[]{:S(2)}, u32[]{:S(2)}) %collective-permute-start.17) | collective-permute-done | bytes 69664 | tf_op jit(solution)/shard_map/ppermute | solution.py:331
  56.1 1.6 %collective-permute-start.19 = (bf16[2,17,16,128]{3,2,1,0:T(8,128)(2,1)S(1)}, bf16[2,17,16,128]{3,2,1,0:T(8,128)(2,1)S(1)}, u32[]{:S(2)}, u32[]{:S(2)}) collective-permute-start(bf16[2,17,16,128]{3,2,1,0:T(8,128)(2,1)S(1)} %pad_maximum_fusion.5), channel_id=1, source_target_pairs={{0,2},{1,3},{2,0},{3,1},{4,6},{5,7},{6,4},{7,5},{8,10},{9,11},{10,... | collective-permute-start | bytes 417800 | tf_op jit(solution)/shard_map/ppermute | solution.py:331
  58.2 4.4 %collective-permute-done.19 = bf16[2,17,16,128]{3,2,1,0:T(8,128)(2,1)S(1)} collective-permute-done((bf16[2,17,16,128]{3,2,1,0:T(8,128)(2,1)S(1)}, bf16[2,17,16,128]{3,2,1,0:T(8,128)(2,1)S(1)}, u32[]{:S(2)}, u32[]{:S(2)}) %collective-permute-start.19) | collective-permute-done | bytes 139296 | tf_op jit(solution)/shard_map/ppermute | solution.py:331
  62.6 2.6 %collective-permute-done.16 = bf16[2,17,16,128]{3,2,1,0:T(8,128)(2,1)S(1)} collective-permute-done((bf16[2,17,16,128]{3,2,1,0:T(8,128)(2,1)S(1)}, bf16[2,17,16,128]{3,2,1,0:T(8,128)(2,1)S(1)}, u32[]{:S(2)}, u32[]{:S(2)}) %collective-permute-start.16) | collective-permute-done | bytes 139296 | tf_op jit(solution)/shard_map/ppermute | solution.py:331
  67.7 1.8 %shard_map.94 = (bf16[65,16,128]{2,1,0:T(8,128)(2,1)S(1)}, f32[16,128]{1,0:T(8,128)S(1)}, f32[16,512]{1,0:T(8,128)S(1)}, f32[16,2048]{1,0:T(8,128)S(1)}, f32[16,128]{1,0:T(8,128)S(1)}) custom-call(bf16[4,17,16,128]{3,2,1,0:T(8,128)(2,1)S(1)} %collective-permute-done.21.panels_ref, bf16[512,2048]{1,0:T(8,128)(2,1)S(1)} %get-tuple-element.60.right_ref, ...), custom_call_target="tpu_custom_call" | custom-call | tf_op jit(solution)/shard_map/pallas_call | solution.py:303
  75.7 3.4 %collective-permute-done.24.got_ref = bf16[17,16,128]{2,1,0:T(8,128)(2,1)S(1)} collective-permute-done((bf16[17,16,128]{2,1,0:T(8,128)(2,1)S(1)}, bf16[17,16,128]{2,1,0:T(8,128)(2,1)S(1)}, u32[]{:S(2)}, u32[]{:S(2)}) %collective-permute-start.24) | collective-permute-done | bytes 69664 | tf_op jit(solution)/shard_map/ppermute | solution.py:331
  80.1 1.9 %collective-permute-start.29 = (bf16[17,16,128]{2,1,0:T(8,128)(2,1)S(1)}, bf16[17,16,128]{2,1,0:T(8,128)(2,1)S(1)}, u32[]{:S(2)}, u32[]{:S(2)}) collective-permute-start(bf16[17,16,128]{2,1,0:T(8,128)(2,1)S(1)} %get-tuple-element.106), channel_id=1, source_target_pairs={{0,12},{1,13},{2,14},{3,15},{4,8},{5,9},{6,10},{7,11},{8,4},{9,5},... | collective-permute-start | bytes 208904 | tf_op jit(solution)/shard_map/ppermute | solution.py:331
  83.5 3.7 %collective-permute-done.28.rest_1_ = bf16[17,16,128]{2,1,0:T(8,128)(2,1)S(1)} collective-permute-done((bf16[17,16,128]{2,1,0:T(8,128)(2,1)S(1)}, bf16[17,16,128]{2,1,0:T(8,128)(2,1)S(1)}, u32[]{:S(2)}, u32[]{:S(2)}) %collective-permute-start.28) | collective-permute-done | bytes 69664 | tf_op jit(solution)/shard_map/ppermute | solution.py:331
  87.7 1.9 %shard_map.103 = (f32[16,2048]{1,0:T(8,128)}, f32[16,2048]{1,0:T(8,128)}) custom-call(f32[16,2048]{1,0:T(8,128)S(1)} %get-tuple-element.91.direction_ref, f32[1,2048]{1,0:T(1,128)S(1)} %get-tuple-element.56.nugget_ref, f32[16,16,128]{2,1,0:T(8,128)S(1)} %get-tuple-element.102.keep_ref, f32[16,128]{1,0:T(8,128)S(1)} %get-tuple-element.100.pair_ref, ...), custom_call_target="tpu_custom_call" | custom-call | tf_op jit(solution)/shard_map/pallas_call | solution.py:303
  (73 shorter events, 26.9 us)
Async XLA Ops:
  1.6 9.8 %collective-permute-start = (bf16[16,16,128]{2,1,0:T(8,128)(2,1)S(1)}, bf16[16,16,128]{2,1,0:T(8,128)(2,1)S(1)}, u32[]{:S(2)}, u32[]{:S(2)}) collective-permute-start(bf16[16,16,128]{2,1,0:T(8,128)(2,1)S(1)} %get-tuple-element.57), channel_id=1, source_target_pairs={{0,4},{1,5},{2,6},{3,7},{4,0},{5,1},{6,2},{7,3},{8,12},{9,13},{10,... | collective-permute-start | bytes 196616 | tf_op jit(solution)/shard_map/ppermute | solution.py:331
  4.6 6.9 %collective-permute-start.3 = (bf16[16,16,128]{2,1,0:T(8,128)(2,1)S(1)}, bf16[16,16,128]{2,1,0:T(8,128)(2,1)S(1)}, u32[]{:S(2)}, u32[]{:S(2)}) collective-permute-start(bf16[16,16,128]{2,1,0:T(8,128)(2,1)S(1)} %get-tuple-element.57), channel_id=1, source_target_pairs={{0,12},{1,13},{2,14},{3,15},{4,8},{5,9},{6,10},{7,11},{8,4},{9,5},... | collective-permute-start | bytes 196616 | tf_op jit(solution)/shard_map/ppermute | solution.py:331
  7.1 6.4 %collective-permute-start.2 = (bf16[16,16,128]{2,1,0:T(8,128)(2,1)S(1)}, bf16[16,16,128]{2,1,0:T(8,128)(2,1)S(1)}, u32[]{:S(2)}, u32[]{:S(2)}) collective-permute-start(bf16[16,16,128]{2,1,0:T(8,128)(2,1)S(1)} %get-tuple-element.57), channel_id=1, source_target_pairs={{0,8},{1,9},{2,10},{3,11},{4,12},{5,13},{6,14},{7,15},{8,0},{9,1},... | collective-permute-start | bytes 196616 | tf_op jit(solution)/shard_map/ppermute | solution.py:331
  13.6 8.9 %collective-permute-start.5 = (bf16[4,16,16,128]{3,2,1,0:T(8,128)(2,1)S(1)}, bf16[4,16,16,128]{3,2,1,0:T(8,128)(2,1)S(1)}, u32[]{:S(2)}, u32[]{:S(2)}) collective-permute-start(bf16[4,16,16,128]{3,2,1,0:T(8,128)(2,1)S(1)} %pad_maximum_fusion.3.rest_0_), channel_id=1, source_target_pairs={{0,1},{1,0},{2,3},{3,2},{4,5},{5,4},{6,7},{7,6},{8,9},{9,8},{10,11... | collective-permute-start | bytes 786440 | tf_op jit(solution)/shard_map/ppermute | solution.py:331
  13.7 6.4 %collective-permute-start.4 = (bf16[2,16,16,128]{3,2,1,0:T(8,128)(2,1)S(1)}, bf16[2,16,16,128]{3,2,1,0:T(8,128)(2,1)S(1)}, u32[]{:S(2)}, u32[]{:S(2)}) collective-permute-start(bf16[2,16,16,128]{3,2,1,0:T(8,128)(2,1)S(1)} %pad_maximum_fusion.7), channel_id=1, source_target_pairs={{0,2},{1,3},{2,0},{3,1},{4,6},{5,7},{6,4},{7,5},{8,10},{9,11},{10,... | collective-permute-start | bytes 393224 | tf_op jit(solution)/shard_map/ppermute | solution.py:331
  15.3 7.2 %collective-permute-start.1 = (bf16[2,16,16,128]{3,2,1,0:T(8,128)(2,1)S(1)}, bf16[2,16,16,128]{3,2,1,0:T(8,128)(2,1)S(1)}, u32[]{:S(2)}, u32[]{:S(2)}) collective-permute-start(bf16[2,16,16,128]{3,2,1,0:T(8,128)(2,1)S(1)} %pad_maximum_fusion.6), channel_id=1, source_target_pairs={{0,2},{1,3},{2,0},{3,1},{4,6},{5,7},{6,4},{7,5},{8,10},{9,11},{10,... | collective-permute-start | bytes 393224 | tf_op jit(solution)/shard_map/ppermute | solution.py:331
  26.9 5.5 %collective-permute-start.8 = (bf16[64,16,128]{2,1,0:T(8,128)(2,1)S(1)}, bf16[64,16,128]{2,1,0:T(8,128)(2,1)S(1)}, u32[]{:S(2)}, u32[]{:S(2)}) collective-permute-start(bf16[64,16,128]{2,1,0:T(8,128)(2,1)S(1)} %shard_map.82), channel_id=1, source_target_pairs={{0,1},{1,0},{2,3},{3,2},{4,5},{5,4},{6,7},{7,6},{8,9},{9,8},{10,11... | collective-permute-start | bytes 786440 | tf_op jit(solution)/shard_map/ppermute | solution.py:331
  28.1 11.0 %collective-permute-start.10 = (bf16[32,16,128]{2,1,0:T(8,128)(2,1)S(1)}, bf16[32,16,128]{2,1,0:T(8,128)(2,1)S(1)}, u32[]{:S(2)}, u32[]{:S(2)}) collective-permute-start(bf16[32,16,128]{2,1,0:T(8,128)(2,1)S(1)} %get-tuple-element.77), channel_id=1, source_target_pairs={{0,2},{1,3},{2,0},{3,1},{4,6},{5,7},{6,4},{7,5},{8,10},{9,11},{10,... | collective-permute-start | bytes 393224 | tf_op jit(solution)/shard_map/ppermute | solution.py:331
  29.6 6.2 %collective-permute-start.9 = (bf16[17,16,128]{2,1,0:T(8,128)(2,1)S(1)}, bf16[17,16,128]{2,1,0:T(8,128)(2,1)S(1)}, u32[]{:S(2)}, u32[]{:S(2)}) collective-permute-start(bf16[17,16,128]{2,1,0:T(8,128)(2,1)S(1)} %get-tuple-element.71), channel_id=1, source_target_pairs={{0,2},{1,3},{2,0},{3,1},{4,6},{5,7},{6,4},{7,5},{8,10},{9,11},{10,... | collective-permute-start | bytes 208904 | tf_op jit(solution)/shard_map/ppermute | solution.py:331
  30.1 6.4 %collective-permute-start.12 = (bf16[16,16,128]{2,1,0:T(8,128)(2,1)S(1)}, bf16[16,16,128]{2,1,0:T(8,128)(2,1)S(1)}, u32[]{:S(2)}, u32[]{:S(2)}) collective-permute-start(bf16[16,16,128]{2,1,0:T(8,128)(2,1)S(1)} %get-tuple-element.80), channel_id=1, source_target_pairs={{0,2},{1,3},{2,0},{3,1},{4,6},{5,7},{6,4},{7,5},{8,10},{9,11},{10,... | collective-permute-start | bytes 196616 | tf_op jit(solution)/shard_map/ppermute | solution.py:331
  36.6 7.8 %collective-permute-start.13 = (bf16[17,16,128]{2,1,0:T(8,128)(2,1)S(1)}, bf16[17,16,128]{2,1,0:T(8,128)(2,1)S(1)}, u32[]{:S(2)}, u32[]{:S(2)}) collective-permute-start(bf16[17,16,128]{2,1,0:T(8,128)(2,1)S(1)} %shard_map.89), channel_id=1, source_target_pairs={{0,8},{1,9},{2,10},{3,11},{4,12},{5,13},{6,14},{7,15},{8,0},{9,1},... | collective-permute-start | bytes 208904 | tf_op jit(solution)/shard_map/ppermute | solution.py:331
  37.4 7.0 %collective-permute-start.14 = (bf16[17,16,128]{2,1,0:T(8,128)(2,1)S(1)}, bf16[17,16,128]{2,1,0:T(8,128)(2,1)S(1)}, u32[]{:S(2)}, u32[]{:S(2)}) collective-permute-start(bf16[17,16,128]{2,1,0:T(8,128)(2,1)S(1)} %get-tuple-element.81), channel_id=1, source_target_pairs={{0,12},{1,13},{2,14},{3,15},{4,8},{5,9},{6,10},{7,11},{8,4},{9,5},... | collective-permute-start | bytes 208904 | tf_op jit(solution)/shard_map/ppermute | solution.py:331
  39.2 5.5 %collective-permute-start.11 = (bf16[17,16,128]{2,1,0:T(8,128)(2,1)S(1)}, bf16[17,16,128]{2,1,0:T(8,128)(2,1)S(1)}, u32[]{:S(2)}, u32[]{:S(2)}) collective-permute-start(bf16[17,16,128]{2,1,0:T(8,128)(2,1)S(1)} %get-tuple-element.79), channel_id=1, source_target_pairs={{0,4},{1,5},{2,6},{3,7},{4,0},{5,1},{6,2},{7,3},{8,12},{9,13},{10,... | collective-permute-start | bytes 208904 | tf_op jit(solution)/shard_map/ppermute | solution.py:331
  47.3 6.4 %collective-permute-start.18 = (bf16[17,16,128]{2,1,0:T(8,128)(2,1)S(1)}, bf16[17,16,128]{2,1,0:T(8,128)(2,1)S(1)}, u32[]{:S(2)}, u32[]{:S(2)}) collective-permute-start(bf16[17,16,128]{2,1,0:T(8,128)(2,1)S(1)} %get-tuple-element.82), channel_id=1, source_target_pairs={{0,12},{1,13},{2,14},{3,15},{4,8},{5,9},{6,10},{7,11},{8,4},{9,5},... | collective-permute-start | bytes 208904 | tf_op jit(solution)/shard_map/ppermute | solution.py:331
  49.2 6.8 %collective-permute-start.17 = (bf16[17,16,128]{2,1,0:T(8,128)(2,1)S(1)}, bf16[17,16,128]{2,1,0:T(8,128)(2,1)S(1)}, u32[]{:S(2)}, u32[]{:S(2)}) collective-permute-start(bf16[17,16,128]{2,1,0:T(8,128)(2,1)S(1)} %get-tuple-element.82), channel_id=1, source_target_pairs={{0,8},{1,9},{2,10},{3,11},{4,12},{5,13},{6,14},{7,15},{8,0},{9,1},... | collective-permute-start | bytes 208904 | tf_op jit(solution)/shard_map/ppermute | solution.py:331
  56.0 9.3 %collective-permute-start.20 = (bf16[4,17,16,128]{3,2,1,0:T(8,128)(2,1)S(1)}, bf16[4,17,16,128]{3,2,1,0:T(8,128)(2,1)S(1)}, u32[]{:S(2)}, u32[]{:S(2)}) collective-permute-start(bf16[4,17,16,128]{3,2,1,0:T(8,128)(2,1)S(1)} %pad_maximum_fusion.1.rest_0_), channel_id=1, source_target_pairs={{0,1},{1,0},{2,3},{3,2},{4,5},{5,4},{6,7},{7,6},{8,9},{9,8},{10,11... | collective-permute-start | bytes 835592 | tf_op jit(solution)/shard_map/ppermute | solution.py:331
  56.1 6.5 %collective-permute-start.19 = (bf16[2,17,16,128]{3,2,1,0:T(8,128)(2,1)S(1)}, bf16[2,17,16,128]{3,2,1,0:T(8,128)(2,1)S(1)}, u32[]{:S(2)}, u32[]{:S(2)}) collective-permute-start(bf16[2,17,16,128]{3,2,1,0:T(8,128)(2,1)S(1)} %pad_maximum_fusion.5), channel_id=1, source_target_pairs={{0,2},{1,3},{2,0},{3,1},{4,6},{5,7},{6,4},{7,5},{8,10},{9,11},{10,... | collective-permute-start | bytes 417800 | tf_op jit(solution)/shard_map/ppermute | solution.py:331
  57.7 7.5 %collective-permute-start.16 = (bf16[2,17,16,128]{3,2,1,0:T(8,128)(2,1)S(1)}, bf16[2,17,16,128]{3,2,1,0:T(8,128)(2,1)S(1)}, u32[]{:S(2)}, u32[]{:S(2)}) collective-permute-start(bf16[2,17,16,128]{3,2,1,0:T(8,128)(2,1)S(1)} %pad_maximum_fusion.4), channel_id=1, source_target_pairs={{0,2},{1,3},{2,0},{3,1},{4,6},{5,7},{6,4},{7,5},{8,10},{9,11},{10,... | collective-permute-start | bytes 417800 | tf_op jit(solution)/shard_map/ppermute | solution.py:331
  71.4 10.7 %collective-permute-start.25 = (bf16[32,16,128]{2,1,0:T(8,128)(2,1)S(1)}, bf16[32,16,128]{2,1,0:T(8,128)(2,1)S(1)}, u32[]{:S(2)}, u32[]{:S(2)}) collective-permute-start(bf16[32,16,128]{2,1,0:T(8,128)(2,1)S(1)} %get-tuple-element.101), channel_id=1, source_target_pairs={{0,2},{1,3},{2,0},{3,1},{4,6},{5,7},{6,4},{7,5},{8,10},{9,11},{10,... | collective-permute-start | bytes 393224 | tf_op jit(solution)/shard_map/ppermute | solution.py:331
  72.9 6.2 %collective-permute-start.24 = (bf16[17,16,128]{2,1,0:T(8,128)(2,1)S(1)}, bf16[17,16,128]{2,1,0:T(8,128)(2,1)S(1)}, u32[]{:S(2)}, u32[]{:S(2)}) collective-permute-start(bf16[17,16,128]{2,1,0:T(8,128)(2,1)S(1)} %get-tuple-element.96), channel_id=1, source_target_pairs={{0,2},{1,3},{2,0},{3,1},{4,6},{5,7},{6,4},{7,5},{8,10},{9,11},{10,... | collective-permute-start | bytes 208904 | tf_op jit(solution)/shard_map/ppermute | solution.py:331
  73.4 6.4 %collective-permute-start.27 = (bf16[16,16,128]{2,1,0:T(8,128)(2,1)S(1)}, bf16[16,16,128]{2,1,0:T(8,128)(2,1)S(1)}, u32[]{:S(2)}, u32[]{:S(2)}) collective-permute-start(bf16[16,16,128]{2,1,0:T(8,128)(2,1)S(1)} %get-tuple-element.105), channel_id=1, source_target_pairs={{0,2},{1,3},{2,0},{3,1},{4,6},{5,7},{6,4},{7,5},{8,10},{9,11},{10,... | collective-permute-start | bytes 196616 | tf_op jit(solution)/shard_map/ppermute | solution.py:331
  79.9 7.3 %collective-permute-start.28 = (bf16[17,16,128]{2,1,0:T(8,128)(2,1)S(1)}, bf16[17,16,128]{2,1,0:T(8,128)(2,1)S(1)}, u32[]{:S(2)}, u32[]{:S(2)}) collective-permute-start(bf16[17,16,128]{2,1,0:T(8,128)(2,1)S(1)} %shard_map.102), channel_id=1, source_target_pairs={{0,8},{1,9},{2,10},{3,11},{4,12},{5,13},{6,14},{7,15},{8,0},{9,1},... | collective-permute-start | bytes 208904 | tf_op jit(solution)/shard_map/ppermute | solution.py:331
  80.1 7.1 %collective-permute-start.29 = (bf16[17,16,128]{2,1,0:T(8,128)(2,1)S(1)}, bf16[17,16,128]{2,1,0:T(8,128)(2,1)S(1)}, u32[]{:S(2)}, u32[]{:S(2)}) collective-permute-start(bf16[17,16,128]{2,1,0:T(8,128)(2,1)S(1)} %get-tuple-element.106), channel_id=1, source_target_pairs={{0,12},{1,13},{2,14},{3,15},{4,8},{5,9},{6,10},{7,11},{8,4},{9,5},... | collective-permute-start | bytes 208904 | tf_op jit(solution)/shard_map/ppermute | solution.py:331
  82.2 5.5 %collective-permute-start.26 = (bf16[17,16,128]{2,1,0:T(8,128)(2,1)S(1)}, bf16[17,16,128]{2,1,0:T(8,128)(2,1)S(1)}, u32[]{:S(2)}, u32[]{:S(2)}) collective-permute-start(bf16[17,16,128]{2,1,0:T(8,128)(2,1)S(1)} %get-tuple-element.104), channel_id=1, source_target_pairs={{0,4},{1,5},{2,6},{3,7},{4,0},{5,1},{6,2},{7,3},{8,12},{9,13},{10,... | collective-permute-start | bytes 208904 | tf_op jit(solution)/shard_map/ppermute | solution.py:331
  (7 other events, 16.9 us)

commit v3 on v2

v3 whole, which is shorter than its diff:
```python
import functools

import jax
import jax.numpy as jnp
from jax import lax
from jax.experimental import pallas as pl
from jax.experimental.pallas import tpu as pltpu
from jax.sharding import PartitionSpec as P

LANES = 128
F32 = jnp.float32
BF16 = jnp.bfloat16
EXACT = lax.Precision.HIGHEST
NN = (((1,), (0,)), ((), ()))
NT = (((1,), (1,)), ((), ()))


def lanes_of(block):
    return lax.broadcasted_iota(jnp.int32, block.shape, len(block.shape) - 1)


def sums_of(parts, rhs):
    rest = jnp.zeros((rhs, LANES - rhs * len(parts)), F32)
    return jnp.concatenate(parts + [rest], axis=1)


def encode(pair, rhs):
    high = pair.astype(BF16).astype(F32)
    rest = pair - high
    middle = rest.astype(BF16).astype(F32)
    low = rest - middle
    return (high + pltpu.roll(middle, 2 * rhs, 1) + pltpu.roll(low, 4 * rhs, 1)).astype(BF16)


def decode(code, rhs):
    total = code + pltpu.roll(code, LANES - 2 * rhs, 1) + pltpu.roll(code, LANES - 4 * rhs, 1)
    return jnp.where(lanes_of(total) < 2 * rhs, total, 0.0)


def second_of(pair, rhs):
    return pltpu.roll(pair, LANES - rhs, 1)


def right_divide(top, bottom, rhs):
    both = jnp.concatenate([top, bottom], axis=0)
    lane = lanes_of(both)
    both = jnp.where(lane < rhs, both, 0.0)
    one = lane[:1]
    for k in range(0, rhs, 2):
        col_0 = jnp.broadcast_to(both[:, k : k + 1], both.shape)
        col_1 = jnp.broadcast_to(both[:, k + 1 : k + 2], both.shape)
        a, b = col_0[k : k + 1], col_1[k : k + 1]
        c, d = col_0[k + 1 : k + 2], col_1[k + 1 : k + 2]
        inverse = 1.0 / (a * d - b * c)
        row_0 = jnp.where(one == k, -1.0, jnp.where(one == k + 1, 0.0, both[k : k + 1]))
        row_1 = jnp.where(one == k, 0.0, jnp.where(one == k + 1, -1.0, both[k + 1 : k + 2]))
        new_0 = (d * row_0 - b * row_1) * inverse
        new_1 = (a * row_1 - c * row_0) * inverse
        both = jnp.where((lane == k) | (lane == k + 1), 0.0, both) - col_0 * new_0 - col_1 * new_1
    return both[rhs:, :]


def left_multiply(square, block, rhs):
    return lax.dot_general(square[:, :rhs], block, NN, precision=EXACT, preferred_element_type=F32)


def gram(former, latter):
    return lax.dot_general(former, latter, NT, precision=EXACT, preferred_element_type=F32)


def rows_of(ref, chunks):
    panels, _, rhs, lanes = ref.shape
    return jnp.concatenate([ref[:, c].reshape(panels * rhs, lanes) for c in range(chunks)], axis=1)


def store_message(message_ref, block, rhs, at=0):
    for c in range(block.shape[1] // LANES):
        message_ref[at + c] = block[:, c * LANES : (c + 1) * LANES].astype(message_ref.dtype)


def far_terms(total, panels, factors, places, bases, rhs, chunks):
    rows = jnp.concatenate([rows_of(ref, chunks) for ref in panels], axis=0)
    far = [lax.dot_general(rows, ref[...], NT, preferred_element_type=F32) for ref in factors]
    far = jnp.concatenate(far, axis=1)
    at = 0
    for base, ref in zip(bases, panels):
        for i in range(ref.shape[0]):
            total = total + jnp.where(places == base + i, far[at : at + rhs], 0.0)
            at += rhs
    return total


def codes_of(panels_ref, chunks):
    count, held = panels_ref.shape[:2]
    code = jnp.zeros(panels_ref.shape[2:], F32)
    for i in range(count if held > chunks else 0):
        code = code + panels_ref[i, chunks].astype(F32)
    return code


def spread_terms(projected, factors, places, wanted, store, rhs, chunks, extra=None):
    masked = [jnp.where(places == place, projected, 0.0).astype(BF16) for place in wanted]
    masked = jnp.concatenate(masked, axis=0)
    width = factors[0].shape[0]
    step = 2 * LANES
    for block in range(chunks // 2):
        at = slice(block * step, (block + 1) * step)
        moved = sum(
            lax.dot_general(
                masked[:, i * width : (i + 1) * width], ref[:, at], NN, preferred_element_type=F32
            )
            for i, ref in enumerate(factors)
        )
        for i in range(len(wanted)):
            for b in range(2):
                piece = moved[i * rhs : (i + 1) * rhs, b * LANES : (b + 1) * LANES]
                if i == 0 and extra is not None:
                    place = block * step + b * LANES
                    piece = piece + extra[:, place : place + LANES]
                store(i, 2 * block + b, piece)


def open_kernel(rhs, right_side_hbm, message_ref, right_side_ref, sem):
    copy = pltpu.make_async_copy(right_side_hbm, right_side_ref, sem)
    copy.start()
    copy.wait()
    store_message(message_ref, right_side_ref[...], rhs)


def load_kernel(
    rhs, rank, own_ref, column_hbm, live_ref, nugget_hbm, left_hbm,
    nugget_ref, left_ref, named_ref, near_ref, sums_ref,
    column_ref, column_sem, nugget_sem, left_sem,
):
    copies = [
        pltpu.make_async_copy(column_hbm, column_ref, column_sem),
        pltpu.make_async_copy(nugget_hbm, nugget_ref, nugget_sem),
        pltpu.make_async_copy(left_hbm, left_ref, left_sem),
    ]
    for copy in copies:
        copy.start()
    own = own_ref[...]
    for copy in copies[:2]:
        copy.wait()
    slot_of = lax.broadcasted_iota(jnp.int32, (1, named_ref.shape[1]), 1) // rank
    named = jnp.full(slot_of.shape, -1, jnp.int32)
    for s in range(column_ref.shape[0]):
        named = jnp.where(slot_of == s, jnp.where(s < live_ref[0], column_ref[s], -1), named)
    named_ref[...] = jnp.broadcast_to(named, named_ref.shape)
    sums_ref[...] = sums_of([gram(own * nugget_ref[...], own), gram(own, own)], rhs)
    copies[2].wait()
    near = lax.dot_general(own.astype(BF16), left_ref[...], NT, preferred_element_type=F32)
    near_ref[...] = jnp.where(named >= 0, near, 0.0)


def load_add_kernel(
    rhs, chunks, place_of, base, held_ref, near_ref, named_ref, other_named_ref, right_hbm, other_ref,
    part_ref, places_ref, right_ref, right_sem,
):
    copy = pltpu.make_async_copy(right_hbm, right_ref, right_sem)
    copy.start()
    named = jnp.concatenate([named_ref[...], other_named_ref[...]], axis=1)
    offset = named ^ lax.axis_index("row")
    places = jnp.where((named >= 0) & ((offset & 1) == 0), place_of(offset), -1)
    places = jnp.concatenate([places] * (rhs // places.shape[0]), axis=0)
    places_ref[...] = places
    near = near_ref[...]
    total = jnp.concatenate([near, jnp.zeros(near.shape, F32)], axis=1)
    copy.wait()
    part_ref[...] = far_terms(total, [held_ref], (right_ref, other_ref), places, [base], rhs, chunks)


def near_add_kernel(
    rhs, chunks, base, held_ref, own_ref, right_side_ref, nugget_ref, left_ref, named_ref, places_ref,
    right_ref, other_ref, part_ref, sums_ref,
):
    own = own_ref[...]
    near = lax.dot_general(own.astype(BF16), left_ref[...], NT, preferred_element_type=F32)
    near = jnp.where(named_ref[:1] >= 0, near, 0.0)
    total = jnp.concatenate([near, jnp.zeros(near.shape, F32)], axis=1)
    part_ref[...] = far_terms(total, [held_ref], (right_ref, other_ref), places_ref[...], [base], rhs, chunks)
    weighted = own * nugget_ref[...]
    code = codes_of(held_ref, chunks)
    none = jnp.zeros((rhs, rhs), F32)
    sums_ref[...] = decode(code, rhs) + sums_of([none, gram(weighted, own), gram(right_side_ref[...], weighted)], rhs)


def add_kernel(
    rhs, chunks, bases, beside_ref, late_ref, right_ref, other_ref, places_ref, part_ref, sums_ref, message_ref
):
    panels = (beside_ref, late_ref)
    total = far_terms(part_ref[...], panels, (right_ref, other_ref), places_ref[...], bases, rhs, chunks)
    width = total.shape[1]
    message_ref[:, :width] = total
    message_ref[:, width:] = sums_ref[...] + decode(codes_of(beside_ref, chunks) + codes_of(late_ref, chunks), rhs)


def both_cores(message_ref, got_ref):
    half = (message_ref.shape[1] - LANES) // 2
    own = message_ref[:, :half] + got_ref[:, half : 2 * half]
    other = message_ref[:, half : 2 * half] + got_ref[:, :half]
    sums = message_ref[:, 2 * half :] + got_ref[:, 2 * half :]
    return jnp.concatenate([own, other], axis=1), sums


def symmetric_product(projected):
    rounded = projected.astype(BF16).astype(F32)
    first = gram(projected, rounded)
    return 0.5 * (first + first.T)


def send_terms(send_ref, projected, factors, places, wanted, pair, rhs, chunks):
    def store(i, c, piece):
        send_ref[i * chunks + c] = piece.astype(BF16)

    spread_terms(projected, factors, places, wanted, store, rhs, chunks)
    send_ref[len(wanted) * chunks] = encode(pair, rhs)


def first_kernel(
    rhs, chunks, wanted, message_ref, got_ref, right_ref, other_ref, places_ref,
    send_ref, pair_ref, projected_ref, sums_ref,
):
    projected, sums = both_cores(message_ref, got_ref)
    projected_ref[...] = projected
    sums_ref[...] = sums
    pair = sums + sums_of([symmetric_product(projected)], rhs)
    pair_ref[...] = pair
    send_terms(send_ref, projected, (right_ref, other_ref), places_ref[...], wanted, pair, rhs, chunks)


def second_kernel(
    rhs, chunks, wanted, message_ref, got_ref, right_ref, other_ref, places_ref,
    gram_ref, weighted_ref, earlier_ref,
    send_ref, pair_ref, projected_ref, next_gram_ref, mix_ref,
):
    projected, sums = both_cores(message_ref, got_ref)
    next_gram_ref[...] = sums
    mix = right_divide(gram_ref[...], sums, rhs)
    projected = projected + left_multiply(mix, earlier_ref[...], rhs)
    projected_ref[...] = projected
    weighted = left_multiply(mix, jnp.concatenate([sums[:, 2 * rhs : 3 * rhs], weighted_ref[:, :rhs]], axis=1), rhs)
    mixed = weighted[:, :rhs]
    curvature = sums[:, rhs : 2 * rhs] + mixed + mixed.T + gram(weighted[:, rhs:], mix[:, :rhs])
    pair = sums_of([curvature + symmetric_product(projected)], rhs)
    pair_ref[...] = pair
    send_terms(send_ref, projected, (right_ref, other_ref), places_ref[...], wanted, pair, rhs, chunks)
    mix_ref[...] = mix


def spread_kernel(
    rhs, chunks, wanted, projected_ref, left_ref, right_ref, other_ref, places_ref, keep_ref, beside_ref
):
    projected = projected_ref[...]
    kept = keep_ref.shape[0] // chunks

    def store(i, c, piece):
        if i < kept:
            keep_ref[i * chunks + c] = piece
        else:
            beside_ref[(i - kept) * chunks + c] = piece.astype(BF16)

    own = projected[:, : projected.shape[1] // 2].astype(BF16)
    own = lax.dot_general(own, left_ref[...], NN, preferred_element_type=F32)
    spread_terms(projected, (right_ref, other_ref), places_ref[...], wanted, store, rhs, chunks, own)


def direction_kernel(rhs, mix_ref, right_side_ref, residual_ref, direction_ref):
    direction_ref[...] = residual_ref[...] + left_multiply(mix_ref[...], right_side_ref[...], rhs)


def join_kernel(keep_ref, got_ref, sum_ref):
    sum_ref[...] = keep_ref[...] + got_ref[...].astype(F32)


def part_kernel(rhs, keep_ref, pair_ref, got_ref, total_ref, *sends):
    size = sends[0].shape[0] - 1
    total = pair_ref[...] + decode(got_ref[got_ref.shape[0] - 1].astype(F32), rhs)
    total_ref[...] = total
    code = encode(total, rhs)
    for i, send in enumerate(sends):
        at = i * size
        send[:size] = (keep_ref[at + size : at + 2 * size] + got_ref[at : at + size].astype(F32)).astype(BF16)
        send[size] = code


def message_kernel(rhs, panel_ref, pair_ref, message_ref):
    message_ref[: panel_ref.shape[0]] = panel_ref[...].astype(BF16)
    message_ref[panel_ref.shape[0]] = encode(pair_ref[...], rhs)


def code_kernel(rhs, pair_ref, code_ref):
    code_ref[...] = encode(pair_ref[...], rhs)


def pair_kernel(rhs, pair_ref, got_ref, total_ref):
    total_ref[...] = pair_ref[...] + decode(got_ref[...].astype(F32), rhs)


def gathered_product(keep_ref, plain_ref, pair_ref, got, direction, nugget, rhs, chunks):
    total = keep_ref[:chunks]
    total = total + plain_ref[...].astype(F32)
    code = jnp.zeros(pair_ref.shape, F32)
    for ref in got:
        total = total + ref[:chunks].astype(F32)
        code = code + ref[chunks].astype(F32)
    applied = nugget * direction + jnp.concatenate([total[c] for c in range(chunks)], axis=1)
    return applied, pair_ref[...] + decode(code, rhs)


def middle_kernel(rhs, chunks, direction_ref, nugget_ref, keep_ref, plain_ref, pair_ref, *rest):
    got, (message_ref, residual_ref, solution_ref, gram_ref) = rest[:-4], rest[-4:]
    direction = direction_ref[...]
    applied, pair = gathered_product(keep_ref, plain_ref, pair_ref, got, direction, nugget_ref[...], rhs, chunks)
    first_gram = second_of(pair, rhs)
    gram_ref[...] = first_gram
    step = right_divide(pair, first_gram, rhs)
    residual = direction - left_multiply(step, applied, rhs)
    residual_ref[...] = residual
    store_message(message_ref, residual, rhs)
    message_ref[chunks] = encode(sums_of([gram(residual, residual)], rhs), rhs)
    solution_ref[...] = left_multiply(step, direction, rhs)


def last_kernel(rhs, chunks, direction_ref, nugget_ref, keep_ref, plain_ref, pair_ref, gram_ref, *rest):
    got, (residual_ref, solution_ref, out_solution_ref, out_residual_ref) = rest[:-4], rest[-4:]
    direction = direction_ref[...]
    applied, pair = gathered_product(keep_ref, plain_ref, pair_ref, got, direction, nugget_ref[...], rhs, chunks)
    step = right_divide(pair, gram_ref[...], rhs)
    out_solution_ref[...] = solution_ref[...] + left_multiply(step, direction, rhs)
    out_residual_ref[...] = residual_ref[...] - left_multiply(step, applied, rhs)


def call(kernel, outs, *args, far=(), scalars=(), fixed=(), scratch=()):
    whole = pl.BlockSpec(memory_space=pltpu.VMEM)
    spaces = {i: pltpu.HBM for i in far} | {i: pltpu.SMEM for i in scalars}
    return pl.pallas_call(
        kernel,
        out_shape=[
            pltpu.VMEM(shape, dtype) if i in fixed else jax.ShapeDtypeStruct(shape, dtype)
            for i, (shape, dtype) in enumerate(outs)
        ],
        in_specs=[pl.BlockSpec(memory_space=spaces[i]) if i in spaces else whole for i in range(len(args))],
        out_specs=[whole] * len(outs),
        scratch_shapes=list(scratch),
        cost_estimate=pl.CostEstimate(flops=0, bytes_accessed=0, transcendentals=0),
        compiler_params=pltpu.CompilerParams(vmem_limit_bytes=32 * 1024 * 1024),
    )(*args)


def after(value, *others):
    return lax.optimization_barrier((value, *others))[0]


def shards(right_sides, nugget, left_factors, right_factors, tile_column, live_slots):
    devices = lax.axis_size("row")
    bits = devices.bit_length() - 1
    low_bits = bits - 2
    slots, rank, width = left_factors.shape
    rhs = right_sides.shape[0]
    chunks = width // LANES
    part = functools.partial

    def swap(array, offset):
        return lax.ppermute(array, "row", [(i, i ^ offset) for i in range(devices)])

    order = (0, 3, 2, 1)
    groups = []
    for k in order:
        group = [k << low_bits]
        for b in range(low_bits - 1, 1, -1):
            group = group + [o | (1 << b) for o in group]
        groups.append(group)
    m = len(groups[0])
    held_offsets = sum(groups, [])
    offsets = held_offsets + [o | 2 for o in held_offsets]
    held, late = 0, 4 * m

    def place_of(offset):
        place = ((4 - (offset >> low_bits)) & 3) * m
        for b in range(low_bits - 1, 1, -1):
            place = place + (((offset >> b) & 1) << (low_bits - 1 - b))
        return place + ((offset >> 1) & 1) * late

    assert [place_of(o) for o in offsets] == list(range(devices // 2))
    stay, go = tuple(range(late + m)), tuple(range(late + m, 2 * late))

    small = ((rhs, LANES), F32)
    panel = ((rhs, width), F32)
    row_block = ((rhs, slots * rank), F32)
    two_rows = ((rhs, 2 * slots * rank), F32)
    core_message = ((rhs, 2 * slots * rank + LANES), F32)
    factor = ((slots * rank, width), BF16)
    semaphore = pltpu.SemaphoreType.DMA

    def plain(count):
        return ((count * chunks, rhs, LANES), BF16)

    def coded(count):
        return ((count * chunks + 1, rhs, LANES), BF16)

    def kept(count):
        return ((count * chunks, rhs, LANES), F32)

    def gather(message, first_terms, *early):
        mine = [message[None]] + [swap(message, k << low_bits)[None] for k in order[1:]]
        for b in range(low_bits - 1, 1, -1):
            mine = [jnp.concatenate([g, swap(g, 1 << b)]) for g in mine]
        beside = swap(mine[0], 2)
        late_panels = swap(after(jnp.concatenate(mine[1:]), beside, *early), 2)
        terms, sums, factors, places = first_terms(jnp.concatenate(mine))
        late_panels = after(late_panels, terms)
        (message,) = call(
            part(add_kernel, rhs, chunks, (late, late + m)),
            [core_message],
            beside, late_panels, *factors, places, terms, sums,
        )
        return message, swap(message, 1), factors, places

    def reduce(send, pair, projected, left, factors, places, *early):
        got = swap(send, 2)
        keep, beside = call(
            part(spread_kernel, rhs, chunks, stay),
            [kept(4 * m), plain(m)],
            projected, left, *factors, places,
        )
        if m == 1:
            pair, *sends = call(
                part(part_kernel, rhs), [small] + [coded(1)] * 3, keep, pair, after(got, keep, *early)
            )
            got = [swap(x, k << low_bits) for x, k in zip(sends, order[1:])]
            return keep, swap(beside, 2), pair, got
        (pair,) = call(part(pair_kernel, rhs), [small], pair, got[-1])
        (keep,) = call(join_kernel, [kept(4 * m)], keep, jnp.concatenate([swap(beside, 2), got[:-1]]))
        size = m * chunks
        four = [keep[i * size : (i + 1) * size] for i in range(4)]
        for b in range(2, low_bits):
            (code,) = call(part(code_kernel, rhs), [((rhs, LANES), BF16)], pair)
            (pair,) = call(part(pair_kernel, rhs), [small], pair, swap(code, 1 << b))
            half = four[0].shape[0] // 2
            four = [x[:half] + swap(x[half:].astype(BF16), 1 << b).astype(F32) for x in four]
        sends = [call(part(message_kernel, rhs), [coded(1)], x, pair)[0] for x in four[1:]]
        nothing = jnp.zeros(*plain(1))
        return four[0], nothing, pair, [swap(x, k << low_bits) for x, k in zip(sends, order[1:])]

    def in_hbm(array):
        return pltpu.with_memory_space_constraint(array, pltpu.HBM)

    message, right_sides = call(
        part(open_kernel, rhs), [plain(1), panel], in_hbm(right_sides), far=(0,), fixed=(1,), scratch=[semaphore]
    )
    right = right_factors.reshape(slots * rank, width)
    other = swap(right, 1)
    named_shape = ((8, slots * rank), jnp.int32)
    nugget, left, named, near, sums = call(
        part(load_kernel, rhs, rank),
        [((1, width), F32), factor, named_shape, row_block, small],
        right_sides, in_hbm(tile_column.reshape(slots)), live_slots, in_hbm(nugget[None, :]),
        in_hbm(left_factors.reshape(slots * rank, width)),
        far=(1, 3, 4), scalars=(2,), fixed=(0, 1), scratch=[pltpu.SMEM((slots,), jnp.int32)] + [semaphore] * 3,
    )
    other_named = swap(named, 1)

    def loading(mine):
        terms, places, here = call(
            part(load_add_kernel, rhs, chunks, place_of, held),
            [two_rows, ((rhs, 2 * slots * rank), jnp.int32), factor],
            mine, near, named, other_named, in_hbm(right), other,
            far=(4,), fixed=(2,), scratch=[semaphore],
        )
        return terms, sums, (here, other), places

    message, got, factors, places = gather(message, loading, near)
    send, pair, earlier, weighted = call(
        part(first_kernel, rhs, chunks, go),
        [coded(3 * m), small, two_rows, small],
        message, got, *factors, places,
    )
    mine, beside, pair, got = reduce(send, pair, earlier, left, factors, places)
    message, residual, solution, first_gram = call(
        part(middle_kernel, rhs, chunks),
        [coded(1), panel, panel, small],
        right_sides, nugget, mine, beside, pair, *got,
    )

    def loaded(mine):
        terms, sums = call(
            part(near_add_kernel, rhs, chunks, held),
            [two_rows, small],
            mine, residual, right_sides, nugget, left, named, places, *factors,
        )
        return terms, sums, factors, places

    message, got, _, _ = gather(message, loaded)
    send, pair, projected, next_gram, mix = call(
        part(second_kernel, rhs, chunks, go),
        [coded(3 * m), small, two_rows, small, small],
        message, got, *factors, places, first_gram, weighted, earlier,
    )
    (direction,) = call(part(direction_kernel, rhs), [panel], mix, right_sides, residual)
    mine, beside, pair, got = reduce(send, pair, projected, left, factors, places, direction)
    return tuple(
        call(
            part(last_kernel, rhs, chunks),
            [panel, panel],
            direction, nugget, mine, beside, pair, next_gram, *got, residual, solution,
        )
    )


def solution(mesh):
    return jax.shard_map(
        shards,
        mesh=mesh,
        in_specs=(
            P(None, ("groups", "row")),
            P(("groups", "row")),
            P(("groups", "row"), None, None),
            P(("groups", "row"), None, None),
            P(("groups", "row"), None),
            P(("groups", "row")),
        ),
        out_specs=(P(None, ("groups", "row")), P(None, ("groups", "row"))),
        check_vma=False,
    )
```

time: 89.8 us -> 78.7 us (0.88)
  waiting for transfers between devices: 39.1 us -> 25.5 us
  starting transfers between devices: 29.1 us -> 31 us
  Pallas kernels: 19 us -> 20.4 us
    ppermute x30 -> x24, waiting for transfers between devices: 39.1 us -> 25.5 us  [swap(): return lax.ppermute(array, 'row', [(i, i ^ offset) for i in range(devices)])]
    ppermute x30 -> x24, starting transfers between devices: 29.1 us -> 31 us  [swap(): return lax.ppermute(array, 'row', [(i, i ^ offset) for i in range(devices)])]
    pallas_call x27 -> x15, Pallas kernels: 19 us -> 20.4 us  [call(): pl.pallas_call(kernel, out_shape=[pltpu.VMEM(shape, dtype) if i in fixed...]
  transfers between devices with their start and end apart: 30 -> 24, of which waited for: 19 -> 12; matrix products, arithmetic and copies ran while one was open for 0% -> 0% of each run, Pallas kernels for 11% -> 14%
where the time goes in v3:
time: 78.7 us; the launch traced here: 78.5 us
  starting transfers between devices  31 us (39%)
  waiting for transfers between devices  25.5 us (32%)
  Pallas kernels  20.4 us (26%)
  between operations  1.42 us (2%)
    ppermute x24, starting transfers between devices, swap(): return lax.ppermute(array, 'row', [(i, i ^ offset) for i in range(devices)])  31 us
    ppermute x24, waiting for transfers between devices, swap(): return lax.ppermute(array, 'row', [(i, i ^ offset) for i in range(devices)])  25.5 us
    pallas_call x15, Pallas kernels, call(): pl.pallas_call(kernel, out_shape=[pltpu.VMEM(shape, dtype) if i in fixed...  20.4 us
  transfers between devices with their start and end apart: 24, of which 12 were waited for; matrix products, arithmetic and copies ran while one was open for 0% of the time, Pallas kernels for 14%

profile of v3, /device:TPU:0, one launch (start us, length us, event | category | flops | bytes accessed | tf_op | source)
XLA Modules:
  0.0 78.5 jit_solution(3488178299224218025)
XLA Ops:
  2.1 2.7 %collective-permute-start.3 = (bf16[16,16,128]{2,1,0:T(8,128)(2,1)S(1)}, bf16[16,16,128]{2,1,0:T(8,128)(2,1)S(1)}, u32[]{:S(2)}, u32[]{:S(2)}) collective-permute-start(bf16[16,16,128]{2,1,0:T(8,128)(2,1)S(1)} %get-tuple-element.47), channel_id=1, source_target_pairs={{0,4},{1,5},{2,6},{3,7},{4,0},{5,1},{6,2},{7,3},{8,12},{9,13},{10,... | collective-permute-start | bytes 196616 | tf_op jit(solution)/shard_map/ppermute | solution.py:365
  4.7 2.6 %collective-permute-start.2 = (bf16[16,16,128]{2,1,0:T(8,128)(2,1)S(1)}, bf16[16,16,128]{2,1,0:T(8,128)(2,1)S(1)}, u32[]{:S(2)}, u32[]{:S(2)}) collective-permute-start(bf16[16,16,128]{2,1,0:T(8,128)(2,1)S(1)} %get-tuple-element.47), channel_id=1, source_target_pairs={{0,8},{1,9},{2,10},{3,11},{4,12},{5,13},{6,14},{7,15},{8,0},{9,1},... | collective-permute-start | bytes 196616 | tf_op jit(solution)/shard_map/ppermute | solution.py:365
  7.3 1.7 %collective-permute-start = (bf16[1,16,16,128]{3,2,1,0:T(8,128)(2,1)S(1)}, bf16[1,16,16,128]{3,2,1,0:T(8,128)(2,1)S(1)}, u32[]{:S(2)}, u32[]{:S(2)}) collective-permute-start(bf16[1,16,16,128]{3,2,1,0:T(8,128)(2,1)S(1)} %bitcast.14), channel_id=1, source_target_pairs={{0,2},{1,3},{2,0},{3,1},{4,6},{5,7},{6,4},{7,5},{8,10},{9,11},{10,... | collective-permute-start | bytes 196616 | tf_op jit(solution)/shard_map/ppermute | solution.py:365
  9.7 2.3 %shard_map.78 = (f32[1,2048]{1,0:T(1,128)S(1)}, bf16[512,2048]{1,0:T(8,128)(2,1)S(1)}, s32[8,512]{1,0:T(8,128)S(1)}, f32[16,512]{1,0:T(8,128)S(1)}, f32[16,128]{1,0:T(8,128)S(1)}) custom-call(f32[16,2048]{1,0:T(8,128)S(1)} %get-tuple-element.45.own_ref.direction_ref.right_side_ref, s32[32]{0:T(128)} %bitcast.32, s32[1]{0:T(128)S(6)} %copy.8.live_ref, ...), custom_call_target="tpu_custom_call" | custom-call | tf_op jit(solution)/shard_map/pallas_call | solution.py:337
  13.5 1.6 %collective-permute-start.4 = (bf16[3,16,16,128]{3,2,1,0:T(8,128)(2,1)S(1)}, bf16[3,16,16,128]{3,2,1,0:T(8,128)(2,1)S(1)}, u32[]{:S(2)}, u32[]{:S(2)}) collective-permute-start(bf16[3,16,16,128]{3,2,1,0:T(8,128)(2,1)S(1)} %pad_maximum_fusion.3), channel_id=1, source_target_pairs={{0,2},{1,3},{2,0},{3,1},{4,6},{5,7},{6,4},{7,5},{8,10},{9,11},{10,... | collective-permute-start | bytes 589832 | tf_op jit(solution)/shard_map/ppermute | solution.py:365
  16.2 3.0 %shard_map.79 = (f32[16,1024]{1,0:T(8,128)S(1)}, s32[16,1024]{1,0:T(8,128)S(1)}, bf16[512,2048]{1,0:T(8,128)(2,1)S(1)}) custom-call(bf16[4,16,16,128]{3,2,1,0:T(8,128)(2,1)S(1)} %pad_maximum_fusion.1.held_ref, f32[16,512]{1,0:T(8,128)S(1)} %get-tuple-element.48.near_ref, s32[8,512]{1,0:T(8,128)S(1)} %get-tuple-element.50.named_ref, ...), custom_call_target="tpu_custom_call" | custom-call | tf_op jit(solution)/shard_map/pallas_call | solution.py:337
  22.8 1.5 %collective-permute-start.9 = (bf16[49,16,128]{2,1,0:T(8,128)(2,1)S(1)}, bf16[49,16,128]{2,1,0:T(8,128)(2,1)S(1)}, u32[]{:S(2)}, u32[]{:S(2)}) collective-permute-start(bf16[49,16,128]{2,1,0:T(8,128)(2,1)S(1)} %get-tuple-element.61), channel_id=1, source_target_pairs={{0,2},{1,3},{2,0},{3,1},{4,6},{5,7},{6,4},{7,5},{8,10},{9,11},{10,... | collective-permute-start | bytes 602120 | tf_op jit(solution)/shard_map/ppermute | solution.py:365
  25.5 4.5 %collective-permute-done.9.got_ref = bf16[49,16,128]{2,1,0:T(8,128)(2,1)S(1)} collective-permute-done((bf16[49,16,128]{2,1,0:T(8,128)(2,1)S(1)}, bf16[49,16,128]{2,1,0:T(8,128)(2,1)S(1)}, u32[]{:S(2)}, u32[]{:S(2)}) %collective-permute-start.9) | collective-permute-done | bytes 200736 | tf_op jit(solution)/shard_map/ppermute | solution.py:365
  30.1 2.7 %collective-permute-start.10 = (bf16[17,16,128]{2,1,0:T(8,128)(2,1)S(1)}, bf16[17,16,128]{2,1,0:T(8,128)(2,1)S(1)}, u32[]{:S(2)}, u32[]{:S(2)}) collective-permute-start(bf16[17,16,128]{2,1,0:T(8,128)(2,1)S(1)} %get-tuple-element.64), channel_id=1, source_target_pairs={{0,12},{1,13},{2,14},{3,15},{4,8},{5,9},{6,10},{7,11},{8,4},{9,5},... | collective-permute-start | bytes 208904 | tf_op jit(solution)/shard_map/ppermute | solution.py:365
  36.0 2.8 %collective-permute-done.8.plain_ref = bf16[16,16,128]{2,1,0:T(8,128)(2,1)S(1)} collective-permute-done((bf16[16,16,128]{2,1,0:T(8,128)(2,1)S(1)}, bf16[16,16,128]{2,1,0:T(8,128)(2,1)S(1)}, u32[]{:S(2)}, u32[]{:S(2)}) %collective-permute-start.8) | collective-permute-done | bytes 65568 | tf_op jit(solution)/shard_map/ppermute | solution.py:365
  39.5 1.5 %shard_map.84 = (bf16[17,16,128]{2,1,0:T(8,128)(2,1)S(1)}, f32[16,2048]{1,0:T(8,128)S(1)}, f32[16,2048]{1,0:T(8,128)S(1)}, f32[16,128]{1,0:T(8,128)S(1)}) custom-call(f32[16,2048]{1,0:T(8,128)S(1)} %get-tuple-element.45.own_ref.direction_ref.right_side_ref, f32[1,2048]{1,0:T(1,128)S(1)} %get-tuple-element.46.nugget_ref, ...), custom_call_target="tpu_custom_call" | custom-call | tf_op jit(solution)/shard_map/pallas_call | solution.py:337
  41.5 2.4 %collective-permute-start.15 = (bf16[17,16,128]{2,1,0:T(8,128)(2,1)S(1)}, bf16[17,16,128]{2,1,0:T(8,128)(2,1)S(1)}, u32[]{:S(2)}, u32[]{:S(2)}) collective-permute-start(bf16[17,16,128]{2,1,0:T(8,128)(2,1)S(1)} %get-tuple-element.67), channel_id=1, source_target_pairs={{0,8},{1,9},{2,10},{3,11},{4,12},{5,13},{6,14},{7,15},{8,0},{9,1},... | collective-permute-start | bytes 208904 | tf_op jit(solution)/shard_map/ppermute | solution.py:365
  43.8 1.6 %collective-permute-start.14 = (bf16[17,16,128]{2,1,0:T(8,128)(2,1)S(1)}, bf16[17,16,128]{2,1,0:T(8,128)(2,1)S(1)}, u32[]{:S(2)}, u32[]{:S(2)}) collective-permute-start(bf16[17,16,128]{2,1,0:T(8,128)(2,1)S(1)} %get-tuple-element.67), channel_id=1, source_target_pairs={{0,12},{1,13},{2,14},{3,15},{4,8},{5,9},{6,10},{7,11},{8,4},{9,5},... | collective-permute-start | bytes 208904 | tf_op jit(solution)/shard_map/ppermute | solution.py:365
  45.4 1.5 %collective-permute-start.13 = (bf16[1,17,16,128]{3,2,1,0:T(8,128)(2,1)S(1)}, bf16[1,17,16,128]{3,2,1,0:T(8,128)(2,1)S(1)}, u32[]{:S(2)}, u32[]{:S(2)}) collective-permute-start(bf16[1,17,16,128]{3,2,1,0:T(8,128)(2,1)S(1)} %bitcast.12), channel_id=1, source_target_pairs={{0,2},{1,3},{2,0},{3,1},{4,6},{5,7},{6,4},{7,5},{8,10},{9,11},{10,... | collective-permute-start | bytes 208904 | tf_op jit(solution)/shard_map/ppermute | solution.py:365
  46.9 1.6 %collective-permute-done.15 = bf16[17,16,128]{2,1,0:T(8,128)(2,1)S(1)} collective-permute-done((bf16[17,16,128]{2,1,0:T(8,128)(2,1)S(1)}, bf16[17,16,128]{2,1,0:T(8,128)(2,1)S(1)}, u32[]{:S(2)}, u32[]{:S(2)}) %collective-permute-start.15) | collective-permute-done | bytes 69664 | tf_op jit(solution)/shard_map/ppermute | solution.py:365
  48.5 1.5 %collective-permute-done.14 = bf16[17,16,128]{2,1,0:T(8,128)(2,1)S(1)} collective-permute-done((bf16[17,16,128]{2,1,0:T(8,128)(2,1)S(1)}, bf16[17,16,128]{2,1,0:T(8,128)(2,1)S(1)}, u32[]{:S(2)}, u32[]{:S(2)}) %collective-permute-start.14) | collective-permute-done | bytes 69664 | tf_op jit(solution)/shard_map/ppermute | solution.py:365
  51.4 2.3 %shard_map.85 = (f32[16,1024]{1,0:T(8,128)S(1)}, f32[16,128]{1,0:T(8,128)S(1)}) custom-call(bf16[4,17,16,128]{3,2,1,0:T(8,128)(2,1)S(1)} %pad_maximum_fusion.held_ref, f32[16,2048]{1,0:T(8,128)S(1)} %get-tuple-element.69.own_ref.residual_ref.rest_3_, f32[16,2048]{1,0:T(8,128)S(1)} %get-tuple-element.45.own_ref.direction_ref.right_side_ref, ...), custom_call_target="tpu_custom_call" | custom-call | tf_op jit(solution)/shard_map/pallas_call | solution.py:337
  53.7 2.2 %collective-permute-done.17.late_ref = bf16[3,17,16,128]{3,2,1,0:T(8,128)(2,1)S(1)} collective-permute-done((bf16[3,17,16,128]{3,2,1,0:T(8,128)(2,1)S(1)}, bf16[3,17,16,128]{3,2,1,0:T(8,128)(2,1)S(1)}, u32[]{:S(2)}, u32[]{:S(2)}) %collective-permute-start.17) | collective-permute-done | bytes 208928 | tf_op jit(solution)/shard_map/ppermute | solution.py:365
  58.6 2.0 %shard_map.87 = (bf16[49,16,128]{2,1,0:T(8,128)(2,1)S(1)}, f32[16,128]{1,0:T(8,128)S(1)}, f32[16,1024]{1,0:T(8,128)S(1)}, f32[16,128]{1,0:T(8,128)S(1)}, f32[16,128]{1,0:T(8,128)S(1)}) custom-call(f32[16,1152]{1,0:T(8,128)S(1)} %shard_map.86.message_ref, f32[16,1152]{1,0:T(8,128)S(1)} %collective-permute-done.18.got_ref, ...), custom_call_target="tpu_custom_call" | custom-call | tf_op jit(solution)/shard_map/pallas_call | solution.py:337
  63.3 4.4 %collective-permute-done.20.got_ref = bf16[49,16,128]{2,1,0:T(8,128)(2,1)S(1)} collective-permute-done((bf16[49,16,128]{2,1,0:T(8,128)(2,1)S(1)}, bf16[49,16,128]{2,1,0:T(8,128)(2,1)S(1)}, u32[]{:S(2)}, u32[]{:S(2)}) %collective-permute-start.20) | collective-permute-done | bytes 200736 | tf_op jit(solution)/shard_map/ppermute | solution.py:365
  67.9 1.9 %collective-permute-start.21 = (bf16[17,16,128]{2,1,0:T(8,128)(2,1)S(1)}, bf16[17,16,128]{2,1,0:T(8,128)(2,1)S(1)}, u32[]{:S(2)}, u32[]{:S(2)}) collective-permute-start(bf16[17,16,128]{2,1,0:T(8,128)(2,1)S(1)} %get-tuple-element.84), channel_id=1, source_target_pairs={{0,12},{1,13},{2,14},{3,15},{4,8},{5,9},{6,10},{7,11},{8,4},{9,5},... | collective-permute-start | bytes 208904 | tf_op jit(solution)/shard_map/ppermute | solution.py:365
  69.8 2.5 %collective-permute-start.23 = (bf16[17,16,128]{2,1,0:T(8,128)(2,1)S(1)}, bf16[17,16,128]{2,1,0:T(8,128)(2,1)S(1)}, u32[]{:S(2)}, u32[]{:S(2)}) collective-permute-start(bf16[17,16,128]{2,1,0:T(8,128)(2,1)S(1)} %get-tuple-element.86), channel_id=1, source_target_pairs={{0,4},{1,5},{2,6},{3,7},{4,0},{5,1},{6,2},{7,3},{8,12},{9,13},{10,... | collective-permute-start | bytes 208904 | tf_op jit(solution)/shard_map/ppermute | solution.py:365
  73.5 3.0 %collective-permute-done.19.plain_ref = bf16[16,16,128]{2,1,0:T(8,128)(2,1)S(1)} collective-permute-done((bf16[16,16,128]{2,1,0:T(8,128)(2,1)S(1)}, bf16[16,16,128]{2,1,0:T(8,128)(2,1)S(1)}, u32[]{:S(2)}, u32[]{:S(2)}) %collective-permute-start.19) | collective-permute-done | bytes 65568 | tf_op jit(solution)/shard_map/ppermute | solution.py:365
  76.5 1.9 %shard_map.91 = (f32[16,2048]{1,0:T(8,128)}, f32[16,2048]{1,0:T(8,128)}) custom-call(f32[16,2048]{1,0:T(8,128)S(1)} %shard_map.88.direction_ref, f32[1,2048]{1,0:T(1,128)S(1)} %get-tuple-element.46.nugget_ref, f32[64,16,128]{2,1,0:T(8,128)S(1)} %get-tuple-element.77.keep_ref, bf16[16,16,128]{2,1,0:T(8,128)(2,1)S(1)} %collective-permute-done.19.plain_ref, ...), custom_call_target="tpu_custom_call" | custom-call | tf_op jit(solution)/shard_map/pallas_call | solution.py:337
  (43 shorter events, 21.4 us)
Async XLA Ops:
  0.6 15.6 %collective-permute-start.6 = (bf16[512,2048]{1,0:T(8,128)(2,1)}, bf16[512,2048]{1,0:T(8,128)(2,1)S(1)}, u32[]{:S(2)}, u32[]{:S(2)}) collective-permute-start(bf16[512,2048]{1,0:T(8,128)(2,1)} %bitcast.17), channel_id=1, source_target_pairs={{0,1},{1,0},{2,3},{3,2},{4,5},{5,4},{6,7},{7,6},{8,9},{9,8},{10,11... | collective-permute-start | bytes 6291464 | tf_op jit(solution)/shard_map/ppermute | solution.py:365
  2.1 9.9 %collective-permute-start.3 = (bf16[16,16,128]{2,1,0:T(8,128)(2,1)S(1)}, bf16[16,16,128]{2,1,0:T(8,128)(2,1)S(1)}, u32[]{:S(2)}, u32[]{:S(2)}) collective-permute-start(bf16[16,16,128]{2,1,0:T(8,128)(2,1)S(1)} %get-tuple-element.47), channel_id=1, source_target_pairs={{0,4},{1,5},{2,6},{3,7},{4,0},{5,1},{6,2},{7,3},{8,12},{9,13},{10,... | collective-permute-start | bytes 196616 | tf_op jit(solution)/shard_map/ppermute | solution.py:365
  4.7 7.3 %collective-permute-start.2 = (bf16[16,16,128]{2,1,0:T(8,128)(2,1)S(1)}, bf16[16,16,128]{2,1,0:T(8,128)(2,1)S(1)}, u32[]{:S(2)}, u32[]{:S(2)}) collective-permute-start(bf16[16,16,128]{2,1,0:T(8,128)(2,1)S(1)} %get-tuple-element.47), channel_id=1, source_target_pairs={{0,8},{1,9},{2,10},{3,11},{4,12},{5,13},{6,14},{7,15},{8,0},{9,1},... | collective-permute-start | bytes 196616 | tf_op jit(solution)/shard_map/ppermute | solution.py:365
  7.3 6.1 %collective-permute-start.1 = (bf16[16,16,128]{2,1,0:T(8,128)(2,1)S(1)}, bf16[16,16,128]{2,1,0:T(8,128)(2,1)S(1)}, u32[]{:S(2)}, u32[]{:S(2)}) collective-permute-start(bf16[16,16,128]{2,1,0:T(8,128)(2,1)S(1)} %get-tuple-element.47), channel_id=1, source_target_pairs={{0,12},{1,13},{2,14},{3,15},{4,8},{5,9},{6,10},{7,11},{8,4},{9,5},... | collective-permute-start | bytes 196616 | tf_op jit(solution)/shard_map/ppermute | solution.py:365
  7.3 6.1 %collective-permute-start = (bf16[1,16,16,128]{3,2,1,0:T(8,128)(2,1)S(1)}, bf16[1,16,16,128]{3,2,1,0:T(8,128)(2,1)S(1)}, u32[]{:S(2)}, u32[]{:S(2)}) collective-permute-start(bf16[1,16,16,128]{3,2,1,0:T(8,128)(2,1)S(1)} %bitcast.14), channel_id=1, source_target_pairs={{0,2},{1,3},{2,0},{3,1},{4,6},{5,7},{6,4},{7,5},{8,10},{9,11},{10,... | collective-permute-start | bytes 196616 | tf_op jit(solution)/shard_map/ppermute | solution.py:365
  13.5 5.8 %collective-permute-start.4 = (bf16[3,16,16,128]{3,2,1,0:T(8,128)(2,1)S(1)}, bf16[3,16,16,128]{3,2,1,0:T(8,128)(2,1)S(1)}, u32[]{:S(2)}, u32[]{:S(2)}) collective-permute-start(bf16[3,16,16,128]{3,2,1,0:T(8,128)(2,1)S(1)} %pad_maximum_fusion.3), channel_id=1, source_target_pairs={{0,2},{1,3},{2,0},{3,1},{4,6},{5,7},{6,4},{7,5},{8,10},{9,11},{10,... | collective-permute-start | bytes 589832 | tf_op jit(solution)/shard_map/ppermute | solution.py:365
  15.1 1.2 %collective-permute-start.5 = (s32[8,512]{1,0:T(8,128)S(1)}, s32[8,512]{1,0:T(8,128)S(1)}, u32[]{:S(2)}, u32[]{:S(2)}) collective-permute-start(s32[8,512]{1,0:T(8,128)S(1)} %get-tuple-element.50.named_ref), channel_id=1, source_target_pairs={{0,1},{1,0},{2,3},{3,2},{4,5},{5,4},{6,7},{7,6},{8,9},{9,8},{10,11... | collective-permute-start | bytes 49160 | tf_op jit(solution)/shard_map/ppermute | solution.py:365
  20.6 1.3 %collective-permute-start.7 = (f32[16,1152]{1,0:T(8,128)S(1)}, f32[16,1152]{1,0:T(8,128)S(1)}, u32[]{:S(2)}, u32[]{:S(2)}) collective-permute-start(f32[16,1152]{1,0:T(8,128)S(1)} %shard_map.80.message_ref), channel_id=1, source_target_pairs={{0,1},{1,0},{2,3},{3,2},{4,5},{5,4},{6,7},{7,6},{8,9},{9,8},{10,11... | collective-permute-start | bytes 221192 | tf_op jit(solution)/shard_map/ppermute | solution.py:365
  22.8 7.1 %collective-permute-start.9 = (bf16[49,16,128]{2,1,0:T(8,128)(2,1)S(1)}, bf16[49,16,128]{2,1,0:T(8,128)(2,1)S(1)}, u32[]{:S(2)}, u32[]{:S(2)}) collective-permute-start(bf16[49,16,128]{2,1,0:T(8,128)(2,1)S(1)} %get-tuple-element.61), channel_id=1, source_target_pairs={{0,2},{1,3},{2,0},{3,1},{4,6},{5,7},{6,4},{7,5},{8,10},{9,11},{10,... | collective-permute-start | bytes 602120 | tf_op jit(solution)/shard_map/ppermute | solution.py:365
  30.1 8.7 %collective-permute-start.10 = (bf16[17,16,128]{2,1,0:T(8,128)(2,1)S(1)}, bf16[17,16,128]{2,1,0:T(8,128)(2,1)S(1)}, u32[]{:S(2)}, u32[]{:S(2)}) collective-permute-start(bf16[17,16,128]{2,1,0:T(8,128)(2,1)S(1)} %get-tuple-element.64), channel_id=1, source_target_pairs={{0,12},{1,13},{2,14},{3,15},{4,8},{5,9},{6,10},{7,11},{8,4},{9,5},... | collective-permute-start | bytes 208904 | tf_op jit(solution)/shard_map/ppermute | solution.py:365
  32.8 6.7 %collective-permute-start.11 = (bf16[17,16,128]{2,1,0:T(8,128)(2,1)S(1)}, bf16[17,16,128]{2,1,0:T(8,128)(2,1)S(1)}, u32[]{:S(2)}, u32[]{:S(2)}) collective-permute-start(bf16[17,16,128]{2,1,0:T(8,128)(2,1)S(1)} %get-tuple-element.65), channel_id=1, source_target_pairs={{0,8},{1,9},{2,10},{3,11},{4,12},{5,13},{6,14},{7,15},{8,0},{9,1},... | collective-permute-start | bytes 208904 | tf_op jit(solution)/shard_map/ppermute | solution.py:365
  33.6 5.9 %collective-permute-start.12 = (bf16[17,16,128]{2,1,0:T(8,128)(2,1)S(1)}, bf16[17,16,128]{2,1,0:T(8,128)(2,1)S(1)}, u32[]{:S(2)}, u32[]{:S(2)}) collective-permute-start(bf16[17,16,128]{2,1,0:T(8,128)(2,1)S(1)} %get-tuple-element.66), channel_id=1, source_target_pairs={{0,4},{1,5},{2,6},{3,7},{4,0},{5,1},{6,2},{7,3},{8,12},{9,13},{10,... | collective-permute-start | bytes 208904 | tf_op jit(solution)/shard_map/ppermute | solution.py:365
  34.5 4.3 %collective-permute-start.8 = (bf16[16,16,128]{2,1,0:T(8,128)(2,1)S(1)}, bf16[16,16,128]{2,1,0:T(8,128)(2,1)S(1)}, u32[]{:S(2)}, u32[]{:S(2)}) collective-permute-start(bf16[16,16,128]{2,1,0:T(8,128)(2,1)S(1)} %get-tuple-element.59), channel_id=1, source_target_pairs={{0,2},{1,3},{2,0},{3,1},{4,6},{5,7},{6,4},{7,5},{8,10},{9,11},{10,... | collective-permute-start | bytes 196616 | tf_op jit(solution)/shard_map/ppermute | solution.py:365
  41.0 5.9 %collective-permute-start.16 = (bf16[17,16,128]{2,1,0:T(8,128)(2,1)S(1)}, bf16[17,16,128]{2,1,0:T(8,128)(2,1)S(1)}, u32[]{:S(2)}, u32[]{:S(2)}) collective-permute-start(bf16[17,16,128]{2,1,0:T(8,128)(2,1)S(1)} %get-tuple-element.67), channel_id=1, source_target_pairs={{0,4},{1,5},{2,6},{3,7},{4,0},{5,1},{6,2},{7,3},{8,12},{9,13},{10,... | collective-permute-start | bytes 208904 | tf_op jit(solution)/shard_map/ppermute | solution.py:365
  41.5 7.0 %collective-permute-start.15 = (bf16[17,16,128]{2,1,0:T(8,128)(2,1)S(1)}, bf16[17,16,128]{2,1,0:T(8,128)(2,1)S(1)}, u32[]{:S(2)}, u32[]{:S(2)}) collective-permute-start(bf16[17,16,128]{2,1,0:T(8,128)(2,1)S(1)} %get-tuple-element.67), channel_id=1, source_target_pairs={{0,8},{1,9},{2,10},{3,11},{4,12},{5,13},{6,14},{7,15},{8,0},{9,1},... | collective-permute-start | bytes 208904 | tf_op jit(solution)/shard_map/ppermute | solution.py:365
  43.8 6.2 %collective-permute-start.14 = (bf16[17,16,128]{2,1,0:T(8,128)(2,1)S(1)}, bf16[17,16,128]{2,1,0:T(8,128)(2,1)S(1)}, u32[]{:S(2)}, u32[]{:S(2)}) collective-permute-start(bf16[17,16,128]{2,1,0:T(8,128)(2,1)S(1)} %get-tuple-element.67), channel_id=1, source_target_pairs={{0,12},{1,13},{2,14},{3,15},{4,8},{5,9},{6,10},{7,11},{8,4},{9,5},... | collective-permute-start | bytes 208904 | tf_op jit(solution)/shard_map/ppermute | solution.py:365
  45.4 4.6 %collective-permute-start.13 = (bf16[1,17,16,128]{3,2,1,0:T(8,128)(2,1)S(1)}, bf16[1,17,16,128]{3,2,1,0:T(8,128)(2,1)S(1)}, u32[]{:S(2)}, u32[]{:S(2)}) collective-permute-start(bf16[1,17,16,128]{3,2,1,0:T(8,128)(2,1)S(1)} %bitcast.12), channel_id=1, source_target_pairs={{0,2},{1,3},{2,0},{3,1},{4,6},{5,7},{6,4},{7,5},{8,10},{9,11},{10,... | collective-permute-start | bytes 208904 | tf_op jit(solution)/shard_map/ppermute | solution.py:365
  50.0 5.9 %collective-permute-start.17 = (bf16[3,17,16,128]{3,2,1,0:T(8,128)(2,1)S(1)}, bf16[3,17,16,128]{3,2,1,0:T(8,128)(2,1)S(1)}, u32[]{:S(2)}, u32[]{:S(2)}) collective-permute-start(bf16[3,17,16,128]{3,2,1,0:T(8,128)(2,1)S(1)} %pad_maximum_fusion.2), channel_id=1, source_target_pairs={{0,2},{1,3},{2,0},{3,1},{4,6},{5,7},{6,4},{7,5},{8,10},{9,11},{10,... | collective-permute-start | bytes 626696 | tf_op jit(solution)/shard_map/ppermute | solution.py:365
  57.3 1.3 %collective-permute-start.18 = (f32[16,1152]{1,0:T(8,128)S(1)}, f32[16,1152]{1,0:T(8,128)S(1)}, u32[]{:S(2)}, u32[]{:S(2)}) collective-permute-start(f32[16,1152]{1,0:T(8,128)S(1)} %shard_map.86.message_ref), channel_id=1, source_target_pairs={{0,1},{1,0},{2,3},{3,2},{4,5},{5,4},{6,7},{7,6},{8,9},{9,8},{10,11... | collective-permute-start | bytes 221192 | tf_op jit(solution)/shard_map/ppermute | solution.py:365
  60.6 7.1 %collective-permute-start.20 = (bf16[49,16,128]{2,1,0:T(8,128)(2,1)S(1)}, bf16[49,16,128]{2,1,0:T(8,128)(2,1)S(1)}, u32[]{:S(2)}, u32[]{:S(2)}) collective-permute-start(bf16[49,16,128]{2,1,0:T(8,128)(2,1)S(1)} %get-tuple-element.80), channel_id=1, source_target_pairs={{0,2},{1,3},{2,0},{3,1},{4,6},{5,7},{6,4},{7,5},{8,10},{9,11},{10,... | collective-permute-start | bytes 602120 | tf_op jit(solution)/shard_map/ppermute | solution.py:365
  67.9 8.7 %collective-permute-start.21 = (bf16[17,16,128]{2,1,0:T(8,128)(2,1)S(1)}, bf16[17,16,128]{2,1,0:T(8,128)(2,1)S(1)}, u32[]{:S(2)}, u32[]{:S(2)}) collective-permute-start(bf16[17,16,128]{2,1,0:T(8,128)(2,1)S(1)} %get-tuple-element.84), channel_id=1, source_target_pairs={{0,12},{1,13},{2,14},{3,15},{4,8},{5,9},{6,10},{7,11},{8,4},{9,5},... | collective-permute-start | bytes 208904 | tf_op jit(solution)/shard_map/ppermute | solution.py:365
  69.8 6.8 %collective-permute-start.22 = (bf16[17,16,128]{2,1,0:T(8,128)(2,1)S(1)}, bf16[17,16,128]{2,1,0:T(8,128)(2,1)S(1)}, u32[]{:S(2)}, u32[]{:S(2)}) collective-permute-start(bf16[17,16,128]{2,1,0:T(8,128)(2,1)S(1)} %get-tuple-element.85), channel_id=1, source_target_pairs={{0,8},{1,9},{2,10},{3,11},{4,12},{5,13},{6,14},{7,15},{8,0},{9,1},... | collective-permute-start | bytes 208904 | tf_op jit(solution)/shard_map/ppermute | solution.py:365
  69.8 6.8 %collective-permute-start.23 = (bf16[17,16,128]{2,1,0:T(8,128)(2,1)S(1)}, bf16[17,16,128]{2,1,0:T(8,128)(2,1)S(1)}, u32[]{:S(2)}, u32[]{:S(2)}) collective-permute-start(bf16[17,16,128]{2,1,0:T(8,128)(2,1)S(1)} %get-tuple-element.86), channel_id=1, source_target_pairs={{0,4},{1,5},{2,6},{3,7},{4,0},{5,1},{6,2},{7,3},{8,12},{9,13},{10,... | collective-permute-start | bytes 208904 | tf_op jit(solution)/shard_map/ppermute | solution.py:365
  72.3 4.3 %collective-permute-start.19 = (bf16[16,16,128]{2,1,0:T(8,128)(2,1)S(1)}, bf16[16,16,128]{2,1,0:T(8,128)(2,1)S(1)}, u32[]{:S(2)}, u32[]{:S(2)}) collective-permute-start(bf16[16,16,128]{2,1,0:T(8,128)(2,1)S(1)} %get-tuple-element.78), channel_id=1, source_target_pairs={{0,2},{1,3},{2,0},{3,1},{4,6},{5,7},{6,4},{7,5},{8,10},{9,11},{10,... | collective-permute-start | bytes 196616 | tf_op jit(solution)/shard_map/ppermute | solution.py:365

commit v4 on v3

--- a/solution.py
+++ b/solution.py
@@ -46,17 +46,34 @@
     lane = lanes_of(both)
     both = jnp.where(lane < rhs, both, 0.0)
     one = lane[:1]
-    for k in range(0, rhs, 2):
-        col_0 = jnp.broadcast_to(both[:, k : k + 1], both.shape)
-        col_1 = jnp.broadcast_to(both[:, k + 1 : k + 2], both.shape)
-        a, b = col_0[k : k + 1], col_1[k : k + 1]
-        c, d = col_0[k + 1 : k + 2], col_1[k + 1 : k + 2]
-        inverse = 1.0 / (a * d - b * c)
-        row_0 = jnp.where(one == k, -1.0, jnp.where(one == k + 1, 0.0, both[k : k + 1]))
-        row_1 = jnp.where(one == k, 0.0, jnp.where(one == k + 1, -1.0, both[k + 1 : k + 2]))
-        new_0 = (d * row_0 - b * row_1) * inverse
-        new_1 = (a * row_1 - c * row_0) * inverse
-        both = jnp.where((lane == k) | (lane == k + 1), 0.0, both) - col_0 * new_0 - col_1 * new_1
+    for k in range(0, rhs, 4):
+        cols = [jnp.broadcast_to(both[:, k + j : k + j + 1], both.shape) for j in range(4)]
+        p = [[cols[j][k + i : k + i + 1] for j in range(4)] for i in range(4)]
+        inside = (one >= k) & (one < k + 4)
+        rows = [
+            jnp.where(inside, jnp.where(one == k + i, -1.0, 0.0), both[k + i : k + i + 1]) for i in range(4)
+        ]
+        inverse = 1.0 / (p[0][0] * p[1][1] - p[0][1] * p[1][0])
+
+        def upper(x, y):
+            return (p[1][1] * x - p[0][1] * y) * inverse, (p[0][0] * y - p[1][0] * x) * inverse
+
+        b_02, b_12 = upper(p[0][2], p[1][2])
+        b_03, b_13 = upper(p[0][3], p[1][3])
+        r_0, r_1 = upper(rows[0], rows[1])
+        s_22 = p[2][2] - p[2][0] * b_02 - p[2][1] * b_12
+        s_23 = p[2][3] - p[2][0] * b_03 - p[2][1] * b_13
+        s_32 = p[3][2] - p[3][0] * b_02 - p[3][1] * b_12
+        s_33 = p[3][3] - p[3][0] * b_03 - p[3][1] * b_13
+        inverse_low = 1.0 / (s_22 * s_33 - s_23 * s_32)
+        q_2 = rows[2] - p[2][0] * r_0 - p[2][1] * r_1
+        q_3 = rows[3] - p[3][0] * r_0 - p[3][1] * r_1
+        w_2 = (s_33 * q_2 - s_23 * q_3) * inverse_low
+        w_3 = (s_22 * q_3 - s_32 * q_2) * inverse_low
+        w_0 = r_0 - b_02 * w_2 - b_03 * w_3
+        w_1 = r_1 - b_12 * w_2 - b_13 * w_3
+        both = jnp.where((lane >= k) & (lane < k + 4), 0.0, both)
+        both = both - cols[0] * w_0 - cols[1] * w_1 - cols[2] * w_2 - cols[3] * w_3
     return both[rhs:, :]
 
 
@@ -78,10 +95,9 @@
         message_ref[at + c] = block[:, c * LANES : (c + 1) * LANES].astype(message_ref.dtype)
 
 
-def far_terms(total, panels, factors, places, bases, rhs, chunks):
+def far_terms(total, panels, turned_ref, places, bases, rhs, chunks):
     rows = jnp.concatenate([rows_of(ref, chunks) for ref in panels], axis=0)
-    far = [lax.dot_general(rows, ref[...], NT, preferred_element_type=F32) for ref in factors]
-    far = jnp.concatenate(far, axis=1)
+    far = lax.dot_general(rows, turned_ref[...], NN, preferred_element_type=F32)
     at = 0
     for base, ref in zip(bases, panels):
         for i in range(ref.shape[0]):
@@ -155,7 +171,7 @@
 
 def load_add_kernel(
     rhs, chunks, place_of, base, held_ref, near_ref, named_ref, other_named_ref, right_hbm, other_ref,
-    part_ref, places_ref, right_ref, right_sem,
+    part_ref, places_ref, right_ref, turned_ref, right_sem,
 ):
     copy = pltpu.make_async_copy(right_hbm, right_ref, right_sem)
     copy.start()
@@ -166,19 +182,22 @@
     places_ref[...] = places
     near = near_ref[...]
     total = jnp.concatenate([near, jnp.zeros(near.shape, F32)], axis=1)
+    half = other_ref.shape[0]
+    turned_ref[:, half:] = other_ref[...].T
     copy.wait()
-    part_ref[...] = far_terms(total, [held_ref], (right_ref, other_ref), places, [base], rhs, chunks)
+    turned_ref[:, :half] = right_ref[...].T
+    part_ref[...] = far_terms(total, [held_ref], turned_ref, places, [base], rhs, chunks)
 
 
 def near_add_kernel(
     rhs, chunks, base, held_ref, own_ref, right_side_ref, nugget_ref, left_ref, named_ref, places_ref,
-    right_ref, other_ref, part_ref, sums_ref,
+    turned_ref, part_ref, sums_ref,
 ):
     own = own_ref[...]
     near = lax.dot_general(own.astype(BF16), left_ref[...], NT, preferred_element_type=F32)
     near = jnp.where(named_ref[:1] >= 0, near, 0.0)
     total = jnp.concatenate([near, jnp.zeros(near.shape, F32)], axis=1)
-    part_ref[...] = far_terms(total, [held_ref], (right_ref, other_ref), places_ref[...], [base], rhs, chunks)
+    part_ref[...] = far_terms(total, [held_ref], turned_ref, places_ref[...], [base], rhs, chunks)
     weighted = own * nugget_ref[...]
     code = codes_of(held_ref, chunks)
     none = jnp.zeros((rhs, rhs), F32)
@@ -186,10 +205,10 @@
 
 
 def add_kernel(
-    rhs, chunks, bases, beside_ref, late_ref, right_ref, other_ref, places_ref, part_ref, sums_ref, message_ref
+    rhs, chunks, bases, beside_ref, late_ref, turned_ref, places_ref, part_ref, sums_ref, message_ref
 ):
     panels = (beside_ref, late_ref)
-    total = far_terms(part_ref[...], panels, (right_ref, other_ref), places_ref[...], bases, rhs, chunks)
+    total = far_terms(part_ref[...], panels, turned_ref, places_ref[...], bases, rhs, chunks)
     width = total.shape[1]
     message_ref[:, :width] = total
     message_ref[:, width:] = sums_ref[...] + decode(codes_of(beside_ref, chunks) + codes_of(late_ref, chunks), rhs)
@@ -203,10 +222,9 @@
     return jnp.concatenate([own, other], axis=1), sums
 
 
-def symmetric_product(projected):
-    rounded = projected.astype(BF16).astype(F32)
-    first = gram(projected, rounded)
-    return 0.5 * (first + first.T)
+def rounded_gram(projected):
+    rounded = projected.astype(BF16)
+    return lax.dot_general(rounded, rounded, NT, preferred_element_type=F32)
 
 
 def send_terms(send_ref, projected, factors, places, wanted, pair, rhs, chunks):
@@ -224,7 +242,7 @@
     projected, sums = both_cores(message_ref, got_ref)
     projected_ref[...] = projected
     sums_ref[...] = sums
-    pair = sums + sums_of([symmetric_product(projected)], rhs)
+    pair = sums + sums_of([rounded_gram(projected)], rhs)
     pair_ref[...] = pair
     send_terms(send_ref, projected, (right_ref, other_ref), places_ref[...], wanted, pair, rhs, chunks)
 
@@ -242,7 +260,7 @@
     weighted = left_multiply(mix, jnp.concatenate([sums[:, 2 * rhs : 3 * rhs], weighted_ref[:, :rhs]], axis=1), rhs)
     mixed = weighted[:, :rhs]
     curvature = sums[:, rhs : 2 * rhs] + mixed + mixed.T + gram(weighted[:, rhs:], mix[:, :rhs])
-    pair = sums_of([curvature + symmetric_product(projected)], rhs)
+    pair = sums_of([curvature + rounded_gram(projected)], rhs)
     pair_ref[...] = pair
     send_terms(send_ref, projected, (right_ref, other_ref), places_ref[...], wanted, pair, rhs, chunks)
     mix_ref[...] = mix
@@ -263,6 +281,10 @@
     own = projected[:, : projected.shape[1] // 2].astype(BF16)
     own = lax.dot_general(own, left_ref[...], NN, preferred_element_type=F32)
     spread_terms(projected, (right_ref, other_ref), places_ref[...], wanted, store, rhs, chunks, own)
+
+
+def solution_kernel(rhs, step_ref, right_side_ref, solution_ref):
+    solution_ref[...] = left_multiply(step_ref[...], right_side_ref[...], rhs)
 
 
 def direction_kernel(rhs, mix_ref, right_side_ref, residual_ref, direction_ref):
@@ -309,7 +331,7 @@
 
 
 def middle_kernel(rhs, chunks, direction_ref, nugget_ref, keep_ref, plain_ref, pair_ref, *rest):
-    got, (message_ref, residual_ref, solution_ref, gram_ref) = rest[:-4], rest[-4:]
+    got, (message_ref, residual_ref, step_ref, gram_ref) = rest[:-4], rest[-4:]
     direction = direction_ref[...]
     applied, pair = gathered_product(keep_ref, plain_ref, pair_ref, got, direction, nugget_ref[...], rhs, chunks)
     first_gram = second_of(pair, rhs)
@@ -319,7 +341,7 @@
     residual_ref[...] = residual
     store_message(message_ref, residual, rhs)
     message_ref[chunks] = encode(sums_of([gram(residual, residual)], rhs), rhs)
-    solution_ref[...] = left_multiply(step, direction, rhs)
+    step_ref[...] = step
 
 
 def last_kernel(rhs, chunks, direction_ref, nugget_ref, keep_ref, plain_ref, pair_ref, gram_ref, *rest):
@@ -408,14 +430,14 @@
             mine = [jnp.concatenate([g, swap(g, 1 << b)]) for g in mine]
         beside = swap(mine[0], 2)
         late_panels = swap(after(jnp.concatenate(mine[1:]), beside, *early), 2)
-        terms, sums, factors, places = first_terms(jnp.concatenate(mine))
+        terms, sums, turned, factors, places = first_terms(jnp.concatenate(mine))
         late_panels = after(late_panels, terms)
         (message,) = call(
             part(add_kernel, rhs, chunks, (late, late + m)),
             [core_message],
-            beside, late_panels, *factors, places, terms, sums,
+            beside, late_panels, turned, places, terms, sums,
         )
-        return message, swap(message, 1), factors, places
+        return message, swap(message, 1), turned, factors, places
 
     def reduce(send, pair, projected, left, factors, places, *early):
         got = swap(send, 2)
@@ -450,7 +472,7 @@
         part(open_kernel, rhs), [plain(1), panel], in_hbm(right_sides), far=(0,), fixed=(1,), scratch=[semaphore]
     )
     right = right_factors.reshape(slots * rank, width)
-    other = swap(right, 1)
+    other = swap(after(right, message), 1)
     named_shape = ((8, slots * rank), jnp.int32)
     nugget, left, named, near, sums = call(
         part(load_kernel, rhs, rank),
@@ -462,36 +484,38 @@
     other_named = swap(named, 1)
 
     def loading(mine):
-        terms, places, here = call(
+        terms, places, here, turned = call(
             part(load_add_kernel, rhs, chunks, place_of, held),
-            [two_rows, ((rhs, 2 * slots * rank), jnp.int32), factor],
+            [two_rows, ((rhs, 2 * slots * rank), jnp.int32), factor, ((width, 2 * slots * rank), BF16)],
             mine, near, named, other_named, in_hbm(right), other,
-            far=(4,), fixed=(2,), scratch=[semaphore],
+            far=(4,), fixed=(2, 3), scratch=[semaphore],
         )
-        return terms, sums, (here, other), places
-
-    message, got, factors, places = gather(message, loading, near)
+        return terms, sums, turned, (here, other), places
+
+    message, got, turned, factors, places = gather(message, loading, near)
     send, pair, earlier, weighted = call(
         part(first_kernel, rhs, chunks, go),
         [coded(3 * m), small, two_rows, small],
         message, got, *factors, places,
     )
     mine, beside, pair, got = reduce(send, pair, earlier, left, factors, places)
-    message, residual, solution, first_gram = call(
+    message, residual, step, first_gram = call(
         part(middle_kernel, rhs, chunks),
-        [coded(1), panel, panel, small],
+        [coded(1), panel, small, small],
         right_sides, nugget, mine, beside, pair, *got,
     )
+
+    (solution,) = call(part(solution_kernel, rhs), [panel], step, right_sides)
 
     def loaded(mine):
         terms, sums = call(
             part(near_add_kernel, rhs, chunks, held),
             [two_rows, small],
-            mine, residual, right_sides, nugget, left, named, places, *factors,
+            after(mine, solution), residual, right_sides, nugget, left, named, places, turned,
         )
-        return terms, sums, factors, places
-
-    message, got, _, _ = gather(message, loaded)
+        return terms, sums, turned, factors, places
+
+    message, got, *_ = gather(message, loaded)
     send, pair, projected, next_gram, mix = call(
         part(second_kernel, rhs, chunks, go),
         [coded(3 * m), small, two_rows, small, small],

time: 78.7 us -> 76.4 us (0.971)
  Pallas kernels: 20.4 us -> 17.8 us
  starting transfers between devices: 31 us -> 31.8 us
    pallas_call x15 -> x16, Pallas kernels: 20.4 us -> 17.8 us  [call(): pl.pallas_call(kernel, out_shape=[pltpu.VMEM(shape, dtype) if i in fixed...]
  transfers between devices with their start and end apart: 24 -> 24, of which waited for: 12 -> 13; matrix products, arithmetic and copies ran while one was open for 0% -> 0% of each run, Pallas kernels for 14% -> 12%
where the time goes in v4:
time: 76.4 us; the launch traced here: 76.2 us
  starting transfers between devices  31.8 us (42%)
  waiting for transfers between devices  25.1 us (33%)
  Pallas kernels  17.8 us (23%)
  between operations  1.44 us (2%)
    ppermute x24, starting transfers between devices, swap(): return lax.ppermute(array, 'row', [(i, i ^ offset) for i in range(devices)])  31.8 us
    ppermute x24, waiting for transfers between devices, swap(): return lax.ppermute(array, 'row', [(i, i ^ offset) for i in range(devices)])  25.1 us
    pallas_call x16, Pallas kernels, call(): pl.pallas_call(kernel, out_shape=[pltpu.VMEM(shape, dtype) if i in fixed...  17.8 us
  transfers between devices with their start and end apart: 24, of which 13 were waited for; matrix products, arithmetic and copies ran while one was open for 0% of the time, Pallas kernels for 12%

profile of v4, /device:TPU:0, one launch (start us, length us, event | category | flops | bytes accessed | tf_op | source)
XLA Modules:
  0.0 76.2 jit_solution(2928257300446508718)
XLA Ops:
  2.1 4.7 %collective-permute-start.1 = (bf16[16,16,128]{2,1,0:T(8,128)(2,1)S(1)}, bf16[16,16,128]{2,1,0:T(8,128)(2,1)S(1)}, u32[]{:S(2)}, u32[]{:S(2)}) collective-permute-start(bf16[16,16,128]{2,1,0:T(8,128)(2,1)S(1)} %get-tuple-element.50), channel_id=1, source_target_pairs={{0,12},{1,13},{2,14},{3,15},{4,8},{5,9},{6,10},{7,11},{8,4},{9,5},... | collective-permute-start | bytes 196616 | tf_op jit(solution)/shard_map/ppermute | solution.py:387
  7.4 1.7 %collective-permute-start = (bf16[1,16,16,128]{3,2,1,0:T(8,128)(2,1)S(1)}, bf16[1,16,16,128]{3,2,1,0:T(8,128)(2,1)S(1)}, u32[]{:S(2)}, u32[]{:S(2)}) collective-permute-start(bf16[1,16,16,128]{3,2,1,0:T(8,128)(2,1)S(1)} %bitcast.14), channel_id=1, source_target_pairs={{0,2},{1,3},{2,0},{3,1},{4,6},{5,7},{6,4},{7,5},{8,10},{9,11},{10,... | collective-permute-start | bytes 196616 | tf_op jit(solution)/shard_map/ppermute | solution.py:387
  9.7 2.3 %shard_map.78 = (f32[1,2048]{1,0:T(1,128)S(1)}, bf16[512,2048]{1,0:T(8,128)(2,1)S(1)}, s32[8,512]{1,0:T(8,128)S(1)}, f32[16,512]{1,0:T(8,128)S(1)}, f32[16,128]{1,0:T(8,128)S(1)}) custom-call(f32[16,2048]{1,0:T(8,128)S(1)} %get-tuple-element.48.own_ref.direction_ref.right_side_ref, s32[32]{0:T(128)} %bitcast.32, s32[1]{0:T(128)S(6)} %copy.8.live_ref, ...), custom_call_target="tpu_custom_call" | custom-call | tf_op jit(solution)/shard_map/pallas_call | solution.py:359
  12.9 1.6 %collective-permute-start.4 = (bf16[3,16,16,128]{3,2,1,0:T(8,128)(2,1)S(1)}, bf16[3,16,16,128]{3,2,1,0:T(8,128)(2,1)S(1)}, u32[]{:S(2)}, u32[]{:S(2)}) collective-permute-start(bf16[3,16,16,128]{3,2,1,0:T(8,128)(2,1)S(1)} %pad_maximum_fusion.3), channel_id=1, source_target_pairs={{0,2},{1,3},{2,0},{3,1},{4,6},{5,7},{6,4},{7,5},{8,10},{9,11},{10,... | collective-permute-start | bytes 589832 | tf_op jit(solution)/shard_map/ppermute | solution.py:387
  15.6 2.6 %shard_map.79 = (f32[16,1024]{1,0:T(8,128)S(1)}, s32[16,1024]{1,0:T(8,128)S(1)}, bf16[512,2048]{1,0:T(8,128)(2,1)S(1)}, bf16[2048,1024]{1,0:T(8,128)(2,1)S(1)}) custom-call(bf16[4,16,16,128]{3,2,1,0:T(8,128)(2,1)S(1)} %pad_maximum_fusion.1.held_ref, f32[16,512]{1,0:T(8,128)S(1)} %get-tuple-element.51.near_ref, s32[8,512]{1,0:T(8,128)S(1)} %get-tuple-element.53.named_ref, ...), custom_call_target="tpu_custom_call" | custom-call | tf_op jit(solution)/shard_map/pallas_call | solution.py:359
  22.4 1.6 %collective-permute-start.9 = (bf16[49,16,128]{2,1,0:T(8,128)(2,1)S(1)}, bf16[49,16,128]{2,1,0:T(8,128)(2,1)S(1)}, u32[]{:S(2)}, u32[]{:S(2)}) collective-permute-start(bf16[49,16,128]{2,1,0:T(8,128)(2,1)S(1)} %get-tuple-element.66), channel_id=1, source_target_pairs={{0,2},{1,3},{2,0},{3,1},{4,6},{5,7},{6,4},{7,5},{8,10},{9,11},{10,... | collective-permute-start | bytes 602120 | tf_op jit(solution)/shard_map/ppermute | solution.py:387
  25.1 4.4 %collective-permute-done.9.got_ref = bf16[49,16,128]{2,1,0:T(8,128)(2,1)S(1)} collective-permute-done((bf16[49,16,128]{2,1,0:T(8,128)(2,1)S(1)}, bf16[49,16,128]{2,1,0:T(8,128)(2,1)S(1)}, u32[]{:S(2)}, u32[]{:S(2)}) %collective-permute-start.9) | collective-permute-done | bytes 200736 | tf_op jit(solution)/shard_map/ppermute | solution.py:387
  29.7 2.5 %collective-permute-start.10 = (bf16[17,16,128]{2,1,0:T(8,128)(2,1)S(1)}, bf16[17,16,128]{2,1,0:T(8,128)(2,1)S(1)}, u32[]{:S(2)}, u32[]{:S(2)}) collective-permute-start(bf16[17,16,128]{2,1,0:T(8,128)(2,1)S(1)} %get-tuple-element.69), channel_id=1, source_target_pairs={{0,12},{1,13},{2,14},{3,15},{4,8},{5,9},{6,10},{7,11},{8,4},{9,5},... | collective-permute-start | bytes 208904 | tf_op jit(solution)/shard_map/ppermute | solution.py:387
  32.4 1.7 %collective-permute-start.12 = (bf16[17,16,128]{2,1,0:T(8,128)(2,1)S(1)}, bf16[17,16,128]{2,1,0:T(8,128)(2,1)S(1)}, u32[]{:S(2)}, u32[]{:S(2)}) collective-permute-start(bf16[17,16,128]{2,1,0:T(8,128)(2,1)S(1)} %get-tuple-element.71), channel_id=1, source_target_pairs={{0,4},{1,5},{2,6},{3,7},{4,0},{5,1},{6,2},{7,3},{8,12},{9,13},{10,... | collective-permute-start | bytes 208904 | tf_op jit(solution)/shard_map/ppermute | solution.py:387
  34.1 1.5 %collective-permute-start.8 = (bf16[16,16,128]{2,1,0:T(8,128)(2,1)S(1)}, bf16[16,16,128]{2,1,0:T(8,128)(2,1)S(1)}, u32[]{:S(2)}, u32[]{:S(2)}) collective-permute-start(bf16[16,16,128]{2,1,0:T(8,128)(2,1)S(1)} %get-tuple-element.64), channel_id=1, source_target_pairs={{0,2},{1,3},{2,0},{3,1},{4,6},{5,7},{6,4},{7,5},{8,10},{9,11},{10,... | collective-permute-start | bytes 196616 | tf_op jit(solution)/shard_map/ppermute | solution.py:387
  35.6 2.7 %collective-permute-done.8.plain_ref = bf16[16,16,128]{2,1,0:T(8,128)(2,1)S(1)} collective-permute-done((bf16[16,16,128]{2,1,0:T(8,128)(2,1)S(1)}, bf16[16,16,128]{2,1,0:T(8,128)(2,1)S(1)}, u32[]{:S(2)}, u32[]{:S(2)}) %collective-permute-start.8) | collective-permute-done | bytes 65568 | tf_op jit(solution)/shard_map/ppermute | solution.py:387
  40.8 2.0 %collective-permute-start.16 = (bf16[17,16,128]{2,1,0:T(8,128)(2,1)S(1)}, bf16[17,16,128]{2,1,0:T(8,128)(2,1)S(1)}, u32[]{:S(2)}, u32[]{:S(2)}) collective-permute-start(bf16[17,16,128]{2,1,0:T(8,128)(2,1)S(1)} %get-tuple-element.72), channel_id=1, source_target_pairs={{0,4},{1,5},{2,6},{3,7},{4,0},{5,1},{6,2},{7,3},{8,12},{9,13},{10,... | collective-permute-start | bytes 208904 | tf_op jit(solution)/shard_map/ppermute | solution.py:387
  42.8 1.6 %collective-permute-start.14 = (bf16[17,16,128]{2,1,0:T(8,128)(2,1)S(1)}, bf16[17,16,128]{2,1,0:T(8,128)(2,1)S(1)}, u32[]{:S(2)}, u32[]{:S(2)}) collective-permute-start(bf16[17,16,128]{2,1,0:T(8,128)(2,1)S(1)} %get-tuple-element.72), channel_id=1, source_target_pairs={{0,12},{1,13},{2,14},{3,15},{4,8},{5,9},{6,10},{7,11},{8,4},{9,5},... | collective-permute-start | bytes 208904 | tf_op jit(solution)/shard_map/ppermute | solution.py:387
  46.6 2.3 %collective-permute-done.14 = bf16[17,16,128]{2,1,0:T(8,128)(2,1)S(1)} collective-permute-done((bf16[17,16,128]{2,1,0:T(8,128)(2,1)S(1)}, bf16[17,16,128]{2,1,0:T(8,128)(2,1)S(1)}, u32[]{:S(2)}, u32[]{:S(2)}) %collective-permute-start.14) | collective-permute-done | bytes 69664 | tf_op jit(solution)/shard_map/ppermute | solution.py:387
  49.0 1.6 %collective-permute-start.17 = (bf16[3,17,16,128]{3,2,1,0:T(8,128)(2,1)S(1)}, bf16[3,17,16,128]{3,2,1,0:T(8,128)(2,1)S(1)}, u32[]{:S(2)}, u32[]{:S(2)}) collective-permute-start(bf16[3,17,16,128]{3,2,1,0:T(8,128)(2,1)S(1)} %pad_maximum_fusion.2), channel_id=1, source_target_pairs={{0,2},{1,3},{2,0},{3,1},{4,6},{5,7},{6,4},{7,5},{8,10},{9,11},{10,... | collective-permute-start | bytes 626696 | tf_op jit(solution)/shard_map/ppermute | solution.py:387
  50.9 1.8 %shard_map.86 = (f32[16,1024]{1,0:T(8,128)S(1)}, f32[16,128]{1,0:T(8,128)S(1)}) custom-call(bf16[4,17,16,128]{3,2,1,0:T(8,128)(2,1)S(1)} %pad_maximum_fusion.held_ref, f32[16,2048]{1,0:T(8,128)S(1)} %get-tuple-element.76.own_ref.residual_ref.rest_3_, f32[16,2048]{1,0:T(8,128)S(1)} %get-tuple-element.48.own_ref.direction_ref.right_side_ref, ...), custom_call_target="tpu_custom_call" | custom-call | tf_op jit(solution)/shard_map/pallas_call | solution.py:359
  52.7 2.2 %collective-permute-done.17.late_ref = bf16[3,17,16,128]{3,2,1,0:T(8,128)(2,1)S(1)} collective-permute-done((bf16[3,17,16,128]{3,2,1,0:T(8,128)(2,1)S(1)}, bf16[3,17,16,128]{3,2,1,0:T(8,128)(2,1)S(1)}, u32[]{:S(2)}, u32[]{:S(2)}) %collective-permute-start.17) | collective-permute-done | bytes 208928 | tf_op jit(solution)/shard_map/ppermute | solution.py:387
  57.0 1.6 %shard_map.88 = (bf16[49,16,128]{2,1,0:T(8,128)(2,1)S(1)}, f32[16,128]{1,0:T(8,128)S(1)}, f32[16,1024]{1,0:T(8,128)S(1)}, f32[16,128]{1,0:T(8,128)S(1)}, f32[16,128]{1,0:T(8,128)S(1)}) custom-call(f32[16,1152]{1,0:T(8,128)S(1)} %shard_map.87.message_ref, f32[16,1152]{1,0:T(8,128)S(1)} %collective-permute-done.18.got_ref, ...), custom_call_target="tpu_custom_call" | custom-call | tf_op jit(solution)/shard_map/pallas_call | solution.py:359
  58.6 1.6 %collective-permute-start.20 = (bf16[49,16,128]{2,1,0:T(8,128)(2,1)S(1)}, bf16[49,16,128]{2,1,0:T(8,128)(2,1)S(1)}, u32[]{:S(2)}, u32[]{:S(2)}) collective-permute-start(bf16[49,16,128]{2,1,0:T(8,128)(2,1)S(1)} %get-tuple-element.87), channel_id=1, source_target_pairs={{0,2},{1,3},{2,0},{3,1},{4,6},{5,7},{6,4},{7,5},{8,10},{9,11},{10,... | collective-permute-start | bytes 602120 | tf_op jit(solution)/shard_map/ppermute | solution.py:387
  61.6 4.1 %collective-permute-done.20.got_ref = bf16[49,16,128]{2,1,0:T(8,128)(2,1)S(1)} collective-permute-done((bf16[49,16,128]{2,1,0:T(8,128)(2,1)S(1)}, bf16[49,16,128]{2,1,0:T(8,128)(2,1)S(1)}, u32[]{:S(2)}, u32[]{:S(2)}) %collective-permute-start.20) | collective-permute-done | bytes 200736 | tf_op jit(solution)/shard_map/ppermute | solution.py:387
  65.9 1.9 %collective-permute-start.21 = (bf16[17,16,128]{2,1,0:T(8,128)(2,1)S(1)}, bf16[17,16,128]{2,1,0:T(8,128)(2,1)S(1)}, u32[]{:S(2)}, u32[]{:S(2)}) collective-permute-start(bf16[17,16,128]{2,1,0:T(8,128)(2,1)S(1)} %get-tuple-element.91), channel_id=1, source_target_pairs={{0,12},{1,13},{2,14},{3,15},{4,8},{5,9},{6,10},{7,11},{8,4},{9,5},... | collective-permute-start | bytes 208904 | tf_op jit(solution)/shard_map/ppermute | solution.py:387
  67.8 2.5 %collective-permute-start.23 = (bf16[17,16,128]{2,1,0:T(8,128)(2,1)S(1)}, bf16[17,16,128]{2,1,0:T(8,128)(2,1)S(1)}, u32[]{:S(2)}, u32[]{:S(2)}) collective-permute-start(bf16[17,16,128]{2,1,0:T(8,128)(2,1)S(1)} %get-tuple-element.93), channel_id=1, source_target_pairs={{0,4},{1,5},{2,6},{3,7},{4,0},{5,1},{6,2},{7,3},{8,12},{9,13},{10,... | collective-permute-start | bytes 208904 | tf_op jit(solution)/shard_map/ppermute | solution.py:387
  71.8 2.7 %collective-permute-done.19.plain_ref = bf16[16,16,128]{2,1,0:T(8,128)(2,1)S(1)} collective-permute-done((bf16[16,16,128]{2,1,0:T(8,128)(2,1)S(1)}, bf16[16,16,128]{2,1,0:T(8,128)(2,1)S(1)}, u32[]{:S(2)}, u32[]{:S(2)}) %collective-permute-start.19) | collective-permute-done | bytes 65568 | tf_op jit(solution)/shard_map/ppermute | solution.py:387
  74.6 1.6 %shard_map.92 = (f32[16,2048]{1,0:T(8,128)}, f32[16,2048]{1,0:T(8,128)}) custom-call(f32[16,2048]{1,0:T(8,128)S(1)} %shard_map.89.direction_ref, f32[1,2048]{1,0:T(1,128)S(1)} %get-tuple-element.49.nugget_ref, f32[64,16,128]{2,1,0:T(8,128)S(1)} %get-tuple-element.84.keep_ref, bf16[16,16,128]{2,1,0:T(8,128)(2,1)S(1)} %collective-permute-done.19.plain_ref, ...), custom_call_target="tpu_custom_call" | custom-call | tf_op jit(solution)/shard_map/pallas_call | solution.py:359
  (44 shorter events, 19.9 us)
Async XLA Ops:
  1.6 14.1 %collective-permute-start.6 = (bf16[512,2048]{1,0:T(8,128)(2,1)}, bf16[512,2048]{1,0:T(8,128)(2,1)S(1)}, u32[]{:S(2)}, u32[]{:S(2)}) collective-permute-start(bf16[512,2048]{1,0:T(8,128)(2,1)} %bitcast.17), channel_id=1, source_target_pairs={{0,1},{1,0},{2,3},{3,2},{4,5},{5,4},{6,7},{7,6},{8,9},{9,8},{10,11... | collective-permute-start | bytes 6291464 | tf_op jit(solution)/shard_map/ppermute | solution.py:387
  2.1 9.9 %collective-permute-start.1 = (bf16[16,16,128]{2,1,0:T(8,128)(2,1)S(1)}, bf16[16,16,128]{2,1,0:T(8,128)(2,1)S(1)}, u32[]{:S(2)}, u32[]{:S(2)}) collective-permute-start(bf16[16,16,128]{2,1,0:T(8,128)(2,1)S(1)} %get-tuple-element.50), channel_id=1, source_target_pairs={{0,12},{1,13},{2,14},{3,15},{4,8},{5,9},{6,10},{7,11},{8,4},{9,5},... | collective-permute-start | bytes 196616 | tf_op jit(solution)/shard_map/ppermute | solution.py:387
  6.8 6.1 %collective-permute-start.2 = (bf16[16,16,128]{2,1,0:T(8,128)(2,1)S(1)}, bf16[16,16,128]{2,1,0:T(8,128)(2,1)S(1)}, u32[]{:S(2)}, u32[]{:S(2)}) collective-permute-start(bf16[16,16,128]{2,1,0:T(8,128)(2,1)S(1)} %get-tuple-element.50), channel_id=1, source_target_pairs={{0,8},{1,9},{2,10},{3,11},{4,12},{5,13},{6,14},{7,15},{8,0},{9,1},... | collective-permute-start | bytes 196616 | tf_op jit(solution)/shard_map/ppermute | solution.py:387
  6.8 6.1 %collective-permute-start.3 = (bf16[16,16,128]{2,1,0:T(8,128)(2,1)S(1)}, bf16[16,16,128]{2,1,0:T(8,128)(2,1)S(1)}, u32[]{:S(2)}, u32[]{:S(2)}) collective-permute-start(bf16[16,16,128]{2,1,0:T(8,128)(2,1)S(1)} %get-tuple-element.50), channel_id=1, source_target_pairs={{0,4},{1,5},{2,6},{3,7},{4,0},{5,1},{6,2},{7,3},{8,12},{9,13},{10,... | collective-permute-start | bytes 196616 | tf_op jit(solution)/shard_map/ppermute | solution.py:387
  7.4 5.5 %collective-permute-start = (bf16[1,16,16,128]{3,2,1,0:T(8,128)(2,1)S(1)}, bf16[1,16,16,128]{3,2,1,0:T(8,128)(2,1)S(1)}, u32[]{:S(2)}, u32[]{:S(2)}) collective-permute-start(bf16[1,16,16,128]{3,2,1,0:T(8,128)(2,1)S(1)} %bitcast.14), channel_id=1, source_target_pairs={{0,2},{1,3},{2,0},{3,1},{4,6},{5,7},{6,4},{7,5},{8,10},{9,11},{10,... | collective-permute-start | bytes 196616 | tf_op jit(solution)/shard_map/ppermute | solution.py:387
  12.9 6.5 %collective-permute-start.4 = (bf16[3,16,16,128]{3,2,1,0:T(8,128)(2,1)S(1)}, bf16[3,16,16,128]{3,2,1,0:T(8,128)(2,1)S(1)}, u32[]{:S(2)}, u32[]{:S(2)}) collective-permute-start(bf16[3,16,16,128]{3,2,1,0:T(8,128)(2,1)S(1)} %pad_maximum_fusion.3), channel_id=1, source_target_pairs={{0,2},{1,3},{2,0},{3,1},{4,6},{5,7},{6,4},{7,5},{8,10},{9,11},{10,... | collective-permute-start | bytes 589832 | tf_op jit(solution)/shard_map/ppermute | solution.py:387
  14.4 1.2 %collective-permute-start.5 = (s32[8,512]{1,0:T(8,128)S(1)}, s32[8,512]{1,0:T(8,128)S(1)}, u32[]{:S(2)}, u32[]{:S(2)}) collective-permute-start(s32[8,512]{1,0:T(8,128)S(1)} %get-tuple-element.53.named_ref), channel_id=1, source_target_pairs={{0,1},{1,0},{2,3},{3,2},{4,5},{5,4},{6,7},{7,6},{8,9},{9,8},{10,11... | collective-permute-start | bytes 49160 | tf_op jit(solution)/shard_map/ppermute | solution.py:387
  20.2 1.3 %collective-permute-start.7 = (f32[16,1152]{1,0:T(8,128)S(1)}, f32[16,1152]{1,0:T(8,128)S(1)}, u32[]{:S(2)}, u32[]{:S(2)}) collective-permute-start(f32[16,1152]{1,0:T(8,128)S(1)} %shard_map.80.message_ref), channel_id=1, source_target_pairs={{0,1},{1,0},{2,3},{3,2},{4,5},{5,4},{6,7},{7,6},{8,9},{9,8},{10,11... | collective-permute-start | bytes 221192 | tf_op jit(solution)/shard_map/ppermute | solution.py:387
  22.4 7.1 %collective-permute-start.9 = (bf16[49,16,128]{2,1,0:T(8,128)(2,1)S(1)}, bf16[49,16,128]{2,1,0:T(8,128)(2,1)S(1)}, u32[]{:S(2)}, u32[]{:S(2)}) collective-permute-start(bf16[49,16,128]{2,1,0:T(8,128)(2,1)S(1)} %get-tuple-element.66), channel_id=1, source_target_pairs={{0,2},{1,3},{2,0},{3,1},{4,6},{5,7},{6,4},{7,5},{8,10},{9,11},{10,... | collective-permute-start | bytes 602120 | tf_op jit(solution)/shard_map/ppermute | solution.py:387
  29.7 8.7 %collective-permute-start.10 = (bf16[17,16,128]{2,1,0:T(8,128)(2,1)S(1)}, bf16[17,16,128]{2,1,0:T(8,128)(2,1)S(1)}, u32[]{:S(2)}, u32[]{:S(2)}) collective-permute-start(bf16[17,16,128]{2,1,0:T(8,128)(2,1)S(1)} %get-tuple-element.69), channel_id=1, source_target_pairs={{0,12},{1,13},{2,14},{3,15},{4,8},{5,9},{6,10},{7,11},{8,4},{9,5},... | collective-permute-start | bytes 208904 | tf_op jit(solution)/shard_map/ppermute | solution.py:387
  32.3 6.4 %collective-permute-start.11 = (bf16[17,16,128]{2,1,0:T(8,128)(2,1)S(1)}, bf16[17,16,128]{2,1,0:T(8,128)(2,1)S(1)}, u32[]{:S(2)}, u32[]{:S(2)}) collective-permute-start(bf16[17,16,128]{2,1,0:T(8,128)(2,1)S(1)} %get-tuple-element.70), channel_id=1, source_target_pairs={{0,8},{1,9},{2,10},{3,11},{4,12},{5,13},{6,14},{7,15},{8,0},{9,1},... | collective-permute-start | bytes 208904 | tf_op jit(solution)/shard_map/ppermute | solution.py:387
  32.4 6.3 %collective-permute-start.12 = (bf16[17,16,128]{2,1,0:T(8,128)(2,1)S(1)}, bf16[17,16,128]{2,1,0:T(8,128)(2,1)S(1)}, u32[]{:S(2)}, u32[]{:S(2)}) collective-permute-start(bf16[17,16,128]{2,1,0:T(8,128)(2,1)S(1)} %get-tuple-element.71), channel_id=1, source_target_pairs={{0,4},{1,5},{2,6},{3,7},{4,0},{5,1},{6,2},{7,3},{8,12},{9,13},{10,... | collective-permute-start | bytes 208904 | tf_op jit(solution)/shard_map/ppermute | solution.py:387
  34.1 4.3 %collective-permute-start.8 = (bf16[16,16,128]{2,1,0:T(8,128)(2,1)S(1)}, bf16[16,16,128]{2,1,0:T(8,128)(2,1)S(1)}, u32[]{:S(2)}, u32[]{:S(2)}) collective-permute-start(bf16[16,16,128]{2,1,0:T(8,128)(2,1)S(1)} %get-tuple-element.64), channel_id=1, source_target_pairs={{0,2},{1,3},{2,0},{3,1},{4,6},{5,7},{6,4},{7,5},{8,10},{9,11},{10,... | collective-permute-start | bytes 196616 | tf_op jit(solution)/shard_map/ppermute | solution.py:387
  40.0 6.6 %collective-permute-start.15 = (bf16[17,16,128]{2,1,0:T(8,128)(2,1)S(1)}, bf16[17,16,128]{2,1,0:T(8,128)(2,1)S(1)}, u32[]{:S(2)}, u32[]{:S(2)}) collective-permute-start(bf16[17,16,128]{2,1,0:T(8,128)(2,1)S(1)} %get-tuple-element.72), channel_id=1, source_target_pairs={{0,8},{1,9},{2,10},{3,11},{4,12},{5,13},{6,14},{7,15},{8,0},{9,1},... | collective-permute-start | bytes 208904 | tf_op jit(solution)/shard_map/ppermute | solution.py:387
  40.8 5.8 %collective-permute-start.16 = (bf16[17,16,128]{2,1,0:T(8,128)(2,1)S(1)}, bf16[17,16,128]{2,1,0:T(8,128)(2,1)S(1)}, u32[]{:S(2)}, u32[]{:S(2)}) collective-permute-start(bf16[17,16,128]{2,1,0:T(8,128)(2,1)S(1)} %get-tuple-element.72), channel_id=1, source_target_pairs={{0,4},{1,5},{2,6},{3,7},{4,0},{5,1},{6,2},{7,3},{8,12},{9,13},{10,... | collective-permute-start | bytes 208904 | tf_op jit(solution)/shard_map/ppermute | solution.py:387
  42.8 6.1 %collective-permute-start.14 = (bf16[17,16,128]{2,1,0:T(8,128)(2,1)S(1)}, bf16[17,16,128]{2,1,0:T(8,128)(2,1)S(1)}, u32[]{:S(2)}, u32[]{:S(2)}) collective-permute-start(bf16[17,16,128]{2,1,0:T(8,128)(2,1)S(1)} %get-tuple-element.72), channel_id=1, source_target_pairs={{0,12},{1,13},{2,14},{3,15},{4,8},{5,9},{6,10},{7,11},{8,4},{9,5},... | collective-permute-start | bytes 208904 | tf_op jit(solution)/shard_map/ppermute | solution.py:387
  44.4 4.6 %collective-permute-start.13 = (bf16[1,17,16,128]{3,2,1,0:T(8,128)(2,1)S(1)}, bf16[1,17,16,128]{3,2,1,0:T(8,128)(2,1)S(1)}, u32[]{:S(2)}, u32[]{:S(2)}) collective-permute-start(bf16[1,17,16,128]{3,2,1,0:T(8,128)(2,1)S(1)} %bitcast.12), channel_id=1, source_target_pairs={{0,2},{1,3},{2,0},{3,1},{4,6},{5,7},{6,4},{7,5},{8,10},{9,11},{10,... | collective-permute-start | bytes 208904 | tf_op jit(solution)/shard_map/ppermute | solution.py:387
  49.0 5.9 %collective-permute-start.17 = (bf16[3,17,16,128]{3,2,1,0:T(8,128)(2,1)S(1)}, bf16[3,17,16,128]{3,2,1,0:T(8,128)(2,1)S(1)}, u32[]{:S(2)}, u32[]{:S(2)}) collective-permute-start(bf16[3,17,16,128]{3,2,1,0:T(8,128)(2,1)S(1)} %pad_maximum_fusion.2), channel_id=1, source_target_pairs={{0,2},{1,3},{2,0},{3,1},{4,6},{5,7},{6,4},{7,5},{8,10},{9,11},{10,... | collective-permute-start | bytes 626696 | tf_op jit(solution)/shard_map/ppermute | solution.py:387
  55.7 1.3 %collective-permute-start.18 = (f32[16,1152]{1,0:T(8,128)S(1)}, f32[16,1152]{1,0:T(8,128)S(1)}, u32[]{:S(2)}, u32[]{:S(2)}) collective-permute-start(f32[16,1152]{1,0:T(8,128)S(1)} %shard_map.87.message_ref), channel_id=1, source_target_pairs={{0,1},{1,0},{2,3},{3,2},{4,5},{5,4},{6,7},{7,6},{8,9},{9,8},{10,11... | collective-permute-start | bytes 221192 | tf_op jit(solution)/shard_map/ppermute | solution.py:387
  58.6 7.1 %collective-permute-start.20 = (bf16[49,16,128]{2,1,0:T(8,128)(2,1)S(1)}, bf16[49,16,128]{2,1,0:T(8,128)(2,1)S(1)}, u32[]{:S(2)}, u32[]{:S(2)}) collective-permute-start(bf16[49,16,128]{2,1,0:T(8,128)(2,1)S(1)} %get-tuple-element.87), channel_id=1, source_target_pairs={{0,2},{1,3},{2,0},{3,1},{4,6},{5,7},{6,4},{7,5},{8,10},{9,11},{10,... | collective-permute-start | bytes 602120 | tf_op jit(solution)/shard_map/ppermute | solution.py:387
  65.9 8.7 %collective-permute-start.21 = (bf16[17,16,128]{2,1,0:T(8,128)(2,1)S(1)}, bf16[17,16,128]{2,1,0:T(8,128)(2,1)S(1)}, u32[]{:S(2)}, u32[]{:S(2)}) collective-permute-start(bf16[17,16,128]{2,1,0:T(8,128)(2,1)S(1)} %get-tuple-element.91), channel_id=1, source_target_pairs={{0,12},{1,13},{2,14},{3,15},{4,8},{5,9},{6,10},{7,11},{8,4},{9,5},... | collective-permute-start | bytes 208904 | tf_op jit(solution)/shard_map/ppermute | solution.py:387
  67.8 6.7 %collective-permute-start.22 = (bf16[17,16,128]{2,1,0:T(8,128)(2,1)S(1)}, bf16[17,16,128]{2,1,0:T(8,128)(2,1)S(1)}, u32[]{:S(2)}, u32[]{:S(2)}) collective-permute-start(bf16[17,16,128]{2,1,0:T(8,128)(2,1)S(1)} %get-tuple-element.92), channel_id=1, source_target_pairs={{0,8},{1,9},{2,10},{3,11},{4,12},{5,13},{6,14},{7,15},{8,0},{9,1},... | collective-permute-start | bytes 208904 | tf_op jit(solution)/shard_map/ppermute | solution.py:387
  67.8 6.7 %collective-permute-start.23 = (bf16[17,16,128]{2,1,0:T(8,128)(2,1)S(1)}, bf16[17,16,128]{2,1,0:T(8,128)(2,1)S(1)}, u32[]{:S(2)}, u32[]{:S(2)}) collective-permute-start(bf16[17,16,128]{2,1,0:T(8,128)(2,1)S(1)} %get-tuple-element.93), channel_id=1, source_target_pairs={{0,4},{1,5},{2,6},{3,7},{4,0},{5,1},{6,2},{7,3},{8,12},{9,13},{10,... | collective-permute-start | bytes 208904 | tf_op jit(solution)/shard_map/ppermute | solution.py:387
  70.3 4.3 %collective-permute-start.19 = (bf16[16,16,128]{2,1,0:T(8,128)(2,1)S(1)}, bf16[16,16,128]{2,1,0:T(8,128)(2,1)S(1)}, u32[]{:S(2)}, u32[]{:S(2)}) collective-permute-start(bf16[16,16,128]{2,1,0:T(8,128)(2,1)S(1)} %get-tuple-element.85), channel_id=1, source_target_pairs={{0,2},{1,3},{2,0},{3,1},{4,6},{5,7},{6,4},{7,5},{8,10},{9,11},{10,... | collective-permute-start | bytes 196616 | tf_op jit(solution)/shard_map/ppermute | solution.py:387

commit v5 on v4

--- a/solution.py
+++ b/solution.py
@@ -205,13 +205,13 @@
 
 
 def add_kernel(
-    rhs, chunks, bases, beside_ref, late_ref, turned_ref, places_ref, part_ref, sums_ref, message_ref
-):
-    panels = (beside_ref, late_ref)
+    rhs, chunks, bases, turned_ref, places_ref, part_ref, sums_ref, *rest
+):
+    *panels, message_ref = rest
     total = far_terms(part_ref[...], panels, turned_ref, places_ref[...], bases, rhs, chunks)
     width = total.shape[1]
     message_ref[:, :width] = total
-    message_ref[:, width:] = sums_ref[...] + decode(codes_of(beside_ref, chunks) + codes_of(late_ref, chunks), rhs)
+    message_ref[:, width:] = sums_ref[...] + decode(sum(codes_of(ref, chunks) for ref in panels), rhs)
 
 
 def both_cores(message_ref, got_ref):
@@ -227,30 +227,35 @@
     return lax.dot_general(rounded, rounded, NT, preferred_element_type=F32)
 
 
-def send_terms(send_ref, projected, factors, places, wanted, pair, rhs, chunks):
+def send_terms(sends, projected, factors, places, wanted, pair, rhs, chunks):
+    slots = [(send, i) for send in sends for i in range(send.shape[0] // chunks)]
+
     def store(i, c, piece):
-        send_ref[i * chunks + c] = piece.astype(BF16)
+        send, j = slots[i]
+        send[j * chunks + c] = piece.astype(BF16)
 
     spread_terms(projected, factors, places, wanted, store, rhs, chunks)
-    send_ref[len(wanted) * chunks] = encode(pair, rhs)
+    code = encode(pair, rhs)
+    for send in sends:
+        send[send.shape[0] - 1] = code
 
 
 def first_kernel(
     rhs, chunks, wanted, message_ref, got_ref, right_ref, other_ref, places_ref,
-    send_ref, pair_ref, projected_ref, sums_ref,
+    pair_ref, projected_ref, sums_ref, *sends,
 ):
     projected, sums = both_cores(message_ref, got_ref)
     projected_ref[...] = projected
     sums_ref[...] = sums
     pair = sums + sums_of([rounded_gram(projected)], rhs)
     pair_ref[...] = pair
-    send_terms(send_ref, projected, (right_ref, other_ref), places_ref[...], wanted, pair, rhs, chunks)
+    send_terms(sends, projected, (right_ref, other_ref), places_ref[...], wanted, pair, rhs, chunks)
 
 
 def second_kernel(
     rhs, chunks, wanted, message_ref, got_ref, right_ref, other_ref, places_ref,
     gram_ref, weighted_ref, earlier_ref,
-    send_ref, pair_ref, projected_ref, next_gram_ref, mix_ref,
+    pair_ref, projected_ref, next_gram_ref, mix_ref, *sends,
 ):
     projected, sums = both_cores(message_ref, got_ref)
     next_gram_ref[...] = sums
@@ -262,25 +267,26 @@
     curvature = sums[:, rhs : 2 * rhs] + mixed + mixed.T + gram(weighted[:, rhs:], mix[:, :rhs])
     pair = sums_of([curvature + rounded_gram(projected)], rhs)
     pair_ref[...] = pair
-    send_terms(send_ref, projected, (right_ref, other_ref), places_ref[...], wanted, pair, rhs, chunks)
+    send_terms(sends, projected, (right_ref, other_ref), places_ref[...], wanted, pair, rhs, chunks)
     mix_ref[...] = mix
 
 
 def spread_kernel(
-    rhs, chunks, wanted, projected_ref, left_ref, right_ref, other_ref, places_ref, keep_ref, beside_ref
+    rhs, chunks, wanted, projected_ref, left_ref, right_ref, other_ref, places_ref, pair_ref, keep_ref, *outs
 ):
     projected = projected_ref[...]
-    kept = keep_ref.shape[0] // chunks
+    slots = [(ref, i) for ref in (keep_ref, *outs) for i in range(ref.shape[0] // chunks)]
 
     def store(i, c, piece):
-        if i < kept:
-            keep_ref[i * chunks + c] = piece
-        else:
-            beside_ref[(i - kept) * chunks + c] = piece.astype(BF16)
+        ref, j = slots[i]
+        ref[j * chunks + c] = piece.astype(ref.dtype)
 
     own = projected[:, : projected.shape[1] // 2].astype(BF16)
     own = lax.dot_general(own, left_ref[...], NN, preferred_element_type=F32)
     spread_terms(projected, (right_ref, other_ref), places_ref[...], wanted, store, rhs, chunks, own)
+    for ref in outs:
+        if ref.shape[0] % chunks:
+            ref[ref.shape[0] - 1] = encode(pair_ref[...], rhs)
 
 
 def solution_kernel(rhs, step_ref, right_side_ref, solution_ref):
@@ -291,8 +297,18 @@
     direction_ref[...] = residual_ref[...] + left_multiply(mix_ref[...], right_side_ref[...], rhs)
 
 
-def join_kernel(keep_ref, got_ref, sum_ref):
-    sum_ref[...] = keep_ref[...] + got_ref[...].astype(F32)
+def join_kernel(keep_ref, *rest):
+    *got, sum_ref = rest
+    total = keep_ref[...]
+    for ref in got:
+        total = total + ref[...].astype(F32)
+    sum_ref[...] = total
+
+
+def pass_kernel(keep_ref, got_ref, message_ref):
+    size = keep_ref.shape[0]
+    message_ref[:size] = (keep_ref[...] + got_ref[:size].astype(F32)).astype(BF16)
+    message_ref[size] = got_ref[size]
 
 
 def part_kernel(rhs, keep_ref, pair_ref, got_ref, total_ref, *sends):
@@ -302,8 +318,19 @@
     code = encode(total, rhs)
     for i, send in enumerate(sends):
         at = i * size
-        send[:size] = (keep_ref[at + size : at + 2 * size] + got_ref[at : at + size].astype(F32)).astype(BF16)
+        send[:size] = (keep_ref[at : at + size] + got_ref[at : at + size].astype(F32)).astype(BF16)
         send[size] = code
+
+
+def join_coded_kernel(rhs, keep_ref, pair_ref, *rest):
+    *got, sum_ref, total_ref = rest
+    size = keep_ref.shape[0]
+    total, code = keep_ref[...], jnp.zeros(pair_ref.shape, F32)
+    for ref in got:
+        total = total + ref[:size].astype(F32)
+        code = code + ref[size].astype(F32)
+    sum_ref[...] = total
+    total_ref[...] = pair_ref[...] + decode(code, rhs)
 
 
 def message_kernel(rhs, panel_ref, pair_ref, message_ref):
@@ -319,9 +346,8 @@
     total_ref[...] = pair_ref[...] + decode(got_ref[...].astype(F32), rhs)
 
 
-def gathered_product(keep_ref, plain_ref, pair_ref, got, direction, nugget, rhs, chunks):
-    total = keep_ref[:chunks]
-    total = total + plain_ref[...].astype(F32)
+def gathered_product(keep_ref, pair_ref, got, direction, nugget, rhs, chunks):
+    total = keep_ref[...]
     code = jnp.zeros(pair_ref.shape, F32)
     for ref in got:
         total = total + ref[:chunks].astype(F32)
@@ -330,10 +356,12 @@
     return applied, pair_ref[...] + decode(code, rhs)
 
 
-def middle_kernel(rhs, chunks, direction_ref, nugget_ref, keep_ref, plain_ref, pair_ref, *rest):
-    got, (message_ref, residual_ref, step_ref, gram_ref) = rest[:-4], rest[-4:]
+def middle_kernel(
+    rhs, chunks, direction_ref, nugget_ref, keep_ref, pair_ref, *rest
+):
+    *got, message_ref, residual_ref, step_ref, gram_ref = rest
     direction = direction_ref[...]
-    applied, pair = gathered_product(keep_ref, plain_ref, pair_ref, got, direction, nugget_ref[...], rhs, chunks)
+    applied, pair = gathered_product(keep_ref, pair_ref, got, direction, nugget_ref[...], rhs, chunks)
     first_gram = second_of(pair, rhs)
     gram_ref[...] = first_gram
     step = right_divide(pair, first_gram, rhs)
@@ -344,16 +372,18 @@
     step_ref[...] = step
 
 
-def last_kernel(rhs, chunks, direction_ref, nugget_ref, keep_ref, plain_ref, pair_ref, gram_ref, *rest):
-    got, (residual_ref, solution_ref, out_solution_ref, out_residual_ref) = rest[:-4], rest[-4:]
+def last_kernel(
+    rhs, chunks, direction_ref, nugget_ref, keep_ref, pair_ref, gram_ref, residual_ref, solution_ref, *rest
+):
+    *got, out_solution_ref, out_residual_ref = rest
     direction = direction_ref[...]
-    applied, pair = gathered_product(keep_ref, plain_ref, pair_ref, got, direction, nugget_ref[...], rhs, chunks)
+    applied, pair = gathered_product(keep_ref, pair_ref, got, direction, nugget_ref[...], rhs, chunks)
     step = right_divide(pair, gram_ref[...], rhs)
     out_solution_ref[...] = solution_ref[...] + left_multiply(step, direction, rhs)
     out_residual_ref[...] = residual_ref[...] - left_multiply(step, applied, rhs)
 
 
-def call(kernel, outs, *args, far=(), scalars=(), fixed=(), scratch=()):
+def call(kernel, outs, *args, far=(), scalars=(), fixed=(), scratch=(), micros=0.0):
     whole = pl.BlockSpec(memory_space=pltpu.VMEM)
     spaces = {i: pltpu.HBM for i in far} | {i: pltpu.SMEM for i in scalars}
     return pl.pallas_call(
@@ -365,7 +395,7 @@
         in_specs=[pl.BlockSpec(memory_space=spaces[i]) if i in spaces else whole for i in range(len(args))],
         out_specs=[whole] * len(outs),
         scratch_shapes=list(scratch),
-        cost_estimate=pl.CostEstimate(flops=0, bytes_accessed=0, transcendentals=0),
+        cost_estimate=pl.CostEstimate(flops=int(micros * 1e9), bytes_accessed=0, transcendentals=0),
         compiler_params=pltpu.CompilerParams(vmem_limit_bytes=32 * 1024 * 1024),
     )(*args)
 
@@ -424,46 +454,66 @@
     def kept(count):
         return ((count * chunks, rhs, LANES), F32)
 
+    late_sends = [coded(2), coded(1)] if m == 1 else [coded(m)] * 3
+
     def gather(message, first_terms, *early):
-        mine = [message[None]] + [swap(message, k << low_bits)[None] for k in order[1:]]
-        for b in range(low_bits - 1, 1, -1):
-            mine = [jnp.concatenate([g, swap(g, 1 << b)]) for g in mine]
-        beside = swap(mine[0], 2)
-        late_panels = swap(after(jnp.concatenate(mine[1:]), beside, *early), 2)
-        terms, sums, turned, factors, places = first_terms(jnp.concatenate(mine))
-        late_panels = after(late_panels, terms)
+        if m == 1:
+            far_3, far_2 = [swap(message, k << low_bits)[None] for k in order[1:3]]
+            beside = swap(message[None], 2)
+            far_1 = swap(message, order[3] << low_bits)[None]
+            last = [
+                swap(after(jnp.concatenate([far_3, far_2]), *early), 2),
+                swap(beside, order[3] << low_bits),
+            ]
+            bases = (late, late + 1, late + 3)
+            held_panels = jnp.concatenate([message[None], far_3, far_2, far_1])
+        else:
+            mine = [message[None]] + [swap(message, k << low_bits)[None] for k in order[1:]]
+            for b in range(low_bits - 1, 1, -1):
+                mine = [jnp.concatenate([g, swap(g, 1 << b)]) for g in mine]
+            beside = swap(mine[0], 2)
+            last = [swap(jnp.concatenate(mine[1:]), 2)]
+            bases = (late, late + m)
+            held_panels = jnp.concatenate(mine)
+        terms, sums, turned, factors, places = first_terms(held_panels)
+        last = [after(x, terms) for x in last]
         (message,) = call(
-            part(add_kernel, rhs, chunks, (late, late + m)),
-            [core_message],
-            beside, late_panels, turned, places, terms, sums,
+            part(add_kernel, rhs, chunks, bases), [core_message], turned, places, terms, sums, beside, *last
         )
         return message, swap(message, 1), turned, factors, places
 
-    def reduce(send, pair, projected, left, factors, places, *early):
-        got = swap(send, 2)
-        keep, beside = call(
-            part(spread_kernel, rhs, chunks, stay),
-            [kept(4 * m), plain(m)],
-            projected, left, *factors, places,
-        )
+    def reduce(sends, pair, projected, left, factors, places):
+        spread = part(spread_kernel, rhs, chunks, stay)
+        operands = (projected, left, *factors, places, pair)
         if m == 1:
-            pair, *sends = call(
-                part(part_kernel, rhs), [small] + [coded(1)] * 3, keep, pair, after(got, keep, *early)
+            got_side = swap(sends[0], 2)
+            got_far = swap(sends[1], order[3] << low_bits)
+            mine, keep, send, beside = call(spread, [kept(1), kept(2), coded(1), kept(1)], *operands)
+            got_1 = swap(send, order[3] << low_bits)
+            (send,) = call(pass_kernel, [coded(1)], beside, got_far)
+            got_beside = swap(send, 2)
+            total, *sends = call(
+                part(part_kernel, rhs), [small] + [coded(1)] * 2, keep, pair, after(got_side, send)
             )
-            got = [swap(x, k << low_bits) for x, k in zip(sends, order[1:])]
-            return keep, swap(beside, 2), pair, got
-        (pair,) = call(part(pair_kernel, rhs), [small], pair, got[-1])
-        (keep,) = call(join_kernel, [kept(4 * m)], keep, jnp.concatenate([swap(beside, 2), got[:-1]]))
-        size = m * chunks
-        four = [keep[i * size : (i + 1) * size] for i in range(4)]
+            got = [swap(x, k << low_bits) for x, k in zip(sends, order[1:3])]
+            mine, pair = call(
+                part(join_coded_kernel, rhs), [kept(1), small], mine, total, got_1, got_beside, micros=5.0
+            )
+            return mine, pair, got
+        got = [swap(x, k << low_bits) for x, k in zip(sends, order[1:])]
+        keep, *sends, beside = call(spread, [kept(m)] + [plain(m)] * 3 + [kept(m)], *operands)
+        got_here = [swap(x, k << low_bits) for x, k in zip(sends, order[1:])]
+        turned, pair = call(part(join_coded_kernel, rhs), [kept(m), small], beside, pair, *got)
+        (keep,) = call(join_kernel, [kept(m)], keep, *got_here)
         for b in range(2, low_bits):
             (code,) = call(part(code_kernel, rhs), [((rhs, LANES), BF16)], pair)
             (pair,) = call(part(pair_kernel, rhs), [small], pair, swap(code, 1 << b))
-            half = four[0].shape[0] // 2
-            four = [x[:half] + swap(x[half:].astype(BF16), 1 << b).astype(F32) for x in four]
-        sends = [call(part(message_kernel, rhs), [coded(1)], x, pair)[0] for x in four[1:]]
-        nothing = jnp.zeros(*plain(1))
-        return four[0], nothing, pair, [swap(x, k << low_bits) for x, k in zip(sends, order[1:])]
+            half = keep.shape[0] // 2
+            keep, turned = [
+                x[:half] + swap(x[half:].astype(BF16), 1 << b).astype(F32) for x in (keep, turned)
+            ]
+        (turned,) = call(part(message_kernel, rhs), [coded(1)], turned, pair)
+        return keep, pair, [swap(turned, 2)]
 
     def in_hbm(array):
         return pltpu.with_memory_space_constraint(array, pltpu.HBM)
@@ -488,21 +538,21 @@
             part(load_add_kernel, rhs, chunks, place_of, held),
             [two_rows, ((rhs, 2 * slots * rank), jnp.int32), factor, ((width, 2 * slots * rank), BF16)],
             mine, near, named, other_named, in_hbm(right), other,
-            far=(4,), fixed=(2, 3), scratch=[semaphore],
+            far=(4,), fixed=(2, 3), scratch=[semaphore], micros=0.0,
         )
         return terms, sums, turned, (here, other), places
 
     message, got, turned, factors, places = gather(message, loading, near)
-    send, pair, earlier, weighted = call(
+    pair, earlier, weighted, *sends = call(
         part(first_kernel, rhs, chunks, go),
-        [coded(3 * m), small, two_rows, small],
+        [small, two_rows, small] + late_sends,
         message, got, *factors, places,
     )
-    mine, beside, pair, got = reduce(send, pair, earlier, left, factors, places)
+    mine, pair, got = reduce(sends, pair, earlier, left, factors, places)
     message, residual, step, first_gram = call(
         part(middle_kernel, rhs, chunks),
         [coded(1), panel, small, small],
-        right_sides, nugget, mine, beside, pair, *got,
+        right_sides, nugget, mine, pair, *got,
     )
 
     (solution,) = call(part(solution_kernel, rhs), [panel], step, right_sides)
@@ -512,22 +562,24 @@
             part(near_add_kernel, rhs, chunks, held),
             [two_rows, small],
             after(mine, solution), residual, right_sides, nugget, left, named, places, turned,
+            micros=0.0,
         )
         return terms, sums, turned, factors, places
 
     message, got, *_ = gather(message, loaded)
-    send, pair, projected, next_gram, mix = call(
+    pair, projected, next_gram, mix, *sends = call(
         part(second_kernel, rhs, chunks, go),
-        [coded(3 * m), small, two_rows, small, small],
+        [small, two_rows, small, small] + late_sends,
         message, got, *factors, places, first_gram, weighted, earlier,
     )
     (direction,) = call(part(direction_kernel, rhs), [panel], mix, right_sides, residual)
-    mine, beside, pair, got = reduce(send, pair, projected, left, factors, places, direction)
+    projected = after(projected, direction)
+    mine, pair, got = reduce(sends, pair, projected, left, factors, places)
     return tuple(
         call(
             part(last_kernel, rhs, chunks),
             [panel, panel],
-            direction, nugget, mine, beside, pair, next_gram, *got, residual, solution,
+            direction, nugget, mine, pair, next_gram, residual, solution, *got,
         )
     )
 

time: 76.4 us -> 72.1 us (0.944)
  waiting for transfers between devices: 25.1 us -> 22.3 us
  starting transfers between devices: 31.8 us -> 30 us
    ppermute x24 -> x28, waiting for transfers between devices: 25.1 us -> 22.3 us  [swap(): return lax.ppermute(array, 'row', [(i, i ^ offset) for i in range(devices)])]
    ppermute x24 -> x28, starting transfers between devices: 31.8 us -> 30 us  [swap(): return lax.ppermute(array, 'row', [(i, i ^ offset) for i in range(devices)])]
    pallas_call x16 -> x20, Pallas kernels: 17.8 us -> 18 us  [call(): pl.pallas_call(kernel, out_shape=[pltpu.VMEM(shape, dtype) if i in fixed...]
  transfers between devices with their start and end apart: 24 -> 28, of which waited for: 13 -> 16; matrix products, arithmetic and copies ran while one was open for 0% -> 0% of each run, Pallas kernels for 12% -> 14%
where the time goes in v5:
time: 72.1 us; the launch traced here: 71.9 us
  starting transfers between devices  30 us (42%)
  waiting for transfers between devices  22.3 us (31%)
  Pallas kernels  18 us (25%)
  between operations  1.44 us (2%)
    ppermute x28, starting transfers between devices, swap(): return lax.ppermute(array, 'row', [(i, i ^ offset) for i in range(devices)])  30 us
    ppermute x28, waiting for transfers between devices, swap(): return lax.ppermute(array, 'row', [(i, i ^ offset) for i in range(devices)])  22.3 us
    pallas_call x20, Pallas kernels, call(): pl.pallas_call(kernel, out_shape=[pltpu.VMEM(shape, dtype) if i in fixed...  18 us
  transfers between devices with their start and end apart: 28, of which 16 were waited for; matrix products, arithmetic and copies ran while one was open for 0% of the time, Pallas kernels for 14%

profile of v5, /device:TPU:0, one launch (start us, length us, event | category | flops | bytes accessed | tf_op | source)
XLA Modules:
  0.0 71.9 jit_solution(14698957929838188545)
XLA Ops:
  2.1 4.7 %collective-permute-start = (bf16[16,16,128]{2,1,0:T(8,128)(2,1)S(1)}, bf16[16,16,128]{2,1,0:T(8,128)(2,1)S(1)}, u32[]{:S(2)}, u32[]{:S(2)}) collective-permute-start(bf16[16,16,128]{2,1,0:T(8,128)(2,1)S(1)} %get-tuple-element.58), channel_id=1, source_target_pairs={{0,12},{1,13},{2,14},{3,15},{4,8},{5,9},{6,10},{7,11},{8,4},{9,5},... | collective-permute-start | bytes 196616 | tf_op jit(solution)/shard_map/ppermute | solution.py:417
  7.4 1.7 %collective-permute-start.5 = (bf16[1,16,16,128]{3,2,1,0:T(8,128)(2,1)S(1)}, bf16[1,16,16,128]{3,2,1,0:T(8,128)(2,1)S(1)}, u32[]{:S(2)}, u32[]{:S(2)}) collective-permute-start(bf16[1,16,16,128]{3,2,1,0:T(8,128)(2,1)S(1)} %bitcast.14), channel_id=1, source_target_pairs={{0,2},{1,3},{2,0},{3,1},{4,6},{5,7},{6,4},{7,5},{8,10},{9,11},{10,... | collective-permute-start | bytes 196616 | tf_op jit(solution)/shard_map/ppermute | solution.py:417
  9.7 2.3 %shard_map.78 = (f32[1,2048]{1,0:T(1,128)S(1)}, bf16[512,2048]{1,0:T(8,128)(2,1)S(1)}, s32[8,512]{1,0:T(8,128)S(1)}, f32[16,512]{1,0:T(8,128)S(1)}, f32[16,128]{1,0:T(8,128)S(1)}) custom-call(f32[16,2048]{1,0:T(8,128)S(1)} %get-tuple-element.59.own_ref.direction_ref.right_side_ref, s32[32]{0:T(128)} %bitcast.30, s32[1]{0:T(128)S(6)} %copy.8.live_ref, ...), custom_call_target="tpu_custom_call" | custom-call | tf_op jit(solution)/shard_map/pallas_call | solution.py:389
  12.8 1.6 %collective-permute-start.6 = (bf16[2,16,16,128]{3,2,1,0:T(8,128)(2,1)S(1)}, bf16[2,16,16,128]{3,2,1,0:T(8,128)(2,1)S(1)}, u32[]{:S(2)}, u32[]{:S(2)}) collective-permute-start(bf16[2,16,16,128]{3,2,1,0:T(8,128)(2,1)S(1)} %pad_maximum_fusion.3), channel_id=1, source_target_pairs={{0,2},{1,3},{2,0},{3,1},{4,6},{5,7},{6,4},{7,5},{8,10},{9,11},{10,... | collective-permute-start | bytes 393224 | tf_op jit(solution)/shard_map/ppermute | solution.py:417
  15.6 2.6 %shard_map.79 = (f32[16,1024]{1,0:T(8,128)S(1)}, s32[16,1024]{1,0:T(8,128)S(1)}, bf16[512,2048]{1,0:T(8,128)(2,1)S(1)}, bf16[2048,1024]{1,0:T(8,128)(2,1)S(1)}) custom-call(bf16[4,16,16,128]{3,2,1,0:T(8,128)(2,1)S(1)} %pad_maximum_fusion.1.held_ref, f32[16,512]{1,0:T(8,128)S(1)} %get-tuple-element.60.near_ref, s32[8,512]{1,0:T(8,128)S(1)} %get-tuple-element.61.named_ref, ...), custom_call_target="tpu_custom_call" | custom-call | tf_op jit(solution)/shard_map/pallas_call | solution.py:389
  19.9 1.3 %collective-permute-done.8.got_ref = f32[16,1152]{1,0:T(8,128)S(1)} collective-permute-done((f32[16,1152]{1,0:T(8,128)S(1)}, f32[16,1152]{1,0:T(8,128)S(1)}, u32[]{:S(2)}, u32[]{:S(2)}) %collective-permute-start.8) | collective-permute-done | bytes 73760 | tf_op jit(solution)/shard_map/ppermute | solution.py:417
  24.1 1.7 %collective-permute-start.11 = (bf16[17,16,128]{2,1,0:T(8,128)(2,1)S(1)}, bf16[17,16,128]{2,1,0:T(8,128)(2,1)S(1)}, u32[]{:S(2)}, u32[]{:S(2)}) collective-permute-start(bf16[17,16,128]{2,1,0:T(8,128)(2,1)S(1)} %get-tuple-element.82), channel_id=1, source_target_pairs={{0,4},{1,5},{2,6},{3,7},{4,0},{5,1},{6,2},{7,3},{8,12},{9,13},{10,... | collective-permute-start | bytes 208904 | tf_op jit(solution)/shard_map/ppermute | solution.py:417
  27.9 2.5 %collective-permute-start.13 = (bf16[17,16,128]{2,1,0:T(8,128)(2,1)S(1)}, bf16[17,16,128]{2,1,0:T(8,128)(2,1)S(1)}, u32[]{:S(2)}, u32[]{:S(2)}) collective-permute-start(bf16[17,16,128]{2,1,0:T(8,128)(2,1)S(1)} %get-tuple-element.85), channel_id=1, source_target_pairs={{0,12},{1,13},{2,14},{3,15},{4,8},{5,9},{6,10},{7,11},{8,4},{9,5},... | collective-permute-start | bytes 208904 | tf_op jit(solution)/shard_map/ppermute | solution.py:417
  30.4 1.4 %collective-permute-start.14 = (bf16[17,16,128]{2,1,0:T(8,128)(2,1)S(1)}, bf16[17,16,128]{2,1,0:T(8,128)(2,1)S(1)}, u32[]{:S(2)}, u32[]{:S(2)}) collective-permute-start(bf16[17,16,128]{2,1,0:T(8,128)(2,1)S(1)} %get-tuple-element.86), channel_id=1, source_target_pairs={{0,8},{1,9},{2,10},{3,11},{4,12},{5,13},{6,14},{7,15},{8,0},{9,1},... | collective-permute-start | bytes 208904 | tf_op jit(solution)/shard_map/ppermute | solution.py:417
  31.9 2.5 %collective-permute-done.13.rest_0_ = bf16[17,16,128]{2,1,0:T(8,128)(2,1)S(1)} collective-permute-done((bf16[17,16,128]{2,1,0:T(8,128)(2,1)S(1)}, bf16[17,16,128]{2,1,0:T(8,128)(2,1)S(1)}, u32[]{:S(2)}, u32[]{:S(2)}) %collective-permute-start.13) | collective-permute-done | bytes 69664 | tf_op jit(solution)/shard_map/ppermute | solution.py:417
  34.4 2.8 %collective-permute-done.14.rest_1_ = bf16[17,16,128]{2,1,0:T(8,128)(2,1)S(1)} collective-permute-done((bf16[17,16,128]{2,1,0:T(8,128)(2,1)S(1)}, bf16[17,16,128]{2,1,0:T(8,128)(2,1)S(1)}, u32[]{:S(2)}, u32[]{:S(2)}) %collective-permute-start.14) | collective-permute-done | bytes 69664 | tf_op jit(solution)/shard_map/ppermute | solution.py:417
  37.2 1.3 %shard_map.86 = (bf16[17,16,128]{2,1,0:T(8,128)(2,1)S(1)}, f32[16,2048]{1,0:T(8,128)S(1)}, f32[16,128]{1,0:T(8,128)S(1)}, f32[16,128]{1,0:T(8,128)S(1)}) custom-call(f32[16,2048]{1,0:T(8,128)S(1)} %get-tuple-element.59.own_ref.direction_ref.right_side_ref, f32[1,2048]{1,0:T(1,128)S(1)} %get-tuple-element.65.nugget_ref, ...), custom_call_target="tpu_custom_call" | custom-call | tf_op jit(solution)/shard_map/pallas_call | solution.py:389
  38.8 2.1 %collective-permute-start.15 = (bf16[17,16,128]{2,1,0:T(8,128)(2,1)S(1)}, bf16[17,16,128]{2,1,0:T(8,128)(2,1)S(1)}, u32[]{:S(2)}, u32[]{:S(2)}) collective-permute-start(bf16[17,16,128]{2,1,0:T(8,128)(2,1)S(1)} %get-tuple-element.87), channel_id=1, source_target_pairs={{0,12},{1,13},{2,14},{3,15},{4,8},{5,9},{6,10},{7,11},{8,4},{9,5},... | collective-permute-start | bytes 208904 | tf_op jit(solution)/shard_map/ppermute | solution.py:417
  42.9 1.2 %collective-permute-done.16 = bf16[17,16,128]{2,1,0:T(8,128)(2,1)S(1)} collective-permute-done((bf16[17,16,128]{2,1,0:T(8,128)(2,1)S(1)}, bf16[17,16,128]{2,1,0:T(8,128)(2,1)S(1)}, u32[]{:S(2)}, u32[]{:S(2)}) %collective-permute-start.16) | collective-permute-done | bytes 69664 | tf_op jit(solution)/shard_map/ppermute | solution.py:417
  48.0 1.8 %shard_map.88 = (f32[16,1024]{1,0:T(8,128)S(1)}, f32[16,128]{1,0:T(8,128)S(1)}) custom-call(bf16[4,17,16,128]{3,2,1,0:T(8,128)(2,1)S(1)} %pad_maximum_fusion.held_ref, f32[16,2048]{1,0:T(8,128)S(1)} %get-tuple-element.90.own_ref.residual_ref, f32[16,2048]{1,0:T(8,128)S(1)} %get-tuple-element.59.own_ref.direction_ref.right_side_ref, ...), custom_call_target="tpu_custom_call" | custom-call | tf_op jit(solution)/shard_map/pallas_call | solution.py:389
  49.8 1.3 %collective-permute-done.20.rest_2_ = bf16[1,17,16,128]{3,2,1,0:T(8,128)(2,1)S(1)} collective-permute-done((bf16[1,17,16,128]{3,2,1,0:T(8,128)(2,1)S(1)}, bf16[1,17,16,128]{3,2,1,0:T(8,128)(2,1)S(1)}, u32[]{:S(2)}, u32[]{:S(2)}) %collective-permute-start.20) | collective-permute-done | bytes 69664 | tf_op jit(solution)/shard_map/ppermute | solution.py:417
  52.0 1.3 %collective-permute-done.21.got_ref = f32[16,1152]{1,0:T(8,128)S(1)} collective-permute-done((f32[16,1152]{1,0:T(8,128)S(1)}, f32[16,1152]{1,0:T(8,128)S(1)}, u32[]{:S(2)}, u32[]{:S(2)}) %collective-permute-start.21) | collective-permute-done | bytes 73760 | tf_op jit(solution)/shard_map/ppermute | solution.py:417
  53.3 1.6 %shard_map.90 = (f32[16,128]{1,0:T(8,128)S(1)}, f32[16,1024]{1,0:T(8,128)S(1)}, f32[16,128]{1,0:T(8,128)S(1)}, f32[16,128]{1,0:T(8,128)S(1)}, bf16[33,16,128]{2,...) custom-call(f32[16,1152]{1,0:T(8,128)S(1)} %shard_map.89.message_ref, f32[16,1152]{1,0:T(8,128)S(1)} %collective-permute-done.21.got_ref, ...), custom_call_target="tpu_custom_call" | custom-call | tf_op jit(solution)/shard_map/pallas_call | solution.py:389
  54.8 1.2 %collective-permute-start.23 = (bf16[17,16,128]{2,1,0:T(8,128)(2,1)S(1)}, bf16[17,16,128]{2,1,0:T(8,128)(2,1)S(1)}, u32[]{:S(2)}, u32[]{:S(2)}) collective-permute-start(bf16[17,16,128]{2,1,0:T(8,128)(2,1)S(1)} %get-tuple-element.105), channel_id=1, source_target_pairs={{0,4},{1,5},{2,6},{3,7},{4,0},{5,1},{6,2},{7,3},{8,12},{9,13},{10,... | collective-permute-start | bytes 208904 | tf_op jit(solution)/shard_map/ppermute | solution.py:417
  58.1 1.4 %collective-permute-start.24 = (bf16[17,16,128]{2,1,0:T(8,128)(2,1)S(1)}, bf16[17,16,128]{2,1,0:T(8,128)(2,1)S(1)}, u32[]{:S(2)}, u32[]{:S(2)}) collective-permute-start(bf16[17,16,128]{2,1,0:T(8,128)(2,1)S(1)} %get-tuple-element.108), channel_id=1, source_target_pairs={{0,4},{1,5},{2,6},{3,7},{4,0},{5,1},{6,2},{7,3},{8,12},{9,13},{10,... | collective-permute-start | bytes 208904 | tf_op jit(solution)/shard_map/ppermute | solution.py:417
  61.6 1.8 %collective-permute-start.26 = (bf16[17,16,128]{2,1,0:T(8,128)(2,1)S(1)}, bf16[17,16,128]{2,1,0:T(8,128)(2,1)S(1)}, u32[]{:S(2)}, u32[]{:S(2)}) collective-permute-start(bf16[17,16,128]{2,1,0:T(8,128)(2,1)S(1)} %get-tuple-element.112), channel_id=1, source_target_pairs={{0,12},{1,13},{2,14},{3,15},{4,8},{5,9},{6,10},{7,11},{8,4},{9,5},... | collective-permute-start | bytes 208904 | tf_op jit(solution)/shard_map/ppermute | solution.py:417
  64.1 3.7 %collective-permute-done.26.rest_0_ = bf16[17,16,128]{2,1,0:T(8,128)(2,1)S(1)} collective-permute-done((bf16[17,16,128]{2,1,0:T(8,128)(2,1)S(1)}, bf16[17,16,128]{2,1,0:T(8,128)(2,1)S(1)}, u32[]{:S(2)}, u32[]{:S(2)}) %collective-permute-start.26) | collective-permute-done | bytes 69664 | tf_op jit(solution)/shard_map/ppermute | solution.py:417
  67.7 2.5 %collective-permute-done.27.rest_1_ = bf16[17,16,128]{2,1,0:T(8,128)(2,1)S(1)} collective-permute-done((bf16[17,16,128]{2,1,0:T(8,128)(2,1)S(1)}, bf16[17,16,128]{2,1,0:T(8,128)(2,1)S(1)}, u32[]{:S(2)}, u32[]{:S(2)}) %collective-permute-start.27) | collective-permute-done | bytes 69664 | tf_op jit(solution)/shard_map/ppermute | solution.py:417
  70.3 1.6 %shard_map.96 = (f32[16,2048]{1,0:T(8,128)}, f32[16,2048]{1,0:T(8,128)}) custom-call(f32[16,2048]{1,0:T(8,128)S(1)} %shard_map.91.direction_ref, f32[1,2048]{1,0:T(1,128)S(1)} %get-tuple-element.65.nugget_ref, f32[16,16,128]{2,1,0:T(8,128)S(1)} %get-tuple-element.109.keep_ref, f32[16,128]{1,0:T(8,128)S(1)} %get-tuple-element.110.pair_ref, ...), custom_call_target="tpu_custom_call" | custom-call | tf_op jit(solution)/shard_map/pallas_call | solution.py:389
  (56 shorter events, 22.7 us)
Async XLA Ops:
  1.6 14.1 %collective-permute-start.4 = (bf16[512,2048]{1,0:T(8,128)(2,1)}, bf16[512,2048]{1,0:T(8,128)(2,1)S(1)}, u32[]{:S(2)}, u32[]{:S(2)}) collective-permute-start(bf16[512,2048]{1,0:T(8,128)(2,1)} %bitcast.17), channel_id=1, source_target_pairs={{0,1},{1,0},{2,3},{3,2},{4,5},{5,4},{6,7},{7,6},{8,9},{9,8},{10,11... | collective-permute-start | bytes 6291464 | tf_op jit(solution)/shard_map/ppermute | solution.py:417
  2.1 9.9 %collective-permute-start = (bf16[16,16,128]{2,1,0:T(8,128)(2,1)S(1)}, bf16[16,16,128]{2,1,0:T(8,128)(2,1)S(1)}, u32[]{:S(2)}, u32[]{:S(2)}) collective-permute-start(bf16[16,16,128]{2,1,0:T(8,128)(2,1)S(1)} %get-tuple-element.58), channel_id=1, source_target_pairs={{0,12},{1,13},{2,14},{3,15},{4,8},{5,9},{6,10},{7,11},{8,4},{9,5},... | collective-permute-start | bytes 196616 | tf_op jit(solution)/shard_map/ppermute | solution.py:417
  6.8 6.1 %collective-permute-start.1 = (bf16[16,16,128]{2,1,0:T(8,128)(2,1)S(1)}, bf16[16,16,128]{2,1,0:T(8,128)(2,1)S(1)}, u32[]{:S(2)}, u32[]{:S(2)}) collective-permute-start(bf16[16,16,128]{2,1,0:T(8,128)(2,1)S(1)} %get-tuple-element.58), channel_id=1, source_target_pairs={{0,8},{1,9},{2,10},{3,11},{4,12},{5,13},{6,14},{7,15},{8,0},{9,1},... | collective-permute-start | bytes 196616 | tf_op jit(solution)/shard_map/ppermute | solution.py:417
  6.8 7.7 %collective-permute-start.2 = (bf16[16,16,128]{2,1,0:T(8,128)(2,1)S(1)}, bf16[16,16,128]{2,1,0:T(8,128)(2,1)S(1)}, u32[]{:S(2)}, u32[]{:S(2)}) collective-permute-start(bf16[16,16,128]{2,1,0:T(8,128)(2,1)S(1)} %get-tuple-element.58), channel_id=1, source_target_pairs={{0,4},{1,5},{2,6},{3,7},{4,0},{5,1},{6,2},{7,3},{8,12},{9,13},{10,... | collective-permute-start | bytes 196616 | tf_op jit(solution)/shard_map/ppermute | solution.py:417
  7.4 7.0 %collective-permute-start.5 = (bf16[1,16,16,128]{3,2,1,0:T(8,128)(2,1)S(1)}, bf16[1,16,16,128]{3,2,1,0:T(8,128)(2,1)S(1)}, u32[]{:S(2)}, u32[]{:S(2)}) collective-permute-start(bf16[1,16,16,128]{3,2,1,0:T(8,128)(2,1)S(1)} %bitcast.14), channel_id=1, source_target_pairs={{0,2},{1,3},{2,0},{3,1},{4,6},{5,7},{6,4},{7,5},{8,10},{9,11},{10,... | collective-permute-start | bytes 196616 | tf_op jit(solution)/shard_map/ppermute | solution.py:417
  12.8 5.4 %collective-permute-start.6 = (bf16[2,16,16,128]{3,2,1,0:T(8,128)(2,1)S(1)}, bf16[2,16,16,128]{3,2,1,0:T(8,128)(2,1)S(1)}, u32[]{:S(2)}, u32[]{:S(2)}) collective-permute-start(bf16[2,16,16,128]{3,2,1,0:T(8,128)(2,1)S(1)} %pad_maximum_fusion.3), channel_id=1, source_target_pairs={{0,2},{1,3},{2,0},{3,1},{4,6},{5,7},{6,4},{7,5},{8,10},{9,11},{10,... | collective-permute-start | bytes 393224 | tf_op jit(solution)/shard_map/ppermute | solution.py:417
  14.4 4.5 %collective-permute-start.7 = (bf16[1,16,16,128]{3,2,1,0:T(8,128)(2,1)S(1)}, bf16[1,16,16,128]{3,2,1,0:T(8,128)(2,1)S(1)}, u32[]{:S(2)}, u32[]{:S(2)}) collective-permute-start(bf16[1,16,16,128]{3,2,1,0:T(8,128)(2,1)S(1)} %collective-permute-done.5.rest_0_), channel_id=1, source_target_pairs={{0,4},{1,5},{2,6},{3,7},{4,0},{5,1},{6,2},{7,3},{8,12},{9,13},{10,... | collective-permute-start | bytes 196616 | tf_op jit(solution)/shard_map/ppermute | solution.py:417
  22.0 4.4 %collective-permute-start.10 = (bf16[17,16,128]{2,1,0:T(8,128)(2,1)S(1)}, bf16[17,16,128]{2,1,0:T(8,128)(2,1)S(1)}, u32[]{:S(2)}, u32[]{:S(2)}) collective-permute-start(bf16[17,16,128]{2,1,0:T(8,128)(2,1)S(1)} %get-tuple-element.79), channel_id=1, source_target_pairs={{0,4},{1,5},{2,6},{3,7},{4,0},{5,1},{6,2},{7,3},{8,12},{9,13},{10,... | collective-permute-start | bytes 208904 | tf_op jit(solution)/shard_map/ppermute | solution.py:417
  22.3 5.4 %collective-permute-start.9 = (bf16[33,16,128]{2,1,0:T(8,128)(2,1)S(1)}, bf16[33,16,128]{2,1,0:T(8,128)(2,1)S(1)}, u32[]{:S(2)}, u32[]{:S(2)}) collective-permute-start(bf16[33,16,128]{2,1,0:T(8,128)(2,1)S(1)} %get-tuple-element.77), channel_id=1, source_target_pairs={{0,2},{1,3},{2,0},{3,1},{4,6},{5,7},{6,4},{7,5},{8,10},{9,11},{10,... | collective-permute-start | bytes 405512 | tf_op jit(solution)/shard_map/ppermute | solution.py:417
  24.1 7.7 %collective-permute-start.11 = (bf16[17,16,128]{2,1,0:T(8,128)(2,1)S(1)}, bf16[17,16,128]{2,1,0:T(8,128)(2,1)S(1)}, u32[]{:S(2)}, u32[]{:S(2)}) collective-permute-start(bf16[17,16,128]{2,1,0:T(8,128)(2,1)S(1)} %get-tuple-element.82), channel_id=1, source_target_pairs={{0,4},{1,5},{2,6},{3,7},{4,0},{5,1},{6,2},{7,3},{8,12},{9,13},{10,... | collective-permute-start | bytes 208904 | tf_op jit(solution)/shard_map/ppermute | solution.py:417
  26.4 5.5 %collective-permute-start.12 = (bf16[17,16,128]{2,1,0:T(8,128)(2,1)S(1)}, bf16[17,16,128]{2,1,0:T(8,128)(2,1)S(1)}, u32[]{:S(2)}, u32[]{:S(2)}) collective-permute-start(bf16[17,16,128]{2,1,0:T(8,128)(2,1)S(1)} %shard_map.83), channel_id=1, source_target_pairs={{0,2},{1,3},{2,0},{3,1},{4,6},{5,7},{6,4},{7,5},{8,10},{9,11},{10,... | collective-permute-start | bytes 208904 | tf_op jit(solution)/shard_map/ppermute | solution.py:417
  27.9 6.5 %collective-permute-start.13 = (bf16[17,16,128]{2,1,0:T(8,128)(2,1)S(1)}, bf16[17,16,128]{2,1,0:T(8,128)(2,1)S(1)}, u32[]{:S(2)}, u32[]{:S(2)}) collective-permute-start(bf16[17,16,128]{2,1,0:T(8,128)(2,1)S(1)} %get-tuple-element.85), channel_id=1, source_target_pairs={{0,12},{1,13},{2,14},{3,15},{4,8},{5,9},{6,10},{7,11},{8,4},{9,5},... | collective-permute-start | bytes 208904 | tf_op jit(solution)/shard_map/ppermute | solution.py:417
  30.4 6.8 %collective-permute-start.14 = (bf16[17,16,128]{2,1,0:T(8,128)(2,1)S(1)}, bf16[17,16,128]{2,1,0:T(8,128)(2,1)S(1)}, u32[]{:S(2)}, u32[]{:S(2)}) collective-permute-start(bf16[17,16,128]{2,1,0:T(8,128)(2,1)S(1)} %get-tuple-element.86), channel_id=1, source_target_pairs={{0,8},{1,9},{2,10},{3,11},{4,12},{5,13},{6,14},{7,15},{8,0},{9,1},... | collective-permute-start | bytes 208904 | tf_op jit(solution)/shard_map/ppermute | solution.py:417
  38.5 5.6 %collective-permute-start.16 = (bf16[17,16,128]{2,1,0:T(8,128)(2,1)S(1)}, bf16[17,16,128]{2,1,0:T(8,128)(2,1)S(1)}, u32[]{:S(2)}, u32[]{:S(2)}) collective-permute-start(bf16[17,16,128]{2,1,0:T(8,128)(2,1)S(1)} %get-tuple-element.87), channel_id=1, source_target_pairs={{0,8},{1,9},{2,10},{3,11},{4,12},{5,13},{6,14},{7,15},{8,0},{9,1},... | collective-permute-start | bytes 208904 | tf_op jit(solution)/shard_map/ppermute | solution.py:417
  38.8 6.3 %collective-permute-start.15 = (bf16[17,16,128]{2,1,0:T(8,128)(2,1)S(1)}, bf16[17,16,128]{2,1,0:T(8,128)(2,1)S(1)}, u32[]{:S(2)}, u32[]{:S(2)}) collective-permute-start(bf16[17,16,128]{2,1,0:T(8,128)(2,1)S(1)} %get-tuple-element.87), channel_id=1, source_target_pairs={{0,12},{1,13},{2,14},{3,15},{4,8},{5,9},{6,10},{7,11},{8,4},{9,5},... | collective-permute-start | bytes 208904 | tf_op jit(solution)/shard_map/ppermute | solution.py:417
  40.9 7.0 %collective-permute-start.17 = (bf16[17,16,128]{2,1,0:T(8,128)(2,1)S(1)}, bf16[17,16,128]{2,1,0:T(8,128)(2,1)S(1)}, u32[]{:S(2)}, u32[]{:S(2)}) collective-permute-start(bf16[17,16,128]{2,1,0:T(8,128)(2,1)S(1)} %get-tuple-element.87), channel_id=1, source_target_pairs={{0,4},{1,5},{2,6},{3,7},{4,0},{5,1},{6,2},{7,3},{8,12},{9,13},{10,... | collective-permute-start | bytes 208904 | tf_op jit(solution)/shard_map/ppermute | solution.py:417
  42.0 4.7 %collective-permute-start.18 = (bf16[1,17,16,128]{3,2,1,0:T(8,128)(2,1)S(1)}, bf16[1,17,16,128]{3,2,1,0:T(8,128)(2,1)S(1)}, u32[]{:S(2)}, u32[]{:S(2)}) collective-permute-start(bf16[1,17,16,128]{3,2,1,0:T(8,128)(2,1)S(1)} %bitcast.12), channel_id=1, source_target_pairs={{0,2},{1,3},{2,0},{3,1},{4,6},{5,7},{6,4},{7,5},{8,10},{9,11},{10,... | collective-permute-start | bytes 208904 | tf_op jit(solution)/shard_map/ppermute | solution.py:417
  45.1 6.0 %collective-permute-start.19 = (bf16[2,17,16,128]{3,2,1,0:T(8,128)(2,1)S(1)}, bf16[2,17,16,128]{3,2,1,0:T(8,128)(2,1)S(1)}, u32[]{:S(2)}, u32[]{:S(2)}) collective-permute-start(bf16[2,17,16,128]{3,2,1,0:T(8,128)(2,1)S(1)} %pad_maximum_fusion.2), channel_id=1, source_target_pairs={{0,2},{1,3},{2,0},{3,1},{4,6},{5,7},{6,4},{7,5},{8,10},{9,11},{10,... | collective-permute-start | bytes 417800 | tf_op jit(solution)/shard_map/ppermute | solution.py:417
  54.8 4.6 %collective-permute-start.23 = (bf16[17,16,128]{2,1,0:T(8,128)(2,1)S(1)}, bf16[17,16,128]{2,1,0:T(8,128)(2,1)S(1)}, u32[]{:S(2)}, u32[]{:S(2)}) collective-permute-start(bf16[17,16,128]{2,1,0:T(8,128)(2,1)S(1)} %get-tuple-element.105), channel_id=1, source_target_pairs={{0,4},{1,5},{2,6},{3,7},{4,0},{5,1},{6,2},{7,3},{8,12},{9,13},{10,... | collective-permute-start | bytes 208904 | tf_op jit(solution)/shard_map/ppermute | solution.py:417
  56.1 5.4 %collective-permute-start.22 = (bf16[33,16,128]{2,1,0:T(8,128)(2,1)S(1)}, bf16[33,16,128]{2,1,0:T(8,128)(2,1)S(1)}, u32[]{:S(2)}, u32[]{:S(2)}) collective-permute-start(bf16[33,16,128]{2,1,0:T(8,128)(2,1)S(1)} %get-tuple-element.103), channel_id=1, source_target_pairs={{0,2},{1,3},{2,0},{3,1},{4,6},{5,7},{6,4},{7,5},{8,10},{9,11},{10,... | collective-permute-start | bytes 405512 | tf_op jit(solution)/shard_map/ppermute | solution.py:417
  58.1 5.9 %collective-permute-start.24 = (bf16[17,16,128]{2,1,0:T(8,128)(2,1)S(1)}, bf16[17,16,128]{2,1,0:T(8,128)(2,1)S(1)}, u32[]{:S(2)}, u32[]{:S(2)}) collective-permute-start(bf16[17,16,128]{2,1,0:T(8,128)(2,1)S(1)} %get-tuple-element.108), channel_id=1, source_target_pairs={{0,4},{1,5},{2,6},{3,7},{4,0},{5,1},{6,2},{7,3},{8,12},{9,13},{10,... | collective-permute-start | bytes 208904 | tf_op jit(solution)/shard_map/ppermute | solution.py:417
  59.5 4.5 %collective-permute-start.25 = (bf16[17,16,128]{2,1,0:T(8,128)(2,1)S(1)}, bf16[17,16,128]{2,1,0:T(8,128)(2,1)S(1)}, u32[]{:S(2)}, u32[]{:S(2)}) collective-permute-start(bf16[17,16,128]{2,1,0:T(8,128)(2,1)S(1)} %shard_map.93), channel_id=1, source_target_pairs={{0,2},{1,3},{2,0},{3,1},{4,6},{5,7},{6,4},{7,5},{8,10},{9,11},{10,... | collective-permute-start | bytes 208904 | tf_op jit(solution)/shard_map/ppermute | solution.py:417
  61.6 6.1 %collective-permute-start.26 = (bf16[17,16,128]{2,1,0:T(8,128)(2,1)S(1)}, bf16[17,16,128]{2,1,0:T(8,128)(2,1)S(1)}, u32[]{:S(2)}, u32[]{:S(2)}) collective-permute-start(bf16[17,16,128]{2,1,0:T(8,128)(2,1)S(1)} %get-tuple-element.112), channel_id=1, source_target_pairs={{0,12},{1,13},{2,14},{3,15},{4,8},{5,9},{6,10},{7,11},{8,4},{9,5},... | collective-permute-start | bytes 208904 | tf_op jit(solution)/shard_map/ppermute | solution.py:417
  63.4 6.8 %collective-permute-start.27 = (bf16[17,16,128]{2,1,0:T(8,128)(2,1)S(1)}, bf16[17,16,128]{2,1,0:T(8,128)(2,1)S(1)}, u32[]{:S(2)}, u32[]{:S(2)}) collective-permute-start(bf16[17,16,128]{2,1,0:T(8,128)(2,1)S(1)} %get-tuple-element.113), channel_id=1, source_target_pairs={{0,8},{1,9},{2,10},{3,11},{4,12},{5,13},{6,14},{7,15},{8,0},{9,1},... | collective-permute-start | bytes 208904 | tf_op jit(solution)/shard_map/ppermute | solution.py:417
  (4 other events, 8.2 us)

commit v6 on v5

--- a/solution.py
+++ b/solution.py
@@ -305,10 +305,11 @@
     sum_ref[...] = total
 
 
-def pass_kernel(keep_ref, got_ref, message_ref):
+def pass_kernel(rhs, keep_ref, *rest):
+    *got, message_ref = rest
     size = keep_ref.shape[0]
-    message_ref[:size] = (keep_ref[...] + got_ref[:size].astype(F32)).astype(BF16)
-    message_ref[size] = got_ref[size]
+    message_ref[:size] = (keep_ref[...] + sum(ref[:size].astype(F32) for ref in got)).astype(BF16)
+    message_ref[size] = encode(decode(sum(ref[size].astype(F32) for ref in got), rhs), rhs)
 
 
 def part_kernel(rhs, keep_ref, pair_ref, got_ref, total_ref, *sends):
@@ -454,7 +455,7 @@
     def kept(count):
         return ((count * chunks, rhs, LANES), F32)
 
-    late_sends = [coded(2), coded(1)] if m == 1 else [coded(m)] * 3
+    late_sends = [coded(m)] * 3
 
     def gather(message, first_terms, *early):
         if m == 1:
@@ -482,29 +483,27 @@
         )
         return message, swap(message, 1), turned, factors, places
 
-    def reduce(sends, pair, projected, left, factors, places):
+    def reduce(sends, pair, projected, left, factors, places, *early):
         spread = part(spread_kernel, rhs, chunks, stay)
         operands = (projected, left, *factors, places, pair)
         if m == 1:
             got_side = swap(sends[0], 2)
-            got_far = swap(sends[1], order[3] << low_bits)
-            mine, keep, send, beside = call(spread, [kept(1), kept(2), coded(1), kept(1)], *operands)
-            got_1 = swap(send, order[3] << low_bits)
-            (send,) = call(pass_kernel, [coded(1)], beside, got_far)
+            got_far = [swap(sends[i], order[i + 1] << low_bits) for i in (1, 2)]
+            mine, keep, *sends, beside = call(spread, [kept(1)] * 2 + [coded(1)] * 2 + [kept(1)], *operands)
+            got_here = [swap(sends[i - 1], order[i + 1] << low_bits) for i in (1, 2)]
+            pair, send = call(part(part_kernel, rhs), [small, coded(1)], keep, pair, got_side)
+            got_last = swap(send, order[1] << low_bits)
+            (send,) = call(part(pass_kernel, rhs), [coded(1)], beside, *got_far)
             got_beside = swap(send, 2)
-            total, *sends = call(
-                part(part_kernel, rhs), [small] + [coded(1)] * 2, keep, pair, after(got_side, send)
-            )
-            got = [swap(x, k << low_bits) for x, k in zip(sends, order[1:3])]
-            mine, pair = call(
-                part(join_coded_kernel, rhs), [kept(1), small], mine, total, got_1, got_beside, micros=5.0
-            )
-            return mine, pair, got
+            join = part(join_coded_kernel, rhs)
+            mine, pair = call(join, [kept(1), small], after(mine, *early), pair, *got_here, micros=0.3)
+            mine, pair = call(join, [kept(1), small], mine, pair, got_last, micros=0.3)
+            return mine, pair, [got_beside]
         got = [swap(x, k << low_bits) for x, k in zip(sends, order[1:])]
         keep, *sends, beside = call(spread, [kept(m)] + [plain(m)] * 3 + [kept(m)], *operands)
         got_here = [swap(x, k << low_bits) for x, k in zip(sends, order[1:])]
         turned, pair = call(part(join_coded_kernel, rhs), [kept(m), small], beside, pair, *got)
-        (keep,) = call(join_kernel, [kept(m)], keep, *got_here)
+        (keep,) = call(join_kernel, [kept(m)], after(keep, *early), *got_here)
         for b in range(2, low_bits):
             (code,) = call(part(code_kernel, rhs), [((rhs, LANES), BF16)], pair)
             (pair,) = call(part(pair_kernel, rhs), [small], pair, swap(code, 1 << b))
@@ -573,8 +572,7 @@
         message, got, *factors, places, first_gram, weighted, earlier,
     )
     (direction,) = call(part(direction_kernel, rhs), [panel], mix, right_sides, residual)
-    projected = after(projected, direction)
-    mine, pair, got = reduce(sends, pair, projected, left, factors, places)
+    mine, pair, got = reduce(sends, pair, projected, left, factors, places, direction)
     return tuple(
         call(
             part(last_kernel, rhs, chunks),

time: 72.1 us -> 69.6 us (0.965)
  waiting for transfers between devices: 22.3 us -> 15.1 us
  starting transfers between devices: 30 us -> 34.4 us
    ppermute x28 -> x30, waiting for transfers between devices: 22.3 us -> 15.1 us  [swap(): return lax.ppermute(array, 'row', [(i, i ^ offset) for i in range(devices)])]
    ppermute x28 -> x30, starting transfers between devices: 30 us -> 34.4 us  [swap(): return lax.ppermute(array, 'row', [(i, i ^ offset) for i in range(devices)])]
    pallas_call x20 -> x22, Pallas kernels: 18 us -> 18.4 us  [call(): pl.pallas_call(kernel, out_shape=[pltpu.VMEM(shape, dtype) if i in fixed...]
  transfers between devices with their start and end apart: 28 -> 30, of which waited for: 16 -> 14; matrix products, arithmetic and copies ran while one was open for 0% -> 0% of each run, Pallas kernels for 14% -> 15%
where the time goes in v6:
time: 69.6 us; the launch traced here: 69.4 us
  starting transfers between devices  34.4 us (49%)
  Pallas kernels  18.4 us (26%)
  waiting for transfers between devices  15.1 us (22%)
  between operations  1.46 us (2%)
    ppermute x30, starting transfers between devices, swap(): return lax.ppermute(array, 'row', [(i, i ^ offset) for i in range(devices)])  34.4 us
    pallas_call x22, Pallas kernels, call(): pl.pallas_call(kernel, out_shape=[pltpu.VMEM(shape, dtype) if i in fixed...  18.4 us
    ppermute x30, waiting for transfers between devices, swap(): return lax.ppermute(array, 'row', [(i, i ^ offset) for i in range(devices)])  15.1 us
  transfers between devices with their start and end apart: 30, of which 14 were waited for; matrix products, arithmetic and copies ran while one was open for 0% of the time, Pallas kernels for 15%

profile of v6, /device:TPU:0, one launch (start us, length us, event | category | flops | bytes accessed | tf_op | source)
XLA Modules:
  0.0 69.4 jit_solution(16191091260999655840)
XLA Ops:
  2.1 4.7 %collective-permute-start = (bf16[16,16,128]{2,1,0:T(8,128)(2,1)S(1)}, bf16[16,16,128]{2,1,0:T(8,128)(2,1)S(1)}, u32[]{:S(2)}, u32[]{:S(2)}) collective-permute-start(bf16[16,16,128]{2,1,0:T(8,128)(2,1)S(1)} %get-tuple-element.62), channel_id=1, source_target_pairs={{0,12},{1,13},{2,14},{3,15},{4,8},{5,9},{6,10},{7,11},{8,4},{9,5},... | collective-permute-start | bytes 196616 | tf_op jit(solution)/shard_map/ppermute | solution.py:418
  7.4 1.7 %collective-permute-start.5 = (bf16[1,16,16,128]{3,2,1,0:T(8,128)(2,1)S(1)}, bf16[1,16,16,128]{3,2,1,0:T(8,128)(2,1)S(1)}, u32[]{:S(2)}, u32[]{:S(2)}) collective-permute-start(bf16[1,16,16,128]{3,2,1,0:T(8,128)(2,1)S(1)} %bitcast.14), channel_id=1, source_target_pairs={{0,2},{1,3},{2,0},{3,1},{4,6},{5,7},{6,4},{7,5},{8,10},{9,11},{10,... | collective-permute-start | bytes 196616 | tf_op jit(solution)/shard_map/ppermute | solution.py:418
  9.7 2.3 %shard_map.78 = (f32[1,2048]{1,0:T(1,128)S(1)}, bf16[512,2048]{1,0:T(8,128)(2,1)S(1)}, s32[8,512]{1,0:T(8,128)S(1)}, f32[16,512]{1,0:T(8,128)S(1)}, f32[16,128]{1,0:T(8,128)S(1)}) custom-call(f32[16,2048]{1,0:T(8,128)S(1)} %get-tuple-element.63.own_ref.direction_ref.right_side_ref, s32[32]{0:T(128)} %bitcast.30, s32[1]{0:T(128)S(6)} %copy.8.live_ref, ...), custom_call_target="tpu_custom_call" | custom-call | tf_op jit(solution)/shard_map/pallas_call | solution.py:390
  12.8 1.6 %collective-permute-start.6 = (bf16[2,16,16,128]{3,2,1,0:T(8,128)(2,1)S(1)}, bf16[2,16,16,128]{3,2,1,0:T(8,128)(2,1)S(1)}, u32[]{:S(2)}, u32[]{:S(2)}) collective-permute-start(bf16[2,16,16,128]{3,2,1,0:T(8,128)(2,1)S(1)} %pad_maximum_fusion.3), channel_id=1, source_target_pairs={{0,2},{1,3},{2,0},{3,1},{4,6},{5,7},{6,4},{7,5},{8,10},{9,11},{10,... | collective-permute-start | bytes 393224 | tf_op jit(solution)/shard_map/ppermute | solution.py:418
  15.6 2.6 %shard_map.79 = (f32[16,1024]{1,0:T(8,128)S(1)}, s32[16,1024]{1,0:T(8,128)S(1)}, bf16[512,2048]{1,0:T(8,128)(2,1)S(1)}, bf16[2048,1024]{1,0:T(8,128)(2,1)S(1)}) custom-call(bf16[4,16,16,128]{3,2,1,0:T(8,128)(2,1)S(1)} %pad_maximum_fusion.1.held_ref, f32[16,512]{1,0:T(8,128)S(1)} %get-tuple-element.64.near_ref, s32[8,512]{1,0:T(8,128)S(1)} %get-tuple-element.65.named_ref, ...), custom_call_target="tpu_custom_call" | custom-call | tf_op jit(solution)/shard_map/pallas_call | solution.py:390
  19.9 1.3 %collective-permute-done.8.got_ref = f32[16,1152]{1,0:T(8,128)S(1)} collective-permute-done((f32[16,1152]{1,0:T(8,128)S(1)}, f32[16,1152]{1,0:T(8,128)S(1)}, u32[]{:S(2)}, u32[]{:S(2)}) %collective-permute-start.8) | collective-permute-done | bytes 73760 | tf_op jit(solution)/shard_map/ppermute | solution.py:418
  22.6 1.6 %collective-permute-start.13 = (bf16[17,16,128]{2,1,0:T(8,128)(2,1)S(1)}, bf16[17,16,128]{2,1,0:T(8,128)(2,1)S(1)}, u32[]{:S(2)}, u32[]{:S(2)}) collective-permute-start(bf16[17,16,128]{2,1,0:T(8,128)(2,1)S(1)} %get-tuple-element.91), channel_id=1, source_target_pairs={{0,8},{1,9},{2,10},{3,11},{4,12},{5,13},{6,14},{7,15},{8,0},{9,1},... | collective-permute-start | bytes 208904 | tf_op jit(solution)/shard_map/ppermute | solution.py:418
  24.2 1.7 %collective-permute-start.14 = (bf16[17,16,128]{2,1,0:T(8,128)(2,1)S(1)}, bf16[17,16,128]{2,1,0:T(8,128)(2,1)S(1)}, u32[]{:S(2)}, u32[]{:S(2)}) collective-permute-start(bf16[17,16,128]{2,1,0:T(8,128)(2,1)S(1)} %get-tuple-element.92), channel_id=1, source_target_pairs={{0,4},{1,5},{2,6},{3,7},{4,0},{5,1},{6,2},{7,3},{8,12},{9,13},{10,... | collective-permute-start | bytes 208904 | tf_op jit(solution)/shard_map/ppermute | solution.py:418
  27.1 1.6 %collective-permute-start.11 = (bf16[17,16,128]{2,1,0:T(8,128)(2,1)S(1)}, bf16[17,16,128]{2,1,0:T(8,128)(2,1)S(1)}, u32[]{:S(2)}, u32[]{:S(2)}) collective-permute-start(bf16[17,16,128]{2,1,0:T(8,128)(2,1)S(1)} %get-tuple-element.84), channel_id=1, source_target_pairs={{0,4},{1,5},{2,6},{3,7},{4,0},{5,1},{6,2},{7,3},{8,12},{9,13},{10,... | collective-permute-start | bytes 208904 | tf_op jit(solution)/shard_map/ppermute | solution.py:418
  28.9 2.8 %collective-permute-start.12 = (bf16[17,16,128]{2,1,0:T(8,128)(2,1)S(1)}, bf16[17,16,128]{2,1,0:T(8,128)(2,1)S(1)}, u32[]{:S(2)}, u32[]{:S(2)}) collective-permute-start(bf16[17,16,128]{2,1,0:T(8,128)(2,1)S(1)} %get-tuple-element.87), channel_id=1, source_target_pairs={{0,12},{1,13},{2,14},{3,15},{4,8},{5,9},{6,10},{7,11},{8,4},{9,5},... | collective-permute-start | bytes 208904 | tf_op jit(solution)/shard_map/ppermute | solution.py:418
  36.2 1.3 %shard_map.87 = (bf16[17,16,128]{2,1,0:T(8,128)(2,1)S(1)}, f32[16,2048]{1,0:T(8,128)S(1)}, f32[16,128]{1,0:T(8,128)S(1)}, f32[16,128]{1,0:T(8,128)S(1)}) custom-call(f32[16,2048]{1,0:T(8,128)S(1)} %get-tuple-element.63.own_ref.direction_ref.right_side_ref, f32[1,2048]{1,0:T(1,128)S(1)} %get-tuple-element.69.nugget_ref, ...), custom_call_target="tpu_custom_call" | custom-call | tf_op jit(solution)/shard_map/pallas_call | solution.py:390
  37.5 2.5 %collective-permute-start.16 = (bf16[17,16,128]{2,1,0:T(8,128)(2,1)S(1)}, bf16[17,16,128]{2,1,0:T(8,128)(2,1)S(1)}, u32[]{:S(2)}, u32[]{:S(2)}) collective-permute-start(bf16[17,16,128]{2,1,0:T(8,128)(2,1)S(1)} %get-tuple-element.93), channel_id=1, source_target_pairs={{0,12},{1,13},{2,14},{3,15},{4,8},{5,9},{6,10},{7,11},{8,4},{9,5},... | collective-permute-start | bytes 208904 | tf_op jit(solution)/shard_map/ppermute | solution.py:418
  44.0 1.2 %collective-permute-start.20 = (bf16[2,17,16,128]{3,2,1,0:T(8,128)(2,1)S(1)}, bf16[2,17,16,128]{3,2,1,0:T(8,128)(2,1)S(1)}, u32[]{:S(2)}, u32[]{:S(2)}) collective-permute-start(bf16[2,17,16,128]{3,2,1,0:T(8,128)(2,1)S(1)} %pad_maximum_fusion.2), channel_id=1, source_target_pairs={{0,2},{1,3},{2,0},{3,1},{4,6},{5,7},{6,4},{7,5},{8,10},{9,11},{10,... | collective-permute-start | bytes 417800 | tf_op jit(solution)/shard_map/ppermute | solution.py:418
  46.9 1.8 %shard_map.89 = (f32[16,1024]{1,0:T(8,128)S(1)}, f32[16,128]{1,0:T(8,128)S(1)}) custom-call(bf16[4,17,16,128]{3,2,1,0:T(8,128)(2,1)S(1)} %pad_maximum_fusion.held_ref, f32[16,2048]{1,0:T(8,128)S(1)} %get-tuple-element.96.own_ref.residual_ref, f32[16,2048]{1,0:T(8,128)S(1)} %get-tuple-element.63.own_ref.direction_ref.right_side_ref, ...), custom_call_target="tpu_custom_call" | custom-call | tf_op jit(solution)/shard_map/pallas_call | solution.py:390
  48.7 1.7 %collective-permute-done.21.rest_2_ = bf16[1,17,16,128]{3,2,1,0:T(8,128)(2,1)S(1)} collective-permute-done((bf16[1,17,16,128]{3,2,1,0:T(8,128)(2,1)S(1)}, bf16[1,17,16,128]{3,2,1,0:T(8,128)(2,1)S(1)}, u32[]{:S(2)}, u32[]{:S(2)}) %collective-permute-start.21) | collective-permute-done | bytes 69664 | tf_op jit(solution)/shard_map/ppermute | solution.py:418
  51.3 1.3 %collective-permute-done.22.got_ref = f32[16,1152]{1,0:T(8,128)S(1)} collective-permute-done((f32[16,1152]{1,0:T(8,128)S(1)}, f32[16,1152]{1,0:T(8,128)S(1)}, u32[]{:S(2)}, u32[]{:S(2)}) %collective-permute-start.22) | collective-permute-done | bytes 73760 | tf_op jit(solution)/shard_map/ppermute | solution.py:418
  52.5 1.6 %shard_map.91 = (f32[16,128]{1,0:T(8,128)S(1)}, f32[16,1024]{1,0:T(8,128)S(1)}, f32[16,128]{1,0:T(8,128)S(1)}, f32[16,128]{1,0:T(8,128)S(1)}, bf16[17,16,128]{2,...) custom-call(f32[16,1152]{1,0:T(8,128)S(1)} %shard_map.90.message_ref, ...), custom_call_target="tpu_custom_call" | custom-call | tf_op jit(solution)/shard_map/pallas_call | solution.py:390
  56.1 1.5 %collective-permute-start.28 = (bf16[17,16,128]{2,1,0:T(8,128)(2,1)S(1)}, bf16[17,16,128]{2,1,0:T(8,128)(2,1)S(1)}, u32[]{:S(2)}, u32[]{:S(2)}) collective-permute-start(bf16[17,16,128]{2,1,0:T(8,128)(2,1)S(1)} %get-tuple-element.121), channel_id=1, source_target_pairs={{0,4},{1,5},{2,6},{3,7},{4,0},{5,1},{6,2},{7,3},{8,12},{9,13},{10,... | collective-permute-start | bytes 208904 | tf_op jit(solution)/shard_map/ppermute | solution.py:418
  58.7 1.5 %collective-permute-start.24 = (bf16[17,16,128]{2,1,0:T(8,128)(2,1)S(1)}, bf16[17,16,128]{2,1,0:T(8,128)(2,1)S(1)}, u32[]{:S(2)}, u32[]{:S(2)}) collective-permute-start(bf16[17,16,128]{2,1,0:T(8,128)(2,1)S(1)} %get-tuple-element.111), channel_id=1, source_target_pairs={{0,8},{1,9},{2,10},{3,11},{4,12},{5,13},{6,14},{7,15},{8,0},{9,1},... | collective-permute-start | bytes 208904 | tf_op jit(solution)/shard_map/ppermute | solution.py:418
  60.2 1.2 %collective-permute-start.25 = (bf16[17,16,128]{2,1,0:T(8,128)(2,1)S(1)}, bf16[17,16,128]{2,1,0:T(8,128)(2,1)S(1)}, u32[]{:S(2)}, u32[]{:S(2)}) collective-permute-start(bf16[17,16,128]{2,1,0:T(8,128)(2,1)S(1)} %get-tuple-element.112), channel_id=1, source_target_pairs={{0,4},{1,5},{2,6},{3,7},{4,0},{5,1},{6,2},{7,3},{8,12},{9,13},{10,... | collective-permute-start | bytes 208904 | tf_op jit(solution)/shard_map/ppermute | solution.py:418
  61.6 1.7 %collective-permute-start.26 = (bf16[17,16,128]{2,1,0:T(8,128)(2,1)S(1)}, bf16[17,16,128]{2,1,0:T(8,128)(2,1)S(1)}, u32[]{:S(2)}, u32[]{:S(2)}) collective-permute-start(bf16[17,16,128]{2,1,0:T(8,128)(2,1)S(1)} %get-tuple-element.115), channel_id=1, source_target_pairs={{0,12},{1,13},{2,14},{3,15},{4,8},{5,9},{6,10},{7,11},{8,4},{9,5},... | collective-permute-start | bytes 208904 | tf_op jit(solution)/shard_map/ppermute | solution.py:418
  64.8 1.4 %collective-permute-done.24.rest_0_ = bf16[17,16,128]{2,1,0:T(8,128)(2,1)S(1)} collective-permute-done((bf16[17,16,128]{2,1,0:T(8,128)(2,1)S(1)}, bf16[17,16,128]{2,1,0:T(8,128)(2,1)S(1)}, u32[]{:S(2)}, u32[]{:S(2)}) %collective-permute-start.24) | collective-permute-done | bytes 69664 | tf_op jit(solution)/shard_map/ppermute | solution.py:418
  66.2 1.5 %collective-permute-done.26.rest_0_ = bf16[17,16,128]{2,1,0:T(8,128)(2,1)S(1)} collective-permute-done((bf16[17,16,128]{2,1,0:T(8,128)(2,1)S(1)}, bf16[17,16,128]{2,1,0:T(8,128)(2,1)S(1)}, u32[]{:S(2)}, u32[]{:S(2)}) %collective-permute-start.26) | collective-permute-done | bytes 69664 | tf_op jit(solution)/shard_map/ppermute | solution.py:418
  67.8 1.6 %shard_map.98 = (f32[16,2048]{1,0:T(8,128)}, f32[16,2048]{1,0:T(8,128)}) custom-call(f32[16,2048]{1,0:T(8,128)S(1)} %shard_map.92.direction_ref, f32[1,2048]{1,0:T(1,128)S(1)} %get-tuple-element.69.nugget_ref, f32[16,16,128]{2,1,0:T(8,128)S(1)} %get-tuple-element.116.keep_ref, f32[16,128]{1,0:T(8,128)S(1)} %get-tuple-element.117.pair_ref, ...), custom_call_target="tpu_custom_call" | custom-call | tf_op jit(solution)/shard_map/pallas_call | solution.py:390
  (62 shorter events, 24.4 us)
Async XLA Ops:
  1.6 14.1 %collective-permute-start.4 = (bf16[512,2048]{1,0:T(8,128)(2,1)}, bf16[512,2048]{1,0:T(8,128)(2,1)S(1)}, u32[]{:S(2)}, u32[]{:S(2)}) collective-permute-start(bf16[512,2048]{1,0:T(8,128)(2,1)} %bitcast.17), channel_id=1, source_target_pairs={{0,1},{1,0},{2,3},{3,2},{4,5},{5,4},{6,7},{7,6},{8,9},{9,8},{10,11... | collective-permute-start | bytes 6291464 | tf_op jit(solution)/shard_map/ppermute | solution.py:418
  2.1 9.9 %collective-permute-start = (bf16[16,16,128]{2,1,0:T(8,128)(2,1)S(1)}, bf16[16,16,128]{2,1,0:T(8,128)(2,1)S(1)}, u32[]{:S(2)}, u32[]{:S(2)}) collective-permute-start(bf16[16,16,128]{2,1,0:T(8,128)(2,1)S(1)} %get-tuple-element.62), channel_id=1, source_target_pairs={{0,12},{1,13},{2,14},{3,15},{4,8},{5,9},{6,10},{7,11},{8,4},{9,5},... | collective-permute-start | bytes 196616 | tf_op jit(solution)/shard_map/ppermute | solution.py:418
  6.8 6.1 %collective-permute-start.1 = (bf16[16,16,128]{2,1,0:T(8,128)(2,1)S(1)}, bf16[16,16,128]{2,1,0:T(8,128)(2,1)S(1)}, u32[]{:S(2)}, u32[]{:S(2)}) collective-permute-start(bf16[16,16,128]{2,1,0:T(8,128)(2,1)S(1)} %get-tuple-element.62), channel_id=1, source_target_pairs={{0,8},{1,9},{2,10},{3,11},{4,12},{5,13},{6,14},{7,15},{8,0},{9,1},... | collective-permute-start | bytes 196616 | tf_op jit(solution)/shard_map/ppermute | solution.py:418
  6.8 7.7 %collective-permute-start.2 = (bf16[16,16,128]{2,1,0:T(8,128)(2,1)S(1)}, bf16[16,16,128]{2,1,0:T(8,128)(2,1)S(1)}, u32[]{:S(2)}, u32[]{:S(2)}) collective-permute-start(bf16[16,16,128]{2,1,0:T(8,128)(2,1)S(1)} %get-tuple-element.62), channel_id=1, source_target_pairs={{0,4},{1,5},{2,6},{3,7},{4,0},{5,1},{6,2},{7,3},{8,12},{9,13},{10,... | collective-permute-start | bytes 196616 | tf_op jit(solution)/shard_map/ppermute | solution.py:418
  7.4 7.0 %collective-permute-start.5 = (bf16[1,16,16,128]{3,2,1,0:T(8,128)(2,1)S(1)}, bf16[1,16,16,128]{3,2,1,0:T(8,128)(2,1)S(1)}, u32[]{:S(2)}, u32[]{:S(2)}) collective-permute-start(bf16[1,16,16,128]{3,2,1,0:T(8,128)(2,1)S(1)} %bitcast.14), channel_id=1, source_target_pairs={{0,2},{1,3},{2,0},{3,1},{4,6},{5,7},{6,4},{7,5},{8,10},{9,11},{10,... | collective-permute-start | bytes 196616 | tf_op jit(solution)/shard_map/ppermute | solution.py:418
  12.8 5.4 %collective-permute-start.6 = (bf16[2,16,16,128]{3,2,1,0:T(8,128)(2,1)S(1)}, bf16[2,16,16,128]{3,2,1,0:T(8,128)(2,1)S(1)}, u32[]{:S(2)}, u32[]{:S(2)}) collective-permute-start(bf16[2,16,16,128]{3,2,1,0:T(8,128)(2,1)S(1)} %pad_maximum_fusion.3), channel_id=1, source_target_pairs={{0,2},{1,3},{2,0},{3,1},{4,6},{5,7},{6,4},{7,5},{8,10},{9,11},{10,... | collective-permute-start | bytes 393224 | tf_op jit(solution)/shard_map/ppermute | solution.py:418
  14.4 4.5 %collective-permute-start.7 = (bf16[1,16,16,128]{3,2,1,0:T(8,128)(2,1)S(1)}, bf16[1,16,16,128]{3,2,1,0:T(8,128)(2,1)S(1)}, u32[]{:S(2)}, u32[]{:S(2)}) collective-permute-start(bf16[1,16,16,128]{3,2,1,0:T(8,128)(2,1)S(1)} %collective-permute-done.5.rest_0_), channel_id=1, source_target_pairs={{0,4},{1,5},{2,6},{3,7},{4,0},{5,1},{6,2},{7,3},{8,12},{9,13},{10,... | collective-permute-start | bytes 196616 | tf_op jit(solution)/shard_map/ppermute | solution.py:418
  22.0 6.8 %collective-permute-start.9 = (bf16[17,16,128]{2,1,0:T(8,128)(2,1)S(1)}, bf16[17,16,128]{2,1,0:T(8,128)(2,1)S(1)}, u32[]{:S(2)}, u32[]{:S(2)}) collective-permute-start(bf16[17,16,128]{2,1,0:T(8,128)(2,1)S(1)} %get-tuple-element.81), channel_id=1, source_target_pairs={{0,2},{1,3},{2,0},{3,1},{4,6},{5,7},{6,4},{7,5},{8,10},{9,11},{10,... | collective-permute-start | bytes 208904 | tf_op jit(solution)/shard_map/ppermute | solution.py:418
  22.6 9.1 %collective-permute-start.13 = (bf16[17,16,128]{2,1,0:T(8,128)(2,1)S(1)}, bf16[17,16,128]{2,1,0:T(8,128)(2,1)S(1)}, u32[]{:S(2)}, u32[]{:S(2)}) collective-permute-start(bf16[17,16,128]{2,1,0:T(8,128)(2,1)S(1)} %get-tuple-element.91), channel_id=1, source_target_pairs={{0,8},{1,9},{2,10},{3,11},{4,12},{5,13},{6,14},{7,15},{8,0},{9,1},... | collective-permute-start | bytes 208904 | tf_op jit(solution)/shard_map/ppermute | solution.py:418
  24.2 7.5 %collective-permute-start.14 = (bf16[17,16,128]{2,1,0:T(8,128)(2,1)S(1)}, bf16[17,16,128]{2,1,0:T(8,128)(2,1)S(1)}, u32[]{:S(2)}, u32[]{:S(2)}) collective-permute-start(bf16[17,16,128]{2,1,0:T(8,128)(2,1)S(1)} %get-tuple-element.92), channel_id=1, source_target_pairs={{0,4},{1,5},{2,6},{3,7},{4,0},{5,1},{6,2},{7,3},{8,12},{9,13},{10,... | collective-permute-start | bytes 208904 | tf_op jit(solution)/shard_map/ppermute | solution.py:418
  27.1 7.1 %collective-permute-start.10 = (bf16[17,16,128]{2,1,0:T(8,128)(2,1)S(1)}, bf16[17,16,128]{2,1,0:T(8,128)(2,1)S(1)}, u32[]{:S(2)}, u32[]{:S(2)}) collective-permute-start(bf16[17,16,128]{2,1,0:T(8,128)(2,1)S(1)} %get-tuple-element.83), channel_id=1, source_target_pairs={{0,8},{1,9},{2,10},{3,11},{4,12},{5,13},{6,14},{7,15},{8,0},{9,1},... | collective-permute-start | bytes 208904 | tf_op jit(solution)/shard_map/ppermute | solution.py:418
  27.1 7.0 %collective-permute-start.11 = (bf16[17,16,128]{2,1,0:T(8,128)(2,1)S(1)}, bf16[17,16,128]{2,1,0:T(8,128)(2,1)S(1)}, u32[]{:S(2)}, u32[]{:S(2)}) collective-permute-start(bf16[17,16,128]{2,1,0:T(8,128)(2,1)S(1)} %get-tuple-element.84), channel_id=1, source_target_pairs={{0,4},{1,5},{2,6},{3,7},{4,0},{5,1},{6,2},{7,3},{8,12},{9,13},{10,... | collective-permute-start | bytes 208904 | tf_op jit(solution)/shard_map/ppermute | solution.py:418
  28.9 6.2 %collective-permute-start.12 = (bf16[17,16,128]{2,1,0:T(8,128)(2,1)S(1)}, bf16[17,16,128]{2,1,0:T(8,128)(2,1)S(1)}, u32[]{:S(2)}, u32[]{:S(2)}) collective-permute-start(bf16[17,16,128]{2,1,0:T(8,128)(2,1)S(1)} %get-tuple-element.87), channel_id=1, source_target_pairs={{0,12},{1,13},{2,14},{3,15},{4,8},{5,9},{6,10},{7,11},{8,4},{9,5},... | collective-permute-start | bytes 208904 | tf_op jit(solution)/shard_map/ppermute | solution.py:418
  37.5 5.9 %collective-permute-start.17 = (bf16[17,16,128]{2,1,0:T(8,128)(2,1)S(1)}, bf16[17,16,128]{2,1,0:T(8,128)(2,1)S(1)}, u32[]{:S(2)}, u32[]{:S(2)}) collective-permute-start(bf16[17,16,128]{2,1,0:T(8,128)(2,1)S(1)} %get-tuple-element.93), channel_id=1, source_target_pairs={{0,8},{1,9},{2,10},{3,11},{4,12},{5,13},{6,14},{7,15},{8,0},{9,1},... | collective-permute-start | bytes 208904 | tf_op jit(solution)/shard_map/ppermute | solution.py:418
  37.5 6.5 %collective-permute-start.16 = (bf16[17,16,128]{2,1,0:T(8,128)(2,1)S(1)}, bf16[17,16,128]{2,1,0:T(8,128)(2,1)S(1)}, u32[]{:S(2)}, u32[]{:S(2)}) collective-permute-start(bf16[17,16,128]{2,1,0:T(8,128)(2,1)S(1)} %get-tuple-element.93), channel_id=1, source_target_pairs={{0,12},{1,13},{2,14},{3,15},{4,8},{5,9},{6,10},{7,11},{8,4},{9,5},... | collective-permute-start | bytes 208904 | tf_op jit(solution)/shard_map/ppermute | solution.py:418
  40.0 6.8 %collective-permute-start.18 = (bf16[17,16,128]{2,1,0:T(8,128)(2,1)S(1)}, bf16[17,16,128]{2,1,0:T(8,128)(2,1)S(1)}, u32[]{:S(2)}, u32[]{:S(2)}) collective-permute-start(bf16[17,16,128]{2,1,0:T(8,128)(2,1)S(1)} %get-tuple-element.93), channel_id=1, source_target_pairs={{0,4},{1,5},{2,6},{3,7},{4,0},{5,1},{6,2},{7,3},{8,12},{9,13},{10,... | collective-permute-start | bytes 208904 | tf_op jit(solution)/shard_map/ppermute | solution.py:418
  41.0 5.1 %collective-permute-start.19 = (bf16[1,17,16,128]{3,2,1,0:T(8,128)(2,1)S(1)}, bf16[1,17,16,128]{3,2,1,0:T(8,128)(2,1)S(1)}, u32[]{:S(2)}, u32[]{:S(2)}) collective-permute-start(bf16[1,17,16,128]{3,2,1,0:T(8,128)(2,1)S(1)} %bitcast.12), channel_id=1, source_target_pairs={{0,2},{1,3},{2,0},{3,1},{4,6},{5,7},{6,4},{7,5},{8,10},{9,11},{10,... | collective-permute-start | bytes 208904 | tf_op jit(solution)/shard_map/ppermute | solution.py:418
  44.0 6.3 %collective-permute-start.20 = (bf16[2,17,16,128]{3,2,1,0:T(8,128)(2,1)S(1)}, bf16[2,17,16,128]{3,2,1,0:T(8,128)(2,1)S(1)}, u32[]{:S(2)}, u32[]{:S(2)}) collective-permute-start(bf16[2,17,16,128]{3,2,1,0:T(8,128)(2,1)S(1)} %pad_maximum_fusion.2), channel_id=1, source_target_pairs={{0,2},{1,3},{2,0},{3,1},{4,6},{5,7},{6,4},{7,5},{8,10},{9,11},{10,... | collective-permute-start | bytes 417800 | tf_op jit(solution)/shard_map/ppermute | solution.py:418
  54.1 7.3 %collective-permute-start.23 = (bf16[17,16,128]{2,1,0:T(8,128)(2,1)S(1)}, bf16[17,16,128]{2,1,0:T(8,128)(2,1)S(1)}, u32[]{:S(2)}, u32[]{:S(2)}) collective-permute-start(bf16[17,16,128]{2,1,0:T(8,128)(2,1)S(1)} %get-tuple-element.109), channel_id=1, source_target_pairs={{0,2},{1,3},{2,0},{3,1},{4,6},{5,7},{6,4},{7,5},{8,10},{9,11},{10,... | collective-permute-start | bytes 208904 | tf_op jit(solution)/shard_map/ppermute | solution.py:418
  55.3 8.0 %collective-permute-start.27 = (bf16[17,16,128]{2,1,0:T(8,128)(2,1)S(1)}, bf16[17,16,128]{2,1,0:T(8,128)(2,1)S(1)}, u32[]{:S(2)}, u32[]{:S(2)}) collective-permute-start(bf16[17,16,128]{2,1,0:T(8,128)(2,1)S(1)} %get-tuple-element.120), channel_id=1, source_target_pairs={{0,8},{1,9},{2,10},{3,11},{4,12},{5,13},{6,14},{7,15},{8,0},{9,1},... | collective-permute-start | bytes 208904 | tf_op jit(solution)/shard_map/ppermute | solution.py:418
  56.1 7.3 %collective-permute-start.28 = (bf16[17,16,128]{2,1,0:T(8,128)(2,1)S(1)}, bf16[17,16,128]{2,1,0:T(8,128)(2,1)S(1)}, u32[]{:S(2)}, u32[]{:S(2)}) collective-permute-start(bf16[17,16,128]{2,1,0:T(8,128)(2,1)S(1)} %get-tuple-element.121), channel_id=1, source_target_pairs={{0,4},{1,5},{2,6},{3,7},{4,0},{5,1},{6,2},{7,3},{8,12},{9,13},{10,... | collective-permute-start | bytes 208904 | tf_op jit(solution)/shard_map/ppermute | solution.py:418
  58.7 7.4 %collective-permute-start.24 = (bf16[17,16,128]{2,1,0:T(8,128)(2,1)S(1)}, bf16[17,16,128]{2,1,0:T(8,128)(2,1)S(1)}, u32[]{:S(2)}, u32[]{:S(2)}) collective-permute-start(bf16[17,16,128]{2,1,0:T(8,128)(2,1)S(1)} %get-tuple-element.111), channel_id=1, source_target_pairs={{0,8},{1,9},{2,10},{3,11},{4,12},{5,13},{6,14},{7,15},{8,0},{9,1},... | collective-permute-start | bytes 208904 | tf_op jit(solution)/shard_map/ppermute | solution.py:418
  60.2 5.9 %collective-permute-start.25 = (bf16[17,16,128]{2,1,0:T(8,128)(2,1)S(1)}, bf16[17,16,128]{2,1,0:T(8,128)(2,1)S(1)}, u32[]{:S(2)}, u32[]{:S(2)}) collective-permute-start(bf16[17,16,128]{2,1,0:T(8,128)(2,1)S(1)} %get-tuple-element.112), channel_id=1, source_target_pairs={{0,4},{1,5},{2,6},{3,7},{4,0},{5,1},{6,2},{7,3},{8,12},{9,13},{10,... | collective-permute-start | bytes 208904 | tf_op jit(solution)/shard_map/ppermute | solution.py:418
  61.6 6.1 %collective-permute-start.26 = (bf16[17,16,128]{2,1,0:T(8,128)(2,1)S(1)}, bf16[17,16,128]{2,1,0:T(8,128)(2,1)S(1)}, u32[]{:S(2)}, u32[]{:S(2)}) collective-permute-start(bf16[17,16,128]{2,1,0:T(8,128)(2,1)S(1)} %get-tuple-element.115), channel_id=1, source_target_pairs={{0,12},{1,13},{2,14},{3,15},{4,8},{5,9},{6,10},{7,11},{8,4},{9,5},... | collective-permute-start | bytes 208904 | tf_op jit(solution)/shard_map/ppermute | solution.py:418
  (6 other events, 16.8 us)

commit v7 on v6

--- a/solution.py
+++ b/solution.py
@@ -114,7 +114,7 @@
     return code
 
 
-def spread_terms(projected, factors, places, wanted, store, rhs, chunks, extra=None):
+def spread_terms(projected, factors, places, wanted, store, rhs, chunks):
     masked = [jnp.where(places == place, projected, 0.0).astype(BF16) for place in wanted]
     masked = jnp.concatenate(masked, axis=0)
     width = factors[0].shape[0]
@@ -130,9 +130,6 @@
         for i in range(len(wanted)):
             for b in range(2):
                 piece = moved[i * rhs : (i + 1) * rhs, b * LANES : (b + 1) * LANES]
-                if i == 0 and extra is not None:
-                    place = block * step + b * LANES
-                    piece = piece + extra[:, place : place + LANES]
                 store(i, 2 * block + b, piece)
 
 
@@ -144,14 +141,15 @@
 
 
 def load_kernel(
-    rhs, rank, own_ref, column_hbm, live_ref, nugget_hbm, left_hbm,
-    nugget_ref, left_ref, named_ref, near_ref, sums_ref,
-    column_ref, column_sem, nugget_sem, left_sem,
+    rhs, rank, own_ref, column_hbm, live_ref, nugget_hbm, left_hbm, right_hbm,
+    nugget_ref, left_ref, right_ref, named_ref, near_ref, sums_ref,
+    column_ref, column_sem, nugget_sem, left_sem, right_sem,
 ):
     copies = [
         pltpu.make_async_copy(column_hbm, column_ref, column_sem),
         pltpu.make_async_copy(nugget_hbm, nugget_ref, nugget_sem),
         pltpu.make_async_copy(left_hbm, left_ref, left_sem),
+        pltpu.make_async_copy(right_hbm, right_ref, right_sem),
     ]
     for copy in copies:
         copy.start()
@@ -167,14 +165,13 @@
     copies[2].wait()
     near = lax.dot_general(own.astype(BF16), left_ref[...], NT, preferred_element_type=F32)
     near_ref[...] = jnp.where(named >= 0, near, 0.0)
+    copies[3].wait()
 
 
 def load_add_kernel(
-    rhs, chunks, place_of, base, held_ref, near_ref, named_ref, other_named_ref, right_hbm, other_ref,
-    part_ref, places_ref, right_ref, turned_ref, right_sem,
-):
-    copy = pltpu.make_async_copy(right_hbm, right_ref, right_sem)
-    copy.start()
+    rhs, chunks, place_of, base, held_ref, near_ref, named_ref, other_named_ref, right_ref, other_ref,
+    part_ref, places_ref, turned_ref,
+):
     named = jnp.concatenate([named_ref[...], other_named_ref[...]], axis=1)
     offset = named ^ lax.axis_index("row")
     places = jnp.where((named >= 0) & ((offset & 1) == 0), place_of(offset), -1)
@@ -184,7 +181,6 @@
     total = jnp.concatenate([near, jnp.zeros(near.shape, F32)], axis=1)
     half = other_ref.shape[0]
     turned_ref[:, half:] = other_ref[...].T
-    copy.wait()
     turned_ref[:, :half] = right_ref[...].T
     part_ref[...] = far_terms(total, [held_ref], turned_ref, places, [base], rhs, chunks)
 
@@ -227,17 +223,18 @@
     return lax.dot_general(rounded, rounded, NT, preferred_element_type=F32)
 
 
-def send_terms(sends, projected, factors, places, wanted, pair, rhs, chunks):
-    slots = [(send, i) for send in sends for i in range(send.shape[0] // chunks)]
+def send_terms(outs, projected, factors, places, wanted, pair, rhs, chunks):
+    slots = [(ref, i) for ref in outs for i in range(ref.shape[0] // chunks)]
 
     def store(i, c, piece):
-        send, j = slots[i]
-        send[j * chunks + c] = piece.astype(BF16)
+        ref, j = slots[i]
+        ref[j * chunks + c] = piece.astype(ref.dtype)
 
     spread_terms(projected, factors, places, wanted, store, rhs, chunks)
     code = encode(pair, rhs)
-    for send in sends:
-        send[send.shape[0] - 1] = code
+    for ref in outs:
+        if ref.shape[0] % chunks:
+            ref[ref.shape[0] - 1] = code
 
 
 def first_kernel(
@@ -271,24 +268,6 @@
     mix_ref[...] = mix
 
 
-def spread_kernel(
-    rhs, chunks, wanted, projected_ref, left_ref, right_ref, other_ref, places_ref, pair_ref, keep_ref, *outs
-):
-    projected = projected_ref[...]
-    slots = [(ref, i) for ref in (keep_ref, *outs) for i in range(ref.shape[0] // chunks)]
-
-    def store(i, c, piece):
-        ref, j = slots[i]
-        ref[j * chunks + c] = piece.astype(ref.dtype)
-
-    own = projected[:, : projected.shape[1] // 2].astype(BF16)
-    own = lax.dot_general(own, left_ref[...], NN, preferred_element_type=F32)
-    spread_terms(projected, (right_ref, other_ref), places_ref[...], wanted, store, rhs, chunks, own)
-    for ref in outs:
-        if ref.shape[0] % chunks:
-            ref[ref.shape[0] - 1] = encode(pair_ref[...], rhs)
-
-
 def solution_kernel(rhs, step_ref, right_side_ref, solution_ref):
     solution_ref[...] = left_multiply(step_ref[...], right_side_ref[...], rhs)
 
@@ -321,6 +300,15 @@
         at = i * size
         send[:size] = (keep_ref[at : at + size] + got_ref[at : at + size].astype(F32)).astype(BF16)
         send[size] = code
+
+
+def own_kernel(rhs, chunks, projected_ref, left_ref, keep_ref, *rest):
+    *_, sum_ref, total_ref = rest
+    join_coded_kernel(rhs, keep_ref, *rest)
+    own = projected_ref[:, : left_ref.shape[0]].astype(BF16)
+    own = lax.dot_general(own, left_ref[...], NN, preferred_element_type=F32)
+    for c in range(chunks):
+        sum_ref[c] = sum_ref[c] + own[:, c * LANES : (c + 1) * LANES]
 
 
 def join_coded_kernel(rhs, keep_ref, pair_ref, *rest):
@@ -455,7 +443,7 @@
     def kept(count):
         return ((count * chunks, rhs, LANES), F32)
 
-    late_sends = [coded(m)] * 3
+    sent = [coded(m)] * 3 + ([kept(1)] * 2 + [coded(1)] * 2 if m == 1 else [kept(m)] + [plain(m)] * 3) + [kept(m)]
 
     def gather(message, first_terms, *early):
         if m == 1:
@@ -483,24 +471,27 @@
         )
         return message, swap(message, 1), turned, factors, places
 
-    def reduce(sends, pair, projected, left, factors, places, *early):
-        spread = part(spread_kernel, rhs, chunks, stay)
-        operands = (projected, left, *factors, places, pair)
+    def reduce(sends, pair, projected, left, *early):
+        sends, stays = sends[:3], sends[3:]
         if m == 1:
             got_side = swap(sends[0], 2)
             got_far = [swap(sends[i], order[i + 1] << low_bits) for i in (1, 2)]
-            mine, keep, *sends, beside = call(spread, [kept(1)] * 2 + [coded(1)] * 2 + [kept(1)], *operands)
+            mine, keep, *sends, beside = stays
             got_here = [swap(sends[i - 1], order[i + 1] << low_bits) for i in (1, 2)]
             pair, send = call(part(part_kernel, rhs), [small, coded(1)], keep, pair, got_side)
             got_last = swap(send, order[1] << low_bits)
             (send,) = call(part(pass_kernel, rhs), [coded(1)], beside, *got_far)
             got_beside = swap(send, 2)
             join = part(join_coded_kernel, rhs)
-            mine, pair = call(join, [kept(1), small], after(mine, *early), pair, *got_here, micros=0.3)
+            mine, pair = call(
+                part(own_kernel, rhs, chunks), [kept(1), small],
+                projected, left, after(mine, *early), pair, *got_here,
+                micros=0.3,
+            )
             mine, pair = call(join, [kept(1), small], mine, pair, got_last, micros=0.3)
             return mine, pair, [got_beside]
         got = [swap(x, k << low_bits) for x, k in zip(sends, order[1:])]
-        keep, *sends, beside = call(spread, [kept(m)] + [plain(m)] * 3 + [kept(m)], *operands)
+        keep, *sends, beside = stays
         got_here = [swap(x, k << low_bits) for x, k in zip(sends, order[1:])]
         turned, pair = call(part(join_coded_kernel, rhs), [kept(m), small], beside, pair, *got)
         (keep,) = call(join_kernel, [kept(m)], after(keep, *early), *got_here)
@@ -512,6 +503,7 @@
                 x[:half] + swap(x[half:].astype(BF16), 1 << b).astype(F32) for x in (keep, turned)
             ]
         (turned,) = call(part(message_kernel, rhs), [coded(1)], turned, pair)
+        keep, pair = call(part(own_kernel, rhs, chunks), [kept(1), small], projected, left, keep, pair)
         return keep, pair, [swap(turned, 2)]
 
     def in_hbm(array):
@@ -523,31 +515,31 @@
     right = right_factors.reshape(slots * rank, width)
     other = swap(after(right, message), 1)
     named_shape = ((8, slots * rank), jnp.int32)
-    nugget, left, named, near, sums = call(
+    nugget, left, here, named, near, sums = call(
         part(load_kernel, rhs, rank),
-        [((1, width), F32), factor, named_shape, row_block, small],
+        [((1, width), F32), factor, factor, named_shape, row_block, small],
         right_sides, in_hbm(tile_column.reshape(slots)), live_slots, in_hbm(nugget[None, :]),
-        in_hbm(left_factors.reshape(slots * rank, width)),
-        far=(1, 3, 4), scalars=(2,), fixed=(0, 1), scratch=[pltpu.SMEM((slots,), jnp.int32)] + [semaphore] * 3,
+        in_hbm(left_factors.reshape(slots * rank, width)), in_hbm(right),
+        far=(1, 3, 4, 5), scalars=(2,), fixed=(0, 1, 2), scratch=[pltpu.SMEM((slots,), jnp.int32)] + [semaphore] * 4,
     )
     other_named = swap(named, 1)
 
     def loading(mine):
-        terms, places, here, turned = call(
+        terms, places, turned = call(
             part(load_add_kernel, rhs, chunks, place_of, held),
-            [two_rows, ((rhs, 2 * slots * rank), jnp.int32), factor, ((width, 2 * slots * rank), BF16)],
-            mine, near, named, other_named, in_hbm(right), other,
-            far=(4,), fixed=(2, 3), scratch=[semaphore], micros=0.0,
+            [two_rows, ((rhs, 2 * slots * rank), jnp.int32), ((width, 2 * slots * rank), BF16)],
+            mine, near, named, other_named, here, other,
+            fixed=(2,),
         )
         return terms, sums, turned, (here, other), places
 
     message, got, turned, factors, places = gather(message, loading, near)
     pair, earlier, weighted, *sends = call(
-        part(first_kernel, rhs, chunks, go),
-        [small, two_rows, small] + late_sends,
+        part(first_kernel, rhs, chunks, go + stay),
+        [small, two_rows, small] + sent,
         message, got, *factors, places,
     )
-    mine, pair, got = reduce(sends, pair, earlier, left, factors, places)
+    mine, pair, got = reduce(sends, pair, earlier, left)
     message, residual, step, first_gram = call(
         part(middle_kernel, rhs, chunks),
         [coded(1), panel, small, small],
@@ -567,12 +559,12 @@
 
     message, got, *_ = gather(message, loaded)
     pair, projected, next_gram, mix, *sends = call(
-        part(second_kernel, rhs, chunks, go),
-        [small, two_rows, small, small] + late_sends,
+        part(second_kernel, rhs, chunks, go + stay),
+        [small, two_rows, small, small] + sent,
         message, got, *factors, places, first_gram, weighted, earlier,
     )
     (direction,) = call(part(direction_kernel, rhs), [panel], mix, right_sides, residual)
-    mine, pair, got = reduce(sends, pair, projected, left, factors, places, direction)
+    mine, pair, got = reduce(sends, pair, projected, left, direction)
     return tuple(
         call(
             part(last_kernel, rhs, chunks),

time: 69.6 us -> 68.4 us (0.983)
  Pallas kernels: 18.4 us -> 15.4 us
  waiting for transfers between devices: 15.1 us -> 16.8 us
    pallas_call x22 -> x20, Pallas kernels: 18.4 us -> 15.4 us  [call(): pl.pallas_call(kernel, out_shape=[pltpu.VMEM(shape, dtype) if i in fixed...]
    ppermute x30, waiting for transfers between devices: 15.1 us -> 16.8 us  [swap(): return lax.ppermute(array, 'row', [(i, i ^ offset) for i in range(devices)])]
  transfers between devices with their start and end apart: 30 -> 30, of which waited for: 14 -> 16; matrix products, arithmetic and copies ran while one was open for 0% -> 0% of each run, Pallas kernels for 15% -> 11%
where the time goes in v7:
time: 68.4 us; the launch traced here: 68.3 us
  starting transfers between devices  34.5 us (50%)
  waiting for transfers between devices  16.8 us (25%)
  Pallas kernels  15.4 us (23%)
  between operations  1.42 us (2%)
    ppermute x30, starting transfers between devices, swap(): return lax.ppermute(array, 'row', [(i, i ^ offset) for i in range(devices)])  34.5 us
    ppermute x30, waiting for transfers between devices, swap(): return lax.ppermute(array, 'row', [(i, i ^ offset) for i in range(devices)])  16.8 us
    pallas_call x20, Pallas kernels, call(): pl.pallas_call(kernel, out_shape=[pltpu.VMEM(shape, dtype) if i in fixed...  15.4 us
  transfers between devices with their start and end apart: 30, of which 16 were waited for; matrix products, arithmetic and copies ran while one was open for 0% of the time, Pallas kernels for 11%

profile of v7, /device:TPU:0, one launch (start us, length us, event | category | flops | bytes accessed | tf_op | source)
XLA Modules:
  0.0 68.3 jit_solution(13874515056821343345)
XLA Ops:
  2.1 4.7 %collective-permute-start = (bf16[16,16,128]{2,1,0:T(8,128)(2,1)S(1)}, bf16[16,16,128]{2,1,0:T(8,128)(2,1)S(1)}, u32[]{:S(2)}, u32[]{:S(2)}) collective-permute-start(bf16[16,16,128]{2,1,0:T(8,128)(2,1)S(1)} %get-tuple-element.62), channel_id=1, source_target_pairs={{0,12},{1,13},{2,14},{3,15},{4,8},{5,9},{6,10},{7,11},{8,4},{9,5},... | collective-permute-start | bytes 196616 | tf_op jit(solution)/shard_map/ppermute | solution.py:406
  7.4 1.7 %collective-permute-start.5 = (bf16[1,16,16,128]{3,2,1,0:T(8,128)(2,1)S(1)}, bf16[1,16,16,128]{3,2,1,0:T(8,128)(2,1)S(1)}, u32[]{:S(2)}, u32[]{:S(2)}) collective-permute-start(bf16[1,16,16,128]{3,2,1,0:T(8,128)(2,1)S(1)} %bitcast.14), channel_id=1, source_target_pairs={{0,2},{1,3},{2,0},{3,1},{4,6},{5,7},{6,4},{7,5},{8,10},{9,11},{10,... | collective-permute-start | bytes 196616 | tf_op jit(solution)/shard_map/ppermute | solution.py:406
  9.7 2.3 %shard_map.78 = (f32[1,2048]{1,0:T(1,128)S(1)}, bf16[512,2048]{1,0:T(8,128)(2,1)S(1)}, bf16[512,2048]{1,0:T(8,128)(2,1)S(1)}, s32[8,512]{1,0:T(8,128)S(1)}, f32[...) custom-call(f32[16,2048]{1,0:T(8,128)S(1)} %get-tuple-element.63.own_ref.direction_ref.right_side_ref, s32[32]{0:T(128)} %bitcast.30, ...), custom_call_target="tpu_custom_call" | custom-call | tf_op jit(solution)/shard_map/pallas_call | solution.py:378
  12.8 1.6 %collective-permute-start.6 = (bf16[2,16,16,128]{3,2,1,0:T(8,128)(2,1)S(1)}, bf16[2,16,16,128]{3,2,1,0:T(8,128)(2,1)S(1)}, u32[]{:S(2)}, u32[]{:S(2)}) collective-permute-start(bf16[2,16,16,128]{3,2,1,0:T(8,128)(2,1)S(1)} %pad_maximum_fusion.3), channel_id=1, source_target_pairs={{0,2},{1,3},{2,0},{3,1},{4,6},{5,7},{6,4},{7,5},{8,10},{9,11},{10,... | collective-permute-start | bytes 393224 | tf_op jit(solution)/shard_map/ppermute | solution.py:406
  15.6 1.5 %shard_map.79 = (f32[16,1024]{1,0:T(8,128)S(1)}, s32[16,1024]{1,0:T(8,128)S(1)}, bf16[2048,1024]{1,0:T(8,128)(2,1)S(1)}) custom-call(bf16[4,16,16,128]{3,2,1,0:T(8,128)(2,1)S(1)} %pad_maximum_fusion.1.held_ref, f32[16,512]{1,0:T(8,128)S(1)} %get-tuple-element.64.near_ref, s32[8,512]{1,0:T(8,128)S(1)} %get-tuple-element.65.named_ref, ...), custom_call_target="tpu_custom_call" | custom-call | tf_op jit(solution)/shard_map/pallas_call | solution.py:378
  19.9 1.3 %collective-permute-done.8.got_ref = f32[16,1152]{1,0:T(8,128)S(1)} collective-permute-done((f32[16,1152]{1,0:T(8,128)S(1)}, f32[16,1152]{1,0:T(8,128)S(1)}, u32[]{:S(2)}, u32[]{:S(2)}) %collective-permute-start.8) | collective-permute-done | bytes 73760 | tf_op jit(solution)/shard_map/ppermute | solution.py:406
  22.5 1.6 %collective-permute-start.13 = (bf16[17,16,128]{2,1,0:T(8,128)(2,1)S(1)}, bf16[17,16,128]{2,1,0:T(8,128)(2,1)S(1)}, u32[]{:S(2)}, u32[]{:S(2)}) collective-permute-start(bf16[17,16,128]{2,1,0:T(8,128)(2,1)S(1)} %get-tuple-element.91), channel_id=1, source_target_pairs={{0,8},{1,9},{2,10},{3,11},{4,12},{5,13},{6,14},{7,15},{8,0},{9,1},... | collective-permute-start | bytes 208904 | tf_op jit(solution)/shard_map/ppermute | solution.py:406
  24.1 1.7 %collective-permute-start.14 = (bf16[17,16,128]{2,1,0:T(8,128)(2,1)S(1)}, bf16[17,16,128]{2,1,0:T(8,128)(2,1)S(1)}, u32[]{:S(2)}, u32[]{:S(2)}) collective-permute-start(bf16[17,16,128]{2,1,0:T(8,128)(2,1)S(1)} %get-tuple-element.92), channel_id=1, source_target_pairs={{0,4},{1,5},{2,6},{3,7},{4,0},{5,1},{6,2},{7,3},{8,12},{9,13},{10,... | collective-permute-start | bytes 208904 | tf_op jit(solution)/shard_map/ppermute | solution.py:406
  25.8 1.6 %collective-permute-start.11 = (bf16[17,16,128]{2,1,0:T(8,128)(2,1)S(1)}, bf16[17,16,128]{2,1,0:T(8,128)(2,1)S(1)}, u32[]{:S(2)}, u32[]{:S(2)}) collective-permute-start(bf16[17,16,128]{2,1,0:T(8,128)(2,1)S(1)} %get-tuple-element.84), channel_id=1, source_target_pairs={{0,4},{1,5},{2,6},{3,7},{4,0},{5,1},{6,2},{7,3},{8,12},{9,13},{10,... | collective-permute-start | bytes 208904 | tf_op jit(solution)/shard_map/ppermute | solution.py:406
  27.6 2.8 %collective-permute-start.12 = (bf16[17,16,128]{2,1,0:T(8,128)(2,1)S(1)}, bf16[17,16,128]{2,1,0:T(8,128)(2,1)S(1)}, u32[]{:S(2)}, u32[]{:S(2)}) collective-permute-start(bf16[17,16,128]{2,1,0:T(8,128)(2,1)S(1)} %get-tuple-element.87), channel_id=1, source_target_pairs={{0,12},{1,13},{2,14},{3,15},{4,8},{5,9},{6,10},{7,11},{8,4},{9,5},... | collective-permute-start | bytes 208904 | tf_op jit(solution)/shard_map/ppermute | solution.py:406
  32.2 1.7 %collective-permute-done.10.rest_1_ = bf16[17,16,128]{2,1,0:T(8,128)(2,1)S(1)} collective-permute-done((bf16[17,16,128]{2,1,0:T(8,128)(2,1)S(1)}, bf16[17,16,128]{2,1,0:T(8,128)(2,1)S(1)}, u32[]{:S(2)}, u32[]{:S(2)}) %collective-permute-start.10) | collective-permute-done | bytes 69664 | tf_op jit(solution)/shard_map/ppermute | solution.py:406
  35.4 1.3 %shard_map.86 = (bf16[17,16,128]{2,1,0:T(8,128)(2,1)S(1)}, f32[16,2048]{1,0:T(8,128)S(1)}, f32[16,128]{1,0:T(8,128)S(1)}, f32[16,128]{1,0:T(8,128)S(1)}) custom-call(f32[16,2048]{1,0:T(8,128)S(1)} %get-tuple-element.63.own_ref.direction_ref.right_side_ref, f32[1,2048]{1,0:T(1,128)S(1)} %get-tuple-element.70.nugget_ref, ...), custom_call_target="tpu_custom_call" | custom-call | tf_op jit(solution)/shard_map/pallas_call | solution.py:378
  37.8 1.3 %collective-permute-start.16 = (bf16[17,16,128]{2,1,0:T(8,128)(2,1)S(1)}, bf16[17,16,128]{2,1,0:T(8,128)(2,1)S(1)}, u32[]{:S(2)}, u32[]{:S(2)}) collective-permute-start(bf16[17,16,128]{2,1,0:T(8,128)(2,1)S(1)} %get-tuple-element.93), channel_id=1, source_target_pairs={{0,12},{1,13},{2,14},{3,15},{4,8},{5,9},{6,10},{7,11},{8,4},{9,5},... | collective-permute-start | bytes 208904 | tf_op jit(solution)/shard_map/ppermute | solution.py:406
  41.4 1.5 %collective-permute-done.17 = bf16[17,16,128]{2,1,0:T(8,128)(2,1)S(1)} collective-permute-done((bf16[17,16,128]{2,1,0:T(8,128)(2,1)S(1)}, bf16[17,16,128]{2,1,0:T(8,128)(2,1)S(1)}, u32[]{:S(2)}, u32[]{:S(2)}) %collective-permute-start.17) | collective-permute-done | bytes 69664 | tf_op jit(solution)/shard_map/ppermute | solution.py:406
  44.1 1.2 %collective-permute-start.20 = (bf16[2,17,16,128]{3,2,1,0:T(8,128)(2,1)S(1)}, bf16[2,17,16,128]{3,2,1,0:T(8,128)(2,1)S(1)}, u32[]{:S(2)}, u32[]{:S(2)}) collective-permute-start(bf16[2,17,16,128]{3,2,1,0:T(8,128)(2,1)S(1)} %pad_maximum_fusion.2), channel_id=1, source_target_pairs={{0,2},{1,3},{2,0},{3,1},{4,6},{5,7},{6,4},{7,5},{8,10},{9,11},{10,... | collective-permute-start | bytes 417800 | tf_op jit(solution)/shard_map/ppermute | solution.py:406
  46.7 1.8 %shard_map.88 = (f32[16,1024]{1,0:T(8,128)S(1)}, f32[16,128]{1,0:T(8,128)S(1)}) custom-call(bf16[4,17,16,128]{3,2,1,0:T(8,128)(2,1)S(1)} %pad_maximum_fusion.held_ref, f32[16,2048]{1,0:T(8,128)S(1)} %get-tuple-element.96.own_ref.residual_ref, f32[16,2048]{1,0:T(8,128)S(1)} %get-tuple-element.63.own_ref.direction_ref.right_side_ref, ...), custom_call_target="tpu_custom_call" | custom-call | tf_op jit(solution)/shard_map/pallas_call | solution.py:378
  48.5 1.4 %collective-permute-done.21.rest_2_ = bf16[1,17,16,128]{3,2,1,0:T(8,128)(2,1)S(1)} collective-permute-done((bf16[1,17,16,128]{3,2,1,0:T(8,128)(2,1)S(1)}, bf16[1,17,16,128]{3,2,1,0:T(8,128)(2,1)S(1)}, u32[]{:S(2)}, u32[]{:S(2)}) %collective-permute-start.21) | collective-permute-done | bytes 69664 | tf_op jit(solution)/shard_map/ppermute | solution.py:406
  50.9 1.3 %collective-permute-done.22.got_ref = f32[16,1152]{1,0:T(8,128)S(1)} collective-permute-done((f32[16,1152]{1,0:T(8,128)S(1)}, f32[16,1152]{1,0:T(8,128)S(1)}, u32[]{:S(2)}, u32[]{:S(2)}) %collective-permute-start.22) | collective-permute-done | bytes 73760 | tf_op jit(solution)/shard_map/ppermute | solution.py:406
  52.1 1.5 %shard_map.90 = (f32[16,128]{1,0:T(8,128)S(1)}, f32[16,1024]{1,0:T(8,128)S(1)}, f32[16,128]{1,0:T(8,128)S(1)}, f32[16,128]{1,0:T(8,128)S(1)}, bf16[17,16,128]{2,...) custom-call(f32[16,1152]{1,0:T(8,128)S(1)} %shard_map.89.message_ref, ...), custom_call_target="tpu_custom_call" | custom-call | tf_op jit(solution)/shard_map/pallas_call | solution.py:378
  54.5 1.5 %collective-permute-start.27 = (bf16[17,16,128]{2,1,0:T(8,128)(2,1)S(1)}, bf16[17,16,128]{2,1,0:T(8,128)(2,1)S(1)}, u32[]{:S(2)}, u32[]{:S(2)}) collective-permute-start(bf16[17,16,128]{2,1,0:T(8,128)(2,1)S(1)} %get-tuple-element.120), channel_id=1, source_target_pairs={{0,8},{1,9},{2,10},{3,11},{4,12},{5,13},{6,14},{7,15},{8,0},{9,1},... | collective-permute-start | bytes 208904 | tf_op jit(solution)/shard_map/ppermute | solution.py:406
  56.8 1.5 %collective-permute-start.24 = (bf16[17,16,128]{2,1,0:T(8,128)(2,1)S(1)}, bf16[17,16,128]{2,1,0:T(8,128)(2,1)S(1)}, u32[]{:S(2)}, u32[]{:S(2)}) collective-permute-start(bf16[17,16,128]{2,1,0:T(8,128)(2,1)S(1)} %get-tuple-element.111), channel_id=1, source_target_pairs={{0,8},{1,9},{2,10},{3,11},{4,12},{5,13},{6,14},{7,15},{8,0},{9,1},... | collective-permute-start | bytes 208904 | tf_op jit(solution)/shard_map/ppermute | solution.py:406
  59.6 1.7 %collective-permute-start.26 = (bf16[17,16,128]{2,1,0:T(8,128)(2,1)S(1)}, bf16[17,16,128]{2,1,0:T(8,128)(2,1)S(1)}, u32[]{:S(2)}, u32[]{:S(2)}) collective-permute-start(bf16[17,16,128]{2,1,0:T(8,128)(2,1)S(1)} %get-tuple-element.115), channel_id=1, source_target_pairs={{0,12},{1,13},{2,14},{3,15},{4,8},{5,9},{6,10},{7,11},{8,4},{9,5},... | collective-permute-start | bytes 208904 | tf_op jit(solution)/shard_map/ppermute | solution.py:406
  63.8 1.3 %collective-permute-done.24.rest_1_ = bf16[17,16,128]{2,1,0:T(8,128)(2,1)S(1)} collective-permute-done((bf16[17,16,128]{2,1,0:T(8,128)(2,1)S(1)}, bf16[17,16,128]{2,1,0:T(8,128)(2,1)S(1)}, u32[]{:S(2)}, u32[]{:S(2)}) %collective-permute-start.24) | collective-permute-done | bytes 69664 | tf_op jit(solution)/shard_map/ppermute | solution.py:406
  66.6 1.6 %shard_map.96 = (f32[16,2048]{1,0:T(8,128)}, f32[16,2048]{1,0:T(8,128)}) custom-call(f32[16,2048]{1,0:T(8,128)S(1)} %shard_map.91.direction_ref, f32[1,2048]{1,0:T(1,128)S(1)} %get-tuple-element.70.nugget_ref, f32[16,16,128]{2,1,0:T(8,128)S(1)} %get-tuple-element.116.keep_ref, f32[16,128]{1,0:T(8,128)S(1)} %get-tuple-element.117.pair_ref, ...), custom_call_target="tpu_custom_call" | custom-call | tf_op jit(solution)/shard_map/pallas_call | solution.py:378
  (60 shorter events, 25.5 us)
Async XLA Ops:
  1.6 14.1 %collective-permute-start.4 = (bf16[512,2048]{1,0:T(8,128)(2,1)}, bf16[512,2048]{1,0:T(8,128)(2,1)S(1)}, u32[]{:S(2)}, u32[]{:S(2)}) collective-permute-start(bf16[512,2048]{1,0:T(8,128)(2,1)} %bitcast.17), channel_id=1, source_target_pairs={{0,1},{1,0},{2,3},{3,2},{4,5},{5,4},{6,7},{7,6},{8,9},{9,8},{10,11... | collective-permute-start | bytes 6291464 | tf_op jit(solution)/shard_map/ppermute | solution.py:406
  2.1 10.0 %collective-permute-start = (bf16[16,16,128]{2,1,0:T(8,128)(2,1)S(1)}, bf16[16,16,128]{2,1,0:T(8,128)(2,1)S(1)}, u32[]{:S(2)}, u32[]{:S(2)}) collective-permute-start(bf16[16,16,128]{2,1,0:T(8,128)(2,1)S(1)} %get-tuple-element.62), channel_id=1, source_target_pairs={{0,12},{1,13},{2,14},{3,15},{4,8},{5,9},{6,10},{7,11},{8,4},{9,5},... | collective-permute-start | bytes 196616 | tf_op jit(solution)/shard_map/ppermute | solution.py:406
  6.8 6.1 %collective-permute-start.1 = (bf16[16,16,128]{2,1,0:T(8,128)(2,1)S(1)}, bf16[16,16,128]{2,1,0:T(8,128)(2,1)S(1)}, u32[]{:S(2)}, u32[]{:S(2)}) collective-permute-start(bf16[16,16,128]{2,1,0:T(8,128)(2,1)S(1)} %get-tuple-element.62), channel_id=1, source_target_pairs={{0,8},{1,9},{2,10},{3,11},{4,12},{5,13},{6,14},{7,15},{8,0},{9,1},... | collective-permute-start | bytes 196616 | tf_op jit(solution)/shard_map/ppermute | solution.py:406
  6.8 7.7 %collective-permute-start.2 = (bf16[16,16,128]{2,1,0:T(8,128)(2,1)S(1)}, bf16[16,16,128]{2,1,0:T(8,128)(2,1)S(1)}, u32[]{:S(2)}, u32[]{:S(2)}) collective-permute-start(bf16[16,16,128]{2,1,0:T(8,128)(2,1)S(1)} %get-tuple-element.62), channel_id=1, source_target_pairs={{0,4},{1,5},{2,6},{3,7},{4,0},{5,1},{6,2},{7,3},{8,12},{9,13},{10,... | collective-permute-start | bytes 196616 | tf_op jit(solution)/shard_map/ppermute | solution.py:406
  7.4 7.0 %collective-permute-start.5 = (bf16[1,16,16,128]{3,2,1,0:T(8,128)(2,1)S(1)}, bf16[1,16,16,128]{3,2,1,0:T(8,128)(2,1)S(1)}, u32[]{:S(2)}, u32[]{:S(2)}) collective-permute-start(bf16[1,16,16,128]{3,2,1,0:T(8,128)(2,1)S(1)} %bitcast.14), channel_id=1, source_target_pairs={{0,2},{1,3},{2,0},{3,1},{4,6},{5,7},{6,4},{7,5},{8,10},{9,11},{10,... | collective-permute-start | bytes 196616 | tf_op jit(solution)/shard_map/ppermute | solution.py:406
  12.8 5.1 %collective-permute-start.6 = (bf16[2,16,16,128]{3,2,1,0:T(8,128)(2,1)S(1)}, bf16[2,16,16,128]{3,2,1,0:T(8,128)(2,1)S(1)}, u32[]{:S(2)}, u32[]{:S(2)}) collective-permute-start(bf16[2,16,16,128]{3,2,1,0:T(8,128)(2,1)S(1)} %pad_maximum_fusion.3), channel_id=1, source_target_pairs={{0,2},{1,3},{2,0},{3,1},{4,6},{5,7},{6,4},{7,5},{8,10},{9,11},{10,... | collective-permute-start | bytes 393224 | tf_op jit(solution)/shard_map/ppermute | solution.py:406
  14.4 4.5 %collective-permute-start.7 = (bf16[1,16,16,128]{3,2,1,0:T(8,128)(2,1)S(1)}, bf16[1,16,16,128]{3,2,1,0:T(8,128)(2,1)S(1)}, u32[]{:S(2)}, u32[]{:S(2)}) collective-permute-start(bf16[1,16,16,128]{3,2,1,0:T(8,128)(2,1)S(1)} %collective-permute-done.5.rest_0_), channel_id=1, source_target_pairs={{0,4},{1,5},{2,6},{3,7},{4,0},{5,1},{6,2},{7,3},{8,12},{9,13},{10,... | collective-permute-start | bytes 196616 | tf_op jit(solution)/shard_map/ppermute | solution.py:406
  21.8 5.6 %collective-permute-start.9 = (bf16[17,16,128]{2,1,0:T(8,128)(2,1)S(1)}, bf16[17,16,128]{2,1,0:T(8,128)(2,1)S(1)}, u32[]{:S(2)}, u32[]{:S(2)}) collective-permute-start(bf16[17,16,128]{2,1,0:T(8,128)(2,1)S(1)} %get-tuple-element.81), channel_id=1, source_target_pairs={{0,2},{1,3},{2,0},{3,1},{4,6},{5,7},{6,4},{7,5},{8,10},{9,11},{10,... | collective-permute-start | bytes 208904 | tf_op jit(solution)/shard_map/ppermute | solution.py:406
  22.5 7.9 %collective-permute-start.13 = (bf16[17,16,128]{2,1,0:T(8,128)(2,1)S(1)}, bf16[17,16,128]{2,1,0:T(8,128)(2,1)S(1)}, u32[]{:S(2)}, u32[]{:S(2)}) collective-permute-start(bf16[17,16,128]{2,1,0:T(8,128)(2,1)S(1)} %get-tuple-element.91), channel_id=1, source_target_pairs={{0,8},{1,9},{2,10},{3,11},{4,12},{5,13},{6,14},{7,15},{8,0},{9,1},... | collective-permute-start | bytes 208904 | tf_op jit(solution)/shard_map/ppermute | solution.py:406
  24.1 6.8 %collective-permute-start.14 = (bf16[17,16,128]{2,1,0:T(8,128)(2,1)S(1)}, bf16[17,16,128]{2,1,0:T(8,128)(2,1)S(1)}, u32[]{:S(2)}, u32[]{:S(2)}) collective-permute-start(bf16[17,16,128]{2,1,0:T(8,128)(2,1)S(1)} %get-tuple-element.92), channel_id=1, source_target_pairs={{0,4},{1,5},{2,6},{3,7},{4,0},{5,1},{6,2},{7,3},{8,12},{9,13},{10,... | collective-permute-start | bytes 208904 | tf_op jit(solution)/shard_map/ppermute | solution.py:406
  25.8 8.1 %collective-permute-start.10 = (bf16[17,16,128]{2,1,0:T(8,128)(2,1)S(1)}, bf16[17,16,128]{2,1,0:T(8,128)(2,1)S(1)}, u32[]{:S(2)}, u32[]{:S(2)}) collective-permute-start(bf16[17,16,128]{2,1,0:T(8,128)(2,1)S(1)} %get-tuple-element.83), channel_id=1, source_target_pairs={{0,8},{1,9},{2,10},{3,11},{4,12},{5,13},{6,14},{7,15},{8,0},{9,1},... | collective-permute-start | bytes 208904 | tf_op jit(solution)/shard_map/ppermute | solution.py:406
  25.8 8.1 %collective-permute-start.11 = (bf16[17,16,128]{2,1,0:T(8,128)(2,1)S(1)}, bf16[17,16,128]{2,1,0:T(8,128)(2,1)S(1)}, u32[]{:S(2)}, u32[]{:S(2)}) collective-permute-start(bf16[17,16,128]{2,1,0:T(8,128)(2,1)S(1)} %get-tuple-element.84), channel_id=1, source_target_pairs={{0,4},{1,5},{2,6},{3,7},{4,0},{5,1},{6,2},{7,3},{8,12},{9,13},{10,... | collective-permute-start | bytes 208904 | tf_op jit(solution)/shard_map/ppermute | solution.py:406
  27.6 6.8 %collective-permute-start.12 = (bf16[17,16,128]{2,1,0:T(8,128)(2,1)S(1)}, bf16[17,16,128]{2,1,0:T(8,128)(2,1)S(1)}, u32[]{:S(2)}, u32[]{:S(2)}) collective-permute-start(bf16[17,16,128]{2,1,0:T(8,128)(2,1)S(1)} %get-tuple-element.87), channel_id=1, source_target_pairs={{0,12},{1,13},{2,14},{3,15},{4,8},{5,9},{6,10},{7,11},{8,4},{9,5},... | collective-permute-start | bytes 208904 | tf_op jit(solution)/shard_map/ppermute | solution.py:406
  36.7 6.2 %collective-permute-start.17 = (bf16[17,16,128]{2,1,0:T(8,128)(2,1)S(1)}, bf16[17,16,128]{2,1,0:T(8,128)(2,1)S(1)}, u32[]{:S(2)}, u32[]{:S(2)}) collective-permute-start(bf16[17,16,128]{2,1,0:T(8,128)(2,1)S(1)} %get-tuple-element.93), channel_id=1, source_target_pairs={{0,8},{1,9},{2,10},{3,11},{4,12},{5,13},{6,14},{7,15},{8,0},{9,1},... | collective-permute-start | bytes 208904 | tf_op jit(solution)/shard_map/ppermute | solution.py:406
  37.8 6.3 %collective-permute-start.16 = (bf16[17,16,128]{2,1,0:T(8,128)(2,1)S(1)}, bf16[17,16,128]{2,1,0:T(8,128)(2,1)S(1)}, u32[]{:S(2)}, u32[]{:S(2)}) collective-permute-start(bf16[17,16,128]{2,1,0:T(8,128)(2,1)S(1)} %get-tuple-element.93), channel_id=1, source_target_pairs={{0,12},{1,13},{2,14},{3,15},{4,8},{5,9},{6,10},{7,11},{8,4},{9,5},... | collective-permute-start | bytes 208904 | tf_op jit(solution)/shard_map/ppermute | solution.py:406
  39.1 7.5 %collective-permute-start.18 = (bf16[17,16,128]{2,1,0:T(8,128)(2,1)S(1)}, bf16[17,16,128]{2,1,0:T(8,128)(2,1)S(1)}, u32[]{:S(2)}, u32[]{:S(2)}) collective-permute-start(bf16[17,16,128]{2,1,0:T(8,128)(2,1)S(1)} %get-tuple-element.93), channel_id=1, source_target_pairs={{0,4},{1,5},{2,6},{3,7},{4,0},{5,1},{6,2},{7,3},{8,12},{9,13},{10,... | collective-permute-start | bytes 208904 | tf_op jit(solution)/shard_map/ppermute | solution.py:406
  40.2 5.4 %collective-permute-start.19 = (bf16[1,17,16,128]{3,2,1,0:T(8,128)(2,1)S(1)}, bf16[1,17,16,128]{3,2,1,0:T(8,128)(2,1)S(1)}, u32[]{:S(2)}, u32[]{:S(2)}) collective-permute-start(bf16[1,17,16,128]{3,2,1,0:T(8,128)(2,1)S(1)} %bitcast.12), channel_id=1, source_target_pairs={{0,2},{1,3},{2,0},{3,1},{4,6},{5,7},{6,4},{7,5},{8,10},{9,11},{10,... | collective-permute-start | bytes 208904 | tf_op jit(solution)/shard_map/ppermute | solution.py:406
  44.1 5.8 %collective-permute-start.20 = (bf16[2,17,16,128]{3,2,1,0:T(8,128)(2,1)S(1)}, bf16[2,17,16,128]{3,2,1,0:T(8,128)(2,1)S(1)}, u32[]{:S(2)}, u32[]{:S(2)}) collective-permute-start(bf16[2,17,16,128]{3,2,1,0:T(8,128)(2,1)S(1)} %pad_maximum_fusion.2), channel_id=1, source_target_pairs={{0,2},{1,3},{2,0},{3,1},{4,6},{5,7},{6,4},{7,5},{8,10},{9,11},{10,... | collective-permute-start | bytes 417800 | tf_op jit(solution)/shard_map/ppermute | solution.py:406
  53.6 5.9 %collective-permute-start.23 = (bf16[17,16,128]{2,1,0:T(8,128)(2,1)S(1)}, bf16[17,16,128]{2,1,0:T(8,128)(2,1)S(1)}, u32[]{:S(2)}, u32[]{:S(2)}) collective-permute-start(bf16[17,16,128]{2,1,0:T(8,128)(2,1)S(1)} %get-tuple-element.109), channel_id=1, source_target_pairs={{0,2},{1,3},{2,0},{3,1},{4,6},{5,7},{6,4},{7,5},{8,10},{9,11},{10,... | collective-permute-start | bytes 208904 | tf_op jit(solution)/shard_map/ppermute | solution.py:406
  54.5 7.6 %collective-permute-start.27 = (bf16[17,16,128]{2,1,0:T(8,128)(2,1)S(1)}, bf16[17,16,128]{2,1,0:T(8,128)(2,1)S(1)}, u32[]{:S(2)}, u32[]{:S(2)}) collective-permute-start(bf16[17,16,128]{2,1,0:T(8,128)(2,1)S(1)} %get-tuple-element.120), channel_id=1, source_target_pairs={{0,8},{1,9},{2,10},{3,11},{4,12},{5,13},{6,14},{7,15},{8,0},{9,1},... | collective-permute-start | bytes 208904 | tf_op jit(solution)/shard_map/ppermute | solution.py:406
  56.0 6.2 %collective-permute-start.28 = (bf16[17,16,128]{2,1,0:T(8,128)(2,1)S(1)}, bf16[17,16,128]{2,1,0:T(8,128)(2,1)S(1)}, u32[]{:S(2)}, u32[]{:S(2)}) collective-permute-start(bf16[17,16,128]{2,1,0:T(8,128)(2,1)S(1)} %get-tuple-element.121), channel_id=1, source_target_pairs={{0,4},{1,5},{2,6},{3,7},{4,0},{5,1},{6,2},{7,3},{8,12},{9,13},{10,... | collective-permute-start | bytes 208904 | tf_op jit(solution)/shard_map/ppermute | solution.py:406
  56.8 8.2 %collective-permute-start.24 = (bf16[17,16,128]{2,1,0:T(8,128)(2,1)S(1)}, bf16[17,16,128]{2,1,0:T(8,128)(2,1)S(1)}, u32[]{:S(2)}, u32[]{:S(2)}) collective-permute-start(bf16[17,16,128]{2,1,0:T(8,128)(2,1)S(1)} %get-tuple-element.111), channel_id=1, source_target_pairs={{0,8},{1,9},{2,10},{3,11},{4,12},{5,13},{6,14},{7,15},{8,0},{9,1},... | collective-permute-start | bytes 208904 | tf_op jit(solution)/shard_map/ppermute | solution.py:406
  58.3 6.7 %collective-permute-start.25 = (bf16[17,16,128]{2,1,0:T(8,128)(2,1)S(1)}, bf16[17,16,128]{2,1,0:T(8,128)(2,1)S(1)}, u32[]{:S(2)}, u32[]{:S(2)}) collective-permute-start(bf16[17,16,128]{2,1,0:T(8,128)(2,1)S(1)} %get-tuple-element.112), channel_id=1, source_target_pairs={{0,4},{1,5},{2,6},{3,7},{4,0},{5,1},{6,2},{7,3},{8,12},{9,13},{10,... | collective-permute-start | bytes 208904 | tf_op jit(solution)/shard_map/ppermute | solution.py:406
  59.6 6.2 %collective-permute-start.26 = (bf16[17,16,128]{2,1,0:T(8,128)(2,1)S(1)}, bf16[17,16,128]{2,1,0:T(8,128)(2,1)S(1)}, u32[]{:S(2)}, u32[]{:S(2)}) collective-permute-start(bf16[17,16,128]{2,1,0:T(8,128)(2,1)S(1)} %get-tuple-element.115), channel_id=1, source_target_pairs={{0,12},{1,13},{2,14},{3,15},{4,8},{5,9},{6,10},{7,11},{8,4},{9,5},... | collective-permute-start | bytes 208904 | tf_op jit(solution)/shard_map/ppermute | solution.py:406
  (6 other events, 16.8 us)

commit v8 on v7

--- a/solution.py
+++ b/solution.py
@@ -187,8 +187,10 @@
 
 def near_add_kernel(
     rhs, chunks, base, held_ref, own_ref, right_side_ref, nugget_ref, left_ref, named_ref, places_ref,
-    turned_ref, part_ref, sums_ref,
-):
+    turned_ref, gram_ref, part_ref, sums_ref, inverse_ref,
+):
+    row = lax.broadcasted_iota(jnp.int32, gram_ref.shape, 0)
+    inverse_ref[...] = right_divide(gram_ref[...], jnp.where(row == lanes_of(row), 1.0, 0.0), rhs)
     own = own_ref[...]
     near = lax.dot_general(own.astype(BF16), left_ref[...], NT, preferred_element_type=F32)
     near = jnp.where(named_ref[:1] >= 0, near, 0.0)
@@ -251,12 +253,12 @@
 
 def second_kernel(
     rhs, chunks, wanted, message_ref, got_ref, right_ref, other_ref, places_ref,
-    gram_ref, weighted_ref, earlier_ref,
+    inverse_ref, weighted_ref, earlier_ref,
     pair_ref, projected_ref, next_gram_ref, mix_ref, *sends,
 ):
     projected, sums = both_cores(message_ref, got_ref)
     next_gram_ref[...] = sums
-    mix = right_divide(gram_ref[...], sums, rhs)
+    mix = left_multiply(sums, inverse_ref[...], rhs)
     projected = projected + left_multiply(mix, earlier_ref[...], rhs)
     projected_ref[...] = projected
     weighted = left_multiply(mix, jnp.concatenate([sums[:, 2 * rhs : 3 * rhs], weighted_ref[:, :rhs]], axis=1), rhs)
@@ -549,22 +551,22 @@
     (solution,) = call(part(solution_kernel, rhs), [panel], step, right_sides)
 
     def loaded(mine):
-        terms, sums = call(
+        terms, sums, inverse = call(
             part(near_add_kernel, rhs, chunks, held),
-            [two_rows, small],
-            after(mine, solution), residual, right_sides, nugget, left, named, places, turned,
+            [two_rows, small, small],
+            mine, residual, right_sides, nugget, left, named, places, turned, first_gram,
             micros=0.0,
         )
-        return terms, sums, turned, factors, places
-
-    message, got, *_ = gather(message, loaded)
+        return terms, sums, turned, (inverse,), places
+
+    message, got, _, (inverse,), _ = gather(message, loaded)
     pair, projected, next_gram, mix, *sends = call(
         part(second_kernel, rhs, chunks, go + stay),
         [small, two_rows, small, small] + sent,
-        message, got, *factors, places, first_gram, weighted, earlier,
+        message, got, *factors, places, inverse, weighted, earlier,
     )
     (direction,) = call(part(direction_kernel, rhs), [panel], mix, right_sides, residual)
-    mine, pair, got = reduce(sends, pair, projected, left, direction)
+    mine, pair, got = reduce(sends, pair, projected, left, direction, solution)
     return tuple(
         call(
             part(last_kernel, rhs, chunks),

time: 68.4 us -> 68 us (level)
  no operation moved by 1% of the time
where the time goes in v8:
time: 68 us; the launch traced here: 67.8 us
  starting transfers between devices  34.5 us (51%)
  waiting for transfers between devices  16.7 us (25%)
  Pallas kernels  15.1 us (22%)
  between operations  1.42 us (2%)
    ppermute x30, starting transfers between devices, swap(): return lax.ppermute(array, 'row', [(i, i ^ offset) for i in range(devices)])  34.5 us
    ppermute x30, waiting for transfers between devices, swap(): return lax.ppermute(array, 'row', [(i, i ^ offset) for i in range(devices)])  16.7 us
    pallas_call x20, Pallas kernels, call(): pl.pallas_call(kernel, out_shape=[pltpu.VMEM(shape, dtype) if i in fixed...  15.1 us
  transfers between devices with their start and end apart: 30, of which 16 were waited for; matrix products, arithmetic and copies ran while one was open for 0% of the time, Pallas kernels for 11%

profile of v8, /device:TPU:0, one launch (start us, length us, event | category | flops | bytes accessed | tf_op | source)
XLA Modules:
  0.0 67.8 jit_solution(4668273099592489528)
XLA Ops:
  2.1 4.7 %collective-permute-start = (bf16[16,16,128]{2,1,0:T(8,128)(2,1)S(1)}, bf16[16,16,128]{2,1,0:T(8,128)(2,1)S(1)}, u32[]{:S(2)}, u32[]{:S(2)}) collective-permute-start(bf16[16,16,128]{2,1,0:T(8,128)(2,1)S(1)} %get-tuple-element.62), channel_id=1, source_target_pairs={{0,12},{1,13},{2,14},{3,15},{4,8},{5,9},{6,10},{7,11},{8,4},{9,5},... | collective-permute-start | bytes 196616 | tf_op jit(solution)/shard_map/ppermute | solution.py:408
  7.4 1.7 %collective-permute-start.5 = (bf16[1,16,16,128]{3,2,1,0:T(8,128)(2,1)S(1)}, bf16[1,16,16,128]{3,2,1,0:T(8,128)(2,1)S(1)}, u32[]{:S(2)}, u32[]{:S(2)}) collective-permute-start(bf16[1,16,16,128]{3,2,1,0:T(8,128)(2,1)S(1)} %bitcast.14), channel_id=1, source_target_pairs={{0,2},{1,3},{2,0},{3,1},{4,6},{5,7},{6,4},{7,5},{8,10},{9,11},{10,... | collective-permute-start | bytes 196616 | tf_op jit(solution)/shard_map/ppermute | solution.py:408
  9.7 2.3 %shard_map.78 = (f32[1,2048]{1,0:T(1,128)S(1)}, bf16[512,2048]{1,0:T(8,128)(2,1)S(1)}, bf16[512,2048]{1,0:T(8,128)(2,1)S(1)}, s32[8,512]{1,0:T(8,128)S(1)}, f32[...) custom-call(f32[16,2048]{1,0:T(8,128)S(1)} %get-tuple-element.63.own_ref.direction_ref.right_side_ref, s32[32]{0:T(128)} %bitcast.30, ...), custom_call_target="tpu_custom_call" | custom-call | tf_op jit(solution)/shard_map/pallas_call | solution.py:380
  12.8 1.6 %collective-permute-start.6 = (bf16[2,16,16,128]{3,2,1,0:T(8,128)(2,1)S(1)}, bf16[2,16,16,128]{3,2,1,0:T(8,128)(2,1)S(1)}, u32[]{:S(2)}, u32[]{:S(2)}) collective-permute-start(bf16[2,16,16,128]{3,2,1,0:T(8,128)(2,1)S(1)} %pad_maximum_fusion.3), channel_id=1, source_target_pairs={{0,2},{1,3},{2,0},{3,1},{4,6},{5,7},{6,4},{7,5},{8,10},{9,11},{10,... | collective-permute-start | bytes 393224 | tf_op jit(solution)/shard_map/ppermute | solution.py:408
  15.6 1.5 %shard_map.79 = (f32[16,1024]{1,0:T(8,128)S(1)}, s32[16,1024]{1,0:T(8,128)S(1)}, bf16[2048,1024]{1,0:T(8,128)(2,1)S(1)}) custom-call(bf16[4,16,16,128]{3,2,1,0:T(8,128)(2,1)S(1)} %pad_maximum_fusion.1.held_ref, f32[16,512]{1,0:T(8,128)S(1)} %get-tuple-element.64.near_ref, s32[8,512]{1,0:T(8,128)S(1)} %get-tuple-element.65.named_ref, ...), custom_call_target="tpu_custom_call" | custom-call | tf_op jit(solution)/shard_map/pallas_call | solution.py:380
  19.9 1.3 %collective-permute-done.8.got_ref = f32[16,1152]{1,0:T(8,128)S(1)} collective-permute-done((f32[16,1152]{1,0:T(8,128)S(1)}, f32[16,1152]{1,0:T(8,128)S(1)}, u32[]{:S(2)}, u32[]{:S(2)}) %collective-permute-start.8) | collective-permute-done | bytes 73760 | tf_op jit(solution)/shard_map/ppermute | solution.py:408
  22.5 1.6 %collective-permute-start.13 = (bf16[17,16,128]{2,1,0:T(8,128)(2,1)S(1)}, bf16[17,16,128]{2,1,0:T(8,128)(2,1)S(1)}, u32[]{:S(2)}, u32[]{:S(2)}) collective-permute-start(bf16[17,16,128]{2,1,0:T(8,128)(2,1)S(1)} %get-tuple-element.91), channel_id=1, source_target_pairs={{0,8},{1,9},{2,10},{3,11},{4,12},{5,13},{6,14},{7,15},{8,0},{9,1},... | collective-permute-start | bytes 208904 | tf_op jit(solution)/shard_map/ppermute | solution.py:408
  24.1 1.7 %collective-permute-start.14 = (bf16[17,16,128]{2,1,0:T(8,128)(2,1)S(1)}, bf16[17,16,128]{2,1,0:T(8,128)(2,1)S(1)}, u32[]{:S(2)}, u32[]{:S(2)}) collective-permute-start(bf16[17,16,128]{2,1,0:T(8,128)(2,1)S(1)} %get-tuple-element.92), channel_id=1, source_target_pairs={{0,4},{1,5},{2,6},{3,7},{4,0},{5,1},{6,2},{7,3},{8,12},{9,13},{10,... | collective-permute-start | bytes 208904 | tf_op jit(solution)/shard_map/ppermute | solution.py:408
  25.8 1.6 %collective-permute-start.11 = (bf16[17,16,128]{2,1,0:T(8,128)(2,1)S(1)}, bf16[17,16,128]{2,1,0:T(8,128)(2,1)S(1)}, u32[]{:S(2)}, u32[]{:S(2)}) collective-permute-start(bf16[17,16,128]{2,1,0:T(8,128)(2,1)S(1)} %get-tuple-element.84), channel_id=1, source_target_pairs={{0,4},{1,5},{2,6},{3,7},{4,0},{5,1},{6,2},{7,3},{8,12},{9,13},{10,... | collective-permute-start | bytes 208904 | tf_op jit(solution)/shard_map/ppermute | solution.py:408
  27.6 2.8 %collective-permute-start.12 = (bf16[17,16,128]{2,1,0:T(8,128)(2,1)S(1)}, bf16[17,16,128]{2,1,0:T(8,128)(2,1)S(1)}, u32[]{:S(2)}, u32[]{:S(2)}) collective-permute-start(bf16[17,16,128]{2,1,0:T(8,128)(2,1)S(1)} %get-tuple-element.87), channel_id=1, source_target_pairs={{0,12},{1,13},{2,14},{3,15},{4,8},{5,9},{6,10},{7,11},{8,4},{9,5},... | collective-permute-start | bytes 208904 | tf_op jit(solution)/shard_map/ppermute | solution.py:408
  32.2 1.7 %collective-permute-done.10.rest_1_ = bf16[17,16,128]{2,1,0:T(8,128)(2,1)S(1)} collective-permute-done((bf16[17,16,128]{2,1,0:T(8,128)(2,1)S(1)}, bf16[17,16,128]{2,1,0:T(8,128)(2,1)S(1)}, u32[]{:S(2)}, u32[]{:S(2)}) %collective-permute-start.10) | collective-permute-done | bytes 69664 | tf_op jit(solution)/shard_map/ppermute | solution.py:408
  35.4 1.3 %shard_map.86 = (bf16[17,16,128]{2,1,0:T(8,128)(2,1)S(1)}, f32[16,2048]{1,0:T(8,128)S(1)}, f32[16,128]{1,0:T(8,128)S(1)}, f32[16,128]{1,0:T(8,128)S(1)}) custom-call(f32[16,2048]{1,0:T(8,128)S(1)} %get-tuple-element.63.own_ref.direction_ref.right_side_ref, f32[1,2048]{1,0:T(1,128)S(1)} %get-tuple-element.70.nugget_ref, ...), custom_call_target="tpu_custom_call" | custom-call | tf_op jit(solution)/shard_map/pallas_call | solution.py:380
  37.8 1.3 %collective-permute-start.16 = (bf16[17,16,128]{2,1,0:T(8,128)(2,1)S(1)}, bf16[17,16,128]{2,1,0:T(8,128)(2,1)S(1)}, u32[]{:S(2)}, u32[]{:S(2)}) collective-permute-start(bf16[17,16,128]{2,1,0:T(8,128)(2,1)S(1)} %get-tuple-element.93), channel_id=1, source_target_pairs={{0,12},{1,13},{2,14},{3,15},{4,8},{5,9},{6,10},{7,11},{8,4},{9,5},... | collective-permute-start | bytes 208904 | tf_op jit(solution)/shard_map/ppermute | solution.py:408
  41.4 1.5 %collective-permute-done.17 = bf16[17,16,128]{2,1,0:T(8,128)(2,1)S(1)} collective-permute-done((bf16[17,16,128]{2,1,0:T(8,128)(2,1)S(1)}, bf16[17,16,128]{2,1,0:T(8,128)(2,1)S(1)}, u32[]{:S(2)}, u32[]{:S(2)}) %collective-permute-start.17) | collective-permute-done | bytes 69664 | tf_op jit(solution)/shard_map/ppermute | solution.py:408
  44.1 1.2 %collective-permute-start.20 = (bf16[2,17,16,128]{3,2,1,0:T(8,128)(2,1)S(1)}, bf16[2,17,16,128]{3,2,1,0:T(8,128)(2,1)S(1)}, u32[]{:S(2)}, u32[]{:S(2)}) collective-permute-start(bf16[2,17,16,128]{3,2,1,0:T(8,128)(2,1)S(1)} %pad_maximum_fusion.2), channel_id=1, source_target_pairs={{0,2},{1,3},{2,0},{3,1},{4,6},{5,7},{6,4},{7,5},{8,10},{9,11},{10,... | collective-permute-start | bytes 417800 | tf_op jit(solution)/shard_map/ppermute | solution.py:408
  46.4 1.8 %shard_map.87 = (f32[16,1024]{1,0:T(8,128)S(1)}, f32[16,128]{1,0:T(8,128)S(1)}, f32[16,128]{1,0:T(8,128)S(1)}) custom-call(bf16[4,17,16,128]{3,2,1,0:T(8,128)(2,1)S(1)} %pad_maximum_fusion.held_ref, f32[16,2048]{1,0:T(8,128)S(1)} %get-tuple-element.94.own_ref.residual_ref, f32[16,2048]{1,0:T(8,128)S(1)} %get-tuple-element.63.own_ref.direction_ref.right_side_ref, ...), custom_call_target="tpu_custom_call" | custom-call | tf_op jit(solution)/shard_map/pallas_call | solution.py:380
  48.2 1.4 %collective-permute-done.21.rest_2_ = bf16[1,17,16,128]{3,2,1,0:T(8,128)(2,1)S(1)} collective-permute-done((bf16[1,17,16,128]{3,2,1,0:T(8,128)(2,1)S(1)}, bf16[1,17,16,128]{3,2,1,0:T(8,128)(2,1)S(1)}, u32[]{:S(2)}, u32[]{:S(2)}) %collective-permute-start.21) | collective-permute-done | bytes 69664 | tf_op jit(solution)/shard_map/ppermute | solution.py:408
  50.6 1.3 %collective-permute-done.22.got_ref = f32[16,1152]{1,0:T(8,128)S(1)} collective-permute-done((f32[16,1152]{1,0:T(8,128)S(1)}, f32[16,1152]{1,0:T(8,128)S(1)}, u32[]{:S(2)}, u32[]{:S(2)}) %collective-permute-start.22) | collective-permute-done | bytes 73760 | tf_op jit(solution)/shard_map/ppermute | solution.py:408
  51.8 1.2 %shard_map.89 = (f32[16,128]{1,0:T(8,128)S(1)}, f32[16,1024]{1,0:T(8,128)S(1)}, f32[16,128]{1,0:T(8,128)S(1)}, f32[16,128]{1,0:T(8,128)S(1)}, bf16[17,16,128]{2,...) custom-call(f32[16,1152]{1,0:T(8,128)S(1)} %shard_map.88.message_ref, ...), custom_call_target="tpu_custom_call" | custom-call | tf_op jit(solution)/shard_map/pallas_call | solution.py:380
  53.9 1.7 %collective-permute-start.27 = (bf16[17,16,128]{2,1,0:T(8,128)(2,1)S(1)}, bf16[17,16,128]{2,1,0:T(8,128)(2,1)S(1)}, u32[]{:S(2)}, u32[]{:S(2)}) collective-permute-start(bf16[17,16,128]{2,1,0:T(8,128)(2,1)S(1)} %get-tuple-element.120), channel_id=1, source_target_pairs={{0,8},{1,9},{2,10},{3,11},{4,12},{5,13},{6,14},{7,15},{8,0},{9,1},... | collective-permute-start | bytes 208904 | tf_op jit(solution)/shard_map/ppermute | solution.py:408
  56.3 1.5 %collective-permute-start.24 = (bf16[17,16,128]{2,1,0:T(8,128)(2,1)S(1)}, bf16[17,16,128]{2,1,0:T(8,128)(2,1)S(1)}, u32[]{:S(2)}, u32[]{:S(2)}) collective-permute-start(bf16[17,16,128]{2,1,0:T(8,128)(2,1)S(1)} %get-tuple-element.111), channel_id=1, source_target_pairs={{0,8},{1,9},{2,10},{3,11},{4,12},{5,13},{6,14},{7,15},{8,0},{9,1},... | collective-permute-start | bytes 208904 | tf_op jit(solution)/shard_map/ppermute | solution.py:408
  59.0 1.8 %collective-permute-start.26 = (bf16[17,16,128]{2,1,0:T(8,128)(2,1)S(1)}, bf16[17,16,128]{2,1,0:T(8,128)(2,1)S(1)}, u32[]{:S(2)}, u32[]{:S(2)}) collective-permute-start(bf16[17,16,128]{2,1,0:T(8,128)(2,1)S(1)} %get-tuple-element.115), channel_id=1, source_target_pairs={{0,12},{1,13},{2,14},{3,15},{4,8},{5,9},{6,10},{7,11},{8,4},{9,5},... | collective-permute-start | bytes 208904 | tf_op jit(solution)/shard_map/ppermute | solution.py:408
  63.5 1.8 %collective-permute-done.24.rest_1_ = bf16[17,16,128]{2,1,0:T(8,128)(2,1)S(1)} collective-permute-done((bf16[17,16,128]{2,1,0:T(8,128)(2,1)S(1)}, bf16[17,16,128]{2,1,0:T(8,128)(2,1)S(1)}, u32[]{:S(2)}, u32[]{:S(2)}) %collective-permute-start.24) | collective-permute-done | bytes 69664 | tf_op jit(solution)/shard_map/ppermute | solution.py:408
  66.2 1.6 %shard_map.96 = (f32[16,2048]{1,0:T(8,128)}, f32[16,2048]{1,0:T(8,128)}) custom-call(f32[16,2048]{1,0:T(8,128)S(1)} %shard_map.90.direction_ref, f32[1,2048]{1,0:T(1,128)S(1)} %get-tuple-element.70.nugget_ref, f32[16,16,128]{2,1,0:T(8,128)S(1)} %get-tuple-element.116.keep_ref, f32[16,128]{1,0:T(8,128)S(1)} %get-tuple-element.117.pair_ref, ...), custom_call_target="tpu_custom_call" | custom-call | tf_op jit(solution)/shard_map/pallas_call | solution.py:380
  (60 shorter events, 24.7 us)
Async XLA Ops:
  1.6 14.1 %collective-permute-start.4 = (bf16[512,2048]{1,0:T(8,128)(2,1)}, bf16[512,2048]{1,0:T(8,128)(2,1)S(1)}, u32[]{:S(2)}, u32[]{:S(2)}) collective-permute-start(bf16[512,2048]{1,0:T(8,128)(2,1)} %bitcast.17), channel_id=1, source_target_pairs={{0,1},{1,0},{2,3},{3,2},{4,5},{5,4},{6,7},{7,6},{8,9},{9,8},{10,11... | collective-permute-start | bytes 6291464 | tf_op jit(solution)/shard_map/ppermute | solution.py:408
  2.1 10.0 %collective-permute-start = (bf16[16,16,128]{2,1,0:T(8,128)(2,1)S(1)}, bf16[16,16,128]{2,1,0:T(8,128)(2,1)S(1)}, u32[]{:S(2)}, u32[]{:S(2)}) collective-permute-start(bf16[16,16,128]{2,1,0:T(8,128)(2,1)S(1)} %get-tuple-element.62), channel_id=1, source_target_pairs={{0,12},{1,13},{2,14},{3,15},{4,8},{5,9},{6,10},{7,11},{8,4},{9,5},... | collective-permute-start | bytes 196616 | tf_op jit(solution)/shard_map/ppermute | solution.py:408
  6.8 6.1 %collective-permute-start.1 = (bf16[16,16,128]{2,1,0:T(8,128)(2,1)S(1)}, bf16[16,16,128]{2,1,0:T(8,128)(2,1)S(1)}, u32[]{:S(2)}, u32[]{:S(2)}) collective-permute-start(bf16[16,16,128]{2,1,0:T(8,128)(2,1)S(1)} %get-tuple-element.62), channel_id=1, source_target_pairs={{0,8},{1,9},{2,10},{3,11},{4,12},{5,13},{6,14},{7,15},{8,0},{9,1},... | collective-permute-start | bytes 196616 | tf_op jit(solution)/shard_map/ppermute | solution.py:408
  6.8 7.7 %collective-permute-start.2 = (bf16[16,16,128]{2,1,0:T(8,128)(2,1)S(1)}, bf16[16,16,128]{2,1,0:T(8,128)(2,1)S(1)}, u32[]{:S(2)}, u32[]{:S(2)}) collective-permute-start(bf16[16,16,128]{2,1,0:T(8,128)(2,1)S(1)} %get-tuple-element.62), channel_id=1, source_target_pairs={{0,4},{1,5},{2,6},{3,7},{4,0},{5,1},{6,2},{7,3},{8,12},{9,13},{10,... | collective-permute-start | bytes 196616 | tf_op jit(solution)/shard_map/ppermute | solution.py:408
  7.4 7.0 %collective-permute-start.5 = (bf16[1,16,16,128]{3,2,1,0:T(8,128)(2,1)S(1)}, bf16[1,16,16,128]{3,2,1,0:T(8,128)(2,1)S(1)}, u32[]{:S(2)}, u32[]{:S(2)}) collective-permute-start(bf16[1,16,16,128]{3,2,1,0:T(8,128)(2,1)S(1)} %bitcast.14), channel_id=1, source_target_pairs={{0,2},{1,3},{2,0},{3,1},{4,6},{5,7},{6,4},{7,5},{8,10},{9,11},{10,... | collective-permute-start | bytes 196616 | tf_op jit(solution)/shard_map/ppermute | solution.py:408
  12.8 5.1 %collective-permute-start.6 = (bf16[2,16,16,128]{3,2,1,0:T(8,128)(2,1)S(1)}, bf16[2,16,16,128]{3,2,1,0:T(8,128)(2,1)S(1)}, u32[]{:S(2)}, u32[]{:S(2)}) collective-permute-start(bf16[2,16,16,128]{3,2,1,0:T(8,128)(2,1)S(1)} %pad_maximum_fusion.3), channel_id=1, source_target_pairs={{0,2},{1,3},{2,0},{3,1},{4,6},{5,7},{6,4},{7,5},{8,10},{9,11},{10,... | collective-permute-start | bytes 393224 | tf_op jit(solution)/shard_map/ppermute | solution.py:408
  14.4 4.5 %collective-permute-start.7 = (bf16[1,16,16,128]{3,2,1,0:T(8,128)(2,1)S(1)}, bf16[1,16,16,128]{3,2,1,0:T(8,128)(2,1)S(1)}, u32[]{:S(2)}, u32[]{:S(2)}) collective-permute-start(bf16[1,16,16,128]{3,2,1,0:T(8,128)(2,1)S(1)} %collective-permute-done.5.rest_0_), channel_id=1, source_target_pairs={{0,4},{1,5},{2,6},{3,7},{4,0},{5,1},{6,2},{7,3},{8,12},{9,13},{10,... | collective-permute-start | bytes 196616 | tf_op jit(solution)/shard_map/ppermute | solution.py:408
  21.8 5.6 %collective-permute-start.9 = (bf16[17,16,128]{2,1,0:T(8,128)(2,1)S(1)}, bf16[17,16,128]{2,1,0:T(8,128)(2,1)S(1)}, u32[]{:S(2)}, u32[]{:S(2)}) collective-permute-start(bf16[17,16,128]{2,1,0:T(8,128)(2,1)S(1)} %get-tuple-element.81), channel_id=1, source_target_pairs={{0,2},{1,3},{2,0},{3,1},{4,6},{5,7},{6,4},{7,5},{8,10},{9,11},{10,... | collective-permute-start | bytes 208904 | tf_op jit(solution)/shard_map/ppermute | solution.py:408
  22.5 7.9 %collective-permute-start.13 = (bf16[17,16,128]{2,1,0:T(8,128)(2,1)S(1)}, bf16[17,16,128]{2,1,0:T(8,128)(2,1)S(1)}, u32[]{:S(2)}, u32[]{:S(2)}) collective-permute-start(bf16[17,16,128]{2,1,0:T(8,128)(2,1)S(1)} %get-tuple-element.91), channel_id=1, source_target_pairs={{0,8},{1,9},{2,10},{3,11},{4,12},{5,13},{6,14},{7,15},{8,0},{9,1},... | collective-permute-start | bytes 208904 | tf_op jit(solution)/shard_map/ppermute | solution.py:408
  24.1 6.8 %collective-permute-start.14 = (bf16[17,16,128]{2,1,0:T(8,128)(2,1)S(1)}, bf16[17,16,128]{2,1,0:T(8,128)(2,1)S(1)}, u32[]{:S(2)}, u32[]{:S(2)}) collective-permute-start(bf16[17,16,128]{2,1,0:T(8,128)(2,1)S(1)} %get-tuple-element.92), channel_id=1, source_target_pairs={{0,4},{1,5},{2,6},{3,7},{4,0},{5,1},{6,2},{7,3},{8,12},{9,13},{10,... | collective-permute-start | bytes 208904 | tf_op jit(solution)/shard_map/ppermute | solution.py:408
  25.8 8.1 %collective-permute-start.10 = (bf16[17,16,128]{2,1,0:T(8,128)(2,1)S(1)}, bf16[17,16,128]{2,1,0:T(8,128)(2,1)S(1)}, u32[]{:S(2)}, u32[]{:S(2)}) collective-permute-start(bf16[17,16,128]{2,1,0:T(8,128)(2,1)S(1)} %get-tuple-element.83), channel_id=1, source_target_pairs={{0,8},{1,9},{2,10},{3,11},{4,12},{5,13},{6,14},{7,15},{8,0},{9,1},... | collective-permute-start | bytes 208904 | tf_op jit(solution)/shard_map/ppermute | solution.py:408
  25.8 8.1 %collective-permute-start.11 = (bf16[17,16,128]{2,1,0:T(8,128)(2,1)S(1)}, bf16[17,16,128]{2,1,0:T(8,128)(2,1)S(1)}, u32[]{:S(2)}, u32[]{:S(2)}) collective-permute-start(bf16[17,16,128]{2,1,0:T(8,128)(2,1)S(1)} %get-tuple-element.84), channel_id=1, source_target_pairs={{0,4},{1,5},{2,6},{3,7},{4,0},{5,1},{6,2},{7,3},{8,12},{9,13},{10,... | collective-permute-start | bytes 208904 | tf_op jit(solution)/shard_map/ppermute | solution.py:408
  27.6 6.7 %collective-permute-start.12 = (bf16[17,16,128]{2,1,0:T(8,128)(2,1)S(1)}, bf16[17,16,128]{2,1,0:T(8,128)(2,1)S(1)}, u32[]{:S(2)}, u32[]{:S(2)}) collective-permute-start(bf16[17,16,128]{2,1,0:T(8,128)(2,1)S(1)} %get-tuple-element.87), channel_id=1, source_target_pairs={{0,12},{1,13},{2,14},{3,15},{4,8},{5,9},{6,10},{7,11},{8,4},{9,5},... | collective-permute-start | bytes 208904 | tf_op jit(solution)/shard_map/ppermute | solution.py:408
  36.7 6.2 %collective-permute-start.17 = (bf16[17,16,128]{2,1,0:T(8,128)(2,1)S(1)}, bf16[17,16,128]{2,1,0:T(8,128)(2,1)S(1)}, u32[]{:S(2)}, u32[]{:S(2)}) collective-permute-start(bf16[17,16,128]{2,1,0:T(8,128)(2,1)S(1)} %get-tuple-element.93), channel_id=1, source_target_pairs={{0,8},{1,9},{2,10},{3,11},{4,12},{5,13},{6,14},{7,15},{8,0},{9,1},... | collective-permute-start | bytes 208904 | tf_op jit(solution)/shard_map/ppermute | solution.py:408
  37.8 6.3 %collective-permute-start.16 = (bf16[17,16,128]{2,1,0:T(8,128)(2,1)S(1)}, bf16[17,16,128]{2,1,0:T(8,128)(2,1)S(1)}, u32[]{:S(2)}, u32[]{:S(2)}) collective-permute-start(bf16[17,16,128]{2,1,0:T(8,128)(2,1)S(1)} %get-tuple-element.93), channel_id=1, source_target_pairs={{0,12},{1,13},{2,14},{3,15},{4,8},{5,9},{6,10},{7,11},{8,4},{9,5},... | collective-permute-start | bytes 208904 | tf_op jit(solution)/shard_map/ppermute | solution.py:408
  39.1 7.2 %collective-permute-start.18 = (bf16[17,16,128]{2,1,0:T(8,128)(2,1)S(1)}, bf16[17,16,128]{2,1,0:T(8,128)(2,1)S(1)}, u32[]{:S(2)}, u32[]{:S(2)}) collective-permute-start(bf16[17,16,128]{2,1,0:T(8,128)(2,1)S(1)} %get-tuple-element.93), channel_id=1, source_target_pairs={{0,4},{1,5},{2,6},{3,7},{4,0},{5,1},{6,2},{7,3},{8,12},{9,13},{10,... | collective-permute-start | bytes 208904 | tf_op jit(solution)/shard_map/ppermute | solution.py:408
  40.2 5.1 %collective-permute-start.19 = (bf16[1,17,16,128]{3,2,1,0:T(8,128)(2,1)S(1)}, bf16[1,17,16,128]{3,2,1,0:T(8,128)(2,1)S(1)}, u32[]{:S(2)}, u32[]{:S(2)}) collective-permute-start(bf16[1,17,16,128]{3,2,1,0:T(8,128)(2,1)S(1)} %bitcast.12), channel_id=1, source_target_pairs={{0,2},{1,3},{2,0},{3,1},{4,6},{5,7},{6,4},{7,5},{8,10},{9,11},{10,... | collective-permute-start | bytes 208904 | tf_op jit(solution)/shard_map/ppermute | solution.py:408
  44.1 5.5 %collective-permute-start.20 = (bf16[2,17,16,128]{3,2,1,0:T(8,128)(2,1)S(1)}, bf16[2,17,16,128]{3,2,1,0:T(8,128)(2,1)S(1)}, u32[]{:S(2)}, u32[]{:S(2)}) collective-permute-start(bf16[2,17,16,128]{3,2,1,0:T(8,128)(2,1)S(1)} %pad_maximum_fusion.2), channel_id=1, source_target_pairs={{0,2},{1,3},{2,0},{3,1},{4,6},{5,7},{6,4},{7,5},{8,10},{9,11},{10,... | collective-permute-start | bytes 417800 | tf_op jit(solution)/shard_map/ppermute | solution.py:408
  53.0 5.9 %collective-permute-start.23 = (bf16[17,16,128]{2,1,0:T(8,128)(2,1)S(1)}, bf16[17,16,128]{2,1,0:T(8,128)(2,1)S(1)}, u32[]{:S(2)}, u32[]{:S(2)}) collective-permute-start(bf16[17,16,128]{2,1,0:T(8,128)(2,1)S(1)} %get-tuple-element.109), channel_id=1, source_target_pairs={{0,2},{1,3},{2,0},{3,1},{4,6},{5,7},{6,4},{7,5},{8,10},{9,11},{10,... | collective-permute-start | bytes 208904 | tf_op jit(solution)/shard_map/ppermute | solution.py:408
  53.9 7.6 %collective-permute-start.27 = (bf16[17,16,128]{2,1,0:T(8,128)(2,1)S(1)}, bf16[17,16,128]{2,1,0:T(8,128)(2,1)S(1)}, u32[]{:S(2)}, u32[]{:S(2)}) collective-permute-start(bf16[17,16,128]{2,1,0:T(8,128)(2,1)S(1)} %get-tuple-element.120), channel_id=1, source_target_pairs={{0,8},{1,9},{2,10},{3,11},{4,12},{5,13},{6,14},{7,15},{8,0},{9,1},... | collective-permute-start | bytes 208904 | tf_op jit(solution)/shard_map/ppermute | solution.py:408
  55.6 6.1 %collective-permute-start.28 = (bf16[17,16,128]{2,1,0:T(8,128)(2,1)S(1)}, bf16[17,16,128]{2,1,0:T(8,128)(2,1)S(1)}, u32[]{:S(2)}, u32[]{:S(2)}) collective-permute-start(bf16[17,16,128]{2,1,0:T(8,128)(2,1)S(1)} %get-tuple-element.121), channel_id=1, source_target_pairs={{0,4},{1,5},{2,6},{3,7},{4,0},{5,1},{6,2},{7,3},{8,12},{9,13},{10,... | collective-permute-start | bytes 208904 | tf_op jit(solution)/shard_map/ppermute | solution.py:408
  56.3 8.9 %collective-permute-start.24 = (bf16[17,16,128]{2,1,0:T(8,128)(2,1)S(1)}, bf16[17,16,128]{2,1,0:T(8,128)(2,1)S(1)}, u32[]{:S(2)}, u32[]{:S(2)}) collective-permute-start(bf16[17,16,128]{2,1,0:T(8,128)(2,1)S(1)} %get-tuple-element.111), channel_id=1, source_target_pairs={{0,8},{1,9},{2,10},{3,11},{4,12},{5,13},{6,14},{7,15},{8,0},{9,1},... | collective-permute-start | bytes 208904 | tf_op jit(solution)/shard_map/ppermute | solution.py:408
  57.8 7.5 %collective-permute-start.25 = (bf16[17,16,128]{2,1,0:T(8,128)(2,1)S(1)}, bf16[17,16,128]{2,1,0:T(8,128)(2,1)S(1)}, u32[]{:S(2)}, u32[]{:S(2)}) collective-permute-start(bf16[17,16,128]{2,1,0:T(8,128)(2,1)S(1)} %get-tuple-element.112), channel_id=1, source_target_pairs={{0,4},{1,5},{2,6},{3,7},{4,0},{5,1},{6,2},{7,3},{8,12},{9,13},{10,... | collective-permute-start | bytes 208904 | tf_op jit(solution)/shard_map/ppermute | solution.py:408
  59.0 6.6 %collective-permute-start.26 = (bf16[17,16,128]{2,1,0:T(8,128)(2,1)S(1)}, bf16[17,16,128]{2,1,0:T(8,128)(2,1)S(1)}, u32[]{:S(2)}, u32[]{:S(2)}) collective-permute-start(bf16[17,16,128]{2,1,0:T(8,128)(2,1)S(1)} %get-tuple-element.115), channel_id=1, source_target_pairs={{0,12},{1,13},{2,14},{3,15},{4,8},{5,9},{6,10},{7,11},{8,4},{9,5},... | collective-permute-start | bytes 208904 | tf_op jit(solution)/shard_map/ppermute | solution.py:408
  (6 other events, 16.8 us)

commit v9 on v8

--- a/solution.py
+++ b/solution.py
@@ -97,6 +97,8 @@
 
 def far_terms(total, panels, turned_ref, places, bases, rhs, chunks):
     rows = jnp.concatenate([rows_of(ref, chunks) for ref in panels], axis=0)
+    if rows.shape[0] * 2 == LANES:
+        rows = jnp.concatenate([rows, rows], axis=0)
     far = lax.dot_general(rows, turned_ref[...], NN, preferred_element_type=F32)
     at = 0
     for base, ref in zip(bases, panels):

time: 68 us -> 67.7 us (level)
  no operation moved by 1% of the time
where the time goes in v9:
time: 67.7 us; the launch traced here: 67.6 us
  starting transfers between devices  34.5 us (51%)
  waiting for transfers between devices  16.8 us (25%)
  Pallas kernels  14.7 us (22%)
  between operations  1.42 us (2%)
    ppermute x30, starting transfers between devices, swap(): return lax.ppermute(array, 'row', [(i, i ^ offset) for i in range(devices)])  34.5 us
    ppermute x30, waiting for transfers between devices, swap(): return lax.ppermute(array, 'row', [(i, i ^ offset) for i in range(devices)])  16.8 us
    pallas_call x20, Pallas kernels, call(): pl.pallas_call(kernel, out_shape=[pltpu.VMEM(shape, dtype) if i in fixed...  14.7 us
  transfers between devices with their start and end apart: 30, of which 16 were waited for; matrix products, arithmetic and copies ran while one was open for 0% of the time, Pallas kernels for 11%

profile of v9, /device:TPU:0, one launch (start us, length us, event | category | flops | bytes accessed | tf_op | source)
XLA Modules:
  0.0 67.6 jit_solution(8037745020807688857)
XLA Ops:
  2.1 4.7 %collective-permute-start = (bf16[16,16,128]{2,1,0:T(8,128)(2,1)S(1)}, bf16[16,16,128]{2,1,0:T(8,128)(2,1)S(1)}, u32[]{:S(2)}, u32[]{:S(2)}) collective-permute-start(bf16[16,16,128]{2,1,0:T(8,128)(2,1)S(1)} %get-tuple-element.62), channel_id=1, source_target_pairs={{0,12},{1,13},{2,14},{3,15},{4,8},{5,9},{6,10},{7,11},{8,4},{9,5},... | collective-permute-start | bytes 196616 | tf_op jit(solution)/shard_map/ppermute | solution.py:410
  7.4 1.7 %collective-permute-start.5 = (bf16[1,16,16,128]{3,2,1,0:T(8,128)(2,1)S(1)}, bf16[1,16,16,128]{3,2,1,0:T(8,128)(2,1)S(1)}, u32[]{:S(2)}, u32[]{:S(2)}) collective-permute-start(bf16[1,16,16,128]{3,2,1,0:T(8,128)(2,1)S(1)} %bitcast.14), channel_id=1, source_target_pairs={{0,2},{1,3},{2,0},{3,1},{4,6},{5,7},{6,4},{7,5},{8,10},{9,11},{10,... | collective-permute-start | bytes 196616 | tf_op jit(solution)/shard_map/ppermute | solution.py:410
  9.7 2.3 %shard_map.78 = (f32[1,2048]{1,0:T(1,128)S(1)}, bf16[512,2048]{1,0:T(8,128)(2,1)S(1)}, bf16[512,2048]{1,0:T(8,128)(2,1)S(1)}, s32[8,512]{1,0:T(8,128)S(1)}, f32[...) custom-call(f32[16,2048]{1,0:T(8,128)S(1)} %get-tuple-element.63.own_ref.direction_ref.right_side_ref, s32[32]{0:T(128)} %bitcast.30, ...), custom_call_target="tpu_custom_call" | custom-call | tf_op jit(solution)/shard_map/pallas_call | solution.py:382
  12.8 1.6 %collective-permute-start.6 = (bf16[2,16,16,128]{3,2,1,0:T(8,128)(2,1)S(1)}, bf16[2,16,16,128]{3,2,1,0:T(8,128)(2,1)S(1)}, u32[]{:S(2)}, u32[]{:S(2)}) collective-permute-start(bf16[2,16,16,128]{3,2,1,0:T(8,128)(2,1)S(1)} %pad_maximum_fusion.3), channel_id=1, source_target_pairs={{0,2},{1,3},{2,0},{3,1},{4,6},{5,7},{6,4},{7,5},{8,10},{9,11},{10,... | collective-permute-start | bytes 393224 | tf_op jit(solution)/shard_map/ppermute | solution.py:410
  15.6 1.5 %shard_map.79 = (f32[16,1024]{1,0:T(8,128)S(1)}, s32[16,1024]{1,0:T(8,128)S(1)}, bf16[2048,1024]{1,0:T(8,128)(2,1)S(1)}) custom-call(bf16[4,16,16,128]{3,2,1,0:T(8,128)(2,1)S(1)} %pad_maximum_fusion.1.held_ref, f32[16,512]{1,0:T(8,128)S(1)} %get-tuple-element.64.near_ref, s32[8,512]{1,0:T(8,128)S(1)} %get-tuple-element.65.named_ref, ...), custom_call_target="tpu_custom_call" | custom-call | tf_op jit(solution)/shard_map/pallas_call | solution.py:382
  19.7 1.3 %collective-permute-done.8.got_ref = f32[16,1152]{1,0:T(8,128)S(1)} collective-permute-done((f32[16,1152]{1,0:T(8,128)S(1)}, f32[16,1152]{1,0:T(8,128)S(1)}, u32[]{:S(2)}, u32[]{:S(2)}) %collective-permute-start.8) | collective-permute-done | bytes 73760 | tf_op jit(solution)/shard_map/ppermute | solution.py:410
  22.3 1.6 %collective-permute-start.13 = (bf16[17,16,128]{2,1,0:T(8,128)(2,1)S(1)}, bf16[17,16,128]{2,1,0:T(8,128)(2,1)S(1)}, u32[]{:S(2)}, u32[]{:S(2)}) collective-permute-start(bf16[17,16,128]{2,1,0:T(8,128)(2,1)S(1)} %get-tuple-element.91), channel_id=1, source_target_pairs={{0,8},{1,9},{2,10},{3,11},{4,12},{5,13},{6,14},{7,15},{8,0},{9,1},... | collective-permute-start | bytes 208904 | tf_op jit(solution)/shard_map/ppermute | solution.py:410
  23.9 1.7 %collective-permute-start.14 = (bf16[17,16,128]{2,1,0:T(8,128)(2,1)S(1)}, bf16[17,16,128]{2,1,0:T(8,128)(2,1)S(1)}, u32[]{:S(2)}, u32[]{:S(2)}) collective-permute-start(bf16[17,16,128]{2,1,0:T(8,128)(2,1)S(1)} %get-tuple-element.92), channel_id=1, source_target_pairs={{0,4},{1,5},{2,6},{3,7},{4,0},{5,1},{6,2},{7,3},{8,12},{9,13},{10,... | collective-permute-start | bytes 208904 | tf_op jit(solution)/shard_map/ppermute | solution.py:410
  25.7 1.6 %collective-permute-start.11 = (bf16[17,16,128]{2,1,0:T(8,128)(2,1)S(1)}, bf16[17,16,128]{2,1,0:T(8,128)(2,1)S(1)}, u32[]{:S(2)}, u32[]{:S(2)}) collective-permute-start(bf16[17,16,128]{2,1,0:T(8,128)(2,1)S(1)} %get-tuple-element.84), channel_id=1, source_target_pairs={{0,4},{1,5},{2,6},{3,7},{4,0},{5,1},{6,2},{7,3},{8,12},{9,13},{10,... | collective-permute-start | bytes 208904 | tf_op jit(solution)/shard_map/ppermute | solution.py:410
  27.5 2.8 %collective-permute-start.12 = (bf16[17,16,128]{2,1,0:T(8,128)(2,1)S(1)}, bf16[17,16,128]{2,1,0:T(8,128)(2,1)S(1)}, u32[]{:S(2)}, u32[]{:S(2)}) collective-permute-start(bf16[17,16,128]{2,1,0:T(8,128)(2,1)S(1)} %get-tuple-element.87), channel_id=1, source_target_pairs={{0,12},{1,13},{2,14},{3,15},{4,8},{5,9},{6,10},{7,11},{8,4},{9,5},... | collective-permute-start | bytes 208904 | tf_op jit(solution)/shard_map/ppermute | solution.py:410
  32.1 1.7 %collective-permute-done.10.rest_1_ = bf16[17,16,128]{2,1,0:T(8,128)(2,1)S(1)} collective-permute-done((bf16[17,16,128]{2,1,0:T(8,128)(2,1)S(1)}, bf16[17,16,128]{2,1,0:T(8,128)(2,1)S(1)}, u32[]{:S(2)}, u32[]{:S(2)}) %collective-permute-start.10) | collective-permute-done | bytes 69664 | tf_op jit(solution)/shard_map/ppermute | solution.py:410
  35.3 1.3 %shard_map.86 = (bf16[17,16,128]{2,1,0:T(8,128)(2,1)S(1)}, f32[16,2048]{1,0:T(8,128)S(1)}, f32[16,128]{1,0:T(8,128)S(1)}, f32[16,128]{1,0:T(8,128)S(1)}) custom-call(f32[16,2048]{1,0:T(8,128)S(1)} %get-tuple-element.63.own_ref.direction_ref.right_side_ref, f32[1,2048]{1,0:T(1,128)S(1)} %get-tuple-element.70.nugget_ref, ...), custom_call_target="tpu_custom_call" | custom-call | tf_op jit(solution)/shard_map/pallas_call | solution.py:382
  37.7 1.3 %collective-permute-start.16 = (bf16[17,16,128]{2,1,0:T(8,128)(2,1)S(1)}, bf16[17,16,128]{2,1,0:T(8,128)(2,1)S(1)}, u32[]{:S(2)}, u32[]{:S(2)}) collective-permute-start(bf16[17,16,128]{2,1,0:T(8,128)(2,1)S(1)} %get-tuple-element.93), channel_id=1, source_target_pairs={{0,12},{1,13},{2,14},{3,15},{4,8},{5,9},{6,10},{7,11},{8,4},{9,5},... | collective-permute-start | bytes 208904 | tf_op jit(solution)/shard_map/ppermute | solution.py:410
  41.2 1.5 %collective-permute-done.17 = bf16[17,16,128]{2,1,0:T(8,128)(2,1)S(1)} collective-permute-done((bf16[17,16,128]{2,1,0:T(8,128)(2,1)S(1)}, bf16[17,16,128]{2,1,0:T(8,128)(2,1)S(1)}, u32[]{:S(2)}, u32[]{:S(2)}) %collective-permute-start.17) | collective-permute-done | bytes 69664 | tf_op jit(solution)/shard_map/ppermute | solution.py:410
  44.0 1.2 %collective-permute-start.20 = (bf16[2,17,16,128]{3,2,1,0:T(8,128)(2,1)S(1)}, bf16[2,17,16,128]{3,2,1,0:T(8,128)(2,1)S(1)}, u32[]{:S(2)}, u32[]{:S(2)}) collective-permute-start(bf16[2,17,16,128]{3,2,1,0:T(8,128)(2,1)S(1)} %pad_maximum_fusion.2), channel_id=1, source_target_pairs={{0,2},{1,3},{2,0},{3,1},{4,6},{5,7},{6,4},{7,5},{8,10},{9,11},{10,... | collective-permute-start | bytes 417800 | tf_op jit(solution)/shard_map/ppermute | solution.py:410
  46.3 1.6 %shard_map.87 = (f32[16,1024]{1,0:T(8,128)S(1)}, f32[16,128]{1,0:T(8,128)S(1)}, f32[16,128]{1,0:T(8,128)S(1)}) custom-call(bf16[4,17,16,128]{3,2,1,0:T(8,128)(2,1)S(1)} %pad_maximum_fusion.held_ref, f32[16,2048]{1,0:T(8,128)S(1)} %get-tuple-element.94.own_ref.residual_ref, f32[16,2048]{1,0:T(8,128)S(1)} %get-tuple-element.63.own_ref.direction_ref.right_side_ref, ...), custom_call_target="tpu_custom_call" | custom-call | tf_op jit(solution)/shard_map/pallas_call | solution.py:382
  47.9 1.6 %collective-permute-done.21.rest_2_ = bf16[1,17,16,128]{3,2,1,0:T(8,128)(2,1)S(1)} collective-permute-done((bf16[1,17,16,128]{3,2,1,0:T(8,128)(2,1)S(1)}, bf16[1,17,16,128]{3,2,1,0:T(8,128)(2,1)S(1)}, u32[]{:S(2)}, u32[]{:S(2)}) %collective-permute-start.21) | collective-permute-done | bytes 69664 | tf_op jit(solution)/shard_map/ppermute | solution.py:410
  50.3 1.3 %collective-permute-done.22.got_ref = f32[16,1152]{1,0:T(8,128)S(1)} collective-permute-done((f32[16,1152]{1,0:T(8,128)S(1)}, f32[16,1152]{1,0:T(8,128)S(1)}, u32[]{:S(2)}, u32[]{:S(2)}) %collective-permute-start.22) | collective-permute-done | bytes 73760 | tf_op jit(solution)/shard_map/ppermute | solution.py:410
  51.6 1.2 %shard_map.89 = (f32[16,128]{1,0:T(8,128)S(1)}, f32[16,1024]{1,0:T(8,128)S(1)}, f32[16,128]{1,0:T(8,128)S(1)}, f32[16,128]{1,0:T(8,128)S(1)}, bf16[17,16,128]{2,...) custom-call(f32[16,1152]{1,0:T(8,128)S(1)} %shard_map.88.message_ref, ...), custom_call_target="tpu_custom_call" | custom-call | tf_op jit(solution)/shard_map/pallas_call | solution.py:382
  53.7 1.7 %collective-permute-start.27 = (bf16[17,16,128]{2,1,0:T(8,128)(2,1)S(1)}, bf16[17,16,128]{2,1,0:T(8,128)(2,1)S(1)}, u32[]{:S(2)}, u32[]{:S(2)}) collective-permute-start(bf16[17,16,128]{2,1,0:T(8,128)(2,1)S(1)} %get-tuple-element.120), channel_id=1, source_target_pairs={{0,8},{1,9},{2,10},{3,11},{4,12},{5,13},{6,14},{7,15},{8,0},{9,1},... | collective-permute-start | bytes 208904 | tf_op jit(solution)/shard_map/ppermute | solution.py:410
  56.1 1.5 %collective-permute-start.24 = (bf16[17,16,128]{2,1,0:T(8,128)(2,1)S(1)}, bf16[17,16,128]{2,1,0:T(8,128)(2,1)S(1)}, u32[]{:S(2)}, u32[]{:S(2)}) collective-permute-start(bf16[17,16,128]{2,1,0:T(8,128)(2,1)S(1)} %get-tuple-element.111), channel_id=1, source_target_pairs={{0,8},{1,9},{2,10},{3,11},{4,12},{5,13},{6,14},{7,15},{8,0},{9,1},... | collective-permute-start | bytes 208904 | tf_op jit(solution)/shard_map/ppermute | solution.py:410
  58.8 1.8 %collective-permute-start.26 = (bf16[17,16,128]{2,1,0:T(8,128)(2,1)S(1)}, bf16[17,16,128]{2,1,0:T(8,128)(2,1)S(1)}, u32[]{:S(2)}, u32[]{:S(2)}) collective-permute-start(bf16[17,16,128]{2,1,0:T(8,128)(2,1)S(1)} %get-tuple-element.115), channel_id=1, source_target_pairs={{0,12},{1,13},{2,14},{3,15},{4,8},{5,9},{6,10},{7,11},{8,4},{9,5},... | collective-permute-start | bytes 208904 | tf_op jit(solution)/shard_map/ppermute | solution.py:410
  63.2 1.7 %collective-permute-done.24.rest_1_ = bf16[17,16,128]{2,1,0:T(8,128)(2,1)S(1)} collective-permute-done((bf16[17,16,128]{2,1,0:T(8,128)(2,1)S(1)}, bf16[17,16,128]{2,1,0:T(8,128)(2,1)S(1)}, u32[]{:S(2)}, u32[]{:S(2)}) %collective-permute-start.24) | collective-permute-done | bytes 69664 | tf_op jit(solution)/shard_map/ppermute | solution.py:410
  66.0 1.6 %shard_map.96 = (f32[16,2048]{1,0:T(8,128)}, f32[16,2048]{1,0:T(8,128)}) custom-call(f32[16,2048]{1,0:T(8,128)S(1)} %shard_map.90.direction_ref, f32[1,2048]{1,0:T(1,128)S(1)} %get-tuple-element.70.nugget_ref, f32[16,16,128]{2,1,0:T(8,128)S(1)} %get-tuple-element.116.keep_ref, f32[16,128]{1,0:T(8,128)S(1)} %get-tuple-element.117.pair_ref, ...), custom_call_target="tpu_custom_call" | custom-call | tf_op jit(solution)/shard_map/pallas_call | solution.py:382
  (60 shorter events, 24.4 us)
Async XLA Ops:
  1.6 14.1 %collective-permute-start.4 = (bf16[512,2048]{1,0:T(8,128)(2,1)}, bf16[512,2048]{1,0:T(8,128)(2,1)S(1)}, u32[]{:S(2)}, u32[]{:S(2)}) collective-permute-start(bf16[512,2048]{1,0:T(8,128)(2,1)} %bitcast.17), channel_id=1, source_target_pairs={{0,1},{1,0},{2,3},{3,2},{4,5},{5,4},{6,7},{7,6},{8,9},{9,8},{10,11... | collective-permute-start | bytes 6291464 | tf_op jit(solution)/shard_map/ppermute | solution.py:410
  2.1 10.0 %collective-permute-start = (bf16[16,16,128]{2,1,0:T(8,128)(2,1)S(1)}, bf16[16,16,128]{2,1,0:T(8,128)(2,1)S(1)}, u32[]{:S(2)}, u32[]{:S(2)}) collective-permute-start(bf16[16,16,128]{2,1,0:T(8,128)(2,1)S(1)} %get-tuple-element.62), channel_id=1, source_target_pairs={{0,12},{1,13},{2,14},{3,15},{4,8},{5,9},{6,10},{7,11},{8,4},{9,5},... | collective-permute-start | bytes 196616 | tf_op jit(solution)/shard_map/ppermute | solution.py:410
  6.8 6.1 %collective-permute-start.1 = (bf16[16,16,128]{2,1,0:T(8,128)(2,1)S(1)}, bf16[16,16,128]{2,1,0:T(8,128)(2,1)S(1)}, u32[]{:S(2)}, u32[]{:S(2)}) collective-permute-start(bf16[16,16,128]{2,1,0:T(8,128)(2,1)S(1)} %get-tuple-element.62), channel_id=1, source_target_pairs={{0,8},{1,9},{2,10},{3,11},{4,12},{5,13},{6,14},{7,15},{8,0},{9,1},... | collective-permute-start | bytes 196616 | tf_op jit(solution)/shard_map/ppermute | solution.py:410
  6.8 7.7 %collective-permute-start.2 = (bf16[16,16,128]{2,1,0:T(8,128)(2,1)S(1)}, bf16[16,16,128]{2,1,0:T(8,128)(2,1)S(1)}, u32[]{:S(2)}, u32[]{:S(2)}) collective-permute-start(bf16[16,16,128]{2,1,0:T(8,128)(2,1)S(1)} %get-tuple-element.62), channel_id=1, source_target_pairs={{0,4},{1,5},{2,6},{3,7},{4,0},{5,1},{6,2},{7,3},{8,12},{9,13},{10,... | collective-permute-start | bytes 196616 | tf_op jit(solution)/shard_map/ppermute | solution.py:410
  7.4 7.0 %collective-permute-start.5 = (bf16[1,16,16,128]{3,2,1,0:T(8,128)(2,1)S(1)}, bf16[1,16,16,128]{3,2,1,0:T(8,128)(2,1)S(1)}, u32[]{:S(2)}, u32[]{:S(2)}) collective-permute-start(bf16[1,16,16,128]{3,2,1,0:T(8,128)(2,1)S(1)} %bitcast.14), channel_id=1, source_target_pairs={{0,2},{1,3},{2,0},{3,1},{4,6},{5,7},{6,4},{7,5},{8,10},{9,11},{10,... | collective-permute-start | bytes 196616 | tf_op jit(solution)/shard_map/ppermute | solution.py:410
  12.8 5.1 %collective-permute-start.6 = (bf16[2,16,16,128]{3,2,1,0:T(8,128)(2,1)S(1)}, bf16[2,16,16,128]{3,2,1,0:T(8,128)(2,1)S(1)}, u32[]{:S(2)}, u32[]{:S(2)}) collective-permute-start(bf16[2,16,16,128]{3,2,1,0:T(8,128)(2,1)S(1)} %pad_maximum_fusion.3), channel_id=1, source_target_pairs={{0,2},{1,3},{2,0},{3,1},{4,6},{5,7},{6,4},{7,5},{8,10},{9,11},{10,... | collective-permute-start | bytes 393224 | tf_op jit(solution)/shard_map/ppermute | solution.py:410
  14.4 4.5 %collective-permute-start.7 = (bf16[1,16,16,128]{3,2,1,0:T(8,128)(2,1)S(1)}, bf16[1,16,16,128]{3,2,1,0:T(8,128)(2,1)S(1)}, u32[]{:S(2)}, u32[]{:S(2)}) collective-permute-start(bf16[1,16,16,128]{3,2,1,0:T(8,128)(2,1)S(1)} %collective-permute-done.5.rest_0_), channel_id=1, source_target_pairs={{0,4},{1,5},{2,6},{3,7},{4,0},{5,1},{6,2},{7,3},{8,12},{9,13},{10,... | collective-permute-start | bytes 196616 | tf_op jit(solution)/shard_map/ppermute | solution.py:410
  21.7 5.6 %collective-permute-start.9 = (bf16[17,16,128]{2,1,0:T(8,128)(2,1)S(1)}, bf16[17,16,128]{2,1,0:T(8,128)(2,1)S(1)}, u32[]{:S(2)}, u32[]{:S(2)}) collective-permute-start(bf16[17,16,128]{2,1,0:T(8,128)(2,1)S(1)} %get-tuple-element.81), channel_id=1, source_target_pairs={{0,2},{1,3},{2,0},{3,1},{4,6},{5,7},{6,4},{7,5},{8,10},{9,11},{10,... | collective-permute-start | bytes 208904 | tf_op jit(solution)/shard_map/ppermute | solution.py:410
  22.3 7.9 %collective-permute-start.13 = (bf16[17,16,128]{2,1,0:T(8,128)(2,1)S(1)}, bf16[17,16,128]{2,1,0:T(8,128)(2,1)S(1)}, u32[]{:S(2)}, u32[]{:S(2)}) collective-permute-start(bf16[17,16,128]{2,1,0:T(8,128)(2,1)S(1)} %get-tuple-element.91), channel_id=1, source_target_pairs={{0,8},{1,9},{2,10},{3,11},{4,12},{5,13},{6,14},{7,15},{8,0},{9,1},... | collective-permute-start | bytes 208904 | tf_op jit(solution)/shard_map/ppermute | solution.py:410
  23.9 6.8 %collective-permute-start.14 = (bf16[17,16,128]{2,1,0:T(8,128)(2,1)S(1)}, bf16[17,16,128]{2,1,0:T(8,128)(2,1)S(1)}, u32[]{:S(2)}, u32[]{:S(2)}) collective-permute-start(bf16[17,16,128]{2,1,0:T(8,128)(2,1)S(1)} %get-tuple-element.92), channel_id=1, source_target_pairs={{0,4},{1,5},{2,6},{3,7},{4,0},{5,1},{6,2},{7,3},{8,12},{9,13},{10,... | collective-permute-start | bytes 208904 | tf_op jit(solution)/shard_map/ppermute | solution.py:410
  25.7 8.1 %collective-permute-start.10 = (bf16[17,16,128]{2,1,0:T(8,128)(2,1)S(1)}, bf16[17,16,128]{2,1,0:T(8,128)(2,1)S(1)}, u32[]{:S(2)}, u32[]{:S(2)}) collective-permute-start(bf16[17,16,128]{2,1,0:T(8,128)(2,1)S(1)} %get-tuple-element.83), channel_id=1, source_target_pairs={{0,8},{1,9},{2,10},{3,11},{4,12},{5,13},{6,14},{7,15},{8,0},{9,1},... | collective-permute-start | bytes 208904 | tf_op jit(solution)/shard_map/ppermute | solution.py:410
  25.7 8.1 %collective-permute-start.11 = (bf16[17,16,128]{2,1,0:T(8,128)(2,1)S(1)}, bf16[17,16,128]{2,1,0:T(8,128)(2,1)S(1)}, u32[]{:S(2)}, u32[]{:S(2)}) collective-permute-start(bf16[17,16,128]{2,1,0:T(8,128)(2,1)S(1)} %get-tuple-element.84), channel_id=1, source_target_pairs={{0,4},{1,5},{2,6},{3,7},{4,0},{5,1},{6,2},{7,3},{8,12},{9,13},{10,... | collective-permute-start | bytes 208904 | tf_op jit(solution)/shard_map/ppermute | solution.py:410
  27.5 6.8 %collective-permute-start.12 = (bf16[17,16,128]{2,1,0:T(8,128)(2,1)S(1)}, bf16[17,16,128]{2,1,0:T(8,128)(2,1)S(1)}, u32[]{:S(2)}, u32[]{:S(2)}) collective-permute-start(bf16[17,16,128]{2,1,0:T(8,128)(2,1)S(1)} %get-tuple-element.87), channel_id=1, source_target_pairs={{0,12},{1,13},{2,14},{3,15},{4,8},{5,9},{6,10},{7,11},{8,4},{9,5},... | collective-permute-start | bytes 208904 | tf_op jit(solution)/shard_map/ppermute | solution.py:410
  36.6 6.2 %collective-permute-start.17 = (bf16[17,16,128]{2,1,0:T(8,128)(2,1)S(1)}, bf16[17,16,128]{2,1,0:T(8,128)(2,1)S(1)}, u32[]{:S(2)}, u32[]{:S(2)}) collective-permute-start(bf16[17,16,128]{2,1,0:T(8,128)(2,1)S(1)} %get-tuple-element.93), channel_id=1, source_target_pairs={{0,8},{1,9},{2,10},{3,11},{4,12},{5,13},{6,14},{7,15},{8,0},{9,1},... | collective-permute-start | bytes 208904 | tf_op jit(solution)/shard_map/ppermute | solution.py:410
  37.7 6.3 %collective-permute-start.16 = (bf16[17,16,128]{2,1,0:T(8,128)(2,1)S(1)}, bf16[17,16,128]{2,1,0:T(8,128)(2,1)S(1)}, u32[]{:S(2)}, u32[]{:S(2)}) collective-permute-start(bf16[17,16,128]{2,1,0:T(8,128)(2,1)S(1)} %get-tuple-element.93), channel_id=1, source_target_pairs={{0,12},{1,13},{2,14},{3,15},{4,8},{5,9},{6,10},{7,11},{8,4},{9,5},... | collective-permute-start | bytes 208904 | tf_op jit(solution)/shard_map/ppermute | solution.py:410
  39.0 7.2 %collective-permute-start.18 = (bf16[17,16,128]{2,1,0:T(8,128)(2,1)S(1)}, bf16[17,16,128]{2,1,0:T(8,128)(2,1)S(1)}, u32[]{:S(2)}, u32[]{:S(2)}) collective-permute-start(bf16[17,16,128]{2,1,0:T(8,128)(2,1)S(1)} %get-tuple-element.93), channel_id=1, source_target_pairs={{0,4},{1,5},{2,6},{3,7},{4,0},{5,1},{6,2},{7,3},{8,12},{9,13},{10,... | collective-permute-start | bytes 208904 | tf_op jit(solution)/shard_map/ppermute | solution.py:410
  40.1 5.1 %collective-permute-start.19 = (bf16[1,17,16,128]{3,2,1,0:T(8,128)(2,1)S(1)}, bf16[1,17,16,128]{3,2,1,0:T(8,128)(2,1)S(1)}, u32[]{:S(2)}, u32[]{:S(2)}) collective-permute-start(bf16[1,17,16,128]{3,2,1,0:T(8,128)(2,1)S(1)} %bitcast.12), channel_id=1, source_target_pairs={{0,2},{1,3},{2,0},{3,1},{4,6},{5,7},{6,4},{7,5},{8,10},{9,11},{10,... | collective-permute-start | bytes 208904 | tf_op jit(solution)/shard_map/ppermute | solution.py:410
  44.0 5.5 %collective-permute-start.20 = (bf16[2,17,16,128]{3,2,1,0:T(8,128)(2,1)S(1)}, bf16[2,17,16,128]{3,2,1,0:T(8,128)(2,1)S(1)}, u32[]{:S(2)}, u32[]{:S(2)}) collective-permute-start(bf16[2,17,16,128]{3,2,1,0:T(8,128)(2,1)S(1)} %pad_maximum_fusion.2), channel_id=1, source_target_pairs={{0,2},{1,3},{2,0},{3,1},{4,6},{5,7},{6,4},{7,5},{8,10},{9,11},{10,... | collective-permute-start | bytes 417800 | tf_op jit(solution)/shard_map/ppermute | solution.py:410
  52.8 5.9 %collective-permute-start.23 = (bf16[17,16,128]{2,1,0:T(8,128)(2,1)S(1)}, bf16[17,16,128]{2,1,0:T(8,128)(2,1)S(1)}, u32[]{:S(2)}, u32[]{:S(2)}) collective-permute-start(bf16[17,16,128]{2,1,0:T(8,128)(2,1)S(1)} %get-tuple-element.109), channel_id=1, source_target_pairs={{0,2},{1,3},{2,0},{3,1},{4,6},{5,7},{6,4},{7,5},{8,10},{9,11},{10,... | collective-permute-start | bytes 208904 | tf_op jit(solution)/shard_map/ppermute | solution.py:410
  53.7 7.6 %collective-permute-start.27 = (bf16[17,16,128]{2,1,0:T(8,128)(2,1)S(1)}, bf16[17,16,128]{2,1,0:T(8,128)(2,1)S(1)}, u32[]{:S(2)}, u32[]{:S(2)}) collective-permute-start(bf16[17,16,128]{2,1,0:T(8,128)(2,1)S(1)} %get-tuple-element.120), channel_id=1, source_target_pairs={{0,8},{1,9},{2,10},{3,11},{4,12},{5,13},{6,14},{7,15},{8,0},{9,1},... | collective-permute-start | bytes 208904 | tf_op jit(solution)/shard_map/ppermute | solution.py:410
  55.3 6.1 %collective-permute-start.28 = (bf16[17,16,128]{2,1,0:T(8,128)(2,1)S(1)}, bf16[17,16,128]{2,1,0:T(8,128)(2,1)S(1)}, u32[]{:S(2)}, u32[]{:S(2)}) collective-permute-start(bf16[17,16,128]{2,1,0:T(8,128)(2,1)S(1)} %get-tuple-element.121), channel_id=1, source_target_pairs={{0,4},{1,5},{2,6},{3,7},{4,0},{5,1},{6,2},{7,3},{8,12},{9,13},{10,... | collective-permute-start | bytes 208904 | tf_op jit(solution)/shard_map/ppermute | solution.py:410
  56.1 8.9 %collective-permute-start.24 = (bf16[17,16,128]{2,1,0:T(8,128)(2,1)S(1)}, bf16[17,16,128]{2,1,0:T(8,128)(2,1)S(1)}, u32[]{:S(2)}, u32[]{:S(2)}) collective-permute-start(bf16[17,16,128]{2,1,0:T(8,128)(2,1)S(1)} %get-tuple-element.111), channel_id=1, source_target_pairs={{0,8},{1,9},{2,10},{3,11},{4,12},{5,13},{6,14},{7,15},{8,0},{9,1},... | collective-permute-start | bytes 208904 | tf_op jit(solution)/shard_map/ppermute | solution.py:410
  57.5 7.4 %collective-permute-start.25 = (bf16[17,16,128]{2,1,0:T(8,128)(2,1)S(1)}, bf16[17,16,128]{2,1,0:T(8,128)(2,1)S(1)}, u32[]{:S(2)}, u32[]{:S(2)}) collective-permute-start(bf16[17,16,128]{2,1,0:T(8,128)(2,1)S(1)} %get-tuple-element.112), channel_id=1, source_target_pairs={{0,4},{1,5},{2,6},{3,7},{4,0},{5,1},{6,2},{7,3},{8,12},{9,13},{10,... | collective-permute-start | bytes 208904 | tf_op jit(solution)/shard_map/ppermute | solution.py:410
  58.8 6.6 %collective-permute-start.26 = (bf16[17,16,128]{2,1,0:T(8,128)(2,1)S(1)}, bf16[17,16,128]{2,1,0:T(8,128)(2,1)S(1)}, u32[]{:S(2)}, u32[]{:S(2)}) collective-permute-start(bf16[17,16,128]{2,1,0:T(8,128)(2,1)S(1)} %get-tuple-element.115), channel_id=1, source_target_pairs={{0,12},{1,13},{2,14},{3,15},{4,8},{5,9},{6,10},{7,11},{8,4},{9,5},... | collective-permute-start | bytes 208904 | tf_op jit(solution)/shard_map/ppermute | solution.py:410
  (6 other events, 16.8 us)

commit v10 on v9

--- a/solution.py
+++ b/solution.py
@@ -83,6 +83,14 @@
 
 def gram(former, latter):
     return lax.dot_general(former, latter, NT, precision=EXACT, preferred_element_type=F32)
+
+
+def split_gram(block, rhs):
+    high = block.astype(BF16)
+    low = (block - high.astype(F32)).astype(BF16)
+    both = jnp.concatenate([high, low], axis=0)
+    total = lax.dot_general(both, both, NT, preferred_element_type=F32)
+    return total[:rhs, :rhs] + total[:rhs, rhs:] + total[rhs:, :rhs]
 
 
 def rows_of(ref, chunks):
@@ -361,7 +369,7 @@
     residual = direction - left_multiply(step, applied, rhs)
     residual_ref[...] = residual
     store_message(message_ref, residual, rhs)
-    message_ref[chunks] = encode(sums_of([gram(residual, residual)], rhs), rhs)
+    message_ref[chunks] = encode(sums_of([split_gram(residual, rhs)], rhs), rhs)
     step_ref[...] = step
 
 

time: 67.7 us -> 67.5 us (level)
  no operation moved by 1% of the time
where the time goes in v10:
time: 67.5 us; the launch traced here: 67.4 us
  starting transfers between devices  34.5 us (51%)
  waiting for transfers between devices  16.8 us (25%)
  Pallas kernels  14.5 us (21%)
  between operations  1.42 us (2%)
    ppermute x30, starting transfers between devices, swap(): return lax.ppermute(array, 'row', [(i, i ^ offset) for i in range(devices)])  34.5 us
    ppermute x30, waiting for transfers between devices, swap(): return lax.ppermute(array, 'row', [(i, i ^ offset) for i in range(devices)])  16.8 us
    pallas_call x20, Pallas kernels, call(): pl.pallas_call(kernel, out_shape=[pltpu.VMEM(shape, dtype) if i in fixed...  14.5 us
  transfers between devices with their start and end apart: 30, of which 16 were waited for; matrix products, arithmetic and copies ran while one was open for 0% of the time, Pallas kernels for 11%

profile of v10, /device:TPU:0, one launch (start us, length us, event | category | flops | bytes accessed | tf_op | source)
XLA Modules:
  0.0 67.4 jit_solution(7177969161061631130)
XLA Ops:
  2.1 4.7 %collective-permute-start = (bf16[16,16,128]{2,1,0:T(8,128)(2,1)S(1)}, bf16[16,16,128]{2,1,0:T(8,128)(2,1)S(1)}, u32[]{:S(2)}, u32[]{:S(2)}) collective-permute-start(bf16[16,16,128]{2,1,0:T(8,128)(2,1)S(1)} %get-tuple-element.62), channel_id=1, source_target_pairs={{0,12},{1,13},{2,14},{3,15},{4,8},{5,9},{6,10},{7,11},{8,4},{9,5},... | collective-permute-start | bytes 196616 | tf_op jit(solution)/shard_map/ppermute | solution.py:418
  7.4 1.7 %collective-permute-start.5 = (bf16[1,16,16,128]{3,2,1,0:T(8,128)(2,1)S(1)}, bf16[1,16,16,128]{3,2,1,0:T(8,128)(2,1)S(1)}, u32[]{:S(2)}, u32[]{:S(2)}) collective-permute-start(bf16[1,16,16,128]{3,2,1,0:T(8,128)(2,1)S(1)} %bitcast.14), channel_id=1, source_target_pairs={{0,2},{1,3},{2,0},{3,1},{4,6},{5,7},{6,4},{7,5},{8,10},{9,11},{10,... | collective-permute-start | bytes 196616 | tf_op jit(solution)/shard_map/ppermute | solution.py:418
  9.7 2.3 %shard_map.78 = (f32[1,2048]{1,0:T(1,128)S(1)}, bf16[512,2048]{1,0:T(8,128)(2,1)S(1)}, bf16[512,2048]{1,0:T(8,128)(2,1)S(1)}, s32[8,512]{1,0:T(8,128)S(1)}, f32[...) custom-call(f32[16,2048]{1,0:T(8,128)S(1)} %get-tuple-element.63.own_ref.direction_ref.right_side_ref, s32[32]{0:T(128)} %bitcast.30, ...), custom_call_target="tpu_custom_call" | custom-call | tf_op jit(solution)/shard_map/pallas_call | solution.py:390
  12.8 1.6 %collective-permute-start.6 = (bf16[2,16,16,128]{3,2,1,0:T(8,128)(2,1)S(1)}, bf16[2,16,16,128]{3,2,1,0:T(8,128)(2,1)S(1)}, u32[]{:S(2)}, u32[]{:S(2)}) collective-permute-start(bf16[2,16,16,128]{3,2,1,0:T(8,128)(2,1)S(1)} %pad_maximum_fusion.3), channel_id=1, source_target_pairs={{0,2},{1,3},{2,0},{3,1},{4,6},{5,7},{6,4},{7,5},{8,10},{9,11},{10,... | collective-permute-start | bytes 393224 | tf_op jit(solution)/shard_map/ppermute | solution.py:418
  15.6 1.5 %shard_map.79 = (f32[16,1024]{1,0:T(8,128)S(1)}, s32[16,1024]{1,0:T(8,128)S(1)}, bf16[2048,1024]{1,0:T(8,128)(2,1)S(1)}) custom-call(bf16[4,16,16,128]{3,2,1,0:T(8,128)(2,1)S(1)} %pad_maximum_fusion.1.held_ref, f32[16,512]{1,0:T(8,128)S(1)} %get-tuple-element.64.near_ref, s32[8,512]{1,0:T(8,128)S(1)} %get-tuple-element.65.named_ref, ...), custom_call_target="tpu_custom_call" | custom-call | tf_op jit(solution)/shard_map/pallas_call | solution.py:390
  19.7 1.3 %collective-permute-done.8.got_ref = f32[16,1152]{1,0:T(8,128)S(1)} collective-permute-done((f32[16,1152]{1,0:T(8,128)S(1)}, f32[16,1152]{1,0:T(8,128)S(1)}, u32[]{:S(2)}, u32[]{:S(2)}) %collective-permute-start.8) | collective-permute-done | bytes 73760 | tf_op jit(solution)/shard_map/ppermute | solution.py:418
  22.3 1.6 %collective-permute-start.13 = (bf16[17,16,128]{2,1,0:T(8,128)(2,1)S(1)}, bf16[17,16,128]{2,1,0:T(8,128)(2,1)S(1)}, u32[]{:S(2)}, u32[]{:S(2)}) collective-permute-start(bf16[17,16,128]{2,1,0:T(8,128)(2,1)S(1)} %get-tuple-element.91), channel_id=1, source_target_pairs={{0,8},{1,9},{2,10},{3,11},{4,12},{5,13},{6,14},{7,15},{8,0},{9,1},... | collective-permute-start | bytes 208904 | tf_op jit(solution)/shard_map/ppermute | solution.py:418
  23.9 1.7 %collective-permute-start.14 = (bf16[17,16,128]{2,1,0:T(8,128)(2,1)S(1)}, bf16[17,16,128]{2,1,0:T(8,128)(2,1)S(1)}, u32[]{:S(2)}, u32[]{:S(2)}) collective-permute-start(bf16[17,16,128]{2,1,0:T(8,128)(2,1)S(1)} %get-tuple-element.92), channel_id=1, source_target_pairs={{0,4},{1,5},{2,6},{3,7},{4,0},{5,1},{6,2},{7,3},{8,12},{9,13},{10,... | collective-permute-start | bytes 208904 | tf_op jit(solution)/shard_map/ppermute | solution.py:418
  25.7 1.6 %collective-permute-start.11 = (bf16[17,16,128]{2,1,0:T(8,128)(2,1)S(1)}, bf16[17,16,128]{2,1,0:T(8,128)(2,1)S(1)}, u32[]{:S(2)}, u32[]{:S(2)}) collective-permute-start(bf16[17,16,128]{2,1,0:T(8,128)(2,1)S(1)} %get-tuple-element.84), channel_id=1, source_target_pairs={{0,4},{1,5},{2,6},{3,7},{4,0},{5,1},{6,2},{7,3},{8,12},{9,13},{10,... | collective-permute-start | bytes 208904 | tf_op jit(solution)/shard_map/ppermute | solution.py:418
  27.5 2.8 %collective-permute-start.12 = (bf16[17,16,128]{2,1,0:T(8,128)(2,1)S(1)}, bf16[17,16,128]{2,1,0:T(8,128)(2,1)S(1)}, u32[]{:S(2)}, u32[]{:S(2)}) collective-permute-start(bf16[17,16,128]{2,1,0:T(8,128)(2,1)S(1)} %get-tuple-element.87), channel_id=1, source_target_pairs={{0,12},{1,13},{2,14},{3,15},{4,8},{5,9},{6,10},{7,11},{8,4},{9,5},... | collective-permute-start | bytes 208904 | tf_op jit(solution)/shard_map/ppermute | solution.py:418
  30.9 1.2 %collective-permute-start.15 = (bf16[17,16,128]{2,1,0:T(8,128)(2,1)S(1)}, bf16[17,16,128]{2,1,0:T(8,128)(2,1)S(1)}, u32[]{:S(2)}, u32[]{:S(2)}) collective-permute-start(bf16[17,16,128]{2,1,0:T(8,128)(2,1)S(1)} %shard_map.85), channel_id=1, source_target_pairs={{0,2},{1,3},{2,0},{3,1},{4,6},{5,7},{6,4},{7,5},{8,10},{9,11},{10,... | collective-permute-start | bytes 208904 | tf_op jit(solution)/shard_map/ppermute | solution.py:418
  32.1 1.7 %collective-permute-done.10.rest_1_ = bf16[17,16,128]{2,1,0:T(8,128)(2,1)S(1)} collective-permute-done((bf16[17,16,128]{2,1,0:T(8,128)(2,1)S(1)}, bf16[17,16,128]{2,1,0:T(8,128)(2,1)S(1)}, u32[]{:S(2)}, u32[]{:S(2)}) %collective-permute-start.10) | collective-permute-done | bytes 69664 | tf_op jit(solution)/shard_map/ppermute | solution.py:418
  37.5 1.3 %collective-permute-start.16 = (bf16[17,16,128]{2,1,0:T(8,128)(2,1)S(1)}, bf16[17,16,128]{2,1,0:T(8,128)(2,1)S(1)}, u32[]{:S(2)}, u32[]{:S(2)}) collective-permute-start(bf16[17,16,128]{2,1,0:T(8,128)(2,1)S(1)} %get-tuple-element.93), channel_id=1, source_target_pairs={{0,12},{1,13},{2,14},{3,15},{4,8},{5,9},{6,10},{7,11},{8,4},{9,5},... | collective-permute-start | bytes 208904 | tf_op jit(solution)/shard_map/ppermute | solution.py:418
  41.0 1.5 %collective-permute-done.17 = bf16[17,16,128]{2,1,0:T(8,128)(2,1)S(1)} collective-permute-done((bf16[17,16,128]{2,1,0:T(8,128)(2,1)S(1)}, bf16[17,16,128]{2,1,0:T(8,128)(2,1)S(1)}, u32[]{:S(2)}, u32[]{:S(2)}) %collective-permute-start.17) | collective-permute-done | bytes 69664 | tf_op jit(solution)/shard_map/ppermute | solution.py:418
  43.8 1.2 %collective-permute-start.20 = (bf16[2,17,16,128]{3,2,1,0:T(8,128)(2,1)S(1)}, bf16[2,17,16,128]{3,2,1,0:T(8,128)(2,1)S(1)}, u32[]{:S(2)}, u32[]{:S(2)}) collective-permute-start(bf16[2,17,16,128]{3,2,1,0:T(8,128)(2,1)S(1)} %pad_maximum_fusion.2), channel_id=1, source_target_pairs={{0,2},{1,3},{2,0},{3,1},{4,6},{5,7},{6,4},{7,5},{8,10},{9,11},{10,... | collective-permute-start | bytes 417800 | tf_op jit(solution)/shard_map/ppermute | solution.py:418
  46.1 1.6 %shard_map.87 = (f32[16,1024]{1,0:T(8,128)S(1)}, f32[16,128]{1,0:T(8,128)S(1)}, f32[16,128]{1,0:T(8,128)S(1)}) custom-call(bf16[4,17,16,128]{3,2,1,0:T(8,128)(2,1)S(1)} %pad_maximum_fusion.held_ref, f32[16,2048]{1,0:T(8,128)S(1)} %get-tuple-element.94.own_ref.residual_ref, f32[16,2048]{1,0:T(8,128)S(1)} %get-tuple-element.63.own_ref.direction_ref.right_side_ref, ...), custom_call_target="tpu_custom_call" | custom-call | tf_op jit(solution)/shard_map/pallas_call | solution.py:390
  47.7 1.6 %collective-permute-done.21.rest_2_ = bf16[1,17,16,128]{3,2,1,0:T(8,128)(2,1)S(1)} collective-permute-done((bf16[1,17,16,128]{3,2,1,0:T(8,128)(2,1)S(1)}, bf16[1,17,16,128]{3,2,1,0:T(8,128)(2,1)S(1)}, u32[]{:S(2)}, u32[]{:S(2)}) %collective-permute-start.21) | collective-permute-done | bytes 69664 | tf_op jit(solution)/shard_map/ppermute | solution.py:418
  50.1 1.3 %collective-permute-done.22.got_ref = f32[16,1152]{1,0:T(8,128)S(1)} collective-permute-done((f32[16,1152]{1,0:T(8,128)S(1)}, f32[16,1152]{1,0:T(8,128)S(1)}, u32[]{:S(2)}, u32[]{:S(2)}) %collective-permute-start.22) | collective-permute-done | bytes 73760 | tf_op jit(solution)/shard_map/ppermute | solution.py:418
  51.4 1.2 %shard_map.89 = (f32[16,128]{1,0:T(8,128)S(1)}, f32[16,1024]{1,0:T(8,128)S(1)}, f32[16,128]{1,0:T(8,128)S(1)}, f32[16,128]{1,0:T(8,128)S(1)}, bf16[17,16,128]{2,...) custom-call(f32[16,1152]{1,0:T(8,128)S(1)} %shard_map.88.message_ref, ...), custom_call_target="tpu_custom_call" | custom-call | tf_op jit(solution)/shard_map/pallas_call | solution.py:390
  53.5 1.6 %collective-permute-start.27 = (bf16[17,16,128]{2,1,0:T(8,128)(2,1)S(1)}, bf16[17,16,128]{2,1,0:T(8,128)(2,1)S(1)}, u32[]{:S(2)}, u32[]{:S(2)}) collective-permute-start(bf16[17,16,128]{2,1,0:T(8,128)(2,1)S(1)} %get-tuple-element.120), channel_id=1, source_target_pairs={{0,8},{1,9},{2,10},{3,11},{4,12},{5,13},{6,14},{7,15},{8,0},{9,1},... | collective-permute-start | bytes 208904 | tf_op jit(solution)/shard_map/ppermute | solution.py:418
  55.9 1.5 %collective-permute-start.24 = (bf16[17,16,128]{2,1,0:T(8,128)(2,1)S(1)}, bf16[17,16,128]{2,1,0:T(8,128)(2,1)S(1)}, u32[]{:S(2)}, u32[]{:S(2)}) collective-permute-start(bf16[17,16,128]{2,1,0:T(8,128)(2,1)S(1)} %get-tuple-element.111), channel_id=1, source_target_pairs={{0,8},{1,9},{2,10},{3,11},{4,12},{5,13},{6,14},{7,15},{8,0},{9,1},... | collective-permute-start | bytes 208904 | tf_op jit(solution)/shard_map/ppermute | solution.py:418
  58.6 1.8 %collective-permute-start.26 = (bf16[17,16,128]{2,1,0:T(8,128)(2,1)S(1)}, bf16[17,16,128]{2,1,0:T(8,128)(2,1)S(1)}, u32[]{:S(2)}, u32[]{:S(2)}) collective-permute-start(bf16[17,16,128]{2,1,0:T(8,128)(2,1)S(1)} %get-tuple-element.115), channel_id=1, source_target_pairs={{0,12},{1,13},{2,14},{3,15},{4,8},{5,9},{6,10},{7,11},{8,4},{9,5},... | collective-permute-start | bytes 208904 | tf_op jit(solution)/shard_map/ppermute | solution.py:418
  63.0 1.8 %collective-permute-done.24.rest_1_ = bf16[17,16,128]{2,1,0:T(8,128)(2,1)S(1)} collective-permute-done((bf16[17,16,128]{2,1,0:T(8,128)(2,1)S(1)}, bf16[17,16,128]{2,1,0:T(8,128)(2,1)S(1)}, u32[]{:S(2)}, u32[]{:S(2)}) %collective-permute-start.24) | collective-permute-done | bytes 69664 | tf_op jit(solution)/shard_map/ppermute | solution.py:418
  65.7 1.6 %shard_map.96 = (f32[16,2048]{1,0:T(8,128)}, f32[16,2048]{1,0:T(8,128)}) custom-call(f32[16,2048]{1,0:T(8,128)S(1)} %shard_map.90.direction_ref, f32[1,2048]{1,0:T(1,128)S(1)} %get-tuple-element.70.nugget_ref, f32[16,16,128]{2,1,0:T(8,128)S(1)} %get-tuple-element.116.keep_ref, f32[16,128]{1,0:T(8,128)S(1)} %get-tuple-element.117.pair_ref, ...), custom_call_target="tpu_custom_call" | custom-call | tf_op jit(solution)/shard_map/pallas_call | solution.py:390
  (60 shorter events, 24.3 us)
Async XLA Ops:
  1.6 14.1 %collective-permute-start.4 = (bf16[512,2048]{1,0:T(8,128)(2,1)}, bf16[512,2048]{1,0:T(8,128)(2,1)S(1)}, u32[]{:S(2)}, u32[]{:S(2)}) collective-permute-start(bf16[512,2048]{1,0:T(8,128)(2,1)} %bitcast.17), channel_id=1, source_target_pairs={{0,1},{1,0},{2,3},{3,2},{4,5},{5,4},{6,7},{7,6},{8,9},{9,8},{10,11... | collective-permute-start | bytes 6291464 | tf_op jit(solution)/shard_map/ppermute | solution.py:418
  2.1 10.0 %collective-permute-start = (bf16[16,16,128]{2,1,0:T(8,128)(2,1)S(1)}, bf16[16,16,128]{2,1,0:T(8,128)(2,1)S(1)}, u32[]{:S(2)}, u32[]{:S(2)}) collective-permute-start(bf16[16,16,128]{2,1,0:T(8,128)(2,1)S(1)} %get-tuple-element.62), channel_id=1, source_target_pairs={{0,12},{1,13},{2,14},{3,15},{4,8},{5,9},{6,10},{7,11},{8,4},{9,5},... | collective-permute-start | bytes 196616 | tf_op jit(solution)/shard_map/ppermute | solution.py:418
  6.8 6.1 %collective-permute-start.1 = (bf16[16,16,128]{2,1,0:T(8,128)(2,1)S(1)}, bf16[16,16,128]{2,1,0:T(8,128)(2,1)S(1)}, u32[]{:S(2)}, u32[]{:S(2)}) collective-permute-start(bf16[16,16,128]{2,1,0:T(8,128)(2,1)S(1)} %get-tuple-element.62), channel_id=1, source_target_pairs={{0,8},{1,9},{2,10},{3,11},{4,12},{5,13},{6,14},{7,15},{8,0},{9,1},... | collective-permute-start | bytes 196616 | tf_op jit(solution)/shard_map/ppermute | solution.py:418
  6.8 7.7 %collective-permute-start.2 = (bf16[16,16,128]{2,1,0:T(8,128)(2,1)S(1)}, bf16[16,16,128]{2,1,0:T(8,128)(2,1)S(1)}, u32[]{:S(2)}, u32[]{:S(2)}) collective-permute-start(bf16[16,16,128]{2,1,0:T(8,128)(2,1)S(1)} %get-tuple-element.62), channel_id=1, source_target_pairs={{0,4},{1,5},{2,6},{3,7},{4,0},{5,1},{6,2},{7,3},{8,12},{9,13},{10,... | collective-permute-start | bytes 196616 | tf_op jit(solution)/shard_map/ppermute | solution.py:418
  7.4 7.0 %collective-permute-start.5 = (bf16[1,16,16,128]{3,2,1,0:T(8,128)(2,1)S(1)}, bf16[1,16,16,128]{3,2,1,0:T(8,128)(2,1)S(1)}, u32[]{:S(2)}, u32[]{:S(2)}) collective-permute-start(bf16[1,16,16,128]{3,2,1,0:T(8,128)(2,1)S(1)} %bitcast.14), channel_id=1, source_target_pairs={{0,2},{1,3},{2,0},{3,1},{4,6},{5,7},{6,4},{7,5},{8,10},{9,11},{10,... | collective-permute-start | bytes 196616 | tf_op jit(solution)/shard_map/ppermute | solution.py:418
  12.8 5.1 %collective-permute-start.6 = (bf16[2,16,16,128]{3,2,1,0:T(8,128)(2,1)S(1)}, bf16[2,16,16,128]{3,2,1,0:T(8,128)(2,1)S(1)}, u32[]{:S(2)}, u32[]{:S(2)}) collective-permute-start(bf16[2,16,16,128]{3,2,1,0:T(8,128)(2,1)S(1)} %pad_maximum_fusion.3), channel_id=1, source_target_pairs={{0,2},{1,3},{2,0},{3,1},{4,6},{5,7},{6,4},{7,5},{8,10},{9,11},{10,... | collective-permute-start | bytes 393224 | tf_op jit(solution)/shard_map/ppermute | solution.py:418
  14.4 4.5 %collective-permute-start.7 = (bf16[1,16,16,128]{3,2,1,0:T(8,128)(2,1)S(1)}, bf16[1,16,16,128]{3,2,1,0:T(8,128)(2,1)S(1)}, u32[]{:S(2)}, u32[]{:S(2)}) collective-permute-start(bf16[1,16,16,128]{3,2,1,0:T(8,128)(2,1)S(1)} %collective-permute-done.5.rest_0_), channel_id=1, source_target_pairs={{0,4},{1,5},{2,6},{3,7},{4,0},{5,1},{6,2},{7,3},{8,12},{9,13},{10,... | collective-permute-start | bytes 196616 | tf_op jit(solution)/shard_map/ppermute | solution.py:418
  21.7 5.6 %collective-permute-start.9 = (bf16[17,16,128]{2,1,0:T(8,128)(2,1)S(1)}, bf16[17,16,128]{2,1,0:T(8,128)(2,1)S(1)}, u32[]{:S(2)}, u32[]{:S(2)}) collective-permute-start(bf16[17,16,128]{2,1,0:T(8,128)(2,1)S(1)} %get-tuple-element.81), channel_id=1, source_target_pairs={{0,2},{1,3},{2,0},{3,1},{4,6},{5,7},{6,4},{7,5},{8,10},{9,11},{10,... | collective-permute-start | bytes 208904 | tf_op jit(solution)/shard_map/ppermute | solution.py:418
  22.3 7.9 %collective-permute-start.13 = (bf16[17,16,128]{2,1,0:T(8,128)(2,1)S(1)}, bf16[17,16,128]{2,1,0:T(8,128)(2,1)S(1)}, u32[]{:S(2)}, u32[]{:S(2)}) collective-permute-start(bf16[17,16,128]{2,1,0:T(8,128)(2,1)S(1)} %get-tuple-element.91), channel_id=1, source_target_pairs={{0,8},{1,9},{2,10},{3,11},{4,12},{5,13},{6,14},{7,15},{8,0},{9,1},... | collective-permute-start | bytes 208904 | tf_op jit(solution)/shard_map/ppermute | solution.py:418
  23.9 6.8 %collective-permute-start.14 = (bf16[17,16,128]{2,1,0:T(8,128)(2,1)S(1)}, bf16[17,16,128]{2,1,0:T(8,128)(2,1)S(1)}, u32[]{:S(2)}, u32[]{:S(2)}) collective-permute-start(bf16[17,16,128]{2,1,0:T(8,128)(2,1)S(1)} %get-tuple-element.92), channel_id=1, source_target_pairs={{0,4},{1,5},{2,6},{3,7},{4,0},{5,1},{6,2},{7,3},{8,12},{9,13},{10,... | collective-permute-start | bytes 208904 | tf_op jit(solution)/shard_map/ppermute | solution.py:418
  25.7 8.1 %collective-permute-start.10 = (bf16[17,16,128]{2,1,0:T(8,128)(2,1)S(1)}, bf16[17,16,128]{2,1,0:T(8,128)(2,1)S(1)}, u32[]{:S(2)}, u32[]{:S(2)}) collective-permute-start(bf16[17,16,128]{2,1,0:T(8,128)(2,1)S(1)} %get-tuple-element.83), channel_id=1, source_target_pairs={{0,8},{1,9},{2,10},{3,11},{4,12},{5,13},{6,14},{7,15},{8,0},{9,1},... | collective-permute-start | bytes 208904 | tf_op jit(solution)/shard_map/ppermute | solution.py:418
  25.7 8.1 %collective-permute-start.11 = (bf16[17,16,128]{2,1,0:T(8,128)(2,1)S(1)}, bf16[17,16,128]{2,1,0:T(8,128)(2,1)S(1)}, u32[]{:S(2)}, u32[]{:S(2)}) collective-permute-start(bf16[17,16,128]{2,1,0:T(8,128)(2,1)S(1)} %get-tuple-element.84), channel_id=1, source_target_pairs={{0,4},{1,5},{2,6},{3,7},{4,0},{5,1},{6,2},{7,3},{8,12},{9,13},{10,... | collective-permute-start | bytes 208904 | tf_op jit(solution)/shard_map/ppermute | solution.py:418
  27.5 6.8 %collective-permute-start.12 = (bf16[17,16,128]{2,1,0:T(8,128)(2,1)S(1)}, bf16[17,16,128]{2,1,0:T(8,128)(2,1)S(1)}, u32[]{:S(2)}, u32[]{:S(2)}) collective-permute-start(bf16[17,16,128]{2,1,0:T(8,128)(2,1)S(1)} %get-tuple-element.87), channel_id=1, source_target_pairs={{0,12},{1,13},{2,14},{3,15},{4,8},{5,9},{6,10},{7,11},{8,4},{9,5},... | collective-permute-start | bytes 208904 | tf_op jit(solution)/shard_map/ppermute | solution.py:418
  36.4 6.2 %collective-permute-start.17 = (bf16[17,16,128]{2,1,0:T(8,128)(2,1)S(1)}, bf16[17,16,128]{2,1,0:T(8,128)(2,1)S(1)}, u32[]{:S(2)}, u32[]{:S(2)}) collective-permute-start(bf16[17,16,128]{2,1,0:T(8,128)(2,1)S(1)} %get-tuple-element.93), channel_id=1, source_target_pairs={{0,8},{1,9},{2,10},{3,11},{4,12},{5,13},{6,14},{7,15},{8,0},{9,1},... | collective-permute-start | bytes 208904 | tf_op jit(solution)/shard_map/ppermute | solution.py:418
  37.5 6.3 %collective-permute-start.16 = (bf16[17,16,128]{2,1,0:T(8,128)(2,1)S(1)}, bf16[17,16,128]{2,1,0:T(8,128)(2,1)S(1)}, u32[]{:S(2)}, u32[]{:S(2)}) collective-permute-start(bf16[17,16,128]{2,1,0:T(8,128)(2,1)S(1)} %get-tuple-element.93), channel_id=1, source_target_pairs={{0,12},{1,13},{2,14},{3,15},{4,8},{5,9},{6,10},{7,11},{8,4},{9,5},... | collective-permute-start | bytes 208904 | tf_op jit(solution)/shard_map/ppermute | solution.py:418
  38.8 7.2 %collective-permute-start.18 = (bf16[17,16,128]{2,1,0:T(8,128)(2,1)S(1)}, bf16[17,16,128]{2,1,0:T(8,128)(2,1)S(1)}, u32[]{:S(2)}, u32[]{:S(2)}) collective-permute-start(bf16[17,16,128]{2,1,0:T(8,128)(2,1)S(1)} %get-tuple-element.93), channel_id=1, source_target_pairs={{0,4},{1,5},{2,6},{3,7},{4,0},{5,1},{6,2},{7,3},{8,12},{9,13},{10,... | collective-permute-start | bytes 208904 | tf_op jit(solution)/shard_map/ppermute | solution.py:418
  39.9 5.1 %collective-permute-start.19 = (bf16[1,17,16,128]{3,2,1,0:T(8,128)(2,1)S(1)}, bf16[1,17,16,128]{3,2,1,0:T(8,128)(2,1)S(1)}, u32[]{:S(2)}, u32[]{:S(2)}) collective-permute-start(bf16[1,17,16,128]{3,2,1,0:T(8,128)(2,1)S(1)} %bitcast.12), channel_id=1, source_target_pairs={{0,2},{1,3},{2,0},{3,1},{4,6},{5,7},{6,4},{7,5},{8,10},{9,11},{10,... | collective-permute-start | bytes 208904 | tf_op jit(solution)/shard_map/ppermute | solution.py:418
  43.8 5.5 %collective-permute-start.20 = (bf16[2,17,16,128]{3,2,1,0:T(8,128)(2,1)S(1)}, bf16[2,17,16,128]{3,2,1,0:T(8,128)(2,1)S(1)}, u32[]{:S(2)}, u32[]{:S(2)}) collective-permute-start(bf16[2,17,16,128]{3,2,1,0:T(8,128)(2,1)S(1)} %pad_maximum_fusion.2), channel_id=1, source_target_pairs={{0,2},{1,3},{2,0},{3,1},{4,6},{5,7},{6,4},{7,5},{8,10},{9,11},{10,... | collective-permute-start | bytes 417800 | tf_op jit(solution)/shard_map/ppermute | solution.py:418
  52.5 5.9 %collective-permute-start.23 = (bf16[17,16,128]{2,1,0:T(8,128)(2,1)S(1)}, bf16[17,16,128]{2,1,0:T(8,128)(2,1)S(1)}, u32[]{:S(2)}, u32[]{:S(2)}) collective-permute-start(bf16[17,16,128]{2,1,0:T(8,128)(2,1)S(1)} %get-tuple-element.109), channel_id=1, source_target_pairs={{0,2},{1,3},{2,0},{3,1},{4,6},{5,7},{6,4},{7,5},{8,10},{9,11},{10,... | collective-permute-start | bytes 208904 | tf_op jit(solution)/shard_map/ppermute | solution.py:418
  53.5 7.6 %collective-permute-start.27 = (bf16[17,16,128]{2,1,0:T(8,128)(2,1)S(1)}, bf16[17,16,128]{2,1,0:T(8,128)(2,1)S(1)}, u32[]{:S(2)}, u32[]{:S(2)}) collective-permute-start(bf16[17,16,128]{2,1,0:T(8,128)(2,1)S(1)} %get-tuple-element.120), channel_id=1, source_target_pairs={{0,8},{1,9},{2,10},{3,11},{4,12},{5,13},{6,14},{7,15},{8,0},{9,1},... | collective-permute-start | bytes 208904 | tf_op jit(solution)/shard_map/ppermute | solution.py:418
  55.1 6.1 %collective-permute-start.28 = (bf16[17,16,128]{2,1,0:T(8,128)(2,1)S(1)}, bf16[17,16,128]{2,1,0:T(8,128)(2,1)S(1)}, u32[]{:S(2)}, u32[]{:S(2)}) collective-permute-start(bf16[17,16,128]{2,1,0:T(8,128)(2,1)S(1)} %get-tuple-element.121), channel_id=1, source_target_pairs={{0,4},{1,5},{2,6},{3,7},{4,0},{5,1},{6,2},{7,3},{8,12},{9,13},{10,... | collective-permute-start | bytes 208904 | tf_op jit(solution)/shard_map/ppermute | solution.py:418
  55.9 8.9 %collective-permute-start.24 = (bf16[17,16,128]{2,1,0:T(8,128)(2,1)S(1)}, bf16[17,16,128]{2,1,0:T(8,128)(2,1)S(1)}, u32[]{:S(2)}, u32[]{:S(2)}) collective-permute-start(bf16[17,16,128]{2,1,0:T(8,128)(2,1)S(1)} %get-tuple-element.111), channel_id=1, source_target_pairs={{0,8},{1,9},{2,10},{3,11},{4,12},{5,13},{6,14},{7,15},{8,0},{9,1},... | collective-permute-start | bytes 208904 | tf_op jit(solution)/shard_map/ppermute | solution.py:418
  57.3 7.5 %collective-permute-start.25 = (bf16[17,16,128]{2,1,0:T(8,128)(2,1)S(1)}, bf16[17,16,128]{2,1,0:T(8,128)(2,1)S(1)}, u32[]{:S(2)}, u32[]{:S(2)}) collective-permute-start(bf16[17,16,128]{2,1,0:T(8,128)(2,1)S(1)} %get-tuple-element.112), channel_id=1, source_target_pairs={{0,4},{1,5},{2,6},{3,7},{4,0},{5,1},{6,2},{7,3},{8,12},{9,13},{10,... | collective-permute-start | bytes 208904 | tf_op jit(solution)/shard_map/ppermute | solution.py:418
  58.6 6.6 %collective-permute-start.26 = (bf16[17,16,128]{2,1,0:T(8,128)(2,1)S(1)}, bf16[17,16,128]{2,1,0:T(8,128)(2,1)S(1)}, u32[]{:S(2)}, u32[]{:S(2)}) collective-permute-start(bf16[17,16,128]{2,1,0:T(8,128)(2,1)S(1)} %get-tuple-element.115), channel_id=1, source_target_pairs={{0,12},{1,13},{2,14},{3,15},{4,8},{5,9},{6,10},{7,11},{8,4},{9,5},... | collective-permute-start | bytes 208904 | tf_op jit(solution)/shard_map/ppermute | solution.py:418
  (6 other events, 16.8 us)

commit v11 on v10

--- a/solution.py
+++ b/solution.py
@@ -380,8 +380,10 @@
     direction = direction_ref[...]
     applied, pair = gathered_product(keep_ref, pair_ref, got, direction, nugget_ref[...], rhs, chunks)
     step = right_divide(pair, gram_ref[...], rhs)
-    out_solution_ref[...] = solution_ref[...] + left_multiply(step, direction, rhs)
-    out_residual_ref[...] = residual_ref[...] - left_multiply(step, applied, rhs)
+    width = direction.shape[1]
+    update = left_multiply(step, jnp.concatenate([direction, applied], axis=1), rhs)
+    out_solution_ref[...] = solution_ref[...] + update[:, :width]
+    out_residual_ref[...] = residual_ref[...] - update[:, width:]
 
 
 def call(kernel, outs, *args, far=(), scalars=(), fixed=(), scratch=(), micros=0.0):

time: 67.5 us -> 67.5 us (level)
  no operation moved by 1% of the time
where the time goes in v11:
time: 67.5 us; the launch traced here: 67.4 us
  starting transfers between devices  34.5 us (51%)
  waiting for transfers between devices  16.8 us (25%)
  Pallas kernels  14.5 us (21%)
  between operations  1.42 us (2%)
    ppermute x30, starting transfers between devices, swap(): return lax.ppermute(array, 'row', [(i, i ^ offset) for i in range(devices)])  34.5 us
    ppermute x30, waiting for transfers between devices, swap(): return lax.ppermute(array, 'row', [(i, i ^ offset) for i in range(devices)])  16.8 us
    pallas_call x20, Pallas kernels, call(): pl.pallas_call(kernel, out_shape=[pltpu.VMEM(shape, dtype) if i in fixed...  14.5 us
  transfers between devices with their start and end apart: 30, of which 16 were waited for; matrix products, arithmetic and copies ran while one was open for 0% of the time, Pallas kernels for 11%

profile of v11, /device:TPU:0, one launch (start us, length us, event | category | flops | bytes accessed | tf_op | source)
XLA Modules:
  0.0 67.4 jit_solution(17660233263235956177)
XLA Ops:
  2.1 4.7 %collective-permute-start = (bf16[16,16,128]{2,1,0:T(8,128)(2,1)S(1)}, bf16[16,16,128]{2,1,0:T(8,128)(2,1)S(1)}, u32[]{:S(2)}, u32[]{:S(2)}) collective-permute-start(bf16[16,16,128]{2,1,0:T(8,128)(2,1)S(1)} %get-tuple-element.62), channel_id=1, source_target_pairs={{0,12},{1,13},{2,14},{3,15},{4,8},{5,9},{6,10},{7,11},{8,4},{9,5},... | collective-permute-start | bytes 196616 | tf_op jit(solution)/shard_map/ppermute | solution.py:420
  7.4 1.7 %collective-permute-start.5 = (bf16[1,16,16,128]{3,2,1,0:T(8,128)(2,1)S(1)}, bf16[1,16,16,128]{3,2,1,0:T(8,128)(2,1)S(1)}, u32[]{:S(2)}, u32[]{:S(2)}) collective-permute-start(bf16[1,16,16,128]{3,2,1,0:T(8,128)(2,1)S(1)} %bitcast.14), channel_id=1, source_target_pairs={{0,2},{1,3},{2,0},{3,1},{4,6},{5,7},{6,4},{7,5},{8,10},{9,11},{10,... | collective-permute-start | bytes 196616 | tf_op jit(solution)/shard_map/ppermute | solution.py:420
  9.7 2.3 %shard_map.78 = (f32[1,2048]{1,0:T(1,128)S(1)}, bf16[512,2048]{1,0:T(8,128)(2,1)S(1)}, bf16[512,2048]{1,0:T(8,128)(2,1)S(1)}, s32[8,512]{1,0:T(8,128)S(1)}, f32[...) custom-call(f32[16,2048]{1,0:T(8,128)S(1)} %get-tuple-element.63.own_ref.direction_ref.right_side_ref, s32[32]{0:T(128)} %bitcast.30, ...), custom_call_target="tpu_custom_call" | custom-call | tf_op jit(solution)/shard_map/pallas_call | solution.py:392
  12.8 1.6 %collective-permute-start.6 = (bf16[2,16,16,128]{3,2,1,0:T(8,128)(2,1)S(1)}, bf16[2,16,16,128]{3,2,1,0:T(8,128)(2,1)S(1)}, u32[]{:S(2)}, u32[]{:S(2)}) collective-permute-start(bf16[2,16,16,128]{3,2,1,0:T(8,128)(2,1)S(1)} %pad_maximum_fusion.3), channel_id=1, source_target_pairs={{0,2},{1,3},{2,0},{3,1},{4,6},{5,7},{6,4},{7,5},{8,10},{9,11},{10,... | collective-permute-start | bytes 393224 | tf_op jit(solution)/shard_map/ppermute | solution.py:420
  15.6 1.5 %shard_map.79 = (f32[16,1024]{1,0:T(8,128)S(1)}, s32[16,1024]{1,0:T(8,128)S(1)}, bf16[2048,1024]{1,0:T(8,128)(2,1)S(1)}) custom-call(bf16[4,16,16,128]{3,2,1,0:T(8,128)(2,1)S(1)} %pad_maximum_fusion.1.held_ref, f32[16,512]{1,0:T(8,128)S(1)} %get-tuple-element.64.near_ref, s32[8,512]{1,0:T(8,128)S(1)} %get-tuple-element.65.named_ref, ...), custom_call_target="tpu_custom_call" | custom-call | tf_op jit(solution)/shard_map/pallas_call | solution.py:392
  19.7 1.3 %collective-permute-done.8.got_ref = f32[16,1152]{1,0:T(8,128)S(1)} collective-permute-done((f32[16,1152]{1,0:T(8,128)S(1)}, f32[16,1152]{1,0:T(8,128)S(1)}, u32[]{:S(2)}, u32[]{:S(2)}) %collective-permute-start.8) | collective-permute-done | bytes 73760 | tf_op jit(solution)/shard_map/ppermute | solution.py:420
  22.3 1.6 %collective-permute-start.13 = (bf16[17,16,128]{2,1,0:T(8,128)(2,1)S(1)}, bf16[17,16,128]{2,1,0:T(8,128)(2,1)S(1)}, u32[]{:S(2)}, u32[]{:S(2)}) collective-permute-start(bf16[17,16,128]{2,1,0:T(8,128)(2,1)S(1)} %get-tuple-element.91), channel_id=1, source_target_pairs={{0,8},{1,9},{2,10},{3,11},{4,12},{5,13},{6,14},{7,15},{8,0},{9,1},... | collective-permute-start | bytes 208904 | tf_op jit(solution)/shard_map/ppermute | solution.py:420
  23.9 1.7 %collective-permute-start.14 = (bf16[17,16,128]{2,1,0:T(8,128)(2,1)S(1)}, bf16[17,16,128]{2,1,0:T(8,128)(2,1)S(1)}, u32[]{:S(2)}, u32[]{:S(2)}) collective-permute-start(bf16[17,16,128]{2,1,0:T(8,128)(2,1)S(1)} %get-tuple-element.92), channel_id=1, source_target_pairs={{0,4},{1,5},{2,6},{3,7},{4,0},{5,1},{6,2},{7,3},{8,12},{9,13},{10,... | collective-permute-start | bytes 208904 | tf_op jit(solution)/shard_map/ppermute | solution.py:420
  25.7 1.6 %collective-permute-start.11 = (bf16[17,16,128]{2,1,0:T(8,128)(2,1)S(1)}, bf16[17,16,128]{2,1,0:T(8,128)(2,1)S(1)}, u32[]{:S(2)}, u32[]{:S(2)}) collective-permute-start(bf16[17,16,128]{2,1,0:T(8,128)(2,1)S(1)} %get-tuple-element.84), channel_id=1, source_target_pairs={{0,4},{1,5},{2,6},{3,7},{4,0},{5,1},{6,2},{7,3},{8,12},{9,13},{10,... | collective-permute-start | bytes 208904 | tf_op jit(solution)/shard_map/ppermute | solution.py:420
  27.5 2.8 %collective-permute-start.12 = (bf16[17,16,128]{2,1,0:T(8,128)(2,1)S(1)}, bf16[17,16,128]{2,1,0:T(8,128)(2,1)S(1)}, u32[]{:S(2)}, u32[]{:S(2)}) collective-permute-start(bf16[17,16,128]{2,1,0:T(8,128)(2,1)S(1)} %get-tuple-element.87), channel_id=1, source_target_pairs={{0,12},{1,13},{2,14},{3,15},{4,8},{5,9},{6,10},{7,11},{8,4},{9,5},... | collective-permute-start | bytes 208904 | tf_op jit(solution)/shard_map/ppermute | solution.py:420
  30.9 1.2 %collective-permute-start.15 = (bf16[17,16,128]{2,1,0:T(8,128)(2,1)S(1)}, bf16[17,16,128]{2,1,0:T(8,128)(2,1)S(1)}, u32[]{:S(2)}, u32[]{:S(2)}) collective-permute-start(bf16[17,16,128]{2,1,0:T(8,128)(2,1)S(1)} %shard_map.85), channel_id=1, source_target_pairs={{0,2},{1,3},{2,0},{3,1},{4,6},{5,7},{6,4},{7,5},{8,10},{9,11},{10,... | collective-permute-start | bytes 208904 | tf_op jit(solution)/shard_map/ppermute | solution.py:420
  32.1 1.7 %collective-permute-done.10.rest_1_ = bf16[17,16,128]{2,1,0:T(8,128)(2,1)S(1)} collective-permute-done((bf16[17,16,128]{2,1,0:T(8,128)(2,1)S(1)}, bf16[17,16,128]{2,1,0:T(8,128)(2,1)S(1)}, u32[]{:S(2)}, u32[]{:S(2)}) %collective-permute-start.10) | collective-permute-done | bytes 69664 | tf_op jit(solution)/shard_map/ppermute | solution.py:420
  37.5 1.3 %collective-permute-start.16 = (bf16[17,16,128]{2,1,0:T(8,128)(2,1)S(1)}, bf16[17,16,128]{2,1,0:T(8,128)(2,1)S(1)}, u32[]{:S(2)}, u32[]{:S(2)}) collective-permute-start(bf16[17,16,128]{2,1,0:T(8,128)(2,1)S(1)} %get-tuple-element.93), channel_id=1, source_target_pairs={{0,12},{1,13},{2,14},{3,15},{4,8},{5,9},{6,10},{7,11},{8,4},{9,5},... | collective-permute-start | bytes 208904 | tf_op jit(solution)/shard_map/ppermute | solution.py:420
  41.0 1.5 %collective-permute-done.17 = bf16[17,16,128]{2,1,0:T(8,128)(2,1)S(1)} collective-permute-done((bf16[17,16,128]{2,1,0:T(8,128)(2,1)S(1)}, bf16[17,16,128]{2,1,0:T(8,128)(2,1)S(1)}, u32[]{:S(2)}, u32[]{:S(2)}) %collective-permute-start.17) | collective-permute-done | bytes 69664 | tf_op jit(solution)/shard_map/ppermute | solution.py:420
  43.8 1.2 %collective-permute-start.20 = (bf16[2,17,16,128]{3,2,1,0:T(8,128)(2,1)S(1)}, bf16[2,17,16,128]{3,2,1,0:T(8,128)(2,1)S(1)}, u32[]{:S(2)}, u32[]{:S(2)}) collective-permute-start(bf16[2,17,16,128]{3,2,1,0:T(8,128)(2,1)S(1)} %pad_maximum_fusion.2), channel_id=1, source_target_pairs={{0,2},{1,3},{2,0},{3,1},{4,6},{5,7},{6,4},{7,5},{8,10},{9,11},{10,... | collective-permute-start | bytes 417800 | tf_op jit(solution)/shard_map/ppermute | solution.py:420
  46.1 1.6 %shard_map.87 = (f32[16,1024]{1,0:T(8,128)S(1)}, f32[16,128]{1,0:T(8,128)S(1)}, f32[16,128]{1,0:T(8,128)S(1)}) custom-call(bf16[4,17,16,128]{3,2,1,0:T(8,128)(2,1)S(1)} %pad_maximum_fusion.held_ref, f32[16,2048]{1,0:T(8,128)S(1)} %get-tuple-element.94.own_ref.residual_ref, f32[16,2048]{1,0:T(8,128)S(1)} %get-tuple-element.63.own_ref.direction_ref.right_side_ref, ...), custom_call_target="tpu_custom_call" | custom-call | tf_op jit(solution)/shard_map/pallas_call | solution.py:392
  47.7 1.6 %collective-permute-done.21.rest_2_ = bf16[1,17,16,128]{3,2,1,0:T(8,128)(2,1)S(1)} collective-permute-done((bf16[1,17,16,128]{3,2,1,0:T(8,128)(2,1)S(1)}, bf16[1,17,16,128]{3,2,1,0:T(8,128)(2,1)S(1)}, u32[]{:S(2)}, u32[]{:S(2)}) %collective-permute-start.21) | collective-permute-done | bytes 69664 | tf_op jit(solution)/shard_map/ppermute | solution.py:420
  50.1 1.3 %collective-permute-done.22.got_ref = f32[16,1152]{1,0:T(8,128)S(1)} collective-permute-done((f32[16,1152]{1,0:T(8,128)S(1)}, f32[16,1152]{1,0:T(8,128)S(1)}, u32[]{:S(2)}, u32[]{:S(2)}) %collective-permute-start.22) | collective-permute-done | bytes 73760 | tf_op jit(solution)/shard_map/ppermute | solution.py:420
  51.4 1.2 %shard_map.89 = (f32[16,128]{1,0:T(8,128)S(1)}, f32[16,1024]{1,0:T(8,128)S(1)}, f32[16,128]{1,0:T(8,128)S(1)}, f32[16,128]{1,0:T(8,128)S(1)}, bf16[17,16,128]{2,...) custom-call(f32[16,1152]{1,0:T(8,128)S(1)} %shard_map.88.message_ref, ...), custom_call_target="tpu_custom_call" | custom-call | tf_op jit(solution)/shard_map/pallas_call | solution.py:392
  53.5 1.6 %collective-permute-start.27 = (bf16[17,16,128]{2,1,0:T(8,128)(2,1)S(1)}, bf16[17,16,128]{2,1,0:T(8,128)(2,1)S(1)}, u32[]{:S(2)}, u32[]{:S(2)}) collective-permute-start(bf16[17,16,128]{2,1,0:T(8,128)(2,1)S(1)} %get-tuple-element.120), channel_id=1, source_target_pairs={{0,8},{1,9},{2,10},{3,11},{4,12},{5,13},{6,14},{7,15},{8,0},{9,1},... | collective-permute-start | bytes 208904 | tf_op jit(solution)/shard_map/ppermute | solution.py:420
  55.9 1.5 %collective-permute-start.24 = (bf16[17,16,128]{2,1,0:T(8,128)(2,1)S(1)}, bf16[17,16,128]{2,1,0:T(8,128)(2,1)S(1)}, u32[]{:S(2)}, u32[]{:S(2)}) collective-permute-start(bf16[17,16,128]{2,1,0:T(8,128)(2,1)S(1)} %get-tuple-element.111), channel_id=1, source_target_pairs={{0,8},{1,9},{2,10},{3,11},{4,12},{5,13},{6,14},{7,15},{8,0},{9,1},... | collective-permute-start | bytes 208904 | tf_op jit(solution)/shard_map/ppermute | solution.py:420
  58.6 1.8 %collective-permute-start.26 = (bf16[17,16,128]{2,1,0:T(8,128)(2,1)S(1)}, bf16[17,16,128]{2,1,0:T(8,128)(2,1)S(1)}, u32[]{:S(2)}, u32[]{:S(2)}) collective-permute-start(bf16[17,16,128]{2,1,0:T(8,128)(2,1)S(1)} %get-tuple-element.115), channel_id=1, source_target_pairs={{0,12},{1,13},{2,14},{3,15},{4,8},{5,9},{6,10},{7,11},{8,4},{9,5},... | collective-permute-start | bytes 208904 | tf_op jit(solution)/shard_map/ppermute | solution.py:420
  63.0 1.8 %collective-permute-done.24.rest_1_ = bf16[17,16,128]{2,1,0:T(8,128)(2,1)S(1)} collective-permute-done((bf16[17,16,128]{2,1,0:T(8,128)(2,1)S(1)}, bf16[17,16,128]{2,1,0:T(8,128)(2,1)S(1)}, u32[]{:S(2)}, u32[]{:S(2)}) %collective-permute-start.24) | collective-permute-done | bytes 69664 | tf_op jit(solution)/shard_map/ppermute | solution.py:420
  65.7 1.6 %shard_map.96 = (f32[16,2048]{1,0:T(8,128)}, f32[16,2048]{1,0:T(8,128)}) custom-call(f32[16,2048]{1,0:T(8,128)S(1)} %shard_map.90.direction_ref, f32[1,2048]{1,0:T(1,128)S(1)} %get-tuple-element.70.nugget_ref, f32[16,16,128]{2,1,0:T(8,128)S(1)} %get-tuple-element.116.keep_ref, f32[16,128]{1,0:T(8,128)S(1)} %get-tuple-element.117.pair_ref, ...), custom_call_target="tpu_custom_call" | custom-call | tf_op jit(solution)/shard_map/pallas_call | solution.py:392
  (60 shorter events, 24.3 us)
Async XLA Ops:
  1.6 14.1 %collective-permute-start.4 = (bf16[512,2048]{1,0:T(8,128)(2,1)}, bf16[512,2048]{1,0:T(8,128)(2,1)S(1)}, u32[]{:S(2)}, u32[]{:S(2)}) collective-permute-start(bf16[512,2048]{1,0:T(8,128)(2,1)} %bitcast.17), channel_id=1, source_target_pairs={{0,1},{1,0},{2,3},{3,2},{4,5},{5,4},{6,7},{7,6},{8,9},{9,8},{10,11... | collective-permute-start | bytes 6291464 | tf_op jit(solution)/shard_map/ppermute | solution.py:420
  2.1 10.0 %collective-permute-start = (bf16[16,16,128]{2,1,0:T(8,128)(2,1)S(1)}, bf16[16,16,128]{2,1,0:T(8,128)(2,1)S(1)}, u32[]{:S(2)}, u32[]{:S(2)}) collective-permute-start(bf16[16,16,128]{2,1,0:T(8,128)(2,1)S(1)} %get-tuple-element.62), channel_id=1, source_target_pairs={{0,12},{1,13},{2,14},{3,15},{4,8},{5,9},{6,10},{7,11},{8,4},{9,5},... | collective-permute-start | bytes 196616 | tf_op jit(solution)/shard_map/ppermute | solution.py:420
  6.8 6.1 %collective-permute-start.1 = (bf16[16,16,128]{2,1,0:T(8,128)(2,1)S(1)}, bf16[16,16,128]{2,1,0:T(8,128)(2,1)S(1)}, u32[]{:S(2)}, u32[]{:S(2)}) collective-permute-start(bf16[16,16,128]{2,1,0:T(8,128)(2,1)S(1)} %get-tuple-element.62), channel_id=1, source_target_pairs={{0,8},{1,9},{2,10},{3,11},{4,12},{5,13},{6,14},{7,15},{8,0},{9,1},... | collective-permute-start | bytes 196616 | tf_op jit(solution)/shard_map/ppermute | solution.py:420
  6.8 7.7 %collective-permute-start.2 = (bf16[16,16,128]{2,1,0:T(8,128)(2,1)S(1)}, bf16[16,16,128]{2,1,0:T(8,128)(2,1)S(1)}, u32[]{:S(2)}, u32[]{:S(2)}) collective-permute-start(bf16[16,16,128]{2,1,0:T(8,128)(2,1)S(1)} %get-tuple-element.62), channel_id=1, source_target_pairs={{0,4},{1,5},{2,6},{3,7},{4,0},{5,1},{6,2},{7,3},{8,12},{9,13},{10,... | collective-permute-start | bytes 196616 | tf_op jit(solution)/shard_map/ppermute | solution.py:420
  7.4 7.0 %collective-permute-start.5 = (bf16[1,16,16,128]{3,2,1,0:T(8,128)(2,1)S(1)}, bf16[1,16,16,128]{3,2,1,0:T(8,128)(2,1)S(1)}, u32[]{:S(2)}, u32[]{:S(2)}) collective-permute-start(bf16[1,16,16,128]{3,2,1,0:T(8,128)(2,1)S(1)} %bitcast.14), channel_id=1, source_target_pairs={{0,2},{1,3},{2,0},{3,1},{4,6},{5,7},{6,4},{7,5},{8,10},{9,11},{10,... | collective-permute-start | bytes 196616 | tf_op jit(solution)/shard_map/ppermute | solution.py:420
  12.8 5.1 %collective-permute-start.6 = (bf16[2,16,16,128]{3,2,1,0:T(8,128)(2,1)S(1)}, bf16[2,16,16,128]{3,2,1,0:T(8,128)(2,1)S(1)}, u32[]{:S(2)}, u32[]{:S(2)}) collective-permute-start(bf16[2,16,16,128]{3,2,1,0:T(8,128)(2,1)S(1)} %pad_maximum_fusion.3), channel_id=1, source_target_pairs={{0,2},{1,3},{2,0},{3,1},{4,6},{5,7},{6,4},{7,5},{8,10},{9,11},{10,... | collective-permute-start | bytes 393224 | tf_op jit(solution)/shard_map/ppermute | solution.py:420
  14.4 4.5 %collective-permute-start.7 = (bf16[1,16,16,128]{3,2,1,0:T(8,128)(2,1)S(1)}, bf16[1,16,16,128]{3,2,1,0:T(8,128)(2,1)S(1)}, u32[]{:S(2)}, u32[]{:S(2)}) collective-permute-start(bf16[1,16,16,128]{3,2,1,0:T(8,128)(2,1)S(1)} %collective-permute-done.5.rest_0_), channel_id=1, source_target_pairs={{0,4},{1,5},{2,6},{3,7},{4,0},{5,1},{6,2},{7,3},{8,12},{9,13},{10,... | collective-permute-start | bytes 196616 | tf_op jit(solution)/shard_map/ppermute | solution.py:420
  21.7 5.6 %collective-permute-start.9 = (bf16[17,16,128]{2,1,0:T(8,128)(2,1)S(1)}, bf16[17,16,128]{2,1,0:T(8,128)(2,1)S(1)}, u32[]{:S(2)}, u32[]{:S(2)}) collective-permute-start(bf16[17,16,128]{2,1,0:T(8,128)(2,1)S(1)} %get-tuple-element.81), channel_id=1, source_target_pairs={{0,2},{1,3},{2,0},{3,1},{4,6},{5,7},{6,4},{7,5},{8,10},{9,11},{10,... | collective-permute-start | bytes 208904 | tf_op jit(solution)/shard_map/ppermute | solution.py:420
  22.3 7.9 %collective-permute-start.13 = (bf16[17,16,128]{2,1,0:T(8,128)(2,1)S(1)}, bf16[17,16,128]{2,1,0:T(8,128)(2,1)S(1)}, u32[]{:S(2)}, u32[]{:S(2)}) collective-permute-start(bf16[17,16,128]{2,1,0:T(8,128)(2,1)S(1)} %get-tuple-element.91), channel_id=1, source_target_pairs={{0,8},{1,9},{2,10},{3,11},{4,12},{5,13},{6,14},{7,15},{8,0},{9,1},... | collective-permute-start | bytes 208904 | tf_op jit(solution)/shard_map/ppermute | solution.py:420
  23.9 6.8 %collective-permute-start.14 = (bf16[17,16,128]{2,1,0:T(8,128)(2,1)S(1)}, bf16[17,16,128]{2,1,0:T(8,128)(2,1)S(1)}, u32[]{:S(2)}, u32[]{:S(2)}) collective-permute-start(bf16[17,16,128]{2,1,0:T(8,128)(2,1)S(1)} %get-tuple-element.92), channel_id=1, source_target_pairs={{0,4},{1,5},{2,6},{3,7},{4,0},{5,1},{6,2},{7,3},{8,12},{9,13},{10,... | collective-permute-start | bytes 208904 | tf_op jit(solution)/shard_map/ppermute | solution.py:420
  25.7 8.1 %collective-permute-start.10 = (bf16[17,16,128]{2,1,0:T(8,128)(2,1)S(1)}, bf16[17,16,128]{2,1,0:T(8,128)(2,1)S(1)}, u32[]{:S(2)}, u32[]{:S(2)}) collective-permute-start(bf16[17,16,128]{2,1,0:T(8,128)(2,1)S(1)} %get-tuple-element.83), channel_id=1, source_target_pairs={{0,8},{1,9},{2,10},{3,11},{4,12},{5,13},{6,14},{7,15},{8,0},{9,1},... | collective-permute-start | bytes 208904 | tf_op jit(solution)/shard_map/ppermute | solution.py:420
  25.7 8.1 %collective-permute-start.11 = (bf16[17,16,128]{2,1,0:T(8,128)(2,1)S(1)}, bf16[17,16,128]{2,1,0:T(8,128)(2,1)S(1)}, u32[]{:S(2)}, u32[]{:S(2)}) collective-permute-start(bf16[17,16,128]{2,1,0:T(8,128)(2,1)S(1)} %get-tuple-element.84), channel_id=1, source_target_pairs={{0,4},{1,5},{2,6},{3,7},{4,0},{5,1},{6,2},{7,3},{8,12},{9,13},{10,... | collective-permute-start | bytes 208904 | tf_op jit(solution)/shard_map/ppermute | solution.py:420
  27.5 6.8 %collective-permute-start.12 = (bf16[17,16,128]{2,1,0:T(8,128)(2,1)S(1)}, bf16[17,16,128]{2,1,0:T(8,128)(2,1)S(1)}, u32[]{:S(2)}, u32[]{:S(2)}) collective-permute-start(bf16[17,16,128]{2,1,0:T(8,128)(2,1)S(1)} %get-tuple-element.87), channel_id=1, source_target_pairs={{0,12},{1,13},{2,14},{3,15},{4,8},{5,9},{6,10},{7,11},{8,4},{9,5},... | collective-permute-start | bytes 208904 | tf_op jit(solution)/shard_map/ppermute | solution.py:420
  36.4 6.2 %collective-permute-start.17 = (bf16[17,16,128]{2,1,0:T(8,128)(2,1)S(1)}, bf16[17,16,128]{2,1,0:T(8,128)(2,1)S(1)}, u32[]{:S(2)}, u32[]{:S(2)}) collective-permute-start(bf16[17,16,128]{2,1,0:T(8,128)(2,1)S(1)} %get-tuple-element.93), channel_id=1, source_target_pairs={{0,8},{1,9},{2,10},{3,11},{4,12},{5,13},{6,14},{7,15},{8,0},{9,1},... | collective-permute-start | bytes 208904 | tf_op jit(solution)/shard_map/ppermute | solution.py:420
  37.5 6.3 %collective-permute-start.16 = (bf16[17,16,128]{2,1,0:T(8,128)(2,1)S(1)}, bf16[17,16,128]{2,1,0:T(8,128)(2,1)S(1)}, u32[]{:S(2)}, u32[]{:S(2)}) collective-permute-start(bf16[17,16,128]{2,1,0:T(8,128)(2,1)S(1)} %get-tuple-element.93), channel_id=1, source_target_pairs={{0,12},{1,13},{2,14},{3,15},{4,8},{5,9},{6,10},{7,11},{8,4},{9,5},... | collective-permute-start | bytes 208904 | tf_op jit(solution)/shard_map/ppermute | solution.py:420
  38.8 7.2 %collective-permute-start.18 = (bf16[17,16,128]{2,1,0:T(8,128)(2,1)S(1)}, bf16[17,16,128]{2,1,0:T(8,128)(2,1)S(1)}, u32[]{:S(2)}, u32[]{:S(2)}) collective-permute-start(bf16[17,16,128]{2,1,0:T(8,128)(2,1)S(1)} %get-tuple-element.93), channel_id=1, source_target_pairs={{0,4},{1,5},{2,6},{3,7},{4,0},{5,1},{6,2},{7,3},{8,12},{9,13},{10,... | collective-permute-start | bytes 208904 | tf_op jit(solution)/shard_map/ppermute | solution.py:420
  39.9 5.1 %collective-permute-start.19 = (bf16[1,17,16,128]{3,2,1,0:T(8,128)(2,1)S(1)}, bf16[1,17,16,128]{3,2,1,0:T(8,128)(2,1)S(1)}, u32[]{:S(2)}, u32[]{:S(2)}) collective-permute-start(bf16[1,17,16,128]{3,2,1,0:T(8,128)(2,1)S(1)} %bitcast.12), channel_id=1, source_target_pairs={{0,2},{1,3},{2,0},{3,1},{4,6},{5,7},{6,4},{7,5},{8,10},{9,11},{10,... | collective-permute-start | bytes 208904 | tf_op jit(solution)/shard_map/ppermute | solution.py:420
  43.8 5.5 %collective-permute-start.20 = (bf16[2,17,16,128]{3,2,1,0:T(8,128)(2,1)S(1)}, bf16[2,17,16,128]{3,2,1,0:T(8,128)(2,1)S(1)}, u32[]{:S(2)}, u32[]{:S(2)}) collective-permute-start(bf16[2,17,16,128]{3,2,1,0:T(8,128)(2,1)S(1)} %pad_maximum_fusion.2), channel_id=1, source_target_pairs={{0,2},{1,3},{2,0},{3,1},{4,6},{5,7},{6,4},{7,5},{8,10},{9,11},{10,... | collective-permute-start | bytes 417800 | tf_op jit(solution)/shard_map/ppermute | solution.py:420
  52.5 5.9 %collective-permute-start.23 = (bf16[17,16,128]{2,1,0:T(8,128)(2,1)S(1)}, bf16[17,16,128]{2,1,0:T(8,128)(2,1)S(1)}, u32[]{:S(2)}, u32[]{:S(2)}) collective-permute-start(bf16[17,16,128]{2,1,0:T(8,128)(2,1)S(1)} %get-tuple-element.109), channel_id=1, source_target_pairs={{0,2},{1,3},{2,0},{3,1},{4,6},{5,7},{6,4},{7,5},{8,10},{9,11},{10,... | collective-permute-start | bytes 208904 | tf_op jit(solution)/shard_map/ppermute | solution.py:420
  53.5 7.6 %collective-permute-start.27 = (bf16[17,16,128]{2,1,0:T(8,128)(2,1)S(1)}, bf16[17,16,128]{2,1,0:T(8,128)(2,1)S(1)}, u32[]{:S(2)}, u32[]{:S(2)}) collective-permute-start(bf16[17,16,128]{2,1,0:T(8,128)(2,1)S(1)} %get-tuple-element.120), channel_id=1, source_target_pairs={{0,8},{1,9},{2,10},{3,11},{4,12},{5,13},{6,14},{7,15},{8,0},{9,1},... | collective-permute-start | bytes 208904 | tf_op jit(solution)/shard_map/ppermute | solution.py:420
  55.1 6.1 %collective-permute-start.28 = (bf16[17,16,128]{2,1,0:T(8,128)(2,1)S(1)}, bf16[17,16,128]{2,1,0:T(8,128)(2,1)S(1)}, u32[]{:S(2)}, u32[]{:S(2)}) collective-permute-start(bf16[17,16,128]{2,1,0:T(8,128)(2,1)S(1)} %get-tuple-element.121), channel_id=1, source_target_pairs={{0,4},{1,5},{2,6},{3,7},{4,0},{5,1},{6,2},{7,3},{8,12},{9,13},{10,... | collective-permute-start | bytes 208904 | tf_op jit(solution)/shard_map/ppermute | solution.py:420
  55.9 8.9 %collective-permute-start.24 = (bf16[17,16,128]{2,1,0:T(8,128)(2,1)S(1)}, bf16[17,16,128]{2,1,0:T(8,128)(2,1)S(1)}, u32[]{:S(2)}, u32[]{:S(2)}) collective-permute-start(bf16[17,16,128]{2,1,0:T(8,128)(2,1)S(1)} %get-tuple-element.111), channel_id=1, source_target_pairs={{0,8},{1,9},{2,10},{3,11},{4,12},{5,13},{6,14},{7,15},{8,0},{9,1},... | collective-permute-start | bytes 208904 | tf_op jit(solution)/shard_map/ppermute | solution.py:420
  57.3 7.5 %collective-permute-start.25 = (bf16[17,16,128]{2,1,0:T(8,128)(2,1)S(1)}, bf16[17,16,128]{2,1,0:T(8,128)(2,1)S(1)}, u32[]{:S(2)}, u32[]{:S(2)}) collective-permute-start(bf16[17,16,128]{2,1,0:T(8,128)(2,1)S(1)} %get-tuple-element.112), channel_id=1, source_target_pairs={{0,4},{1,5},{2,6},{3,7},{4,0},{5,1},{6,2},{7,3},{8,12},{9,13},{10,... | collective-permute-start | bytes 208904 | tf_op jit(solution)/shard_map/ppermute | solution.py:420
  58.6 6.6 %collective-permute-start.26 = (bf16[17,16,128]{2,1,0:T(8,128)(2,1)S(1)}, bf16[17,16,128]{2,1,0:T(8,128)(2,1)S(1)}, u32[]{:S(2)}, u32[]{:S(2)}) collective-permute-start(bf16[17,16,128]{2,1,0:T(8,128)(2,1)S(1)} %get-tuple-element.115), channel_id=1, source_target_pairs={{0,12},{1,13},{2,14},{3,15},{4,8},{5,9},{6,10},{7,11},{8,4},{9,5},... | collective-permute-start | bytes 208904 | tf_op jit(solution)/shard_map/ppermute | solution.py:420
  (6 other events, 16.8 us)
